TPU v7x, 32 devices: a whole 2x2x4 slice. The times are simulated.
32 devices in a mesh: rep: 8 (over z, core), shard: 4 (over y, x).
Axes of the slice: x: 2, y: 2, z: 4, core: 2. Of those that a mesh axis runs over, the one named last changes fastest.
Arguments:
- tokens: bfloat16 [32, 256, 1024], P(('rep', 'shard')), may hold values from -6 to 6
- cotangent: bfloat16 [32, 256, 1024], P(('rep', 'shard')), may hold values from -6 to 6
- lengths: int32 [8, 4], P('rep'), may hold values from 1 to 256, 768 in all within a row
- sequence_deal: int32 [8, 4], P('rep'), may hold values from 0 to 3, each once within a row
- routes: int32 [32, 256, 2], P(('rep', 'shard')), may hold values from 0 to 3, all different within a row
- fill_order: int32 [32, 256], P(('rep', 'shard')), may hold values from 0 to 255, each once within a row
- norm_attn: bfloat16 [1024], P('shard'), may hold values from 0.5 to 1.5
- w_query: bfloat16 [1024, 1024], P('shard'), may hold values from -0.1875 to 0.1875
- w_key: bfloat16 [1024, 1024], P('shard'), may hold values from -0.1875 to 0.1875
- w_value: bfloat16 [1024, 1024], P('shard'), may hold values from -0.1875 to 0.1875
- w_out: bfloat16 [1024, 1024], P('shard'), may hold values from -0.75 to 0.75
- rel_bias: bfloat16 [32, 16], P('shard'), may hold values from -3 to 3
- norm_ffn: bfloat16 [1024], P('shard'), may hold values from 0.5 to 1.5
- w_router: bfloat16 [1024, 4], P('shard'), may hold values from -0.1875 to 0.1875
- w_gate: bfloat16 [4, 1024, 2816], P(None, None, 'shard'), may hold values from -0.1875 to 0.1875
- w_up: bfloat16 [4, 1024, 2816], P(None, None, 'shard'), may hold values from -0.1875 to 0.1875
- w_down: bfloat16 [4, 2816, 1024], P(None, 'shard'), may hold values from -0.4375 to 0.4375
Outputs:
- output: bfloat16 [32, 256, 1024], P(('rep', 'shard'))
- grad_tokens: bfloat16 [32, 256, 1024], P(('rep', 'shard'))
- grad_norm_attn: float32 [1024], P('shard')
- grad_query: float32 [1024, 1024], P('shard')
- grad_key: float32 [1024, 1024], P('shard')
- grad_value: float32 [1024, 1024], P('shard')
- grad_out: float32 [1024, 1024], P('shard')
- grad_bias: float32 [32, 16], P('shard')
- grad_norm_ffn: float32 [1024], P('shard')
- grad_router: float32 [1024, 4], P('shard')
- grad_gate: float32 [4, 1024, 2816], P(None, None, 'shard')
- grad_up: float32 [4, 1024, 2816], P(None, None, 'shard')
- grad_down: float32 [4, 2816, 1024], P(None, 'shard')
Inputs may be any that keep to these rules, and one draw needn't show every extreme that they name: Each row holds the lengths of the 4 sequences of a replica group; they sum to 768 and the largest is 256; positions at or past a length are padding. `sequence_deal`: each row is a permutation of 0 to 3. `routes`: a token's two experts differ; every expert is named somewhere. `fill_order`: each row is a permutation of 0 to 255.
All inputs are finite; a program needn't handle non-finite values.
Results may differ from a plain program's by a relative error of at most 0.022.
Values may be sent and summed in bfloat16 or wider, within the bound.
No kernel may reach another device: no remote copies, remote signals or barrier semaphores. Data moves between devices by JAX's collectives and lax.ppermute only.
A program may use at most 448 MiB of HBM per device.

v0:
```python
import math

import jax
import jax.numpy as jnp
from jax import lax
from jax.sharding import PartitionSpec as P

HEADS = 16
HEAD_DIM = 64
EXPERTS = 4
BUCKETS = 32
CAP = 144


eps = 1e-06
bucket_edges = [int(math.ceil(16.0 * 8.0 ** (level / 16.0))) for level in range(1, 16)]


def dot_plain(left_side, right_side):
    return jnp.dot(left_side, right_side, preferred_element_type=jnp.float32)


def dot_rows(left_side, right_side):
    return lax.dot_general(
        left_side, right_side, (((0,), (0,)), ((), ())), preferred_element_type=jnp.float32
    )


def dot_cols(left_side, right_side):
    return lax.dot_general(
        left_side, right_side, (((1,), (1,)), ((), ())), preferred_element_type=jnp.float32
    )


def rms_forward(values, gain_row):
    scale = lax.rsqrt(jnp.mean(values * values, axis=-1, keepdims=True) + eps)
    return (values * scale * gain_row, scale)


def rms_backward(values, scale, gain_row, upward):
    grad_gain = jnp.sum(upward * values * scale, axis=0)
    weighted = upward * gain_row
    grad_values = scale * weighted - values * scale * scale * scale * jnp.mean(
        values * weighted, axis=-1, keepdims=True
    )
    return (grad_values, grad_gain)


def bucket_onehot(slot_count):
    query_pos = lax.broadcasted_iota(jnp.int32, (slot_count, slot_count), 0)
    key_pos = lax.broadcasted_iota(jnp.int32, (slot_count, slot_count), 1)
    distance = jnp.maximum(query_pos - key_pos, 0)
    bucket = jnp.minimum(distance, 16)
    for border in bucket_edges:
        bucket = bucket + (distance >= border).astype(jnp.int32)
    labels = lax.broadcasted_iota(jnp.int32, (BUCKETS, 1), 0)
    onehot = (bucket.reshape(1, -1) == labels).astype(jnp.bfloat16)
    return (onehot, query_pos, key_pos)


def slot_plan(seq_routes, seq_order, length):
    slot_count = seq_order.shape[0]
    positions = jnp.arange(slot_count, dtype=jnp.int32)
    valid_rows = positions < length
    ranked_token = jnp.zeros((slot_count,), jnp.int32).at[seq_order].set(positions)
    ranked_routes = seq_routes[ranked_token]
    ranked_valid = valid_rows[ranked_token]
    picked = jnp.concatenate([ranked_routes[:, 0], ranked_routes[:, 1]])
    picked_valid = jnp.concatenate([ranked_valid, ranked_valid])
    expert_ids = jnp.arange(EXPERTS, dtype=jnp.int32)
    expert_hits = ((picked[:, None] == expert_ids[None, :]) & picked_valid[:, None]).astype(
        jnp.int32
    )
    running = jnp.cumsum(expert_hits, axis=0)
    place_rank = jnp.sum(running * expert_hits, axis=1) - 1
    kept_pair = picked_valid & (place_rank < CAP)
    flat_slot = jnp.where(kept_pair, picked * CAP + place_rank, EXPERTS * CAP)
    owner_token = jnp.concatenate([ranked_token, ranked_token])
    branch = jnp.concatenate(
        [jnp.zeros((slot_count,), jnp.int32), jnp.ones((slot_count,), jnp.int32)]
    )
    slot_token = (
        jnp.full((EXPERTS * CAP + 1,), slot_count, jnp.int32)
        .at[flat_slot]
        .set(owner_token)[: EXPERTS * CAP]
    )
    slot_choice = (
        jnp.zeros((EXPERTS * CAP + 1,), jnp.int32).at[flat_slot].set(branch)[: EXPERTS * CAP]
    )
    token_slot = jnp.zeros((slot_count, 2), jnp.int32).at[owner_token, branch].set(flat_slot)
    return (slot_token, slot_choice, token_slot)


def head_scores(query_head, key_head, bias_column, onehot, allowed):
    slot_count = query_head.shape[0]
    bias_full = dot_rows(bias_column, onehot).reshape(slot_count, slot_count)
    return jnp.where(allowed, dot_cols(query_head, key_head) * 0.125 + bias_full, -1000000000.0)


def attention_forward(queries, keys_in, values_in, bias_table, onehot, allowed):
    slot_count = queries.shape[0]

    def head_step(head_index, carry):
        context, log_totals = carry
        start = head_index * HEAD_DIM
        query_head = lax.dynamic_slice_in_dim(queries, start, HEAD_DIM, 1)
        key_head = lax.dynamic_slice_in_dim(keys_in, start, HEAD_DIM, 1)
        value_head = lax.dynamic_slice_in_dim(values_in, start, HEAD_DIM, 1)
        bias_column = lax.dynamic_slice_in_dim(bias_table, head_index, 1, 1)
        scores = head_scores(query_head, key_head, bias_column, onehot, allowed)
        row_max = jnp.max(scores, axis=-1, keepdims=True)
        log_total = row_max + jnp.log(jnp.sum(jnp.exp(scores - row_max), axis=-1, keepdims=True))
        attention = jnp.exp(scores - log_total).astype(jnp.bfloat16)
        context_head = dot_plain(attention, value_head).astype(jnp.bfloat16)
        context = lax.dynamic_update_slice_in_dim(context, context_head, start, 1)
        log_totals = lax.dynamic_update_slice_in_dim(
            log_totals, log_total.reshape(1, -1), head_index, 0
        )
        return (context, log_totals)

    initial = (jnp.zeros(queries.shape, jnp.bfloat16), jnp.zeros((HEADS, slot_count), jnp.float32))
    return lax.fori_loop(0, HEADS, head_step, initial)


def attention_backward(
    queries, keys_in, values_in, bias_table, onehot, allowed, log_totals, grad_context
):

    def head_step(head_index, carry):
        grad_query, grad_key, grad_value, grad_table = carry
        start = head_index * HEAD_DIM
        query_head = lax.dynamic_slice_in_dim(queries, start, HEAD_DIM, 1)
        key_head = lax.dynamic_slice_in_dim(keys_in, start, HEAD_DIM, 1)
        value_head = lax.dynamic_slice_in_dim(values_in, start, HEAD_DIM, 1)
        grad_head = lax.dynamic_slice_in_dim(grad_context, start, HEAD_DIM, 1)
        bias_column = lax.dynamic_slice_in_dim(bias_table, head_index, 1, 1)
        scores = head_scores(query_head, key_head, bias_column, onehot, allowed)
        log_total = lax.dynamic_slice_in_dim(log_totals, head_index, 1, 0).reshape(-1, 1)
        attention = jnp.exp(scores - log_total)
        grad_att = dot_cols(grad_head, value_head)
        row_sum = jnp.sum(attention * grad_att, axis=-1, keepdims=True)
        grad_scores = (attention * (grad_att - row_sum)).astype(jnp.bfloat16)
        query_part = (dot_plain(grad_scores, key_head) * 0.125).astype(jnp.bfloat16)
        key_part = (dot_rows(grad_scores, query_head) * 0.125).astype(jnp.bfloat16)
        value_part = dot_rows(attention.astype(jnp.bfloat16), grad_head).astype(jnp.bfloat16)
        table_part = dot_cols(onehot, grad_scores.reshape(1, -1))
        grad_query = lax.dynamic_update_slice_in_dim(grad_query, query_part, start, 1)
        grad_key = lax.dynamic_update_slice_in_dim(grad_key, key_part, start, 1)
        grad_value = lax.dynamic_update_slice_in_dim(grad_value, value_part, start, 1)
        grad_table = lax.dynamic_update_slice_in_dim(grad_table, table_part, head_index, 1)
        return (grad_query, grad_key, grad_value, grad_table)

    blank = jnp.zeros(queries.shape, jnp.bfloat16)
    initial = (blank, blank, blank, jnp.zeros((BUCKETS, HEADS), jnp.float32))
    return lax.fori_loop(0, HEADS, head_step, initial)


def expert_forward(rows_in, gate_cols, up_cols, down_rows):
    gate_act = dot_plain(rows_in, gate_cols)
    up_act = dot_plain(rows_in, up_cols)
    hidden = (jax.nn.gelu(gate_act, approximate=True) * up_act).astype(jnp.bfloat16)
    return dot_plain(hidden, down_rows)


def expert_backward(rows_in, gate_cols, up_cols, down_rows, grad_out):
    gate_act = dot_plain(rows_in, gate_cols)
    up_act = dot_plain(rows_in, up_cols)
    activated, gelu_back = jax.vjp(lambda values: jax.nn.gelu(values, approximate=True), gate_act)
    hidden = (activated * up_act).astype(jnp.bfloat16)
    grad_hidden = dot_cols(grad_out, down_rows)
    grad_gate = gelu_back(grad_hidden * up_act)[0].astype(jnp.bfloat16)
    grad_up = (grad_hidden * activated).astype(jnp.bfloat16)
    grad_down_w = dot_rows(hidden, grad_out)
    grad_gate_w = dot_rows(rows_in, grad_gate)
    grad_up_w = dot_rows(rows_in, grad_up)
    grad_rows = dot_cols(grad_gate, gate_cols) + dot_cols(grad_up, up_cols)
    return (grad_rows, grad_gate_w, grad_up_w, grad_down_w)


def shards(
    tokens,
    cotangent,
    lengths,
    sequence_deal,
    routes,
    fill_order,
    norm_attn,
    w_query,
    w_key,
    w_value,
    w_out,
    rel_bias,
    norm_ffn,
    w_router,
    w_gate,
    w_up,
    w_down,
):
    group_size = lax.axis_size("shard")
    my_index = lax.axis_index("shard")
    deal_row = sequence_deal[0]
    source = lax.dynamic_index_in_dim(deal_row, my_index, 0, keepdims=False)
    home = jnp.sum(
        jnp.arange(group_size, dtype=jnp.int32) * (deal_row == my_index).astype(jnp.int32)
    )
    arrived, arrived_grad = (
        lax.all_gather(tokens, "shard", axis=0, tiled=True),
        lax.all_gather(cotangent, "shard", axis=0, tiled=True),
    )
    inputs = lax.dynamic_index_in_dim(arrived, source, 0, keepdims=False).astype(jnp.float32)
    upstream = lax.dynamic_index_in_dim(arrived_grad, source, 0, keepdims=False).astype(jnp.float32)
    length = lax.dynamic_index_in_dim(lengths[0], source, 0, keepdims=False)
    seq_routes = routes[0]
    seq_order = fill_order[0]
    slot_count = inputs.shape[0]
    model_width = inputs.shape[1]
    gain_attn, query_w, key_w, value_w, out_w, bias_table, gain_ffn, router_w = (
        lax.all_gather(norm_attn, "shard", axis=0, tiled=True),
        lax.all_gather(w_query, "shard", axis=0, tiled=True),
        lax.all_gather(w_key, "shard", axis=0, tiled=True),
        lax.all_gather(w_value, "shard", axis=0, tiled=True),
        lax.all_gather(w_out, "shard", axis=0, tiled=True),
        lax.all_gather(rel_bias, "shard", axis=0, tiled=True),
        lax.all_gather(norm_ffn, "shard", axis=0, tiled=True),
        lax.all_gather(w_router, "shard", axis=0, tiled=True),
    )
    gain_one = gain_attn.astype(jnp.float32)
    normed, scale_one = rms_forward(inputs, gain_one)
    normed_low = normed.astype(jnp.bfloat16)
    queries = dot_plain(normed_low, query_w).astype(jnp.bfloat16)
    keys_in = dot_plain(normed_low, key_w).astype(jnp.bfloat16)
    values_in = dot_plain(normed_low, value_w).astype(jnp.bfloat16)
    onehot, query_pos, key_pos = bucket_onehot(slot_count)
    allowed = (key_pos <= query_pos) & (key_pos < length)
    context, log_totals = attention_forward(
        queries, keys_in, values_in, bias_table, onehot, allowed
    )
    middle = inputs + dot_plain(context, out_w)
    gain_two = gain_ffn.astype(jnp.float32)
    normed_two, scale_two = rms_forward(middle, gain_two)
    ffn_in = normed_two.astype(jnp.bfloat16)
    router = jax.nn.softmax(dot_plain(ffn_in, router_w), axis=-1)
    slot_token, slot_choice, token_slot = slot_plan(seq_routes, seq_order, length)
    padded = jnp.concatenate([ffn_in, jnp.zeros((1, model_width), jnp.bfloat16)])
    buffers = jnp.take(padded, slot_token, axis=0).reshape(EXPERTS, CAP, model_width)
    out_list = []
    for expert in range(EXPERTS):
        gate_full, up_full, down_full = (
            lax.all_gather(w_gate[expert], "shard", axis=1, tiled=True),
            lax.all_gather(w_up[expert], "shard", axis=1, tiled=True),
            lax.all_gather(w_down[expert], "shard", axis=0, tiled=True),
        )
        out_list.append(expert_forward(buffers[expert], gate_full, up_full, down_full))
    expert_out = jnp.stack(out_list, 0).astype(jnp.bfloat16)
    flat_out = jnp.concatenate(
        [expert_out.reshape(EXPERTS * CAP, model_width), jnp.zeros((1, model_width), jnp.bfloat16)]
    )
    gathered = jnp.take(flat_out, token_slot, axis=0).astype(jnp.float32)
    kept_pair = (token_slot < EXPERTS * CAP).astype(jnp.float32)
    route_hits = (
        seq_routes[:, :, None] == jnp.arange(EXPERTS, dtype=jnp.int32)[None, None, :]
    ).astype(jnp.float32)
    gates = jnp.sum(router[:, None, :] * route_hits, axis=-1) * kept_pair
    result = middle + jnp.sum(gates[:, :, None] * gathered, axis=1)
    grad_gates = jnp.sum(upstream[:, None, :] * gathered, axis=-1)
    grad_probs = jnp.sum((grad_gates * kept_pair)[:, :, None] * route_hits, axis=1)
    grad_logits = router * (grad_probs - jnp.sum(router * grad_probs, axis=-1, keepdims=True))
    gate_pad = jnp.concatenate([gates, jnp.zeros((1, 2), jnp.float32)])
    upstream_pad = jnp.concatenate([upstream, jnp.zeros((1, model_width), jnp.float32)])
    gate_at_slot = gate_pad[slot_token, slot_choice]
    grad_buffers = (
        (gate_at_slot[:, None] * jnp.take(upstream_pad, slot_token, axis=0))
        .astype(jnp.bfloat16)
        .reshape(EXPERTS, CAP, model_width)
    )
    gate_list, up_list, down_list = ([], [], [])
    rows_list = []
    for expert in range(EXPERTS):
        gate_full, up_full, down_full = (
            lax.all_gather(w_gate[expert], "shard", axis=1, tiled=True),
            lax.all_gather(w_up[expert], "shard", axis=1, tiled=True),
            lax.all_gather(w_down[expert], "shard", axis=0, tiled=True),
        )
        grad_rows, grad_gate_w, grad_up_w, grad_down_w = expert_backward(
            buffers[expert], gate_full, up_full, down_full, grad_buffers[expert]
        )
        owned_gate, owned_up, owned_down = (
            lax.psum_scatter(
                grad_gate_w.astype(jnp.bfloat16), "shard", scatter_dimension=1, tiled=True
            ).astype(jnp.float32),
            lax.psum_scatter(
                grad_up_w.astype(jnp.bfloat16), "shard", scatter_dimension=1, tiled=True
            ).astype(jnp.float32),
            lax.psum_scatter(
                grad_down_w.astype(jnp.bfloat16), "shard", scatter_dimension=0, tiled=True
            ).astype(jnp.float32),
        )
        rows_list.append(grad_rows)
        gate_list.append(owned_gate)
        up_list.append(owned_up)
        down_list.append(owned_down)
    grad_rows_all = jnp.stack(rows_list, 0)
    gate_total, up_total, down_total = (
        lax.psum(jnp.stack(gate_list, 0).astype(jnp.bfloat16), "rep").astype(jnp.float32),
        lax.psum(jnp.stack(up_list, 0).astype(jnp.bfloat16), "rep").astype(jnp.float32),
        lax.psum(jnp.stack(down_list, 0).astype(jnp.bfloat16), "rep").astype(jnp.float32),
    )
    rows_pad = jnp.concatenate(
        [
            grad_rows_all.reshape(EXPERTS * CAP, model_width),
            jnp.zeros((1, model_width), jnp.float32),
        ]
    )
    router_full = router_w.astype(jnp.float32)
    grad_ffn_in = jnp.sum(jnp.take(rows_pad, token_slot, axis=0), axis=1)
    grad_ffn_in = grad_ffn_in + lax.dot_general(
        grad_logits,
        router_full,
        (((1,), (1,)), ((), ())),
        precision=lax.Precision.HIGHEST,
        preferred_element_type=jnp.float32,
    )
    grad_router_w = lax.dot_general(
        ffn_in.astype(jnp.float32),
        grad_logits,
        (((0,), (0,)), ((), ())),
        precision=lax.Precision.HIGHEST,
        preferred_element_type=jnp.float32,
    )
    grad_middle, grad_gain_two = rms_backward(middle, scale_two, gain_two, grad_ffn_in)
    grad_middle = grad_middle + upstream
    grad_attn_low = grad_middle.astype(jnp.bfloat16)
    grad_out_w = dot_rows(context, grad_attn_low)
    grad_context = dot_cols(grad_attn_low, out_w).astype(jnp.bfloat16)
    grad_query, grad_key, grad_value, grad_table = attention_backward(
        queries, keys_in, values_in, bias_table, onehot, allowed, log_totals, grad_context
    )
    grad_normed = (
        dot_cols(grad_query, query_w) + dot_cols(grad_key, key_w) + dot_cols(grad_value, value_w)
    )
    grad_query_w = dot_rows(normed_low, grad_query)
    grad_key_w = dot_rows(normed_low, grad_key)
    grad_value_w = dot_rows(normed_low, grad_value)
    grad_inputs, grad_gain_one = rms_backward(inputs, scale_one, gain_one, grad_normed)
    grad_inputs = grad_inputs + grad_middle
    owned_parts = (
        lax.psum_scatter(
            grad_gain_one.astype(jnp.bfloat16), "shard", scatter_dimension=0, tiled=True
        ).astype(jnp.float32),
        lax.psum_scatter(
            grad_query_w.astype(jnp.bfloat16), "shard", scatter_dimension=0, tiled=True
        ).astype(jnp.float32),
        lax.psum_scatter(
            grad_key_w.astype(jnp.bfloat16), "shard", scatter_dimension=0, tiled=True
        ).astype(jnp.float32),
        lax.psum_scatter(
            grad_value_w.astype(jnp.bfloat16), "shard", scatter_dimension=0, tiled=True
        ).astype(jnp.float32),
        lax.psum_scatter(
            grad_out_w.astype(jnp.bfloat16), "shard", scatter_dimension=0, tiled=True
        ).astype(jnp.float32),
        lax.psum_scatter(
            grad_table.astype(jnp.bfloat16), "shard", scatter_dimension=0, tiled=True
        ).astype(jnp.float32),
        lax.psum_scatter(
            grad_gain_two.astype(jnp.bfloat16), "shard", scatter_dimension=0, tiled=True
        ).astype(jnp.float32),
        lax.psum_scatter(
            grad_router_w.astype(jnp.bfloat16), "shard", scatter_dimension=0, tiled=True
        ).astype(jnp.float32),
    )
    dense_totals = (
        lax.psum(owned_parts[0].astype(jnp.bfloat16), "rep").astype(jnp.float32),
        lax.psum(owned_parts[1].astype(jnp.bfloat16), "rep").astype(jnp.float32),
        lax.psum(owned_parts[2].astype(jnp.bfloat16), "rep").astype(jnp.float32),
        lax.psum(owned_parts[3].astype(jnp.bfloat16), "rep").astype(jnp.float32),
        lax.psum(owned_parts[4].astype(jnp.bfloat16), "rep").astype(jnp.float32),
        lax.psum(owned_parts[5].astype(jnp.bfloat16), "rep").astype(jnp.float32),
        lax.psum(owned_parts[6].astype(jnp.bfloat16), "rep").astype(jnp.float32),
        lax.psum(owned_parts[7].astype(jnp.bfloat16), "rep").astype(jnp.float32),
    )
    back_out, back_grad = (
        lax.all_gather(result.astype(jnp.bfloat16)[None], "shard", axis=0, tiled=True),
        lax.all_gather(grad_inputs.astype(jnp.bfloat16)[None], "shard", axis=0, tiled=True),
    )
    output = lax.dynamic_slice_in_dim(back_out, home, 1, 0)
    grad_tokens = lax.dynamic_slice_in_dim(back_grad, home, 1, 0)
    return (
        output,
        grad_tokens,
        dense_totals[0],
        dense_totals[1],
        dense_totals[2],
        dense_totals[3],
        dense_totals[4],
        dense_totals[5],
        dense_totals[6],
        dense_totals[7],
        gate_total,
        up_total,
        down_total,
    )


def solution(mesh):
    return jax.shard_map(
        shards,
        mesh=mesh,
        in_specs=(
            P(("rep", "shard"), None, None),
            P(("rep", "shard"), None, None),
            P("rep", None),
            P("rep", None),
            P(("rep", "shard"), None, None),
            P(("rep", "shard"), None),
            P("shard"),
            P("shard", None),
            P("shard", None),
            P("shard", None),
            P("shard", None),
            P("shard", None),
            P("shard"),
            P("shard", None),
            P(None, None, "shard"),
            P(None, None, "shard"),
            P(None, "shard", None),
        ),
        out_specs=(
            P(("rep", "shard"), None, None),
            P(("rep", "shard"), None, None),
            P("shard"),
            P("shard", None),
            P("shard", None),
            P("shard", None),
            P("shard", None),
            P("shard", None),
            P("shard"),
            P("shard", None),
            P(None, None, "shard"),
            P(None, None, "shard"),
            P(None, "shard", None),
        ),
        check_vma=False,
    )
```

profile of v0, /device:TPU:0, one launch (start us, length us, event | category | flops | bytes accessed | tf_op | source)
XLA Modules:
  0.0 2552.4 jit_solution(14643499661359837519)
XLA Ops:
  83.3 24.2 scatter_fusion
  125.0 34.5 %all-gather.43.cloned.1.call-done = bf16[1024,1024]{1,0:T(8,128)(2,1)} async-done(((bf16[256,1024]{1,0:T(8,128)(2,1)}), bf16[1024,1024]{1,0:T(8,128)(2,1)}) %all-gather.43.cloned.1.call-update) | async-done | bytes 2097168 | tf_op jit(solution)/shard_map/all_gather | solution.py:221
  162.8 69.2 %while.37 = (s32[]{:T(128)}, bf16[256,1024]{0,1:T(8,128)(2,1)S(1)}, f32[16,256]{1,0:T(8,128)}, bf16[256,1024]{1,0:T(8,128)(2,1)S(1)}, bf16[256,1024]{1,0:T(8,128...) while((s32[]{:T(128)}, bf16[256,1024]{0,1:T(8,128)(2,1)S(1)}, ...), condition=%wide.region_4.5_spmd.clone, body=%wide.region_1.0_spmd.clone.sunk | while | flops 25837316 | bytes 10727611 | solution.py:122
  252.5 49.4 %all-gather.71.cloned.1.call-done = bf16[1,2816,1024]{2,1,0:T(8,128)(2,1)} async-done(((bf16[1,704,1024]{2,1,0:T(8,128)(2,1)}), bf16[1,2816,1024]{2,1,0:T(8,128)(2,1)}) %all-gather.71.cloned.1.call-update) | async-done | bytes 5767184 | tf_op jit(solution)/shard_map/all_gather | solution.py:251
  307.7 61.8 %all-gather.69.cloned.1.call-done = bf16[1,1024,2816]{1,2,0:T(8,128)(2,1)} async-done(((bf16[1,1024,704]{1,2,0:T(8,128)(2,1)}), bf16[1,1024,2816]{1,2,0:T(8,128)(2,1)}) %all-gather.69.cloned.1.call-update) | async-done | bytes 5767184 | tf_op jit(solution)/shard_map/all_gather | solution.py:250
  375.4 61.8 %all-gather.67.cloned.1.call-done = bf16[1,1024,2816]{1,2,0:T(8,128)(2,1)} async-done(((bf16[1,1024,704]{1,2,0:T(8,128)(2,1)}), bf16[1,1024,2816]{1,2,0:T(8,128)(2,1)}) %all-gather.67.cloned.1.call-update) | async-done | bytes 5767184 | tf_op jit(solution)/shard_map/all_gather | solution.py:249
  450.6 54.7 %all-gather.65.cloned.1.call-done = bf16[1,2816,1024]{2,1,0:T(8,128)(2,1)} async-done(((bf16[1,704,1024]{2,1,0:T(8,128)(2,1)}), bf16[1,2816,1024]{2,1,0:T(8,128)(2,1)}) %all-gather.65.cloned.1.call-update) | async-done | bytes 5767184 | tf_op jit(solution)/shard_map/all_gather | solution.py:251
  511.2 61.8 %all-gather.63.cloned.1.call-done = bf16[1,1024,2816]{1,2,0:T(8,128)(2,1)} async-done(((bf16[1,1024,704]{1,2,0:T(8,128)(2,1)}), bf16[1,1024,2816]{1,2,0:T(8,128)(2,1)}) %all-gather.63.cloned.1.call-update) | async-done | bytes 5767184 | tf_op jit(solution)/shard_map/all_gather | solution.py:250
  578.9 61.7 %all-gather.61.cloned.1.call-done = bf16[1,1024,2816]{1,2,0:T(8,128)(2,1)} async-done(((bf16[1,1024,704]{1,2,0:T(8,128)(2,1)}), bf16[1,1024,2816]{1,2,0:T(8,128)(2,1)}) %all-gather.61.cloned.1.call-update) | async-done | bytes 5767184 | tf_op jit(solution)/shard_map/all_gather | solution.py:249
  653.9 54.3 %all-gather.59.cloned.1.call-done = bf16[1,2816,1024]{2,1,0:T(8,128)(2,1)} async-done(((bf16[1,704,1024]{2,1,0:T(8,128)(2,1)}), bf16[1,2816,1024]{2,1,0:T(8,128)(2,1)}) %all-gather.59.cloned.1.call-update) | async-done | bytes 5767184 | tf_op jit(solution)/shard_map/all_gather | solution.py:251
  714.1 61.7 %all-gather.57.cloned.1.call-done = bf16[1,1024,2816]{1,2,0:T(8,128)(2,1)} async-done(((bf16[1,1024,704]{1,2,0:T(8,128)(2,1)}), bf16[1,1024,2816]{1,2,0:T(8,128)(2,1)}) %all-gather.57.cloned.1.call-update) | async-done | bytes 5767184 | tf_op jit(solution)/shard_map/all_gather | solution.py:250
  781.6 61.6 %all-gather.55.cloned.1.call-done = bf16[1,1024,2816]{1,2,0:T(8,128)(2,1)} async-done(((bf16[1,1024,704]{1,2,0:T(8,128)(2,1)}), bf16[1,1024,2816]{1,2,0:T(8,128)(2,1)}) %all-gather.55.cloned.1.call-update) | async-done | bytes 5767184 | tf_op jit(solution)/shard_map/all_gather | solution.py:249
  856.7 54.1 %all-gather.53.cloned.1.call-done = bf16[1,2816,1024]{2,1,0:T(8,128)(2,1)} async-done(((bf16[1,704,1024]{2,1,0:T(8,128)(2,1)}), bf16[1,2816,1024]{2,1,0:T(8,128)(2,1)}) %all-gather.53.cloned.1.call-update) | async-done | bytes 5767184 | tf_op jit(solution)/shard_map/all_gather | solution.py:251
  916.7 61.6 %all-gather.51.cloned.1.call-done = bf16[1,1024,2816]{1,2,0:T(8,128)(2,1)} async-done(((bf16[1,1024,704]{1,2,0:T(8,128)(2,1)}), bf16[1,1024,2816]{1,2,0:T(8,128)(2,1)}) %all-gather.51.cloned.1.call-update) | async-done | bytes 5767184 | tf_op jit(solution)/shard_map/all_gather | solution.py:250
  984.2 61.7 %all-gather.49.cloned.1.call-done = bf16[1,1024,2816]{1,2,0:T(8,128)(2,1)} async-done(((bf16[1,1024,704]{1,2,0:T(8,128)(2,1)}), bf16[1,1024,2816]{1,2,0:T(8,128)(2,1)}) %all-gather.49.cloned.1.call-update) | async-done | bytes 5767184 | tf_op jit(solution)/shard_map/all_gather | solution.py:249
  1164.6 173.2 %while.38 = (s32[]{:T(128)}, bf16[256,1024]{0,1:T(8,128)(2,1)S(1)}, bf16[256,1024]{0,1:T(8,128)(2,1)S(1)}, bf16[256,1024]{0,1:T(8,128)(2,1)}, bf16[32,16]{0,1:T(...) while((s32[]{:T(128)}, bf16[256,1024]{0,1:T(8,128)(2,1)S(1)}, ...), condition=%wide.region_25.26_spmd.clone.clone, body=%wide.region_23.25_spmd.clone.clone.sunk | while | flops 59588356 | bytes 13151391 | solution.py:155
  1365.8 25.9 %reduce-scatter.42.cloned.1.call-done = bf16[1024,704]{0,1:T(8,128)(2,1)} async-done(((bf16[1024,2816]{0,1:T(8,128)(2,1)}), bf16[1024,704]{0,1:T(8,128)(2,1)}) %reduce-scatter.42.cloned.1.call-update) | async-done | bytes 1441808 | tf_op jit(solution)/shard_map/reduce_scatter | solution.py:291
  1391.7 68.7 %reduce-scatter.40.cloned.1.call-done = bf16[1024,704]{0,1:T(8,128)(2,1)} async-done(((bf16[1024,2816]{0,1:T(8,128)(2,1)}), bf16[1024,704]{0,1:T(8,128)(2,1)}) %reduce-scatter.40.cloned.1.call-update) | async-done | bytes 1441808 | tf_op jit(solution)/shard_map/reduce_scatter | solution.py:291
  1460.4 68.8 %reduce-scatter.38.cloned.1.call-done = bf16[1024,704]{0,1:T(8,128)(2,1)} async-done(((bf16[1024,2816]{0,1:T(8,128)(2,1)}), bf16[1024,704]{0,1:T(8,128)(2,1)}) %reduce-scatter.38.cloned.1.call-update) | async-done | bytes 1441808 | tf_op jit(solution)/shard_map/reduce_scatter | solution.py:291
  1529.2 68.7 %reduce-scatter.36.cloned.1.call-done = bf16[1024,704]{0,1:T(8,128)(2,1)} async-done(((bf16[1024,2816]{0,1:T(8,128)(2,1)}), bf16[1024,704]{0,1:T(8,128)(2,1)}) %reduce-scatter.36.cloned.1.call-update) | async-done | bytes 1441808 | tf_op jit(solution)/shard_map/reduce_scatter | solution.py:291
  1604.1 62.5 %reduce-scatter.50.cloned.1.call-done = bf16[704,1024]{1,0:T(8,128)(2,1)} async-done(((bf16[2816,1024]{1,0:T(8,128)(2,1)}), bf16[704,1024]{1,0:T(8,128)(2,1)}) %reduce-scatter.50.cloned.1.call-update) | async-done | bytes 1441808 | tf_op jit(solution)/shard_map/reduce_scatter | solution.py:294
  1666.6 68.8 %reduce-scatter.48.cloned.1.call-done = bf16[704,1024]{1,0:T(8,128)(2,1)} async-done(((bf16[2816,1024]{1,0:T(8,128)(2,1)}), bf16[704,1024]{1,0:T(8,128)(2,1)}) %reduce-scatter.48.cloned.1.call-update) | async-done | bytes 1441808 | tf_op jit(solution)/shard_map/reduce_scatter | solution.py:294
  1735.4 68.8 %reduce-scatter.46.cloned.1.call-done = bf16[704,1024]{1,0:T(8,128)(2,1)} async-done(((bf16[2816,1024]{1,0:T(8,128)(2,1)}), bf16[704,1024]{1,0:T(8,128)(2,1)}) %reduce-scatter.46.cloned.1.call-update) | async-done | bytes 1441808 | tf_op jit(solution)/shard_map/reduce_scatter | solution.py:294
  1804.3 68.7 %reduce-scatter.44.cloned.1.call-done = bf16[704,1024]{1,0:T(8,128)(2,1)} async-done(((bf16[2816,1024]{1,0:T(8,128)(2,1)}), bf16[704,1024]{1,0:T(8,128)(2,1)}) %reduce-scatter.44.cloned.1.call-update) | async-done | bytes 1441808 | tf_op jit(solution)/shard_map/reduce_scatter | solution.py:294
  1879.1 32.1 %reduce-scatter.20.cloned.1.call-done = bf16[256,1024]{1,0:T(8,128)(2,1)} async-done(((bf16[1024,1024]{1,0:T(8,128)(2,1)}), bf16[256,1024]{1,0:T(8,128)(2,1)}) %reduce-scatter.20.cloned.1.call-update) | async-done | bytes 524304 | tf_op jit(solution)/shard_map/reduce_scatter | solution.py:350
  1911.2 38.4 %reduce-scatter.22.cloned.1.call-done = bf16[256,1024]{1,0:T(8,128)(2,1)} async-done(((bf16[1024,1024]{1,0:T(8,128)(2,1)}), bf16[256,1024]{1,0:T(8,128)(2,1)}) %reduce-scatter.22.cloned.1.call-update) | async-done | bytes 524304 | tf_op jit(solution)/shard_map/reduce_scatter | solution.py:353
  1949.6 38.0 %reduce-scatter.24.cloned.1.call-done = bf16[256,1024]{1,0:T(8,128)(2,1)} async-done(((bf16[1024,1024]{1,0:T(8,128)(2,1)}), bf16[256,1024]{1,0:T(8,128)(2,1)}) %reduce-scatter.24.cloned.1.call-update) | async-done | bytes 524304 | tf_op jit(solution)/shard_map/reduce_scatter | solution.py:356
  1987.7 38.5 %reduce-scatter.26.cloned.1.call-done = bf16[256,1024]{1,0:T(8,128)(2,1)} async-done(((bf16[1024,1024]{1,0:T(8,128)(2,1)}), bf16[256,1024]{1,0:T(8,128)(2,1)}) %reduce-scatter.26.cloned.1.call-update) | async-done | bytes 524304 | tf_op jit(solution)/shard_map/reduce_scatter | solution.py:359
  2054.5 16.1 all-reduce.8
  2072.9 18.4 all-gather.73.cloned.1.call-done
  2093.2 35.9 %all-gather.75.cloned.1.call-done = bf16[1024,1024]{1,0:T(8,128)(2,1)} async-done(((bf16[256,1024]{1,0:T(8,128)(2,1)}), bf16[1024,1024]{1,0:T(8,128)(2,1)}) %all-gather.75.cloned.1.call-update) | async-done | bytes 2097168 | tf_op jit(solution)/shard_map/all_gather | solution.py:384
  2131.0 389.0 %all-reduce.13.cloned.1.call-done = (bf16[256,1024]{1,0:T(8,128)(2,1)}, bf16[256,1024]{1,0:T(8,128)(2,1)}, bf16[256,1024]{1,0:T(8,128)(2,1)}, bf16[256,1024]{1,0...) async-done(((bf16[256,1024]{1,0:T(8,128)(2,1)}, bf16[256,1024]{1,0:T(8,128)(2,1)}, ...) | async-done | bytes 19398672 | tf_op jit(solution)/shard_map/psum | solution.py:374
  (793 shorter events, 656.9 us)
Async XLA Ops:
  11.2 290.7 %all-gather.71.cloned.1.call-start = ((), (), s32[]{:S(2)}) async-start(), calls=%async_computation.50 | async-start | bytes 7208960 | tf_op jit(solution)/shard_map/all_gather | solution.py:251
  16.5 353.0 %all-gather.69.cloned.1.call-start = ((), (), s32[]{:S(2)}) async-start(), calls=%async_computation.49 | async-start | bytes 7208960 | tf_op jit(solution)/shard_map/all_gather | solution.py:250
  22.0 415.2 %all-gather.67.cloned.1.call-start = ((), (), s32[]{:S(2)}) async-start(), calls=%async_computation.48 | async-start | bytes 7208960 | tf_op jit(solution)/shard_map/all_gather | solution.py:249
  27.3 478.0 %all-gather.65.cloned.1.call-start = ((), (), s32[]{:S(2)}) async-start(), calls=%async_computation.47 | async-start | bytes 7208960 | tf_op jit(solution)/shard_map/all_gather | solution.py:251
  27.9 545.1 %all-gather.63.cloned.1.call-start = ((), (), s32[]{:S(2)}) async-start(), calls=%async_computation.46 | async-start | bytes 7208960 | tf_op jit(solution)/shard_map/all_gather | solution.py:250
  28.6 611.9 %all-gather.61.cloned.1.call-start = ((), (), s32[]{:S(2)}) async-start(), calls=%async_computation.45 | async-start | bytes 7208960 | tf_op jit(solution)/shard_map/all_gather | solution.py:249
  29.2 679.0 %all-gather.59.cloned.1.call-start = ((), (), s32[]{:S(2)}) async-start(), calls=%async_computation.44 | async-start | bytes 7208960 | tf_op jit(solution)/shard_map/all_gather | solution.py:251
  30.0 745.8 %all-gather.57.cloned.1.call-start = ((), (), s32[]{:S(2)}) async-start(), calls=%async_computation.43 | async-start | bytes 7208960 | tf_op jit(solution)/shard_map/all_gather | solution.py:250
  30.6 812.7 %all-gather.55.cloned.1.call-start = ((), (), s32[]{:S(2)}) async-start(), calls=%async_computation.42 | async-start | bytes 7208960 | tf_op jit(solution)/shard_map/all_gather | solution.py:249
  31.1 879.7 %all-gather.53.cloned.1.call-start = ((), (), s32[]{:S(2)}) async-start(), calls=%async_computation.41 | async-start | bytes 7208960 | tf_op jit(solution)/shard_map/all_gather | solution.py:251
  31.7 946.6 %all-gather.51.cloned.1.call-start = ((), (), s32[]{:S(2)}) async-start(), calls=%async_computation.40 | async-start | bytes 7208960 | tf_op jit(solution)/shard_map/all_gather | solution.py:250
  32.3 1013.6 %all-gather.49.cloned.1.call-start = ((), (), s32[]{:S(2)}) async-start(), calls=%async_computation.39 | async-start | bytes 7208960 | tf_op jit(solution)/shard_map/all_gather | solution.py:249
  32.9 1326.7 %reduce-scatter.34.cloned.1.call-start = ((), (), s32[]{:S(2)}) async-start(), calls=%async_computation.30 | async-start | bytes 7208960 | tf_op jit(solution)/shard_map/reduce_scatter | solution.py:288
  450.1 909.5 %reduce-scatter.32.cloned.1.call-start = ((), (), s32[]{:S(2)}) async-start(), calls=%async_computation.29 | async-start | bytes 7208960 | tf_op jit(solution)/shard_map/reduce_scatter | solution.py:288
  653.7 706.0 %reduce-scatter.30.cloned.1.call-start = ((), (), s32[]{:S(2)}) async-start(), calls=%async_computation.28 | async-start | bytes 7208960 | tf_op jit(solution)/shard_map/reduce_scatter | solution.py:288
  856.5 503.2 %reduce-scatter.28.cloned.1.call-start = ((), (), s32[]{:S(2)}) async-start(), calls=%async_computation.27 | async-start | bytes 7208960 | tf_op jit(solution)/shard_map/reduce_scatter | solution.py:288
  1058.9 332.8 %reduce-scatter.42.cloned.1.call-start = ((), (), s32[]{:S(2)}) async-start(), calls=%async_computation.34 | async-start | bytes 7208960 | tf_op jit(solution)/shard_map/reduce_scatter | solution.py:291
  1064.4 396.0 %reduce-scatter.40.cloned.1.call-start = ((), (), s32[]{:S(2)}) async-start(), calls=%async_computation.33 | async-start | bytes 7208960 | tf_op jit(solution)/shard_map/reduce_scatter | solution.py:291
  1069.8 459.4 %reduce-scatter.38.cloned.1.call-start = ((), (), s32[]{:S(2)}) async-start(), calls=%async_computation.32 | async-start | bytes 7208960 | tf_op jit(solution)/shard_map/reduce_scatter | solution.py:291
  1075.3 522.6 %reduce-scatter.36.cloned.1.call-start = ((), (), s32[]{:S(2)}) async-start(), calls=%async_computation.31 | async-start | bytes 7208960 | tf_op jit(solution)/shard_map/reduce_scatter | solution.py:291
  1081.2 585.4 %reduce-scatter.50.cloned.1.call-start = ((), (), s32[]{:S(2)}) async-start(), calls=%async_computation.38 | async-start | bytes 7208960 | tf_op jit(solution)/shard_map/reduce_scatter | solution.py:294
  1085.6 649.8 %reduce-scatter.48.cloned.1.call-start = ((), (), s32[]{:S(2)}) async-start(), calls=%async_computation.37 | async-start | bytes 7208960 | tf_op jit(solution)/shard_map/reduce_scatter | solution.py:294
  1091.0 713.2 %reduce-scatter.46.cloned.1.call-start = ((), (), s32[]{:S(2)}) async-start(), calls=%async_computation.36 | async-start | bytes 7208960 | tf_op jit(solution)/shard_map/reduce_scatter | solution.py:294
  1096.6 776.4 %reduce-scatter.44.cloned.1.call-start = ((), (), s32[]{:S(2)}) async-start(), calls=%async_computation.35 | async-start | bytes 7208960 | tf_op jit(solution)/shard_map/reduce_scatter | solution.py:294
  1158.0 753.1 %reduce-scatter.20.cloned.1.call-start = ((), (), s32[]{:S(2)}) async-start(), calls=%async_computation.23 | async-start | bytes 2621440 | tf_op jit(solution)/shard_map/reduce_scatter | solution.py:350
  1341.1 608.5 %reduce-scatter.22.cloned.1.call-start = ((), (), s32[]{:S(2)}) async-start(), calls=%async_computation.24 | async-start | bytes 2621440 | tf_op jit(solution)/shard_map/reduce_scatter | solution.py:353
  1344.5 643.2 %reduce-scatter.24.cloned.1.call-start = ((), (), s32[]{:S(2)}) async-start(), calls=%async_computation.25 | async-start | bytes 2621440 | tf_op jit(solution)/shard_map/reduce_scatter | solution.py:356
  1347.9 678.2 %reduce-scatter.26.cloned.1.call-start = ((), (), s32[]{:S(2)}) async-start(), calls=%async_computation.26 | async-start | bytes 2621440 | tf_op jit(solution)/shard_map/reduce_scatter | solution.py:359
  1350.0 703.6 %reduce-scatter.52.cloned.1.call-start = ((), (), s32[]{:S(2)}) async-start(), calls=%async_computation.53 | async-start | bytes 327680
  1351.3 740.0 %all-gather.73.cloned.1.call-start = ((), (), s32[]{:S(2)}) async-start(), calls=%async_computation.51 | async-start | bytes 2621440 | tf_op jit(solution)/shard_map/all_gather | solution.py:383
  1351.9 777.2 %all-gather.75.cloned.1.call-start = ((), (), s32[]{:S(2)}) async-start(), calls=%async_computation.52 | async-start | bytes 2621440 | tf_op jit(solution)/shard_map/all_gather | solution.py:384
  1359.5 1160.5 %all-reduce.13.cloned.1.call-start = ((), (), s32[]{:S(2)}) async-start(), calls=%async_computation.54 | async-start | bytes 38797312 | tf_op jit(solution)/shard_map/psum | solution.py:374
  (87 other events, 3324.5 us)
Sparse Core Ops, SparseCore 0:
  9.9 38.0 all-gather.36
  49.8 35.3 all-gather.38
  87.1 35.3 all-gather.40
  124.1 35.2 all-gather.42
  161.1 35.3 all-gather.46
  198.2 35.3 all-gather.44
  236.0 65.8 all-gather.70
  303.7 65.7 all-gather.68
  371.4 65.7 all-gather.66
  439.5 65.7 all-gather.64
  507.2 65.7 all-gather.62
  574.7 65.7 all-gather.60
  642.4 65.7 all-gather.58
  709.9 65.7 all-gather.56
  777.4 65.7 all-gather.54
  845.0 65.7 all-gather.52
  912.5 65.7 all-gather.50
  980.0 65.7 all-gather.48
  1049.4 65.8 reduce-scatter.33
  1118.7 65.8 reduce-scatter.31
  1188.1 65.8 reduce-scatter.29
  1257.0 65.8 reduce-scatter.27
  1325.8 65.8 reduce-scatter.41
  1394.5 65.8 reduce-scatter.39
  1463.4 65.8 reduce-scatter.37
  1532.1 65.8 reduce-scatter.35
  1600.8 65.8 reduce-scatter.49
  1669.6 65.8 reduce-scatter.47
  1738.4 65.8 reduce-scatter.45
  1807.1 65.8 reduce-scatter.43
  2056.0 35.2 all-gather.72
  2133.5 386.3 all-reduce.12
  (6 shorter events, 199.8 us)
where the time goes:
time: 2570 us; the launch traced here: 2550 us
  waiting for transfers between devices  1860 us (72%)
  matrix products  367 us (14%)
  local copies, waits for them, and re-layouts  144 us (6%)
  other arithmetic  91 us (4%)
  blocking collectives  64.3 us (3%)
    psum x1, waiting for transfers between devices, shards(): lax.psum(owned_parts[1].astype(jnp.bfloat16), 'rep').astype(jnp.float32)  389 us
    reduce_scatter x4, waiting for transfers between devices, shards(): lax.psum_scatter(grad_down_w.astype(jnp.bfloat16), 'shard', scatter_dimen...  269 us
    all_gather x4, waiting for transfers between devices, shards(): lax.all_gather(w_up[expert], 'shard', axis=1, tiled=True)  247 us
    all_gather x4, waiting for transfers between devices, shards(): lax.all_gather(w_gate[expert], 'shard', axis=1, tiled=True)  247 us
    reduce_scatter x4, waiting for transfers between devices, shards(): lax.psum_scatter(grad_up_w.astype(jnp.bfloat16), 'shard', scatter_dimensi...  232 us
    all_gather x4, waiting for transfers between devices, shards(): lax.all_gather(w_down[expert], 'shard', axis=0, tiled=True)  213 us
    dot_general x80, matrix products, dot_rows(): lax.dot_general(left_side, right_side, (((0,), (0,)), ((), ())), preferre...  147 us
    dot_general x49, matrix products, dot_plain(): return jnp.dot(left_side, right_side, preferred_element_type=jnp.float32)  112 us
  transfers between devices with their start and end apart: 38, of which 30 were waited for; matrix products, arithmetic and copies ran while one was open for 22% of the time, Pallas kernels for 0%

commit v1 on v0

v1 whole, which is shorter than its diff:
```python
import functools
import math

import jax
import jax.numpy as jnp
from jax import lax
from jax.experimental import pallas as pl
from jax.experimental.pallas import tpu as pltpu
from jax.sharding import PartitionSpec as P

HEADS = 16
HEAD_DIM = 64
EXPERTS = 4
BUCKETS = 32
CAP = 144
LANES = 128

eps = 1e-06
bucket_edges = [int(math.ceil(16.0 * 8.0 ** (level / 16.0))) for level in range(1, 16)]
bf16 = jnp.bfloat16
f32 = jnp.float32


def dot_nn(a, b):
    return lax.dot_general(a, b, (((1,), (0,)), ((), ())), preferred_element_type=f32)


def dot_nt(a, b):
    return lax.dot_general(a, b, (((1,), (1,)), ((), ())), preferred_element_type=f32)


def dot_tn(a, b):
    return lax.dot_general(a, b, (((0,), (0,)), ((), ())), preferred_element_type=f32)


def params(mib):
    return pltpu.CompilerParams(vmem_limit_bytes=mib * 1024 * 1024)


def vmem():
    return pl.BlockSpec(memory_space=pltpu.VMEM)


def anywhere():
    return pl.BlockSpec(memory_space=pl.ANY)


def smem():
    return pl.BlockSpec(memory_space=pltpu.SMEM)


def bias_kernel(len_ref, base_ref, out_ref):
    n = base_ref.shape[2]
    rows = lax.broadcasted_iota(jnp.int32, (n, n), 0)
    cols = lax.broadcasted_iota(jnp.int32, (n, n), 1)
    allowed = (cols <= rows) & (cols < len_ref[0])
    for h in range(2):
        row = jnp.broadcast_to(base_ref[0, h : h + 1, :], (n, n))
        bias = pltpu.roll(row, 0, 1, stride=1, stride_axis=0)
        out_ref[h] = jnp.where(allowed, bias, -1000000000.0).astype(bf16)


def bias_of(length, base):
    pairs, _, n = base.shape
    return pl.pallas_call(
        bias_kernel,
        grid_spec=pltpu.PrefetchScalarGridSpec(
            num_scalar_prefetch=1,
            grid=(pairs,),
            in_specs=[pl.BlockSpec((1, 2, n), lambda i, l: (i, 0, 0))],
            out_specs=pl.BlockSpec((2, n, n), lambda i, l: (i, 0, 0)),
        ),
        out_shape=jax.ShapeDtypeStruct((2 * pairs, n, n), bf16),
        compiler_params=params(16),
        name="bias",
    )(length, base)


def softmax_of(q, k, bias):
    s = dot_nt(q, k) * 0.125 + bias.astype(f32)
    e = jnp.exp(s - jnp.max(s, axis=-1, keepdims=True))
    return e * (1.0 / jnp.sum(e, axis=-1, keepdims=True))


def gather_rows(off_ref, pieces, dest, sems):
    rows = pieces[0].shape[0]
    copies = []
    for p, piece in enumerate(pieces):
        start = pl.multiple_of(off_ref[p] * rows, rows)
        copies.append(pltpu.make_async_copy(piece, dest.at[pl.ds(start, rows)], sems.at[p]))
        copies[-1].start()
    return copies


def attn_fwd_kernel(N, *refs):
    off_ref, x_ref, gain_ref, bias_ref = refs[:4]
    pieces = refs[4 : 4 + N]
    h_ref, qkv_ref, c_ref, wout_ref, w_s, sems = refs[4 + N :]
    width = x_ref.shape[1]
    copies = gather_rows(off_ref, pieces, w_s, sems)
    x = x_ref[...].astype(f32)
    scale = lax.rsqrt(jnp.mean(x * x, axis=-1, keepdims=True) + eps)
    h_ref[...] = (x * scale * gain_ref[...]).astype(bf16)
    for copy in copies:
        copy.wait()
    out = pltpu.make_async_copy(w_s, wout_ref, sems.at[N])
    out.start()
    step = width // 2

    def project(i, carry):
        cut = pl.ds(pl.multiple_of(i * step, step), step)
        qkv_ref[:, cut] = dot_nn(h_ref[...], w_s[:, cut]).astype(bf16)
        return carry

    lax.fori_loop(0, 3 * width // step, project, 0)

    def pair(i, carry):
        def at(j):
            return pl.ds(pl.multiple_of(j * width + i * LANES, LANES), LANES)

        q2, k2, v2 = qkv_ref[:, at(0)], qkv_ref[:, at(1)], qkv_ref[:, at(2)]
        heads = []
        for h in range(2):
            cut = slice(h * HEAD_DIM, (h + 1) * HEAD_DIM)
            p = softmax_of(q2[:, cut], k2[:, cut], bias_ref[2 * i + h]).astype(bf16)
            heads.append(dot_nn(p, v2[:, cut]).astype(bf16))
        c_ref[:, at(0)] = jnp.concatenate(heads, axis=1)
        return carry

    lax.fori_loop(0, HEADS // 2, pair, 0)
    out.wait()


def attn_fwd(offsets, x, gain, bias, pieces):
    n, width = x.shape
    N = len(pieces)
    full = jax.ShapeDtypeStruct((n, width), bf16)
    return pl.pallas_call(
        functools.partial(attn_fwd_kernel, N),
        in_specs=[smem(), vmem(), vmem(), vmem()] + [anywhere()] * N,
        out_specs=[vmem(), vmem(), vmem(), anywhere()],
        out_shape=[
            full,
            jax.ShapeDtypeStruct((n, 3 * width), bf16),
            full,
            jax.ShapeDtypeStruct((width, 3 * width), bf16),
        ],
        scratch_shapes=[pltpu.VMEM((width, 3 * width), bf16), pltpu.SemaphoreType.DMA((N + 1,))],
        compiler_params=params(24),
        name="attn_fwd",
    )(offsets, x, gain, bias, *pieces)


def mid_kernel(N, *refs):
    off_ref, x_ref, gain_ref, c_ref = refs[:4]
    pieces = refs[4 : 4 + N]
    mid_ref, h_ref, wout_ref, w_s, sems = refs[4 + N :]
    for copy in gather_rows(off_ref, pieces, w_s, sems):
        copy.wait()
    out = pltpu.make_async_copy(w_s, wout_ref, sems.at[N])
    out.start()
    mid = x_ref[...].astype(f32) + dot_nn(c_ref[...], w_s[...])
    scale = lax.rsqrt(jnp.mean(mid * mid, axis=-1, keepdims=True) + eps)
    mid_ref[...] = mid
    h_ref[...] = (mid * scale * gain_ref[...]).astype(bf16)
    out.wait()


def mid_of(offsets, x, gain, context, pieces):
    n, width = x.shape
    N = len(pieces)
    return pl.pallas_call(
        functools.partial(mid_kernel, N),
        in_specs=[smem(), vmem(), vmem(), vmem()] + [anywhere()] * N,
        out_specs=[vmem(), vmem(), anywhere()],
        out_shape=[
            jax.ShapeDtypeStruct((n, width), f32),
            jax.ShapeDtypeStruct((n, width), bf16),
            jax.ShapeDtypeStruct((width, width), bf16),
        ],
        scratch_shapes=[pltpu.VMEM((width, width), bf16), pltpu.SemaphoreType.DMA((N + 1,))],
        compiler_params=params(16),
        name="middle",
    )(offsets, x, gain, context, *pieces)


def attn_bwd_kernel(q_ref, k_ref, v_ref, bias_ref, dc_ref, dq_ref, dk_ref, dv_ref, diag_ref):
    n = q_ref.shape[0]
    rows = lax.broadcasted_iota(jnp.int32, (n, n), 0)
    cols = lax.broadcasted_iota(jnp.int32, (n, n), 1)
    reverse = (rows + cols == n - 1).astype(bf16)
    for h in range(2):
        cut = slice(h * HEAD_DIM, (h + 1) * HEAD_DIM)
        q, k, v, dc = q_ref[:, cut], k_ref[:, cut], v_ref[:, cut], dc_ref[:, cut]
        p = softmax_of(q, k, bias_ref[h])
        dp = dot_nt(dc, v)
        ds = p * (dp - jnp.sum(p * dp, axis=-1, keepdims=True))
        low = ds.astype(bf16)
        dq_ref[:, cut] = (dot_nn(low, k) * 0.125).astype(bf16)
        dk_ref[:, cut] = (dot_tn(low, q) * 0.125).astype(bf16)
        dv_ref[:, cut] = dot_tn(p.astype(bf16), dc).astype(bf16)
        turned = pltpu.roll(dot_nn(reverse, low), 1, 1, stride=1, stride_axis=0)
        diag_ref[0, h : h + 1, :] = jnp.sum(turned, axis=0, keepdims=True)


def attn_bwd(qkv, bias, dc):
    n = qkv.shape[0]
    pairs = HEADS // 2
    blk = pl.BlockSpec((n, LANES), lambda i: (0, i))
    row = pl.BlockSpec((1, 2, n), lambda i: (i, 0, 0))
    full = jax.ShapeDtypeStruct((n, HEADS * HEAD_DIM), bf16)
    return pl.pallas_call(
        attn_bwd_kernel,
        grid=(pairs,),
        in_specs=[
            blk,
            pl.BlockSpec((n, LANES), lambda i: (0, pairs + i)),
            pl.BlockSpec((n, LANES), lambda i: (0, 2 * pairs + i)),
            pl.BlockSpec((2, n, n), lambda i: (i, 0, 0)),
            blk,
        ],
        out_specs=[blk, blk, blk, row],
        out_shape=[full, full, full, jax.ShapeDtypeStruct((pairs, 2, n), f32)],
        compiler_params=params(16),
        name="attn_bwd",
    )(qkv, qkv, qkv, bias, dc)


def ffn_kernel(S, e, *refs):
    core_ref, pos_ref, aux_ref = refs[:3]
    h2 = refs[3 : 3 + S]
    ct = refs[3 + S : 3 + 2 * S]
    wg_hbm, wu_hbm, wd_hbm = refs[3 + 2 * S : 6 + 2 * S]
    refs = refs[6 + 2 * S + (1 if e else 0) :]
    gk, gs, uk, us, dk, ds, eodx, dr = refs[:8]
    refs = refs[8:]
    if e == 0:
        prob_ref, refs = refs[0], refs[1:]
    else:
        prob_ref = aux_ref
    wg, wu, wd, x_s, c_s, gate_s, a_s, u_s, d_s, hid_s, da_s, du_s, g_o, u_o, d_o, ed_o, sems = refs
    n, width = h2[0].shape
    loads = []
    for i, (src, dst) in enumerate(((wg_hbm, wg), (wu_hbm, wu), (wd_hbm, wd))):
        loads.append(pltpu.make_async_copy(src.at[e], dst, sems.at[i]))
        loads[-1].start()
    lanes = lax.broadcasted_iota(jnp.int32, (n, LANES), 1)
    slots = lax.broadcasted_iota(jnp.int32, (CAP, n), 0)
    if e == 0:
        for s in range(S):
            logits = jnp.where(lanes < EXPERTS, dot_nn(h2[s][...], aux_ref[...]), -1e30)
            ex = jnp.exp(logits - jnp.max(logits, axis=-1, keepdims=True))
            prob = ex / jnp.sum(ex, axis=-1, keepdims=True)
            high = prob.astype(bf16).astype(f32)
            rest = pltpu.roll(prob - high, EXPERTS, 1)
            prob_ref[s] = jnp.where(lanes < EXPERTS, high, rest).astype(bf16)
    for s in range(S):
        rows = slice(s * CAP, (s + 1) * CAP)
        hot = (slots == pos_ref[s, e : e + 1, :]).astype(bf16)
        x_s[rows, :] = dot_nn(hot, h2[s][...]).astype(bf16)
        c_s[rows, :] = dot_nn(hot, ct[s][...]).astype(bf16)
        picked = dot_nn(hot, prob_ref[s])
        gate_s[rows, :] = jnp.broadcast_to(
            picked[:, e : e + 1] + picked[:, EXPERTS + e : EXPERTS + e + 1], (CAP, LANES)
        )
    loads[0].wait()
    a_s[...] = dot_nt(x_s[...], wg[...])
    loads[1].wait()
    u_s[...] = dot_nt(x_s[...], wu[...])
    loads[2].wait()
    d_s[...] = dot_nt(c_s[...], wd[...])
    const = math.sqrt(2.0 / math.pi)
    for s in range(S):
        rows = slice(s * CAP, (s + 1) * CAP)
        a, u, d0, gate = a_s[rows, :], u_s[rows, :], d_s[rows, :], gate_s[rows, 0:1]
        t = jnp.tanh(const * (a + 0.044715 * a * a * a))
        half = 0.5 * (1.0 + t)
        act = a * half
        slope = half + 0.5 * a * (1.0 - t * t) * (const * (1.0 + 3 * 0.044715 * a * a))
        hid = act * u
        dg = jnp.sum(hid * d0, axis=-1, keepdims=True)
        hid_s[rows, :] = (gate * hid).astype(bf16)
        dh = gate * d0
        da_s[rows, :] = (dh * u * slope).astype(bf16)
        du_s[rows, :] = (dh * act).astype(bf16)
        hot = (slots == pos_ref[s, e : e + 1, :]).astype(f32)
        dr[s : s + 1, :] = jnp.sum(hot * dg, axis=0, keepdims=True)
    half_w = width // 2
    core = core_ref[0]
    mine = pl.ds(pl.multiple_of(core * half_w, half_w), half_w)
    other = pl.ds(pl.multiple_of((1 - core) * half_w, half_w), half_w)
    stores = []

    def store(src, dst):
        stores.append(pltpu.make_async_copy(src, dst, sems.at[3 + len(stores)]))
        stores[-1].start()

    for left, right, buf, keep, send in (
        (hid_s, c_s, d_o, dk, ds),
        (da_s, x_s, g_o, gk, gs),
        (du_s, x_s, u_o, uk, us),
    ):
        buf[...] = dot_tn(left[...], right[...]).astype(bf16)
        store(buf.at[:, other], send)
        store(buf.at[:, mine], keep)
    ed_o[:, :width] = dot_nn(hid_s[...], wd[...]).astype(bf16)
    ed_o[:, width:] = (dot_nn(da_s[...], wg[...]) + dot_nn(du_s[...], wu[...])).astype(bf16)
    for s in range(S):
        store(ed_o.at[pl.ds(s * CAP, CAP)], eodx.at[s, pl.ds(e * CAP, CAP)])
    for copy in stores:
        copy.wait()


def ffn(e, core, pos, aux, h2, ct, w_gate, w_up, w_down, chain):
    S = len(h2)
    n, width = h2[0].shape
    cols = w_gate.shape[1]
    rows = S * CAP
    half = jax.ShapeDtypeStruct((cols, width // 2), bf16)
    shapes = [half] * 6 + [
        jax.ShapeDtypeStruct((S, EXPERTS * CAP, 2 * width), bf16),
        jax.ShapeDtypeStruct((S, n), f32),
    ]
    specs = [anywhere()] * 7 + [vmem()]
    if e == 0:
        shapes.append(jax.ShapeDtypeStruct((S, n, LANES), bf16))
        specs.append(vmem())
    return pl.pallas_call(
        functools.partial(ffn_kernel, S, e),
        in_specs=[smem()] + [vmem()] * (2 + 2 * S) + [anywhere()] * (4 if e else 3),
        out_specs=specs,
        out_shape=shapes,
        input_output_aliases={6 + 2 * S: 6} if e else {},
        scratch_shapes=[pltpu.VMEM((cols, width), bf16)] * 3
        + [pltpu.VMEM((rows, width), bf16)] * 2
        + [pltpu.VMEM((rows, LANES), f32)]
        + [pltpu.VMEM((rows, cols), f32)] * 3
        + [pltpu.VMEM((rows, cols), bf16)] * 3
        + [pltpu.VMEM((cols, width), bf16)] * 3
        + [pltpu.VMEM((rows, 2 * width), bf16), pltpu.SemaphoreType.DMA((9 + S,))],
        compiler_params=params(44),
        cost_estimate=pl.CostEstimate(
            flops=18 * rows * width * cols, bytes_accessed=20_000_000, transcendentals=0
        ),
        name=f"ffn{e}",
    )(core, pos, aux, *h2, *ct, w_gate, w_up, w_down, *([chain] if e else []))


def combine_kernel(S, pos_ref, src_ref, *outs):
    n, width = outs[0].shape
    lanes = lax.broadcasted_iota(jnp.int32, (n, EXPERTS * CAP), 1)
    s = pl.program_id(0)
    hot = lanes == pos_ref[:, 0:1]
    for e in range(1, EXPERTS):
        hot = hot | (lanes == pos_ref[:, e : e + 1])
    total = dot_nn(hot.astype(bf16), src_ref[...]).astype(bf16)
    for i in range(S):

        @pl.when(s == i)
        def _(i=i):
            outs[i][...] = total


def combine(pos_col, eodx):
    S, n = pos_col.shape[:2]
    width = eodx.shape[2]
    return pl.pallas_call(
        functools.partial(combine_kernel, S),
        grid=(S,),
        in_specs=[
            pl.BlockSpec((None, n, LANES), lambda s: (s, 0, 0)),
            pl.BlockSpec((None, EXPERTS * CAP, width), lambda s: (s, 0, 0)),
        ],
        out_specs=[pl.BlockSpec((n, width), lambda s: (0, 0))] * S,
        out_shape=[jax.ShapeDtypeStruct((n, width), bf16)] * S,
        compiler_params=params(40),
        name="combine",
    )(pos_col, eodx)


def stages_of(size):
    n = size // 2
    h = n // 2
    swap = [(i, i ^ 1) for i in range(size)]
    plan = [(swap, "add")]
    for k in range(h - 1):
        plan.append((line_perm([(k, k + 1), (n - 1 - k, n - 2 - k)]), "add"))
    plan.append((line_perm([(h - 1, h), (h, h - 1)]), "add"))
    for k in reversed(range(h - 1)):
        plan.append((line_perm([(k + 1, k), (n - 2 - k, n - 1 - k)]), k))
    plan.append((swap, "final"))
    return plan


def wave_kernel(size, kinds, *refs):
    place_ref = refs[0]
    line, core = place_ref[0], place_ref[1]
    n_in = 2 * len(kinds)
    ins = refs[1 : 1 + n_in]
    outs = refs[-len(kinds) :]
    last = size // 2 - 1
    for i, kind in enumerate(kinds):
        have, got, out = ins[2 * i], ins[2 * i + 1], outs[i]
        half = have.shape[1]
        if kind == "add":
            out[...] = (have[...].astype(f32) + got[...].astype(f32)).astype(bf16)
        elif kind == "final":
            a, b = have[...].astype(f32), got[...].astype(f32)
            out[:, :half] = jnp.where(core == 0, a, b)
            out[:, half:] = jnp.where(core == 0, b, a)
        else:
            take = (line == kind) | (line == last - kind)
            out[...] = jnp.where(take, got[...], have[...])


def row_block(rows):
    return max(b for b in range(16, min(rows, 256) + 1, 16) if rows % b == 0)


def wave(size, place, entries):
    kinds = tuple(e[0] for e in entries)
    rows, half = entries[0][1].shape
    blk = row_block(rows)
    spec = pl.BlockSpec((blk, half), lambda r: (r, 0))
    ins, outs, shapes, extra, aliases = [], [], [], [], {}
    for kind, have, got, final in entries:
        ins += [have, got]
    for i, (kind, have, got, final) in enumerate(entries):
        if kind == "final":
            expert, target = final
            outs.append(pl.BlockSpec((None, blk, 2 * half), lambda r, e=expert: (e, r, 0)))
            shapes.append(jax.ShapeDtypeStruct((EXPERTS, rows, 2 * half), f32))
            if target is not None:
                aliases[1 + len(ins) + len(extra)] = i
                extra.append(target)
        else:
            outs.append(spec)
            shapes.append(jax.ShapeDtypeStruct((rows, half), bf16))
    return pl.pallas_call(
        functools.partial(wave_kernel, size, kinds),
        grid=(rows // blk,),
        in_specs=[smem()] + [spec] * len(ins) + [anywhere()] * len(extra),
        out_specs=outs,
        out_shape=shapes,
        input_output_aliases=aliases,
        compiler_params=params(24),
        name="wave",
    )(place, *ins, *extra)


def pipelined_sums(size, place, chunks):
    plan = stages_of(size)
    targets = {}
    state = {}
    for w in range(len(chunks) + len(plan) - 1):
        entries, where = [], []
        for k in range(max(0, w - len(plan) + 1), min(w + 1, len(chunks))):
            pairs, kind = plan[w - k]
            keep, send, out, expert = chunks[k]
            have = keep if w == k else state[k]
            got = lax.ppermute(send if w == k else have, "rep", pairs)
            entries.append((kind, have, got, (expert, targets.get(out))))
            where.append((k, out, kind))
        for (k, out, kind), value in zip(where, wave(size, place, entries)):
            if kind == "final":
                targets[out] = value
            else:
                state[k] = value
    return targets


def swap_core(x, size):
    return lax.ppermute(x, "rep", [(i, i ^ 1) for i in range(size)])


def swap_shard(x, size, mask):
    return lax.ppermute(x, "shard", [(i, i ^ mask) for i in range(size)])


def line_perm(pairs):
    return [(2 * a + c, 2 * b + c) for a, b in pairs for c in range(2)]


def line_sum(x, size, line):
    n = size // 2
    h = n // 2
    for k in range(h - 1):
        x = x + lax.ppermute(x, "rep", line_perm([(k, k + 1), (n - 1 - k, n - 2 - k)]))
    x = x + lax.ppermute(x, "rep", line_perm([(h - 1, h), (h, h - 1)]))
    for k in reversed(range(h - 1)):
        got = lax.ppermute(x, "rep", line_perm([(k + 1, k), (n - 2 - k, n - 1 - k)]))
        x = jnp.where((line == k) | (line == n - 1 - k), got, x)
    return x


def rms_backward(values, scale, gain_row, upward):
    grad_gain = jnp.sum(upward * values * scale, axis=0)
    weighted = upward * gain_row
    grad_values = scale * weighted - values * scale * scale * scale * jnp.mean(
        values * weighted, axis=-1, keepdims=True
    )
    return (grad_values, grad_gain)


def bucket_of(distance):
    bucket = jnp.minimum(distance, 16)
    for border in bucket_edges:
        bucket = bucket + (distance >= border).astype(jnp.int32)
    return bucket


def slot_positions(routes, order, lengths):
    n = order.shape[1]
    valid = jnp.arange(n, dtype=jnp.int32)[None, :] < lengths[:, None]
    experts = jnp.arange(EXPERTS, dtype=jnp.int32)
    hits = (routes[:, :, :, None] == experts) & valid[:, :, None, None]
    hits = hits.reshape(routes.shape[0], n, 2 * EXPERTS)
    before = (order[:, None, :] < order[:, :, None]).astype(bf16)
    count = jnp.einsum("stk,sut->sku", hits.astype(bf16), before, preferred_element_type=f32)
    total = jnp.sum(hits[:, :, :EXPERTS].astype(f32), axis=1)
    hits = jnp.swapaxes(hits, 1, 2)
    first, second = count[:, :EXPERTS], count[:, EXPERTS:] + total[:, :, None]
    slot = jnp.where(
        hits[:, :EXPERTS], first, jnp.where(hits[:, EXPERTS:], second, float(2 * CAP + n))
    )
    return jnp.where(slot < CAP, slot, -1.0).astype(jnp.int32)


def shards(
    R,
    S,
    tokens,
    cotangent,
    lengths,
    sequence_deal,
    routes,
    fill_order,
    norm_attn,
    w_query,
    w_key,
    w_value,
    w_out,
    rel_bias,
    norm_ffn,
    w_router,
    w_gate,
    w_up,
    w_down,
):
    me = lax.axis_index("shard")
    rep = lax.axis_index("rep")
    core = rep % 2
    line = rep // 2
    x_low, ct_low = tokens[0], cotangent[0]
    n, width = x_low.shape
    part = width // S
    half = part // 2
    group = jnp.arange(S, dtype=jnp.int32)

    bias_flat = jnp.pad(rel_bias.reshape(-1), (0, part - rel_bias.size))
    small = jnp.concatenate(
        [norm_attn[:, None], norm_ffn[:, None], w_router, bias_flat[:, None]], axis=1
    )
    plan = jnp.concatenate([routes[0], fill_order[0][:, None]], axis=1)
    small_all = jnp.zeros((S,) + small.shape, bf16)
    plan_all = jnp.zeros((S,) + plan.shape, jnp.int32)
    for m in range(S):
        got_s = small if m == 0 else swap_shard(small, S, m)
        got_p = plan if m == 0 else swap_shard(plan, S, m)
        small_all = lax.dynamic_update_slice(small_all, got_s[None], (me ^ m, 0, 0))
        plan_all = lax.dynamic_update_slice(plan_all, got_p[None], (me ^ m, 0, 0))
    gain_one = small_all[:, :, 0].reshape(-1).astype(f32)
    gain_two = small_all[:, :, 1].reshape(-1).astype(f32)
    router_w = small_all[:, :, 2 : 2 + EXPERTS].reshape(width, EXPERTS)
    bias_table = small_all[:, : rel_bias.size, 2 + EXPERTS].reshape(BUCKETS, HEADS)

    low_half = [
        lax.dynamic_slice_in_dim(w, core * half, half, 0) for w in (w_query, w_key, w_value, w_out)
    ]
    stack_qkv = jnp.concatenate(low_half[:3], axis=1)
    qkv_pieces, out_pieces, offsets = [], [], []
    for stack, pieces in ((stack_qkv, qkv_pieces), (low_half[3], out_pieces)):
        for m in range(S):
            got = stack if m == 0 else swap_shard(stack, S, m)
            pieces += [got, swap_core(got, R)]
    for m in range(S):
        offsets += [2 * (me ^ m) + core, 2 * (me ^ m) + 1 - core]
    offsets = jnp.stack(offsets).astype(jnp.int32)
    ct_all = [ct_low] + [swap_shard(ct_low, S, m) for m in range(1, S)]

    deal = sequence_deal[0]
    row_of = jnp.sum(group[:, None] * (deal[:, None] == group[None, :]).astype(jnp.int32), axis=0)
    homes = me ^ group
    rows = jnp.take(row_of, homes)
    plans = jnp.take(plan_all, rows, axis=0)
    pos = slot_positions(plans[:, :, :2], plans[:, :, 2], jnp.take(lengths[0], homes))
    length = lax.dynamic_slice_in_dim(lengths[0], me, 1, 0)

    turned = jnp.arange(n, dtype=jnp.int32)
    hot = (bucket_of((n - turned) % n)[None, :] == jnp.arange(BUCKETS)[:, None]).astype(bf16)
    base = dot_tn(bias_table, hot).reshape(HEADS // 2, 2, n)

    bias = bias_of(length, base)
    normed_low, qkv, context, qkv_w = attn_fwd(offsets, x_low, gain_one[None], bias, qkv_pieces)
    middle, ffn_in, out_w = mid_of(offsets, x_low, gain_two[None], context, out_pieces)

    h2_all = [ffn_in] + [swap_shard(ffn_in, S, m) for m in range(1, S)]
    router_pad = jnp.pad(router_w, ((0, 0), (0, LANES - EXPERTS)))
    core_one = core.reshape(1).astype(jnp.int32)
    place = jnp.stack([line, core]).astype(jnp.int32)
    gate_t, up_t = jnp.swapaxes(w_gate, 1, 2), jnp.swapaxes(w_up, 1, 2)
    eodx, aux, drs, chunks = None, router_pad, [], []
    for e in range(EXPERTS):
        got = ffn(e, core_one, pos, aux, h2_all, ct_all, gate_t, up_t, w_down, eodx)
        gk, gs, uk, us, dk, ds, eodx, dr = got[:8]
        if e == 0:
            aux = got[8]
        drs.append(dr)
        chunks += [(dk, ds, 2, e), (gk, gs, 0, e), (uk, us, 1, e)]
    flat = jnp.arange(EXPERTS, dtype=jnp.int32) * CAP
    pos_col = jnp.swapaxes(jnp.where(pos < 0, -1, pos + flat[None, :, None]), 1, 2)
    pos_col = jnp.pad(pos_col, ((0, 0), (0, 0), (0, LANES - EXPERTS)))
    parts = combine(pos_col, eodx)
    dr_all = jnp.stack(drs, axis=1)
    total = parts[0].astype(f32)
    drouter = dr_all[0]
    for m in range(1, S):
        total = total + swap_shard(parts[m], S, m).astype(f32)
        drouter = drouter + swap_shard(dr_all[m], S, m)

    sums = pipelined_sums(R, place, chunks)
    gate_total, up_total, down_total = jnp.swapaxes(sums[0], 1, 2), jnp.swapaxes(sums[1], 1, 2), sums[2]

    result = middle + total[:, :width]
    upstream = ct_low.astype(f32)
    inputs = x_low.astype(f32)
    scale_one = lax.rsqrt(jnp.mean(inputs * inputs, axis=-1, keepdims=True) + eps)
    scale_two = lax.rsqrt(jnp.mean(middle * middle, axis=-1, keepdims=True) + eps)
    probs = jax.nn.softmax(dot_nn(ffn_in, router_w), axis=-1)
    drouter = drouter.T
    dlogit = probs * (drouter - jnp.sum(probs * drouter, axis=-1, keepdims=True))
    grad_ffn_in = total[:, width:] + lax.dot_general(
        dlogit,
        router_w.astype(f32),
        (((1,), (1,)), ((), ())),
        precision=lax.Precision.HIGHEST,
        preferred_element_type=f32,
    )
    grad_router_w = lax.dot_general(
        ffn_in.astype(f32),
        dlogit,
        (((0,), (0,)), ((), ())),
        precision=lax.Precision.HIGHEST,
        preferred_element_type=f32,
    )
    grad_middle, grad_gain_two = rms_backward(middle, scale_two, gain_two, grad_ffn_in)
    grad_middle = grad_middle + upstream
    grad_attn_low = grad_middle.astype(bf16)
    grad_out_w = dot_tn(context, grad_attn_low).astype(bf16)
    grad_context = dot_nt(grad_attn_low, out_w).astype(bf16)
    dq, dk, dv, diag = attn_bwd(qkv, bias, grad_context)
    grad_table = dot_nt(hot.astype(f32), diag.reshape(HEADS, n))
    dqkv = jnp.concatenate([dq, dk, dv], axis=1)
    grad_normed = dot_nt(dqkv, qkv_w)
    grad_qkv_w = dot_tn(normed_low, dqkv).astype(bf16)
    grad_inputs, grad_gain_one = rms_backward(inputs, scale_one, gain_one, grad_normed)
    grad_inputs = grad_inputs + grad_middle

    table = jnp.pad(grad_table.reshape(S, -1), ((0, 0), (0, part - rel_bias.size)))
    extra = jnp.concatenate(
        [grad_gain_one[:, None], grad_gain_two[:, None], grad_router_w, table.reshape(-1, 1)],
        axis=1,
    ).astype(bf16)
    extra = jnp.pad(extra, ((0, 0), (0, LANES - extra.shape[1])))
    dense = jnp.concatenate([grad_qkv_w, grad_out_w, extra], axis=1)
    dense = dense.reshape(S, 2, half, -1)
    keep = lax.dynamic_index_in_dim(dense, core, 1, keepdims=False)
    send = lax.dynamic_index_in_dim(dense, 1 - core, 1, keepdims=False)
    keep = keep + swap_core(send, R)
    owned = lax.dynamic_index_in_dim(keep, me, 0, keepdims=False).astype(f32)
    for m in range(1, S):
        block = lax.dynamic_index_in_dim(keep, me ^ m, 0, keepdims=False)
        owned = owned + swap_shard(block, S, m).astype(f32)
    mine = line_sum(owned.astype(bf16), R, line)
    other = swap_core(mine, R)
    dense = jnp.concatenate(
        [jnp.where(core == 0, mine, other), jnp.where(core == 0, other, mine)], axis=0
    ).astype(f32)
    extra = dense[:, 4 * width :]
    return (
        result.astype(bf16)[None],
        grad_inputs.astype(bf16)[None],
        extra[:, 0],
        dense[:, :width],
        dense[:, width : 2 * width],
        dense[:, 2 * width : 3 * width],
        dense[:, 3 * width : 4 * width],
        extra[: rel_bias.size, 2 + EXPERTS].reshape(rel_bias.shape),
        extra[:, 1],
        extra[:, 2 : 2 + EXPERTS],
        gate_total,
        up_total,
        down_total,
    )


def solution(mesh):
    R, S = mesh.shape["rep"], mesh.shape["shard"]
    rows = P(("rep", "shard"), None, None)
    mat = P("shard", None)
    return jax.shard_map(
        functools.partial(shards, R, S),
        mesh=mesh,
        in_specs=(rows, rows, P("rep", None), P("rep", None), rows, P(("rep", "shard"), None))
        + (P("shard"), mat, mat, mat, mat, mat, P("shard"), mat)
        + (P(None, None, "shard"), P(None, None, "shard"), P(None, "shard", None)),
        out_specs=(rows, rows, P("shard"), mat, mat, mat, mat, mat, P("shard"), mat)
        + (P(None, None, "shard"), P(None, None, "shard"), P(None, "shard", None)),
        check_vma=False,
    )
```

time: 2570 us -> 774 us (0.30)
  waiting for transfers between devices: 1860 us -> 336 us
  matrix products: 367 us -> 15.6 us
  Pallas kernels: 0 us -> 162 us
  starting transfers between devices: 3.03 us -> 160 us
  local copies, waits for them, and re-layouts: 144 us -> 72.2 us
  other arithmetic: 91 us -> 20.7 us
  blocking collectives: 64.3 us -> 0 us
    all_gather x20 -> x0, waiting for transfers between devices: 806 us -> none  [the longest x4 247 us: shards(): lax.all_gather(w_up[expert], 'shard', axis=1, tiled=True)]
    reduce_scatter x16 -> x0, waiting for transfers between devices: 648 us -> none  [the longest x4 269 us: shards(): lax.psum_scatter(grad_down_w.astype(jnp.bfloat16), 'shard', scatter_dimen...]
    psum x1 -> x0, waiting for transfers between devices: 389 us -> none  [shards(): lax.psum(owned_parts[1].astype(jnp.bfloat16), 'rep').astype(jnp.float32)]
    dot_general x211 -> x10, matrix products: 367 us -> 15.6 us  [the longest x3 7.21 us: dot_nt(): lax.dot_general(a, b, (((1,), (1,)), ((), ())), preferred_element_type=f32)]
    ppermute x0 -> x100, waiting for transfers between devices: none -> 336 us  [the longest x60 195 us: pipelined_sums(): got = lax.ppermute(send if w == k else have, 'rep', pairs)]
    pallas_call x0 -> x25, Pallas kernels: none -> 162 us  [the longest x4 74.8 us: ffn(): pl.pallas_call(functools.partial(ffn_kernel, S, e), in_specs=[smem()] + [...]
    ppermute x0 -> x100, starting transfers between devices: none -> 160 us  [the longest x60 119 us: pipelined_sums(): got = lax.ppermute(send if w == k else have, 'rep', pairs)]
    convert_element_type x66 -> x2, other arithmetic: 52.9 us -> 2.98 us  [the longest x1 2.38 us: shards(): dense = jnp.concatenate([jnp.where(core == 0, mine, other), jnp.where(cor...]
  transfers between devices with their start and end apart: 38 -> 100, of which waited for: 30 -> 35; matrix products, arithmetic and copies ran while one was open for 22% -> 10% of each run, Pallas kernels for 0% -> 10%
where the time goes in v1:
time: 774 us; the launch traced here: 769 us
  waiting for transfers between devices  336 us (43%)
  Pallas kernels  162 us (21%)
  starting transfers between devices  160 us (21%)
  local copies, waits for them, and re-layouts  72.2 us (9%)
  other arithmetic  20.7 us (3%)
  matrix products  15.6 us (2%)
    ppermute x60, waiting for transfers between devices, pipelined_sums(): got = lax.ppermute(send if w == k else have, 'rep', pairs)  195 us
    ppermute x27, waiting for transfers between devices, swap_shard(): return lax.ppermute(x, 'shard', [(i, i ^ mask) for i in range(size)])  123 us
    ppermute x60, starting transfers between devices, pipelined_sums(): got = lax.ppermute(send if w == k else have, 'rep', pairs)  119 us
    pallas_call x4, Pallas kernels, ffn(): pl.pallas_call(functools.partial(ffn_kernel, S, e), in_specs=[smem()] + [...  74.8 us
    pallas_call x16, Pallas kernels, wave(): pl.pallas_call(functools.partial(wave_kernel, size, kinds), grid=(rows //...  48.5 us
    unnamed x170, local copies, waits for them, and re-layouts  38.3 us
    ppermute x27, starting transfers between devices, swap_shard(): return lax.ppermute(x, 'shard', [(i, i ^ mask) for i in range(size)])  36 us
    ppermute x1, waiting for transfers between devices, line_sum(): lax.ppermute(x, 'rep', line_perm([(k, k + 1), (n - 1 - k, n - 2 - k)]))  18.5 us
  transfers between devices with their start and end apart: 100, of which 35 were waited for; matrix products, arithmetic and copies ran while one was open for 10% of the time, Pallas kernels for 10%

profile of v1, /device:TPU:0, one launch (start us, length us, event | category | flops | bytes accessed | tf_op | source)
XLA Modules:
  0.0 768.8 jit_solution(1302310618390949291)
XLA Ops:
  18.3 25.7 %collective-permute-done.1 = bf16[256,7]{0,1:T(8,128)(2,1)S(1)} collective-permute-done((bf16[256,7]{0,1:T(8,128)(2,1)S(1)}, bf16[256,7]{0,1:T(8,128)(2,1)S(1)}, u32[]{:S(2)}, u32[]{:S(2)}) %collective-permute-start.1) | collective-permute-done | bytes 3616 | tf_op jit(solution)/shard_map/ppermute | solution.py:477
  73.7 14.0 %attn_fwd.1 = (bf16[256,1024]{1,0:T(8,128)(2,1)S(1)}, bf16[256,3072]{1,0:T(8,128)(2,1)S(1)}, bf16[256,1024]{1,0:T(8,128)(2,1)S(1)}, bf16[1024,3072]{1,0:T(8,128)(2,1)S(1)}) custom-call(s32[8]{0:T(128)S(1)} %stack.57.refs_0_, bf16[256,1024]{1,0:T(8,128)(2,1)S(1)} %bitcast.140, f32[1,1024]{1,0:T(1,128)S(1)} %bitcast.143, ...), custom_call_target="tpu_custom_call" | custom-call | tf_op jit(solution)/shard_map/attn_fwd/pallas_call | solution.py:138
  105.9 10.7 %collective-permute-done.22.refs_6_ = bf16[256,1024]{1,0:T(8,128)(2,1)} collective-permute-done((bf16[256,1024]{1,0:T(8,128)(2,1)S(1)}, bf16[256,1024]{1,0:T(8,128)(2,1)}, u32[]{:S(2)}, u32[]{:S(2)}) %collective-permute-start.22) | collective-permute-done | bytes 524320 | tf_op jit(solution)/shard_map/ppermute | solution.py:477
  116.6 8.8 %collective-permute-done.21.refs_5_ = bf16[256,1024]{1,0:T(8,128)(2,1)} collective-permute-done((bf16[256,1024]{1,0:T(8,128)(2,1)S(1)}, bf16[256,1024]{1,0:T(8,128)(2,1)}, u32[]{:S(2)}, u32[]{:S(2)}) %collective-permute-start.21) | collective-permute-done | bytes 524320 | tf_op jit(solution)/shard_map/ppermute | solution.py:477
  126.8 19.1 %ffn0.1 = (bf16[704,512]{1,0:T(8,128)(2,1)S(1)}, bf16[704,512]{1,0:T(8,128)(2,1)}, bf16[704,512]{1,0:T(8,128)(2,1)S(1)}, bf16[704,512]{1,0:T(8,128)(2,1)}, bf16[...) custom-call(s32[1]{0:T(128)} %bitcast.28.refs_0_, ...), custom_call_target="tpu_custom_call" | custom-call | flops 7474249728 | bytes 20000000 | tf_op jit(solution)/shard_map/ffn0/pallas_call | solution.py:328
  147.7 18.6 %ffn1.1 = (bf16[704,512]{1,0:T(8,128)(2,1)S(1)}, bf16[704,512]{1,0:T(8,128)(2,1)S(1)}, bf16[704,512]{1,0:T(8,128)(2,1)S(1)}, bf16[704,512]{1,0:T(8,128)(2,1)S(1)...) custom-call(s32[1]{0:T(128)} %bitcast.28.refs_0_, ...), custom_call_target="tpu_custom_call", output_to_operand_aliasing={{6}: (14, {})} | custom-call | flops 7474249728 | bytes 20000000 | tf_op jit(solution)/shard_map/ffn1/pallas_call | solution.py:328
  170.7 18.5 %ffn2.1 = (bf16[704,512]{1,0:T(8,128)(2,1)S(1)}, bf16[704,512]{1,0:T(8,128)(2,1)S(1)}, bf16[704,512]{1,0:T(8,128)(2,1)S(1)}, bf16[704,512]{1,0:T(8,128)(2,1)S(1)...) custom-call(s32[1]{0:T(128)} %bitcast.28.refs_0_, ...), custom_call_target="tpu_custom_call", output_to_operand_aliasing={{6}: (14, {})} | custom-call | flops 7474249728 | bytes 20000000 | tf_op jit(solution)/shard_map/ffn2/pallas_call | solution.py:328
  194.5 18.6 %ffn3.1 = (bf16[704,512]{1,0:T(8,128)(2,1)S(1)}, bf16[704,512]{1,0:T(8,128)(2,1)S(1)}, bf16[704,512]{1,0:T(8,128)(2,1)S(1)}, bf16[704,512]{1,0:T(8,128)(2,1)S(1)...) custom-call(s32[1]{0:T(128)} %bitcast.28.refs_0_, ...), custom_call_target="tpu_custom_call", output_to_operand_aliasing={{6}: (14, {})} | custom-call | flops 7474249728 | bytes 20000000 | tf_op jit(solution)/shard_map/ffn3/pallas_call | solution.py:328
  231.9 42.5 %collective-permute-done.30 = f32[4,256]{1,0:T(4,128)S(1)} collective-permute-done((f32[4,256]{1,0:T(4,128)S(1)}, f32[4,256]{1,0:T(4,128)S(1)}, u32[]{:S(2)}, u32[]{:S(2)}) %collective-permute-start.30) | collective-permute-done | bytes 4128 | tf_op jit(solution)/shard_map/ppermute | solution.py:477
  296.6 13.9 %attn_bwd.1 = (bf16[256,1024]{1,0:T(8,128)(2,1)S(1)}, bf16[256,1024]{1,0:T(8,128)(2,1)S(1)}, bf16[256,1024]{1,0:T(8,128)(2,1)S(1)}, f32[8,2,256]{2,1,0:T(2,128)S(1)}) custom-call(bf16[256,3072]{1,0:T(8,128)(2,1)S(1)} %copy-done.4, bf16[256,3072]{1,0:T(8,128)(2,1)S(1)} %copy-done.4, bf16[256,3072]{1,0:T(8,128)(2,1)S(1)} %copy-done.4, ...), custom_call_target="tpu_custom_call" | custom-call | tf_op jit(solution)/shard_map/attn_bwd/pallas_call | solution.py:212
  336.3 6.6 copy.177
  358.0 11.1 %collective-permute-done.46.refs_2_ = bf16[704,512]{1,0:T(8,128)(2,1)S(1)} collective-permute-done((bf16[704,512]{1,0:T(8,128)(2,1)S(1)}, bf16[704,512]{1,0:T(8,128)(2,1)S(1)}, u32[]{:S(2)}, u32[]{:S(2)}) %collective-permute-start.46) | collective-permute-done | bytes 720928 | tf_op jit(solution)/shard_map/ppermute | solution.py:461
  377.0 7.4 collective-permute-start.53
  384.5 11.0 %collective-permute-done.51.refs_4_ = bf16[704,512]{1,0:T(8,128)(2,1)S(1)} collective-permute-done((bf16[704,512]{1,0:T(8,128)(2,1)S(1)}, bf16[704,512]{1,0:T(8,128)(2,1)S(1)}, u32[]{:S(2)}, u32[]{:S(2)}) %collective-permute-start.51) | collective-permute-done | bytes 720928 | tf_op jit(solution)/shard_map/ppermute | solution.py:461
  411.2 12.1 %collective-permute-done.56.refs_4_ = bf16[704,512]{1,0:T(8,128)(2,1)S(1)} collective-permute-done((bf16[704,512]{1,0:T(8,128)(2,1)S(1)}, bf16[704,512]{1,0:T(8,128)(2,1)S(1)}, u32[]{:S(2)}, u32[]{:S(2)}) %collective-permute-start.56) | collective-permute-done | bytes 720928 | tf_op jit(solution)/shard_map/ppermute | solution.py:461
  432.5 8.2 %collective-permute-start.63 = (bf16[704,512]{1,0:T(8,128)(2,1)}, bf16[704,512]{1,0:T(8,128)(2,1)}, u32[]{:S(2)}, u32[]{:S(2)}) collective-permute-start(bf16[704,512]{1,0:T(8,128)(2,1)} %get-tuple-element.172.refs_7_), channel_id=1, source_target_pairs={{0,8},{4,12},{24,16},{28,20},{1,9},{5,13},{25,17},{29,21},{2,10},{... | collective-permute-start | bytes 2162696 | tf_op jit(solution)/shard_map/ppermute | solution.py:461
  440.8 6.5 copy.176
  469.5 11.9 %collective-permute-done.66.refs_4_ = bf16[704,512]{1,0:T(8,128)(2,1)S(1)} collective-permute-done((bf16[704,512]{1,0:T(8,128)(2,1)S(1)}, bf16[704,512]{1,0:T(8,128)(2,1)S(1)}, u32[]{:S(2)}, u32[]{:S(2)}) %collective-permute-start.66) | collective-permute-done | bytes 720928 | tf_op jit(solution)/shard_map/ppermute | solution.py:461
  483.1 15.2 %collective-permute-done.68.refs_8_ = bf16[704,512]{1,0:T(8,128)(2,1)S(1)} collective-permute-done((bf16[704,512]{1,0:T(8,128)(2,1)S(1)}, bf16[704,512]{1,0:T(8,128)(2,1)S(1)}, u32[]{:S(2)}, u32[]{:S(2)}) %collective-permute-start.68) | collective-permute-done | bytes 720928 | tf_op jit(solution)/shard_map/ppermute | solution.py:461
  502.4 13.3 %collective-permute-done.35 = bf16[128,4224]{0,1:T(8,128)(2,1)S(1)} collective-permute-done((bf16[128,4224]{0,1:T(8,128)(2,1)S(1)}, bf16[128,4224]{0,1:T(8,128)(2,1)S(1)}, u32[]{:S(2)}, u32[]{:S(2)}) %collective-permute-start.35) | collective-permute-done | bytes 1081376 | tf_op jit(solution)/shard_map/ppermute | solution.py:477
  524.8 14.4 %collective-permute-done.73.refs_8_ = bf16[704,512]{1,0:T(8,128)(2,1)S(1)} collective-permute-done((bf16[704,512]{1,0:T(8,128)(2,1)S(1)}, bf16[704,512]{1,0:T(8,128)(2,1)S(1)}, u32[]{:S(2)}, u32[]{:S(2)}) %collective-permute-start.73) | collective-permute-done | bytes 720928 | tf_op jit(solution)/shard_map/ppermute | solution.py:461
  542.1 18.5 %collective-permute-done.36 = bf16[128,4224]{0,1:T(8,128)(2,1)S(1)} collective-permute-done((bf16[128,4224]{0,1:T(8,128)(2,1)S(1)}, bf16[128,4224]{0,1:T(8,128)(2,1)S(1)}, u32[]{:S(2)}, u32[]{:S(2)}) %collective-permute-start.36) | collective-permute-done | bytes 1081376 | tf_op jit(solution)/shard_map/ppermute | solution.py:488
  563.6 8.9 %collective-permute-start.78 = (bf16[704,512]{1,0:T(8,128)(2,1)S(1)}, bf16[704,512]{1,0:T(8,128)(2,1)S(1)}, u32[]{:S(2)}, u32[]{:S(2)}) collective-permute-start(bf16[704,512]{1,0:T(8,128)(2,1)S(1)} %get-tuple-element.192.refs_7_), channel_id=1, source_target_pairs={{0,8},{4,12},{24,16},{28,20},{1,9},{5,13},{25,17},{29,21},{2,10},{... | collective-permute-start | bytes 2162696 | tf_op jit(solution)/shard_map/ppermute | solution.py:461
  572.6 9.8 %collective-permute-done.76.refs_4_ = bf16[704,512]{1,0:T(8,128)(2,1)S(1)} collective-permute-done((bf16[704,512]{1,0:T(8,128)(2,1)S(1)}, bf16[704,512]{1,0:T(8,128)(2,1)S(1)}, u32[]{:S(2)}, u32[]{:S(2)}) %collective-permute-start.76) | collective-permute-done | bytes 720928 | tf_op jit(solution)/shard_map/ppermute | solution.py:461
  590.7 23.8 %collective-permute-start.83 = (bf16[704,512]{1,0:T(8,128)(2,1)S(1)}, bf16[704,512]{1,0:T(8,128)(2,1)S(1)}, u32[]{:S(2)}, u32[]{:S(2)}) collective-permute-start(bf16[704,512]{1,0:T(8,128)(2,1)S(1)} %get-tuple-element.199.refs_7_), channel_id=1, source_target_pairs={{0,8},{4,12},{24,16},{28,20},{1,9},{5,13},{25,17},{29,21},{2,10},{... | collective-permute-start | bytes 2162696 | tf_op jit(solution)/shard_map/ppermute | solution.py:461
  617.2 8.8 %collective-permute-done.81.refs_4_ = bf16[704,512]{1,0:T(8,128)(2,1)S(1)} collective-permute-done((bf16[704,512]{1,0:T(8,128)(2,1)S(1)}, bf16[704,512]{1,0:T(8,128)(2,1)S(1)}, u32[]{:S(2)}, u32[]{:S(2)}) %collective-permute-start.81) | collective-permute-done | bytes 720928 | tf_op jit(solution)/shard_map/ppermute | solution.py:461
  635.9 7.1 collective-permute-start.88
  643.0 21.3 %collective-permute-done.86.refs_4_ = bf16[704,512]{1,0:T(8,128)(2,1)} collective-permute-done((bf16[704,512]{1,0:T(8,128)(2,1)S(1)}, bf16[704,512]{1,0:T(8,128)(2,1)}, u32[]{:S(2)}, u32[]{:S(2)}) %collective-permute-start.86) | collective-permute-done | bytes 720928 | tf_op jit(solution)/shard_map/ppermute | solution.py:461
  671.0 7.4 collective-permute-start.93
  680.8 8.6 %collective-permute-done.91.refs_4_ = bf16[704,512]{1,0:T(8,128)(2,1)S(1)} collective-permute-done((bf16[704,512]{1,0:T(8,128)(2,1)S(1)}, bf16[704,512]{1,0:T(8,128)(2,1)S(1)}, u32[]{:S(2)}, u32[]{:S(2)}) %collective-permute-start.91) | collective-permute-done | bytes 720928 | tf_op jit(solution)/shard_map/ppermute | solution.py:461
  702.1 15.1 %collective-permute-done.95.refs_4_ = bf16[704,512]{1,0:T(8,128)(2,1)} collective-permute-done((bf16[704,512]{1,0:T(8,128)(2,1)S(1)}, bf16[704,512]{1,0:T(8,128)(2,1)}, u32[]{:S(2)}, u32[]{:S(2)}) %collective-permute-start.95) | collective-permute-done | bytes 720928 | tf_op jit(solution)/shard_map/ppermute | solution.py:461
  724.2 19.6 %collective-permute-done.98.refs_4_ = bf16[704,512]{1,0:T(8,128)(2,1)S(1)} collective-permute-done((bf16[704,512]{1,0:T(8,128)(2,1)S(1)}, bf16[704,512]{1,0:T(8,128)(2,1)S(1)}, u32[]{:S(2)}, u32[]{:S(2)}) %collective-permute-start.98) | collective-permute-done | bytes 720928 | tf_op jit(solution)/shard_map/ppermute | solution.py:461
  (473 shorter events, 309.3 us)
Async XLA Ops:
  7.2 46.7 %collective-permute-start.8 = (bf16[128,3072]{1,0:T(8,128)(2,1)S(1)}, bf16[128,3072]{1,0:T(8,128)(2,1)S(1)}, u32[]{:S(2)}, u32[]{:S(2)}) collective-permute-start(bf16[128,3072]{1,0:T(8,128)(2,1)S(1)} %pad_maximum_fusion.refs_4_), channel_id=1, source_target_pairs={{0,3},{1,2},{2,1},{3,0},{4,7},{5,6},{6,5},{7,4},{8,11},{9,10},{10,... | collective-permute-start | bytes 2359304 | tf_op jit(solution)/shard_map/ppermute | solution.py:477
  10.2 45.2 %collective-permute-start.6 = (bf16[128,3072]{1,0:T(8,128)(2,1)S(1)}, bf16[128,3072]{1,0:T(8,128)(2,1)}, u32[]{:S(2)}, u32[]{:S(2)}) collective-permute-start(bf16[128,3072]{1,0:T(8,128)(2,1)S(1)} %pad_maximum_fusion.refs_4_), channel_id=1, source_target_pairs={{0,2},{1,3},{2,0},{3,1},{4,6},{5,7},{6,4},{7,5},{8,10},{9,11},{10,... | collective-permute-start | bytes 2359304 | tf_op jit(solution)/shard_map/ppermute | solution.py:477
  13.7 41.7 %collective-permute-start.4 = (bf16[128,3072]{1,0:T(8,128)(2,1)S(1)}, bf16[128,3072]{1,0:T(8,128)(2,1)}, u32[]{:S(2)}, u32[]{:S(2)}) collective-permute-start(bf16[128,3072]{1,0:T(8,128)(2,1)S(1)} %pad_maximum_fusion.refs_4_), channel_id=1, source_target_pairs={{0,1},{1,0},{2,3},{3,2},{4,5},{5,4},{6,7},{7,6},{8,9},{9,8},{10,11... | collective-permute-start | bytes 2359304 | tf_op jit(solution)/shard_map/ppermute | solution.py:477
  14.8 29.2 %collective-permute-start.1 = (bf16[256,7]{0,1:T(8,128)(2,1)S(1)}, bf16[256,7]{0,1:T(8,128)(2,1)S(1)}, u32[]{:S(2)}, u32[]{:S(2)}) collective-permute-start(bf16[256,7]{0,1:T(8,128)(2,1)S(1)} %pad_maximum_fusion.3), channel_id=1, source_target_pairs={{0,2},{1,3},{2,0},{3,1},{4,6},{5,7},{6,4},{7,5},{8,10},{9,11},{10,... | collective-permute-start | bytes 10760 | tf_op jit(solution)/shard_map/ppermute | solution.py:477
  16.8 28.9 %collective-permute-start = (bf16[256,7]{0,1:T(8,128)(2,1)S(1)}, bf16[256,7]{0,1:T(8,128)(2,1)S(1)}, u32[]{:S(2)}, u32[]{:S(2)}) collective-permute-start(bf16[256,7]{0,1:T(8,128)(2,1)S(1)} %pad_maximum_fusion.3), channel_id=1, source_target_pairs={{0,1},{1,0},{2,3},{3,2},{4,5},{5,4},{6,7},{7,6},{8,9},{9,8},{10,11... | collective-permute-start | bytes 10760 | tf_op jit(solution)/shard_map/ppermute | solution.py:477
  68.3 31.1 %collective-permute-start.25 = (bf16[256,1024]{1,0:T(8,128)(2,1)S(1)}, bf16[256,1024]{1,0:T(8,128)(2,1)}, u32[]{:S(2)}, u32[]{:S(2)}) collective-permute-start(bf16[256,1024]{1,0:T(8,128)(2,1)S(1)} %bitcast.133), channel_id=1, source_target_pairs={{0,3},{1,2},{2,1},{3,0},{4,7},{5,6},{6,5},{7,4},{8,11},{9,10},{10,... | collective-permute-start | bytes 1572872 | tf_op jit(solution)/shard_map/ppermute | solution.py:477
  227.6 57.9 %collective-permute-start.26 = (bf16[256,2048]{1,0:T(8,128)(2,1)S(1)}, bf16[256,2048]{1,0:T(8,128)(2,1)S(1)}, u32[]{:S(2)}, u32[]{:S(2)}) collective-permute-start(bf16[256,2048]{1,0:T(8,128)(2,1)S(1)} %get-tuple-element.129), channel_id=1, source_target_pairs={{0,1},{1,0},{2,3},{3,2},{4,5},{5,4},{6,7},{7,6},{8,9},{9,8},{10,11... | collective-permute-start | bytes 3145736 | tf_op jit(solution)/shard_map/ppermute | solution.py:477
  228.0 57.6 %collective-permute-start.27 = (bf16[256,2048]{1,0:T(8,128)(2,1)S(1)}, bf16[256,2048]{1,0:T(8,128)(2,1)S(1)}, u32[]{:S(2)}, u32[]{:S(2)}) collective-permute-start(bf16[256,2048]{1,0:T(8,128)(2,1)S(1)} %get-tuple-element.130), channel_id=1, source_target_pairs={{0,2},{1,3},{2,0},{3,1},{4,6},{5,7},{6,4},{7,5},{8,10},{9,11},{10,... | collective-permute-start | bytes 3145736 | tf_op jit(solution)/shard_map/ppermute | solution.py:477
  229.6 60.3 %collective-permute-start.28 = (bf16[256,2048]{1,0:T(8,128)(2,1)S(1)}, bf16[256,2048]{1,0:T(8,128)(2,1)S(1)}, u32[]{:S(2)}, u32[]{:S(2)}) collective-permute-start(bf16[256,2048]{1,0:T(8,128)(2,1)S(1)} %get-tuple-element.131), channel_id=1, source_target_pairs={{0,3},{1,2},{2,1},{3,0},{4,7},{5,6},{6,5},{7,4},{8,11},{9,10},{10,... | collective-permute-start | bytes 3145736 | tf_op jit(solution)/shard_map/ppermute | solution.py:477
  231.2 43.3 %collective-permute-start.30 = (f32[4,256]{1,0:T(4,128)S(1)}, f32[4,256]{1,0:T(4,128)S(1)}, u32[]{:S(2)}, u32[]{:S(2)}) collective-permute-start(f32[4,256]{1,0:T(4,128)S(1)} %bitcast.179), channel_id=1, source_target_pairs={{0,2},{1,3},{2,0},{3,1},{4,6},{5,7},{6,4},{7,5},{8,10},{9,11},{10,... | collective-permute-start | bytes 12296 | tf_op jit(solution)/shard_map/ppermute | solution.py:477
  231.8 51.1 %collective-permute-start.40 = (bf16[704,512]{1,0:T(8,128)(2,1)S(1)}, bf16[704,512]{1,0:T(8,128)(2,1)S(1)}, u32[]{:S(2)}, u32[]{:S(2)}) collective-permute-start(bf16[704,512]{1,0:T(8,128)(2,1)S(1)} %get-tuple-element.145), channel_id=1, source_target_pairs={{0,4},{4,0},{8,12},{12,8},{16,20},{20,16},{24,28},{28,24},{1,5},{5... | collective-permute-start | bytes 2162696 | tf_op jit(solution)/shard_map/ppermute | solution.py:461
  282.5 41.7 %collective-permute-start.42 = (bf16[704,512]{1,0:T(8,128)(2,1)}, bf16[704,512]{1,0:T(8,128)(2,1)}, u32[]{:S(2)}, u32[]{:S(2)}) collective-permute-start(bf16[704,512]{1,0:T(8,128)(2,1)} %get-tuple-element.147), channel_id=1, source_target_pairs={{0,4},{4,0},{8,12},{12,8},{16,20},{20,16},{24,28},{28,24},{1,5},{5... | collective-permute-start | bytes 2162696 | tf_op jit(solution)/shard_map/ppermute | solution.py:461
  282.9 60.0 %collective-permute-start.45 = (bf16[704,512]{1,0:T(8,128)(2,1)}, bf16[704,512]{1,0:T(8,128)(2,1)}, u32[]{:S(2)}, u32[]{:S(2)}) collective-permute-start(bf16[704,512]{1,0:T(8,128)(2,1)} %get-tuple-element.151), channel_id=1, source_target_pairs={{0,4},{4,0},{8,12},{12,8},{16,20},{20,16},{24,28},{28,24},{1,5},{5... | collective-permute-start | bytes 2162696 | tf_op jit(solution)/shard_map/ppermute | solution.py:461
  285.5 72.4 %collective-permute-start.49 = (bf16[704,512]{1,0:T(8,128)(2,1)}, bf16[704,512]{1,0:T(8,128)(2,1)}, u32[]{:S(2)}, u32[]{:S(2)}) collective-permute-start(bf16[704,512]{1,0:T(8,128)(2,1)} %get-tuple-element.156), channel_id=1, source_target_pairs={{0,4},{4,0},{8,12},{12,8},{16,20},{20,16},{24,28},{28,24},{1,5},{5... | collective-permute-start | bytes 2162696 | tf_op jit(solution)/shard_map/ppermute | solution.py:461
  285.5 38.7 %collective-permute-start.41 = (bf16[704,512]{1,0:T(8,128)(2,1)}, bf16[704,512]{1,0:T(8,128)(2,1)}, u32[]{:S(2)}, u32[]{:S(2)}) collective-permute-start(bf16[704,512]{1,0:T(8,128)(2,1)} %wave.16.refs_1_), channel_id=1, source_target_pairs={{0,8},{4,12},{24,16},{28,20},{1,9},{5,13},{25,17},{29,21},{2,10},{... | collective-permute-start | bytes 2162696 | tf_op jit(solution)/shard_map/ppermute | solution.py:461
  342.9 119.2 %collective-permute-start.32 = (bf16[4,128,4224]{1,2,0:T(8,128)(2,1)}, bf16[4,128,4224]{1,2,0:T(8,128)(2,1)}, u32[]{:S(2)}, u32[]{:S(2)}) collective-permute-start(bf16[4,128,4224]{1,2,0:T(8,128)(2,1)} %bitcast.160), channel_id=1, source_target_pairs={{0,4},{4,0},{8,12},{12,8},{16,20},{20,16},{24,28},{28,24},{1,5},{5... | collective-permute-start | bytes 12976136 | tf_op jit(solution)/shard_map/ppermute | solution.py:473
  465.2 35.9 %collective-permute-start.33 = (bf16[128,4224]{0,1:T(8,128)(2,1)S(1)}, bf16[128,4224]{0,1:T(8,128)(2,1)S(1)}, u32[]{:S(2)}, u32[]{:S(2)}) collective-permute-start(bf16[128,4224]{0,1:T(8,128)(2,1)S(1)} %get-tuple-element.307), channel_id=1, source_target_pairs={{0,1},{1,0},{2,3},{3,2},{4,5},{5,4},{6,7},{7,6},{8,9},{9,8},{10,11... | collective-permute-start | bytes 3244040 | tf_op jit(solution)/shard_map/ppermute | solution.py:477
  466.8 48.9 %collective-permute-start.35 = (bf16[128,4224]{0,1:T(8,128)(2,1)S(1)}, bf16[128,4224]{0,1:T(8,128)(2,1)S(1)}, u32[]{:S(2)}, u32[]{:S(2)}) collective-permute-start(bf16[128,4224]{0,1:T(8,128)(2,1)S(1)} %get-tuple-element.308), channel_id=1, source_target_pairs={{0,3},{1,2},{2,1},{3,0},{4,7},{5,6},{6,5},{7,4},{8,11},{9,10},{10,... | collective-permute-start | bytes 3244040 | tf_op jit(solution)/shard_map/ppermute | solution.py:477
  468.2 48.9 %collective-permute-start.34 = (bf16[128,4224]{0,1:T(8,128)(2,1)S(1)}, bf16[128,4224]{0,1:T(8,128)(2,1)S(1)}, u32[]{:S(2)}, u32[]{:S(2)}) collective-permute-start(bf16[128,4224]{0,1:T(8,128)(2,1)S(1)} %get-tuple-element.309), channel_id=1, source_target_pairs={{0,2},{1,3},{2,0},{3,1},{4,6},{5,7},{6,4},{7,5},{8,10},{9,11},{10,... | collective-permute-start | bytes 3244040 | tf_op jit(solution)/shard_map/ppermute | solution.py:477
  483.0 40.3 %collective-permute-start.74 = (bf16[704,512]{1,0:T(8,128)(2,1)S(1)}, bf16[704,512]{1,0:T(8,128)(2,1)S(1)}, u32[]{:S(2)}, u32[]{:S(2)}) collective-permute-start(bf16[704,512]{1,0:T(8,128)(2,1)S(1)} %copy-done.53), channel_id=1, source_target_pairs={{0,4},{4,0},{8,12},{12,8},{16,20},{20,16},{24,28},{28,24},{1,5},{5... | collective-permute-start | bytes 2162696 | tf_op jit(solution)/shard_map/ppermute | solution.py:461
  523.3 37.3 %collective-permute-start.36 = (bf16[128,4224]{0,1:T(8,128)(2,1)S(1)}, bf16[128,4224]{0,1:T(8,128)(2,1)S(1)}, u32[]{:S(2)}, u32[]{:S(2)}) collective-permute-start(bf16[128,4224]{0,1:T(8,128)(2,1)S(1)} %fusion.4), channel_id=1, source_target_pairs={{0,8},{4,12},{24,16},{28,20},{1,9},{5,13},{25,17},{29,21},{2,10},{... | collective-permute-start | bytes 3244040 | tf_op jit(solution)/shard_map/ppermute | solution.py:488
  524.7 38.9 %collective-permute-start.79 = (bf16[704,512]{1,0:T(8,128)(2,1)S(1)}, bf16[704,512]{1,0:T(8,128)(2,1)S(1)}, u32[]{:S(2)}, u32[]{:S(2)}) collective-permute-start(bf16[704,512]{1,0:T(8,128)(2,1)S(1)} %copy-done.51), channel_id=1, source_target_pairs={{0,4},{4,0},{8,12},{12,8},{16,20},{20,16},{24,28},{28,24},{1,5},{5... | collective-permute-start | bytes 2162696 | tf_op jit(solution)/shard_map/ppermute | solution.py:461
  542.1 30.5 %collective-permute-start.75 = (bf16[704,512]{1,0:T(8,128)(2,1)S(1)}, bf16[704,512]{1,0:T(8,128)(2,1)S(1)}, u32[]{:S(2)}, u32[]{:S(2)}) collective-permute-start(bf16[704,512]{1,0:T(8,128)(2,1)S(1)} %get-tuple-element.189.refs_1_), channel_id=1, source_target_pairs={{0,4},{4,0},{8,12},{12,8},{16,20},{20,16},{24,28},{28,24},{1,5},{5... | collective-permute-start | bytes 2162696 | tf_op jit(solution)/shard_map/ppermute | solution.py:461
  560.9 53.7 %collective-permute-start.37 = (bf16[128,4224]{0,1:T(8,128)(2,1)S(1)}, bf16[128,4224]{0,1:T(8,128)(2,1)S(1)}, u32[]{:S(2)}, u32[]{:S(2)}) collective-permute-start(bf16[128,4224]{0,1:T(8,128)(2,1)S(1)} %add.362), channel_id=1, source_target_pairs={{8,16},{12,20},{16,8},{20,12},{9,17},{13,21},{17,9},{21,13},{10,18... | collective-permute-start | bytes 3244040 | tf_op jit(solution)/shard_map/ppermute | solution.py:489
  588.5 37.4 %collective-permute-start.81 = (bf16[704,512]{1,0:T(8,128)(2,1)S(1)}, bf16[704,512]{1,0:T(8,128)(2,1)S(1)}, u32[]{:S(2)}, u32[]{:S(2)}) collective-permute-start(bf16[704,512]{1,0:T(8,128)(2,1)S(1)} %get-tuple-element.197.refs_3_), channel_id=1, source_target_pairs={{8,0},{12,4},{16,24},{20,28},{9,1},{13,5},{17,25},{21,29},{10,2},{... | collective-permute-start | bytes 2162696 | tf_op jit(solution)/shard_map/ppermute | solution.py:461
  590.0 36.0 %collective-permute-start.82 = (bf16[704,512]{1,0:T(8,128)(2,1)S(1)}, bf16[704,512]{1,0:T(8,128)(2,1)S(1)}, u32[]{:S(2)}, u32[]{:S(2)}) collective-permute-start(bf16[704,512]{1,0:T(8,128)(2,1)S(1)} %get-tuple-element.198.refs_5_), channel_id=1, source_target_pairs={{8,16},{12,20},{16,8},{20,12},{9,17},{13,21},{17,9},{21,13},{10,18... | collective-permute-start | bytes 2162696 | tf_op jit(solution)/shard_map/ppermute | solution.py:461
  590.7 39.4 %collective-permute-start.83 = (bf16[704,512]{1,0:T(8,128)(2,1)S(1)}, bf16[704,512]{1,0:T(8,128)(2,1)S(1)}, u32[]{:S(2)}, u32[]{:S(2)}) collective-permute-start(bf16[704,512]{1,0:T(8,128)(2,1)S(1)} %get-tuple-element.199.refs_7_), channel_id=1, source_target_pairs={{0,8},{4,12},{24,16},{28,20},{1,9},{5,13},{25,17},{29,21},{2,10},{... | collective-permute-start | bytes 2162696 | tf_op jit(solution)/shard_map/ppermute | solution.py:461
  615.9 62.5 %collective-permute-start.38 = (bf16[128,4224]{0,1:T(8,128)(2,1)}, bf16[128,4224]{0,1:T(8,128)(2,1)}, u32[]{:S(2)}, u32[]{:S(2)}) collective-permute-start(bf16[128,4224]{0,1:T(8,128)(2,1)} %add.363), channel_id=1, source_target_pairs={{8,0},{12,4},{16,24},{20,28},{9,1},{13,5},{17,25},{21,29},{10,2},{... | collective-permute-start | bytes 3244040 | tf_op jit(solution)/shard_map/ppermute | solution.py:491
  633.1 31.3 %collective-permute-start.86 = (bf16[704,512]{1,0:T(8,128)(2,1)S(1)}, bf16[704,512]{1,0:T(8,128)(2,1)}, u32[]{:S(2)}, u32[]{:S(2)}) collective-permute-start(bf16[704,512]{1,0:T(8,128)(2,1)S(1)} %get-tuple-element.204.refs_3_), channel_id=1, source_target_pairs={{8,0},{12,4},{16,24},{20,28},{9,1},{13,5},{17,25},{21,29},{10,2},{... | collective-permute-start | bytes 2162696 | tf_op jit(solution)/shard_map/ppermute | solution.py:461
  634.4 30.0 %collective-permute-start.87 = (bf16[704,512]{1,0:T(8,128)(2,1)}, bf16[704,512]{1,0:T(8,128)(2,1)}, u32[]{:S(2)}, u32[]{:S(2)}) collective-permute-start(bf16[704,512]{1,0:T(8,128)(2,1)} %get-tuple-element.205.refs_5_), channel_id=1, source_target_pairs={{8,16},{12,20},{16,8},{20,12},{9,17},{13,21},{17,9},{21,13},{10,18... | collective-permute-start | bytes 2162696 | tf_op jit(solution)/shard_map/ppermute | solution.py:461
  635.9 28.5 %collective-permute-start.88 = (bf16[704,512]{1,0:T(8,128)(2,1)}, bf16[704,512]{1,0:T(8,128)(2,1)}, u32[]{:S(2)}, u32[]{:S(2)}) collective-permute-start(bf16[704,512]{1,0:T(8,128)(2,1)} %get-tuple-element.206.refs_7_), channel_id=1, source_target_pairs={{0,8},{4,12},{24,16},{28,20},{1,9},{5,13},{25,17},{29,21},{2,10},{... | collective-permute-start | bytes 2162696 | tf_op jit(solution)/shard_map/ppermute | solution.py:461
  680.8 41.7 %collective-permute-start.39 = (bf16[128,4224]{0,1:T(8,128)(2,1)}, bf16[128,4224]{0,1:T(8,128)(2,1)}, u32[]{:S(2)}, u32[]{:S(2)}) collective-permute-start(bf16[128,4224]{0,1:T(8,128)(2,1)} %broadcast_select_fusion), channel_id=1, source_target_pairs={{0,4},{4,0},{8,12},{12,8},{16,20},{20,16},{24,28},{28,24},{1,5},{5... | collective-permute-start | bytes 3244040 | tf_op jit(solution)/shard_map/ppermute | solution.py:473
  (145 other events, 1955.1 us)

commit v2 on v1

v2 whole, which is shorter than its diff:
```python
import functools
import math

import jax
import jax.numpy as jnp
from jax import lax
from jax.experimental import pallas as pl
from jax.experimental.pallas import tpu as pltpu
from jax.sharding import PartitionSpec as P

HEADS = 16
HEAD_DIM = 64
EXPERTS = 4
BUCKETS = 32
CAP = 144
LANES = 128

eps = 1e-06
bucket_edges = [int(math.ceil(16.0 * 8.0 ** (level / 16.0))) for level in range(1, 16)]
bf16 = jnp.bfloat16
f32 = jnp.float32


def dot_nn(a, b):
    return lax.dot_general(a, b, (((1,), (0,)), ((), ())), preferred_element_type=f32)


def dot_nt(a, b):
    return lax.dot_general(a, b, (((1,), (1,)), ((), ())), preferred_element_type=f32)


def dot_tn(a, b):
    return lax.dot_general(a, b, (((0,), (0,)), ((), ())), preferred_element_type=f32)


def params(mib):
    return pltpu.CompilerParams(vmem_limit_bytes=mib * 1024 * 1024)


def vmem():
    return pl.BlockSpec(memory_space=pltpu.VMEM)


def anywhere():
    return pl.BlockSpec(memory_space=pl.ANY)


TOKEN = jax.ShapeDtypeStruct((8, LANES), f32)


def token_spec():
    return pl.BlockSpec((8, LANES), lambda *i: (0, 0))


def give(token):
    token[...] = jnp.zeros(token.shape, token.dtype)


def short():
    return pl.CostEstimate(flops=1, bytes_accessed=1, transcendentals=0)


def hbm():
    return pl.BlockSpec(memory_space=pltpu.HBM)


def pin(x):
    return pltpu.with_memory_space_constraint(x, pltpu.HBM)


def smem():
    return pl.BlockSpec(memory_space=pltpu.SMEM)


def bias_kernel(len_ref, base_ref, out_ref):
    n = base_ref.shape[2]
    rows = lax.broadcasted_iota(jnp.int32, (n, n), 0)
    cols = lax.broadcasted_iota(jnp.int32, (n, n), 1)
    allowed = (cols <= rows) & (cols < len_ref[0])
    for h in range(2):
        row = jnp.broadcast_to(base_ref[0, h : h + 1, :], (n, n))
        bias = pltpu.roll(row, 0, 1, stride=1, stride_axis=0)
        out_ref[h] = jnp.where(allowed, bias, -1000000000.0).astype(bf16)


def bias_of(length, base):
    pairs, _, n = base.shape
    return pl.pallas_call(
        bias_kernel,
        grid_spec=pltpu.PrefetchScalarGridSpec(
            num_scalar_prefetch=1,
            grid=(pairs,),
            in_specs=[pl.BlockSpec((1, 2, n), lambda i, l: (i, 0, 0))],
            out_specs=pl.BlockSpec((2, n, n), lambda i, l: (i, 0, 0)),
        ),
        out_shape=jax.ShapeDtypeStruct((2 * pairs, n, n), bf16),
        compiler_params=params(60),
        name="bias",
    )(length, base)


def softmax_of(q, k, bias):
    s = dot_nt(q, k) * 0.125 + bias.astype(f32)
    e = jnp.exp(s - jnp.max(s, axis=-1, keepdims=True))
    return e * (1.0 / jnp.sum(e, axis=-1, keepdims=True))


def attn_fwd_kernel(N, *refs):
    off_ref, x_ref, gain_ref, bias_ref = refs[:4]
    own, pieces = refs[4:8], refs[8 : 8 + N]
    h_ref, qkv_ref, c_ref, wout_ref, w_s, sem = refs[8 + N :]
    width = x_ref.shape[1]
    unit = min(piece.shape[0] for piece in pieces)
    first = pl.multiple_of(off_ref[N] * unit, unit)
    for j in range(4):
        w_s[pl.ds(first, own[j].shape[0]), j * width : (j + 1) * width] = own[j][...]
    for p, piece in enumerate(pieces):
        start = pl.multiple_of(off_ref[p] * unit, unit)
        w_s[pl.ds(start, piece.shape[0]), :] = piece[...]
    out = pltpu.make_async_copy(w_s, wout_ref, sem)
    out.start()
    x = x_ref[...].astype(f32)
    scale = lax.rsqrt(jnp.mean(x * x, axis=-1, keepdims=True) + eps)
    h_ref[...] = (x * scale * gain_ref[...]).astype(bf16)
    step = width // 2

    def project(i, carry):
        cut = pl.ds(pl.multiple_of(i * step, step), step)
        qkv_ref[:, cut] = dot_nn(h_ref[...], w_s[:, cut]).astype(bf16)
        return carry

    lax.fori_loop(0, 3 * width // step, project, 0)

    def pair(i, carry):
        def at(j):
            return pl.ds(pl.multiple_of(j * width + i * LANES, LANES), LANES)

        q2, k2, v2 = qkv_ref[:, at(0)], qkv_ref[:, at(1)], qkv_ref[:, at(2)]
        heads = []
        for h in range(2):
            cut = slice(h * HEAD_DIM, (h + 1) * HEAD_DIM)
            p = softmax_of(q2[:, cut], k2[:, cut], bias_ref[2 * i + h]).astype(bf16)
            heads.append(dot_nn(p, v2[:, cut]).astype(bf16))
        c_ref[:, at(0)] = jnp.concatenate(heads, axis=1)
        return carry

    lax.fori_loop(0, HEADS // 2, pair, 0)
    out.wait()


def attn_fwd(offsets, x, gain, bias, own, pieces):
    n, width = x.shape
    N = len(pieces)
    full = jax.ShapeDtypeStruct((n, width), bf16)
    return pl.pallas_call(
        functools.partial(attn_fwd_kernel, N),
        in_specs=[smem(), vmem(), vmem(), vmem()] + [vmem()] * (4 + N),
        out_specs=[vmem(), vmem(), vmem(), hbm()],
        out_shape=[
            full,
            jax.ShapeDtypeStruct((n, 3 * width), bf16),
            full,
            pltpu.HBM((width, 4 * width), bf16),
        ],
        scratch_shapes=[pltpu.VMEM((width, 4 * width), bf16), pltpu.SemaphoreType.DMA],
        compiler_params=params(60),
        cost_estimate=short(),
        name="attn_fwd",
    )(offsets, x, gain, bias, *own, *pieces)


def mid_kernel(x_ref, gain_ref, c_ref, w_hbm, *refs):
    mid_ref, h_ref, w_s, sem = refs[-4:]
    width = x_ref.shape[1]
    load = pltpu.make_async_copy(w_hbm.at[:, pl.ds(3 * width, width)], w_s, sem)
    load.start()
    load.wait()
    mid = x_ref[...].astype(f32) + dot_nn(c_ref[...], w_s[...])
    scale = lax.rsqrt(jnp.mean(mid * mid, axis=-1, keepdims=True) + eps)
    mid_ref[...] = mid
    h_ref[...] = (mid * scale * gain_ref[...]).astype(bf16)


def mid_of(x, gain, context, weights, tokens):
    n, width = x.shape
    return pl.pallas_call(
        mid_kernel,
        in_specs=[vmem(), vmem(), vmem(), hbm()] + [anywhere()] * len(tokens),
        out_specs=[vmem(), vmem()],
        out_shape=[
            jax.ShapeDtypeStruct((n, width), f32),
            jax.ShapeDtypeStruct((n, width), bf16),
        ],
        scratch_shapes=[pltpu.VMEM((width, width), bf16), pltpu.SemaphoreType.DMA],
        compiler_params=params(60),
        cost_estimate=short(),
        name="middle",
    )(x, gain, context, weights, *tokens)


def attn_bwd_kernel(q_ref, k_ref, v_ref, bias_ref, dc_ref, *refs):
    dq_ref, dk_ref, dv_ref, diag_ref, token = refs[-5:]
    give(token)
    n = q_ref.shape[0]
    rows = lax.broadcasted_iota(jnp.int32, (n, n), 0)
    cols = lax.broadcasted_iota(jnp.int32, (n, n), 1)
    reverse = (rows + cols == n - 1).astype(bf16)
    for h in range(2):
        cut = slice(h * HEAD_DIM, (h + 1) * HEAD_DIM)
        q, k, v, dc = q_ref[:, cut], k_ref[:, cut], v_ref[:, cut], dc_ref[:, cut]
        p = softmax_of(q, k, bias_ref[h])
        dp = dot_nt(dc, v)
        ds = p * (dp - jnp.sum(p * dp, axis=-1, keepdims=True))
        low = ds.astype(bf16)
        dq_ref[:, cut] = (dot_nn(low, k) * 0.125).astype(bf16)
        dk_ref[:, cut] = (dot_tn(low, q) * 0.125).astype(bf16)
        dv_ref[:, cut] = dot_tn(p.astype(bf16), dc).astype(bf16)
        turned = pltpu.roll(dot_nn(reverse, low), 1, 1, stride=1, stride_axis=0)
        diag_ref[0, h : h + 1, :] = jnp.sum(turned, axis=0, keepdims=True)


def attn_bwd(qkv, bias, dc, tokens):
    n = qkv.shape[0]
    pairs = HEADS // 2
    blk = pl.BlockSpec((n, LANES), lambda i: (0, i))
    row = pl.BlockSpec((1, 2, n), lambda i: (i, 0, 0))
    full = jax.ShapeDtypeStruct((n, HEADS * HEAD_DIM), bf16)
    return pl.pallas_call(
        attn_bwd_kernel,
        grid=(pairs,),
        in_specs=[
            blk,
            pl.BlockSpec((n, LANES), lambda i: (0, pairs + i)),
            pl.BlockSpec((n, LANES), lambda i: (0, 2 * pairs + i)),
            pl.BlockSpec((2, n, n), lambda i: (i, 0, 0)),
            blk,
        ]
        + [anywhere()] * len(tokens),
        out_specs=[blk, blk, blk, row, token_spec()],
        out_shape=[full, full, full, jax.ShapeDtypeStruct((pairs, 2, n), f32), TOKEN],
        compiler_params=params(60),
        cost_estimate=short(),
        name="attn_bwd",
    )(qkv, qkv, qkv, bias, dc, *tokens)


def rows_of(refs):
    return refs[0][...] if len(refs) == 1 else jnp.concatenate([r[...] for r in refs], axis=0)


def ffn_kernel(shape, experts, groups, n_after, *refs):
    S, n_seq, first = len(shape), sum(shape), experts[0] == 0
    where_ref, pos_ref, aux_ref = refs[:3]
    refs = refs[3:]

    def sequences(parts):
        out, at = [], 0
        for count in shape:
            out.append(parts[at : at + count])
            at += count
        return out

    h2, ct = sequences(refs[:n_seq]), sequences(refs[n_seq : 2 * n_seq])
    refs = refs[2 * n_seq :]
    w_hbm = refs[:3]
    refs = refs[3 + n_after + (0 if first else 2) :]
    keeps, sends, (e_all, d_all, token) = refs[0], refs[1 : 1 + len(groups)], refs[1 + len(groups) : 4 + len(groups)]
    give(token)
    refs = refs[4 + len(groups) :]
    where_to = [(g, k) for g, size in enumerate(groups) for k in range(size)]
    if first:
        prob_ref, refs = refs[0], refs[1:]
    else:
        prob_ref = aux_ref
    w_v, x_s, c_s, gate_s, a_s, u_s, d_s, hid_s, da_s, du_s, o_s, eo_s, dx_s, sem_l, sem_s = refs
    n, width = pos_ref.shape[2], x_s.shape[1]
    loads = [[] for _ in experts]
    for i, e in enumerate(experts):
        for j in range(3):
            copy = pltpu.make_async_copy(w_hbm[j].at[e], w_v.at[i, j], sem_l.at[i, j])
            copy.start()
            loads[i].append(copy)
    lanes = lax.broadcasted_iota(jnp.int32, (n, LANES), 1)
    slot_lanes = lax.broadcasted_iota(jnp.int32, (CAP, LANES), 1)
    slots = lax.broadcasted_iota(jnp.int32, (CAP, n), 0)
    if first:
        for s in range(S):
            logits = jnp.where(lanes < EXPERTS, dot_nn(rows_of(h2[s]), aux_ref[...]), -1e30)
            ex = jnp.exp(logits - jnp.max(logits, axis=-1, keepdims=True))
            prob = ex / jnp.sum(ex, axis=-1, keepdims=True)
            high = prob.astype(bf16).astype(f32)
            rest = pltpu.roll(prob - high, EXPERTS, 1)
            prob_ref[s] = jnp.where(lanes < EXPERTS, high, rest).astype(bf16)
    half_w = width // 2
    core = where_ref[1]
    mine = pl.ds(pl.multiple_of(core * half_w, half_w), half_w)
    other = pl.ds(pl.multiple_of((1 - core) * half_w, half_w), half_w)
    const = math.sqrt(2.0 / math.pi)
    pending = {}

    def store(key, i, j, src, dst):
        copy = pltpu.make_async_copy(src, dst, sem_s.at[i, j])
        copy.start()
        pending.setdefault(key, []).append(copy)

    def settle(key):
        for copy in pending.pop(key, []):
            copy.wait()

    for i, e in enumerate(experts):
        wg, wu, wd = w_v.at[i, 0], w_v.at[i, 1], w_v.at[i, 2]
        for s in range(S):
            rows = slice(s * CAP, (s + 1) * CAP)
            hot = (slots == pos_ref[s, e : e + 1, :]).astype(bf16)
            x_s[rows, :] = dot_nn(hot, rows_of(h2[s])).astype(bf16)
            c_s[rows, :] = dot_nn(hot, rows_of(ct[s])).astype(bf16)
            picked = dot_nn(hot, prob_ref[s])
            gate_s[rows, :] = jnp.broadcast_to(
                picked[:, e : e + 1] + picked[:, EXPERTS + e : EXPERTS + e + 1], (CAP, LANES)
            )
        loads[i][0].wait()
        a_s[...] = dot_nt(x_s[...], wg[...])
        loads[i][1].wait()
        u_s[...] = dot_nt(x_s[...], wu[...])
        loads[i][2].wait()
        d_s[...] = dot_nt(c_s[...], wd[...])
        settle("dx")
        for s in range(S):
            rows = slice(s * CAP, (s + 1) * CAP)
            a, u, d0, gate = a_s[rows, :], u_s[rows, :], d_s[rows, :], gate_s[rows, 0:1]
            t = jnp.tanh(const * (a + 0.044715 * a * a * a))
            half = 0.5 * (1.0 + t)
            act = a * half
            slope = half + 0.5 * a * (1.0 - t * t) * (const * (1.0 + 3 * 0.044715 * a * a))
            hid = act * u
            dg = jnp.sum(hid * d0, axis=-1, keepdims=True)
            hid_s[rows, :] = (gate * hid).astype(bf16)
            dh = gate * d0
            da_s[rows, :] = (dh * u * slope).astype(bf16)
            du_s[rows, :] = (dh * act).astype(bf16)
            dx_s[rows, width:] = jnp.where(slot_lanes == e, dg, 0.0).astype(bf16)
        for j, (left, right) in enumerate(((hid_s, c_s), (da_s, x_s), (du_s, x_s))):
            settle(j)
            o_s[j] = dot_tn(left[...], right[...]).astype(bf16)
            g, k = where_to[3 * i + j]
            store(j, i, 2 * j, o_s.at[j, :, other], sends[g].at[k])
            store(j, i, 2 * j + 1, o_s.at[j, :, mine], keeps.at[3 * i + j])
        settle("eo")
        eo_s[...] = dot_nn(hid_s[...], wd[...]).astype(bf16)
        for s in range(S):
            rows = pl.ds(s * CAP, CAP)
            store("eo", i, 6 + s, eo_s.at[rows], e_all.at[s, pl.ds(e * CAP, CAP)])
        dx_s[:, :width] = (dot_nn(da_s[...], wg[...]) + dot_nn(du_s[...], wu[...])).astype(bf16)
        for s in range(S):
            rows = pl.ds(s * CAP, CAP)
            store("dx", i, 6 + S + s, dx_s.at[rows], d_all.at[s, pl.ds(e * CAP, CAP)])
    for key in list(pending):
        settle(key)


def ffn(experts, groups, core, pos, aux, h2, ct, weights, chain, after):
    shape = tuple(len(blocks) for blocks in h2)
    S, n_seq, N = len(shape), sum(shape), len(experts)
    n = pos.shape[2]
    cols, width = weights[0].shape[1:]
    rows = S * CAP
    first = experts[0] == 0
    shapes = [pltpu.HBM((k, cols, width // 2), bf16) for k in (3 * N,) + groups] + [
        pltpu.HBM((S, EXPERTS * CAP, width), bf16),
        pltpu.HBM((S, EXPERTS * CAP, width + LANES), bf16),
        TOKEN,
    ]
    M = 1 + len(groups)
    specs = [hbm()] * (M + 2) + [vmem()]
    if first:
        shapes.append(jax.ShapeDtypeStruct((S, n, LANES), bf16))
        specs.append(vmem())
    at = 6 + 2 * n_seq + len(after)
    return pl.pallas_call(
        functools.partial(ffn_kernel, shape, experts, groups, len(after)),
        in_specs=[smem()]
        + [vmem()] * (2 + 2 * n_seq)
        + [hbm()] * 3
        + [anywhere()] * len(after)
        + [hbm()] * (0 if first else 2),
        out_specs=specs,
        out_shape=shapes,
        input_output_aliases={} if first else {at: M, at + 1: M + 1},
        scratch_shapes=[pltpu.VMEM((N, 3, cols, width), bf16)]
        + [pltpu.VMEM((rows, width), bf16)] * 2
        + [pltpu.VMEM((rows, LANES), f32)]
        + [pltpu.VMEM((rows, cols), f32)] * 3
        + [pltpu.VMEM((rows, cols), bf16)] * 3
        + [pltpu.VMEM((3, cols, width), bf16)]
        + [pltpu.VMEM((rows, width), bf16), pltpu.VMEM((rows, width + LANES), bf16)]
        + [pltpu.SemaphoreType.DMA((N, 3)), pltpu.SemaphoreType.DMA((N, 6 + 2 * S))],
        compiler_params=params(60),
        cost_estimate=short(),
        name=f"ffn{experts[0]}",
    )(
        core,
        pos,
        aux,
        *[b for blocks in h2 for b in blocks],
        *[b for blocks in ct for b in blocks],
        *weights,
        *after,
        *([] if first else [pin(x) for x in chain]),
    )


def combine_kernel(me_ref, pos_ref, src_ref, *refs):
    out, token = refs[-2:]
    give(token)
    n = pos_ref.shape[0]
    lanes = lax.broadcasted_iota(jnp.int32, (n, EXPERTS * CAP), 1)
    hot = lanes == pos_ref[:, 0:1]
    for e in range(1, EXPERTS):
        hot = hot | (lanes == pos_ref[:, e : e + 1])
    out[...] = dot_nn(hot.astype(bf16), src_ref[...]).astype(bf16)


def combine(me, pos_col, src, tokens):
    S, n = pos_col.shape[:2]
    width = src.shape[2]
    out, token = pl.pallas_call(
        combine_kernel,
        grid_spec=pltpu.PrefetchScalarGridSpec(
            num_scalar_prefetch=1,
            grid=(S,),
            in_specs=[
                pl.BlockSpec((None, n, LANES), lambda s, me: (s, 0, 0)),
                pl.BlockSpec((None, EXPERTS * CAP, width), lambda s, me: (s, 0, 0)),
            ]
            + [anywhere()] * len(tokens),
            out_specs=[
                pl.BlockSpec((None, n, width), lambda s, me: (jnp.bitwise_xor(me[0], s), 0, 0)),
                token_spec(),
            ],
        ),
        out_shape=[jax.ShapeDtypeStruct((S, n, width), bf16), TOKEN],
        compiler_params=params(60),
        cost_estimate=short(),
        name="combine",
    )(me, pos_col, src, *tokens)
    return out, [token]


PANEL = 512


def split_rows(src, core, S, keep, send, sems):
    half, panels = src.shape[0] // (2 * S), src.shape[1] // PANEL
    copies = []
    for m in range(S):
        for c, dest in enumerate((keep, send)):
            who = core if c == 0 else 1 - core
            start = pl.multiple_of((2 * m + who) * half, half)
            for p in range(panels):
                copies.append(
                    pltpu.make_async_copy(
                        src.at[pl.ds(start, half), pl.ds(p * PANEL, PANEL)],
                        dest.at[m, pl.ds(p * half, half)],
                        sems.at[(2 * m + c) * panels + p],
                    )
                )
                copies[-1].start()
    return copies


def hi_lo(x):
    high = x.astype(bf16)
    return high, (x - high.astype(f32)).astype(bf16)


def sum_columns(x):
    ones = jnp.ones((x.shape[0], LANES), bf16)
    high, rest = hi_lo(x)
    return dot_tn(high, ones) + dot_tn(rest, ones)


def back_mid_kernel(S, *refs):
    core_ref, mid_ref, ct_ref, gain_ref, h2_ref, wr_ref, c_ref, wo_hbm = refs[:8]
    parts_ref = refs[8]
    dmid_ref, dc_ref, extra_ref, keep, send, token, wo, go_s, sem_w, sems = refs[-10:]
    give(token)
    n, width = mid_ref.shape
    load = pltpu.make_async_copy(wo_hbm.at[:, pl.ds(3 * width, width)], wo, sem_w)
    load.start()

    dh = parts_ref[0].astype(f32)
    for m in range(1, S):
        dh = dh + parts_ref[m].astype(f32)
    lanes = lax.broadcasted_iota(jnp.int32, (n, LANES), 1)
    logits = jnp.where(lanes < EXPERTS, dot_nn(h2_ref[...], wr_ref[...]), -1e30)
    ex = jnp.exp(logits - jnp.max(logits, axis=-1, keepdims=True))
    prob = ex / jnp.sum(ex, axis=-1, keepdims=True)
    drouter = dh[:, width:]
    dlogit = prob * (drouter - jnp.sum(prob * drouter, axis=-1, keepdims=True))
    high, rest = hi_lo(dlogit)
    dh2 = dh[:, :width] + dot_nt(high, wr_ref[...]) + dot_nt(rest, wr_ref[...])
    grad_router = dot_tn(h2_ref[...], high) + dot_tn(h2_ref[...], rest)
    mid = mid_ref[...]
    scale = lax.rsqrt(jnp.mean(mid * mid, axis=-1, keepdims=True) + eps)
    weighted = dh2 * gain_ref[...]
    dz = scale * weighted - mid * (scale * scale * scale) * jnp.mean(
        mid * weighted, axis=-1, keepdims=True
    )
    dmid = ct_ref[...].astype(f32) + dz
    dmid_ref[...] = dmid
    low = dmid.astype(bf16)
    go_s[...] = dot_tn(c_ref[...], low).astype(bf16)
    copies = split_rows(go_s, core_ref[0], S, keep, send, sems)
    load.wait()
    dc_ref[...] = dot_nt(low, wo[...]).astype(bf16)
    wide = lax.broadcasted_iota(jnp.int32, (width, LANES), 1)
    gain_column = sum_columns(dh2 * mid * scale)
    extra_ref[...] = jnp.where(wide == 1, gain_column, pltpu.roll(grad_router, 2, 1))
    for copy in copies:
        copy.wait()


def back_mid(core, S, mid, ct, gain, h2, router_w, context, out_w, parts, tokens):
    n, width = mid.shape
    panels = width // PANEL
    part = pltpu.HBM((S, panels * width // (2 * S), PANEL), bf16)
    return pl.pallas_call(
        functools.partial(back_mid_kernel, S),
        in_specs=[smem()]
        + [vmem()] * 6
        + [hbm()]
        + [vmem()]
        + [anywhere()] * len(tokens),
        out_specs=[vmem(), vmem(), vmem(), hbm(), hbm(), vmem()],
        out_shape=[
            jax.ShapeDtypeStruct((n, width), f32),
            jax.ShapeDtypeStruct((n, width), bf16),
            jax.ShapeDtypeStruct((width, LANES), f32),
            part,
            part,
            TOKEN,
        ],
        scratch_shapes=[
            pltpu.VMEM((width, width), bf16),
            pltpu.VMEM((width, width), bf16),
            pltpu.SemaphoreType.DMA,
            pltpu.SemaphoreType.DMA((2 * S * panels,)),
        ],
        compiler_params=params(60),
        cost_estimate=short(),
        name="back_mid",
    )(core, mid, ct, gain, h2, router_w, context, out_w, parts, *tokens)


def back_in_kernel(S, *refs):
    core_ref, x_ref, gain_ref, h_ref, dq_ref, dk_ref, dv_ref, diag_ref, hot_ref = refs[:9]
    extra_ref, dmid_ref, w_hbm = refs[9:12]
    dx_ref, keep, send, token, w_s, g_s, sem_w, sems = refs[-8:]
    give(token)
    n, width = x_ref.shape
    load = pltpu.make_async_copy(w_hbm.at[:, pl.ds(0, 3 * width)], w_s, sem_w)
    load.start()
    for j, d_ref in enumerate((dq_ref, dk_ref, dv_ref)):
        g_s[:, j * width : (j + 1) * width] = dot_tn(h_ref[...], d_ref[...]).astype(bf16)
    load.wait()
    dh = dot_nt(dq_ref[...], w_s[:, :width])
    dh = dh + dot_nt(dk_ref[...], w_s[:, width : 2 * width])
    dh = dh + dot_nt(dv_ref[...], w_s[:, 2 * width :])
    x = x_ref[...].astype(f32)
    scale = lax.rsqrt(jnp.mean(x * x, axis=-1, keepdims=True) + eps)
    wide = lax.broadcasted_iota(jnp.int32, (width, LANES), 1)
    extra = jnp.where(wide == 0, sum_columns(dh * x * scale), extra_ref[...])
    end = 3 * width + LANES
    g_s[:, 3 * width : end] = jnp.where(wide < 2 + EXPERTS, extra, 0.0).astype(bf16)
    g_s[:, end:] = jnp.zeros((width, PANEL - LANES), bf16)
    diag = jnp.concatenate(
        [jnp.zeros((8, n), f32), diag_ref[...], jnp.zeros((LANES - 8 - HEADS, n), f32)], axis=0
    )
    high, rest = hi_lo(diag)
    table = dot_nt(hot_ref[...], high) + dot_nt(hot_ref[...], rest)
    part, count = width // S, BUCKETS // S
    places = lax.broadcasted_iota(jnp.int32, (16, BUCKETS), 0)
    buckets = lax.broadcasted_iota(jnp.int32, (16, BUCKETS), 1)
    high, rest = hi_lo(table)
    for s in range(S):
        pick = ((places < count) & (buckets == places + s * count)).astype(bf16)
        rows = dot_nn(pick, high) + dot_nn(pick, rest)
        rows = rows + g_s[s * part : s * part + 16, 3 * width : end].astype(f32)
        g_s[s * part : s * part + 16, 3 * width : end] = rows.astype(bf16)
    copies = split_rows(g_s, core_ref[0], S, keep, send, sems)
    weighted = dh * gain_ref[...]
    dz = scale * weighted - x * (scale * scale * scale) * jnp.mean(
        x * weighted, axis=-1, keepdims=True
    )
    dx_ref[...] = (dz + dmid_ref[...]).astype(bf16)
    for copy in copies:
        copy.wait()


def back_in(core, S, x, gain, h1, dq, dk, dv, diag, hot, extra, dmid, qkv_w, tokens):
    n, width = x.shape
    cols = 3 * width + PANEL
    panels = cols // PANEL
    part = pltpu.HBM((S, panels * width // (2 * S), PANEL), bf16)
    return pl.pallas_call(
        functools.partial(back_in_kernel, S),
        in_specs=[smem()] + [vmem()] * 10 + [hbm()] + [anywhere()] * len(tokens),
        out_specs=[vmem(), hbm(), hbm(), vmem()],
        out_shape=[jax.ShapeDtypeStruct((n, width), bf16), part, part, TOKEN],
        scratch_shapes=[
            pltpu.VMEM((width, 3 * width), bf16),
            pltpu.VMEM((width, cols), bf16),
            pltpu.SemaphoreType.DMA,
            pltpu.SemaphoreType.DMA((2 * S * panels,)),
        ],
        compiler_params=params(60),
        cost_estimate=short(),
        name="back_in",
    )(core, x, gain, h1, dq, dk, dv, diag, hot, extra, dmid, qkv_w, *tokens)


def wave_kernel(shapes_in, shapes_out, *refs):
    place_ref = refs[0]
    line, core = place_ref[0], place_ref[1]
    inner = (line == 1) | (line == 2)
    get = dict(zip(shapes_in, refs[1:]))
    put = dict(zip(shapes_out, refs[len(refs) - len(shapes_out) :]))
    give(put["token"])

    def add(a, b):
        return (get[a][...].astype(f32) + get[b][...].astype(f32)).astype(bf16)

    if "mid" in put:
        put["mid"][...] = add("s0", "got_pair")
    if "core" in put:
        put["core"][...] = jnp.where(inner, get["pair"][...], get["got_pair"][...])
    new = None
    if "keep" in get:
        new = add("keep", "recv") if "recv" in get else get["keep"][...]
    full = add("mid", "got_mid") if "mid" in get else None
    if new is not None:
        put["s0"][...] = new
    if "pair" in put:
        if new is None or full is None:
            put["pair"][...] = full if new is None else new
        else:
            put["pair"][...] = jnp.where(inner, full, new)
    if "final" in put:
        a, b = get["core"][...].astype(f32), get["got_core"][...].astype(f32)
        half = a.shape[1]
        put["final"][:, :half] = jnp.where(core == 0, a, b)
        put["final"][:, half:] = jnp.where(core == 0, b, a)


class Sums:
    def __init__(self, size, place):
        self.size, self.place = size, place
        self.line = size // 2 == 4
        self.queues = [[], []]
        self.state = [{}, {}]
        self.ids = [{}, {}]
        self.turn = 0
        self.added = 0
        self.final = None
        self.targets = {}
        self.last = []

    def add(self, keep, k, recv, j, name, expert):
        if self.line:
            self.queues[self.added % 2].append((keep, k, recv, j, name, expert))
            self.added += 1
            return
        mine = line_sum((keep[k].astype(f32) + recv[j].astype(f32)).astype(bf16), self.size)
        other = swap_core(mine, self.size)
        first = self.place[1] == 0
        whole = jnp.concatenate([jnp.where(first, mine, other), jnp.where(first, other, mine)], 1)
        if name not in self.targets:
            self.targets[name] = jnp.zeros((EXPERTS,) + whole.shape, f32)
        self.targets[name] = self.targets[name].at[expert].set(whole.astype(f32))

    def busy(self):
        return any(self.queues) or any(self.state) or self.final is not None

    def step(self, more=()):
        self.last = self.last + list(more)
        stream = self.turn
        self.turn = 1 - stream
        queue, state, ids = self.queues[stream], self.state[stream], self.ids[stream]
        rep_axis = "rep"
        ins, outs = {}, []
        if "s0" in state or "pair" in state:
            pairs = line_perm([(0, 1), (1, 0), (2, 3), (3, 2)])
            ins["got_pair"] = lax.ppermute(state["pair"], rep_axis, pairs)
        if "mid" in state:
            ins["mid"] = state["mid"]
            ins["got_mid"] = lax.ppermute(state["mid"], rep_axis, line_perm([(1, 2), (2, 1)]))
        new_ids = {}
        if "in" in ids:
            ins["s0"] = state["s0"]
            outs.append("mid")
            new_ids["mid"] = ids["in"]
        if "out" in ids:
            ins["pair"] = state["pair"]
            outs.append("core")
        if "mid" in ids:
            new_ids["out"] = ids["mid"]
        if queue:
            keep, k, recv, j, name, expert = queue.pop(0)
            ins["keep"] = (keep, k)
            if recv is not None:
                ins["recv"] = (recv, j)
            outs.append("s0")
            new_ids["in"] = (name, expert)
        if "in" in new_ids or "out" in new_ids:
            outs.append("pair")
        if self.final is not None:
            value, (name, expert) = self.final
            ins["core"] = value
            ins["got_core"] = swap_core(value, self.size)
            outs.append("final")
        if not outs:
            self.state[stream] = {}
            return
        result = self.kernel(ins, outs, self.final[1] if self.final is not None else None)
        if self.final is not None:
            self.targets[self.final[1][0]] = result["final"]
        self.final = (result["core"], ids["out"]) if "core" in outs else None
        self.last = [result["token"]]
        self.state[stream] = {key: result[key] for key in ("s0", "mid", "pair") if key in outs}
        self.ids[stream] = new_ids

    def kernel(self, ins, outs, final):
        arrays, specs = [], []
        rows, cols = next(
            (x[0].shape[1:] if isinstance(x, tuple) else x.shape) for x in ins.values()
        )
        steps = max(g for g in (1, 2, 4) if rows % (16 * g) == 0)
        spec = pl.BlockSpec((rows // steps, cols), lambda r: (r, 0))
        for x in ins.values():
            if isinstance(x, tuple):
                arrays.append(pin(x[0]))
                specs.append(
                    pl.BlockSpec((None, rows // steps, cols), lambda r, k=x[1]: (k, r, 0))
                )
            else:
                arrays.append(pin(x))
                specs.append(spec)
        shape = pltpu.HBM((rows, cols), bf16)
        out_specs, out_shapes, extra, aliases = [], [], [], {}
        for i, key in enumerate(outs):
            if key == "final":
                name, expert = final
                out_specs.append(
                    pl.BlockSpec((None, rows // steps, 2 * cols), lambda r: (expert, r, 0))
                )
                count = EXPERTS if name in ("gate", "up", "down") else 1
                out_shapes.append(pltpu.HBM((count, rows, 2 * cols), f32))
                if name in self.targets:
                    extra.append(pin(self.targets[name]))
                    aliases[1 + len(arrays)] = i
            else:
                out_specs.append(spec)
                out_shapes.append(shape)
        values = pl.pallas_call(
            functools.partial(wave_kernel, tuple(ins), tuple(outs) + ("token",)),
            grid=(steps,),
            in_specs=[smem()] + specs + [anywhere()] * (len(extra) + len(self.last)),
            out_specs=out_specs + [token_spec()],
            out_shape=out_shapes + [TOKEN],
            input_output_aliases=aliases,
            compiler_params=params(60),
            cost_estimate=short(),
            name="wave",
        )(self.place, *arrays, *extra, *self.last)
        return dict(zip(tuple(outs) + ("token",), values))


def swap_core(x, size):
    return lax.ppermute(x, "rep", [(i, i ^ 1) for i in range(size)])


def swap_shard(x, size, mask):
    return lax.ppermute(x, "shard", [(i, i ^ mask) for i in range(size)])


def line_perm(pairs):
    return [(2 * a + c, 2 * b + c) for a, b in pairs for c in range(2)]


def after(x, *others):
    return lax.optimization_barrier((x,) + others)[0]


def relay_gather(x, S):
    if S != 4:
        return [[x]] + [[swap_shard(x, S, m)] for m in range(1, S)]
    cut = x.shape[0] // 2
    one, two = swap_shard(x, S, 1), swap_shard(x, S, 2)
    return [[x], [one], [two], [swap_shard(one[:cut], S, 2), swap_shard(two[cut:], S, 1)]]


def line_sum(x, size):
    n = size // 2
    h = n // 2
    line = lax.axis_index("rep") // 2
    for k in range(h - 1):
        x = x + lax.ppermute(x, "rep", line_perm([(k, k + 1), (n - 1 - k, n - 2 - k)]))
    x = x + lax.ppermute(x, "rep", line_perm([(h - 1, h), (h, h - 1)]))
    for k in reversed(range(h - 1)):
        got = lax.ppermute(x, "rep", line_perm([(k + 1, k), (n - 2 - k, n - 1 - k)]))
        x = jnp.where((line == k) | (line == n - 1 - k), got, x)
    return x


def deal_out(x):
    return lax.all_to_all(x, "shard", 0, 0, tiled=True)


def bucket_of(distance):
    bucket = jnp.minimum(distance, 16)
    for border in bucket_edges:
        bucket = bucket + (distance >= border).astype(jnp.int32)
    return bucket


def slot_positions(routes, order, lengths):
    n = order.shape[1]
    valid = jnp.arange(n, dtype=jnp.int32)[None, :] < lengths[:, None]
    experts = jnp.arange(EXPERTS, dtype=jnp.int32)
    hits = (routes[:, :, :, None] == experts) & valid[:, :, None, None]
    hits = hits.reshape(routes.shape[0], n, 2 * EXPERTS)
    before = (order[:, None, :] < order[:, :, None]).astype(bf16)
    count = jnp.einsum("stk,sut->sku", hits.astype(bf16), before, preferred_element_type=f32)
    total = jnp.sum(hits[:, :, :EXPERTS].astype(f32), axis=1)
    hits = jnp.swapaxes(hits, 1, 2)
    first, second = count[:, :EXPERTS], count[:, EXPERTS:] + total[:, :, None]
    slot = jnp.where(
        hits[:, :EXPERTS], first, jnp.where(hits[:, EXPERTS:], second, float(2 * CAP + n))
    )
    return jnp.where(slot < CAP, slot, -1.0).astype(jnp.int32)


def shards(
    R,
    S,
    tokens,
    cotangent,
    lengths,
    sequence_deal,
    routes,
    fill_order,
    norm_attn,
    w_query,
    w_key,
    w_value,
    w_out,
    rel_bias,
    norm_ffn,
    w_router,
    w_gate,
    w_up,
    w_down,
):
    me = lax.axis_index("shard")
    rep = lax.axis_index("rep")
    core = rep % 2
    line = rep // 2
    x_low, ct_low = tokens[0], cotangent[0]
    n, width = x_low.shape
    part = width // S
    half = part // 2
    group = jnp.arange(S, dtype=jnp.int32)

    dense = (w_query, w_key, w_value, w_out)
    stack = jnp.where(
        core == 0,
        jnp.concatenate([w[:half] for w in dense], axis=1),
        jnp.concatenate([w[half:] for w in dense], axis=1),
    )
    blocks = relay_gather(stack, S)
    count = len(blocks[-1])
    pieces, places = [], []
    for m in range(1, S):
        place = 2 * count * (me ^ m)
        each = count // len(blocks[m])
        pieces += blocks[m]
        places += [place + count * core + j * each for j in range(len(blocks[m]))]
        for j, block in enumerate(blocks[m]):
            pieces.append(swap_core(block, R))
            places.append(place + count * (1 - core) + j * each)
    offsets = jnp.stack(places + [2 * count * me]).astype(jnp.int32)
    ct_all = relay_gather(after(ct_low, *blocks[-1]), S)

    bias_flat = jnp.pad(rel_bias.reshape(-1), (0, part - rel_bias.size))
    small = jnp.concatenate(
        [norm_attn[:, None], norm_ffn[:, None], w_router, bias_flat[:, None]], axis=1
    )
    small = jnp.pad(small, ((0, n - part), (0, 0)))
    plan = jnp.concatenate([routes[0], fill_order[0][:, None]], axis=1).astype(bf16)
    small = jnp.concatenate([small, plan], axis=1)
    small = after(small, blocks[1][0])
    small_all = deal_out(jnp.broadcast_to(small[None], (S,) + small.shape))
    plan_all = small_all[:, :, 3 + EXPERTS :]
    small_all = small_all[:, :part]
    gain_one = small_all[:, :, 0].reshape(-1).astype(f32)
    gain_two = small_all[:, :, 1].reshape(-1).astype(f32)
    router_w = small_all[:, :, 2 : 2 + EXPERTS].reshape(width, EXPERTS)
    bias_table = small_all[:, : rel_bias.size, 2 + EXPERTS].reshape(BUCKETS, HEADS)

    length = lax.dynamic_slice_in_dim(lengths[0], me, 1, 0)

    turned = jnp.arange(n, dtype=jnp.int32)
    hot = (bucket_of((n - turned) % n)[None, :] == jnp.arange(BUCKETS)[:, None]).astype(bf16)
    base = dot_tn(bias_table, hot).reshape(HEADS // 2, 2, n)

    bias = bias_of(length, base)
    normed_low, qkv, context, dense_w = attn_fwd(offsets, x_low, gain_one[None], bias, dense, pieces)
    ct_tokens = [ct_all[m][0] for m in range(1, 3)]
    middle, ffn_in = mid_of(x_low, gain_two[None], context, dense_w, ct_tokens)

    plan_all = after(plan_all, ffn_in).astype(jnp.int32)
    deal = sequence_deal[0]
    row_of = jnp.sum(group[:, None] * (deal[:, None] == group[None, :]).astype(jnp.int32), axis=0)
    homes = me ^ group
    plans = jnp.take(plan_all, jnp.take(row_of, homes), axis=0)
    pos = slot_positions(plans[:, :, :2], plans[:, :, 2], jnp.take(lengths[0], homes))

    h2_all = relay_gather(ffn_in, S)
    router_pad = jnp.pad(router_w, ((0, 0), (0, LANES - EXPERTS)))
    core_one = core.reshape(1).astype(jnp.int32)
    place = jnp.stack([line, core]).astype(jnp.int32)
    me_one = me.reshape(1).astype(jnp.int32)
    where = jnp.stack([me, core]).astype(jnp.int32)
    weights = [pin(w) for w in (jnp.swapaxes(w_gate, 1, 2), jnp.swapaxes(w_up, 1, 2), w_down)]
    sums = Sums(R, place)
    chain, aux = (), router_pad
    for experts, groups in (((0, 1), (2, 2, 2)), ((2, 3), (2, 2, 2))):
        got = ffn(experts, groups, where, pos, aux, h2_all, ct_all, weights, chain, sums.last)
        M = 1 + len(groups)
        keep, sends, chain = got[0], got[1:M], got[M : M + 2]
        sums.last = [got[M + 2]]
        if experts[0] == 0:
            aux = got[-1]
        where_to = [(g, k) for g, size in enumerate(groups) for k in range(size)]
        recvs = [swap_core(x, R) for x in sends]
        for i, e in enumerate(experts):
            for j, name in enumerate(("down", "gate", "up")):
                g, k = where_to[3 * i + j]
                sums.add(keep, 3 * i + j, recvs[g], k, name, e)
        if experts[0] == 0 and sums.line:
            sums.step()
            sums.step()

    def run(steps, more=()):
        for _ in range(steps):
            if sums.line and sums.busy():
                sums.step(more)

    run(1)
    flat = jnp.arange(EXPERTS, dtype=jnp.int32) * CAP
    pos_col = jnp.swapaxes(jnp.where(pos < 0, -1, pos + flat[None, :, None]), 1, 2)
    pos_col = jnp.pad(pos_col, ((0, 0), (0, 0), (0, LANES - EXPERTS)))
    d_parts, sums.last = combine(me_one, pos_col, chain[1], sums.last)
    d_parts = deal_out(d_parts)
    run(3)

    dmid, dc, extra, keep, send, token = back_mid(
        core_one, S, middle, ct_low, gain_two[None], ffn_in, router_pad, context, dense_w, d_parts, sums.last
    )
    recv = swap_core(send, R)
    dq, dk, dv, diag, token = attn_bwd(qkv, bias, dc, [token])
    sums.last = [token]
    run(2)
    grad_x, keep_in, send, token = back_in(
        core_one, S, x_low, gain_one[None], normed_low, dq, dk, dv, diag.reshape(HEADS, n), hot, extra, dmid, dense_w, sums.last
    )
    sums.last = [token]

    recv_in = swap_core(send, R)
    run(1)
    halves = jnp.concatenate(
        [
            (keep_in.astype(f32) + recv_in.astype(f32)).astype(bf16),
            (keep.astype(f32) + recv.astype(f32)).astype(bf16),
        ],
        axis=1,
    )
    run(1, [halves])
    owned = jnp.sum(deal_out(halves).astype(f32), axis=0).astype(bf16)
    rows, cut = owned.shape[0], weights[0].shape[1]
    if sums.line:
        owned = jnp.pad(owned, ((0, 2 * cut - rows), (0, 0)))[None]
        run(1)
        sums.add(owned[:, :cut], 0, None, 0, "dense0", 0)
        sums.add(owned[:, cut:], 0, None, 0, "dense1", 0)
    else:
        owned = line_sum(owned, R)
        other = swap_core(owned, R)
        owned = jnp.concatenate(
            [jnp.where(core == 0, owned, other), jnp.where(core == 0, other, owned)], axis=1
        ).astype(f32)
    run(1)
    out_parts, sums.last = combine(me_one, pos_col, chain[0], sums.last)
    out_parts = deal_out(out_parts)
    run(4)
    result = (middle + jnp.sum(out_parts.astype(f32), axis=0)).astype(bf16)
    run(1, [result])
    run(100)
    if sums.line:
        owned = jnp.concatenate([sums.targets["dense0"][0], sums.targets["dense1"][0]], axis=0)

    def matrix(first, count):
        x = owned[first * half : (first + count) * half].reshape(count, half, 2, PANEL)
        return jnp.transpose(x, (2, 1, 0, 3)).reshape(part, count * PANEL)

    many = width // PANEL
    small = matrix(3 * many, 1)
    grad_in_w = [matrix(j * many, many) for j in range(3)]
    grad_out_w = matrix(3 * many + 1, many)
    return (
        result[None],
        grad_x[None],
        small[:, 0],
        *grad_in_w,
        grad_out_w,
        small[: BUCKETS // S, 8 : 8 + HEADS],
        small[:, 1],
        small[:, 2 : 2 + EXPERTS],
        jnp.swapaxes(sums.targets["gate"], 1, 2),
        jnp.swapaxes(sums.targets["up"], 1, 2),
        sums.targets["down"],
    )


def solution(mesh):
    R, S = mesh.shape["rep"], mesh.shape["shard"]
    rows = P(("rep", "shard"), None, None)
    mat = P("shard", None)
    return jax.shard_map(
        functools.partial(shards, R, S),
        mesh=mesh,
        in_specs=(rows, rows, P("rep", None), P("rep", None), rows, P(("rep", "shard"), None))
        + (P("shard"), mat, mat, mat, mat, mat, P("shard"), mat)
        + (P(None, None, "shard"), P(None, None, "shard"), P(None, "shard", None)),
        out_specs=(rows, rows, P("shard"), mat, mat, mat, mat, mat, P("shard"), mat)
        + (P(None, None, "shard"), P(None, None, "shard"), P(None, "shard", None)),
        check_vma=False,
    )
```

time: 774 us -> 573 us (0.74)
  waiting for transfers between devices: 336 us -> 139 us
  Pallas kernels: 162 us -> 240 us
  starting transfers between devices: 160 us -> 107 us
  matrix products: 15.6 us -> 0.47 us
  local copies, waits for them, and re-layouts: 72.2 us -> 60.2 us
    ppermute x63 -> x32, waiting for transfers between devices: 213 us -> 86.8 us  [the longest x18 86.8 us: step(): ins['got_pair'] = lax.ppermute(state['pair'], rep_axis, pairs)]
    ppermute x27 -> x12, waiting for transfers between devices: 123 us -> 41.4 us  [swap_shard(): return lax.ppermute(x, 'shard', [(i, i ^ mask) for i in range(size)])]
    pallas_call x22 -> x28, Pallas kernels: 132 us -> 203 us  [the longest x21 101 us: kernel(): pl.pallas_call(functools.partial(wave_kernel, tuple(ins), tuple(outs) + (...]
    ppermute x63 -> x32, starting transfers between devices: 122 us -> 69.6 us  [the longest x18 49.8 us: step(): ins['got_pair'] = lax.ppermute(state['pair'], rep_axis, pairs)]
    dynamic_slice x6 -> x0, local copies, waits for them, and re-layouts: 19.4 us -> none  [the longest x2 10.8 us: shards(): keep = lax.dynamic_index_in_dim(dense, core, 1, keepdims=False)]
    ppermute x27 -> x12, starting transfers between devices: 36 us -> 16.8 us  [swap_shard(): return lax.ppermute(x, 'shard', [(i, i ^ mask) for i in range(size)])]
    all_to_all x0 -> x4, starting transfers between devices: none -> 16.6 us  [deal_out(): return lax.all_to_all(x, 'shard', 0, 0, tiled=True)]
    unnamed x170 -> x119, local copies, waits for them, and re-layouts: 38.3 us -> 24.1 us
  transfers between devices with their start and end apart: 100 -> 74, of which waited for: 35 -> 21; matrix products, arithmetic and copies ran while one was open for 10% -> 7% of each run, Pallas kernels for 10% -> 31%
where the time goes in v2:
time: 573 us; the launch traced here: 565 us
  Pallas kernels  240 us (42%)
  waiting for transfers between devices  139 us (24%)
  starting transfers between devices  107 us (19%)
  local copies, waits for them, and re-layouts  60.2 us (11%)
  other arithmetic  17.7 us (3%)
    pallas_call x21, Pallas kernels, kernel(): pl.pallas_call(functools.partial(wave_kernel, tuple(ins), tuple(outs) + (...  101 us
    ppermute x18, waiting for transfers between devices, step(): ins['got_pair'] = lax.ppermute(state['pair'], rep_axis, pairs)  86.8 us
    pallas_call x2, Pallas kernels, ffn(): pl.pallas_call(functools.partial(ffn_kernel, shape, experts, groups, len(...  64.7 us
    ppermute x18, starting transfers between devices, step(): ins['got_pair'] = lax.ppermute(state['pair'], rep_axis, pairs)  49.8 us
    ppermute x12, waiting for transfers between devices, swap_shard(): return lax.ppermute(x, 'shard', [(i, i ^ mask) for i in range(size)])  41.4 us
    unnamed x119, local copies, waits for them, and re-layouts  24.1 us
    ppermute x14, starting transfers between devices, step(): lax.ppermute(state['mid'], rep_axis, line_perm([(1, 2), (2, 1)]))  19.8 us
    pallas_call x1, Pallas kernels, attn_fwd(): pl.pallas_call(functools.partial(attn_fwd_kernel, N), in_specs=[smem(), v...  17.2 us
  transfers between devices with their start and end apart: 74, of which 21 were waited for; matrix products, arithmetic and copies ran while one was open for 7% of the time, Pallas kernels for 31%

profile of v2, /device:TPU:0, one launch (start us, length us, event | category | flops | bytes accessed | tf_op | source)
XLA Modules:
  0.0 565.4 jit_solution(18117222282559371323)
XLA Ops:
  9.5 20.3 %collective-permute-done.2.refs_10_ = bf16[128,4096]{1,0:T(8,128)(2,1)S(1)} collective-permute-done((bf16[128,4096]{1,0:T(8,128)(2,1)S(1)}, bf16[128,4096]{1,0:T(8,128)(2,1)S(1)}, u32[]{:S(2)}, u32[]{:S(2)}) %collective-permute-start.2) | collective-permute-done | bytes 1048608 | tf_op jit(solution)/shard_map/ppermute | solution.py:783
  34.9 8.2 %collective-permute-done.5.refs_13_ = bf16[64,4096]{1,0:T(8,128)(2,1)S(1)} collective-permute-done((bf16[64,4096]{1,0:T(8,128)(2,1)S(1)}, bf16[64,4096]{1,0:T(8,128)(2,1)S(1)}, u32[]{:S(2)}, u32[]{:S(2)}) %collective-permute-start.5) | collective-permute-done | bytes 524320 | tf_op jit(solution)/shard_map/ppermute | solution.py:783
  57.1 5.4 bias.1.refs_3_.bias_ref
  62.6 17.2 %attn_fwd.1 = (bf16[256,1024]{1,0:T(8,128)(2,1)}, bf16[256,3072]{1,0:T(8,128)(2,1)}, bf16[256,1024]{1,0:T(8,128)(2,1)}, bf16[1024,4096]{1,0:T(8,128)(2,1)}) custom-call(s32[9]{0:T(128)} %stack.53.refs_0_, bf16[256,1024]{1,0:T(8,128)(2,1)} %bitcast.90, f32[1,1024]{1,0:T(1,128)} %convert.14.refs_2_, bf16[16,256,256]{2,1,0:T(8,128)(2,1)} %bias.1.refs_3_.bias_ref, ...), custom_call_target="tpu_custom_call" | custom-call | flops 1 | bytes 1 | tf_op jit(solution)/shard_map/attn_fwd/pallas_call | solution.py:155
  94.8 5.7 %collective-permute-done.11.refs_5_ = bf16[256,1024]{1,0:T(8,128)(2,1)S(1)} collective-permute-done((bf16[256,1024]{1,0:T(8,128)(2,1)}, bf16[256,1024]{1,0:T(8,128)(2,1)S(1)}, u32[]{:S(2)}, u32[]{:S(2)}) %collective-permute-start.11) | collective-permute-done | bytes 524320 | tf_op jit(solution)/shard_map/ppermute | solution.py:783
  112.5 32.7 %ffn0.1 = (bf16[6,704,512]{2,1,0:T(8,128)(2,1)}, bf16[2,704,512]{2,1,0:T(8,128)(2,1)}, bf16[2,704,512]{2,1,0:T(8,128)(2,1)}, bf16[2,704,512]{2,1,0:T(8,128)(2,1)...) custom-call(s32[2]{0:T(128)} %pad_add_fusion.refs_0_, ...), custom_call_target="tpu_custom_call" | custom-call | flops 1 | bytes 1 | tf_op jit(solution)/shard_map/ffn0/pallas_call | solution.py:379
  159.5 32.0 %ffn2.1 = (bf16[6,704,512]{2,1,0:T(8,128)(2,1)}, bf16[2,704,512]{2,1,0:T(8,128)(2,1)}, bf16[2,704,512]{2,1,0:T(8,128)(2,1)}, bf16[2,704,512]{2,1,0:T(8,128)(2,1)...) custom-call(s32[2]{0:T(128)} %pad_add_fusion.refs_0_, ...), custom_call_target="tpu_custom_call", output_to_operand_aliasing={{4}: (17, {}), {5}: (18, {})} | custom-call | flops 1 | bytes 1 | tf_op jit(solution)/shard_map/ffn2/pallas_call | solution.py:379
  196.9 6.6 %combine.2 = (bf16[4,256,1152]{2,1,0:T(8,128)(2,1)}, f32[8,128]{1,0:T(8,128)}) custom-call(s32[1]{0:T(128)} %bitcast.19.me_ref, s32[4,256,128]{2,1,0:T(8,128)} %pad.17.pos_ref, bf16[4,576,1152]{2,1,0:T(8,128)(2,1)} %get-tuple-element.170.src_ref, f32[8,128]{1,0:T(8,128)} %get-tuple-element.174.refs_0_), custom_call_target="tpu_custom_call" | custom-call | flops 1 | bytes 1 | tf_op jit(solution)/shard_map/combine/pallas_call | solution.py:426
  210.7 15.6 %collective-permute-done.17.refs_1_ = bf16[704,512]{1,0:T(8,128)(2,1)S(1)} collective-permute-done((bf16[704,512]{1,0:T(8,128)(2,1)}, bf16[704,512]{1,0:T(8,128)(2,1)S(1)}, u32[]{:S(2)}, u32[]{:S(2)}) %collective-permute-start.17) | collective-permute-done | bytes 720928 | tf_op jit(solution)/shard_map/ppermute | solution.py:693
  233.2 8.6 %collective-permute-done.23.refs_1_ = bf16[704,512]{1,0:T(8,128)(2,1)} collective-permute-done((bf16[704,512]{1,0:T(8,128)(2,1)}, bf16[704,512]{1,0:T(8,128)(2,1)}, u32[]{:S(2)}, u32[]{:S(2)}) %collective-permute-start.23) | collective-permute-done | bytes 720928 | tf_op jit(solution)/shard_map/ppermute | solution.py:693
  248.2 9.0 %collective-permute-done.20.refs_1_ = bf16[704,512]{1,0:T(8,128)(2,1)S(1)} collective-permute-done((bf16[704,512]{1,0:T(8,128)(2,1)}, bf16[704,512]{1,0:T(8,128)(2,1)S(1)}, u32[]{:S(2)}, u32[]{:S(2)}) %collective-permute-start.20) | collective-permute-done | bytes 720928 | tf_op jit(solution)/shard_map/ppermute | solution.py:693
  266.2 7.8 %back_mid.1 = (f32[256,1024]{1,0:T(8,128)}, bf16[256,1024]{1,0:T(8,128)(2,1)}, f32[1024,128]{1,0:T(8,128)}, bf16[4,256,512]{2,1,0:T(8,128)(2,1)}, bf16[4,256,512]{2,1,0:T(8,128)(2,1)}, /*index=5*/f32[8,128]{1,0:T(8,128)}) custom-call(s32[1]{0:T(128)} %bitcast.25.refs_0_, f32[256,1024]{1,0:T(8,128)} %get-tuple-element.155.refs_1_, ...), custom_call_target="tpu_custom_call" | custom-call | flops 1 | bytes 1 | tf_op jit(solution)/shard_map/back_mid/pallas_call | solution.py:527
  274.0 14.2 %attn_bwd.1 = (bf16[256,1024]{1,0:T(8,128)(2,1)}, bf16[256,1024]{1,0:T(8,128)(2,1)}, bf16[256,1024]{1,0:T(8,128)(2,1)}, f32[8,2,256]{2,1,0:T(2,128)}, f32[8,128]{1,0:T(8,128)}) custom-call(bf16[256,3072]{1,0:T(8,128)(2,1)} %get-tuple-element.193.q_ref.k_ref.v_ref, bf16[256,3072]{1,0:T(8,128)(2,1)} %get-tuple-element.193.q_ref.k_ref.v_ref, ...), custom_call_target="tpu_custom_call" | custom-call | flops 1 | bytes 1 | tf_op jit(solution)/shard_map/attn_bwd/pallas_call | solution.py:228
  296.3 5.7 %wave.28 = (bf16[704,512]{1,0:T(8,128)(2,1)}, bf16[704,512]{1,0:T(8,128)(2,1)}, bf16[704,512]{1,0:T(8,128)(2,1)}, bf16[704,512]{1,0:T(8,128)(2,1)}, f32[4,704,1024]{2,1,0:T(8,128)}, /*index=5*/f32[8,128]{1,0:T(8,128)}) custom-call(s32[2]{0:T(128)} %pad_add_fusion.1.refs_0_, bf16[704,512]{1,0:T(8,128)(2,1)} %copy-done.31, ...), custom_call_target="tpu_custom_call" | custom-call | flops 1 | bytes 1 | tf_op jit(solution)/shard_map/wave/pallas_call | solution.py:764
  302.1 12.1 %back_in.1 = (bf16[256,1024]{1,0:T(8,128)(2,1)}, bf16[4,896,512]{2,1,0:T(8,128)(2,1)}, bf16[4,896,512]{2,1,0:T(8,128)(2,1)}, f32[8,128]{1,0:T(8,128)}) custom-call(s32[1]{0:T(128)} %bitcast.25.refs_0_, bf16[256,1024]{1,0:T(8,128)(2,1)} %bitcast.92, f32[1,1024]{1,0:T(1,128)} %convert.14.refs_2_, bf16[256,1024]{1,0:T(8,128)(2,1)} %get-tuple-element.209.refs_3_, ...), custom_call_target="tpu_custom_call" | custom-call | flops 1 | bytes 1 | tf_op jit(solution)/shard_map/back_in/pallas_call | solution.py:605
  314.8 7.0 %collective-permute-done.39 = bf16[4,256,512]{2,1,0:T(8,128)(2,1)S(1)} collective-permute-done((bf16[4,256,512]{2,1,0:T(8,128)(2,1)S(1)}, bf16[4,256,512]{2,1,0:T(8,128)(2,1)S(1)}, u32[]{:S(2)}, u32[]{:S(2)}) %collective-permute-start.39) | collective-permute-done | bytes 1048608 | tf_op jit(solution)/shard_map/ppermute | solution.py:779
  341.8 12.2 %collective-permute-done.34.refs_1_ = bf16[704,512]{1,0:T(8,128)(2,1)} collective-permute-done((bf16[704,512]{1,0:T(8,128)(2,1)}, bf16[704,512]{1,0:T(8,128)(2,1)}, u32[]{:S(2)}, u32[]{:S(2)}) %collective-permute-start.34) | collective-permute-done | bytes 720928 | tf_op jit(solution)/shard_map/ppermute | solution.py:693
  354.0 5.8 %wave.29 = (bf16[704,512]{1,0:T(8,128)(2,1)}, bf16[704,512]{1,0:T(8,128)(2,1)}, bf16[704,512]{1,0:T(8,128)(2,1)}, bf16[704,512]{1,0:T(8,128)(2,1)}, f32[4,704,1024]{2,1,0:T(8,128)}, /*index=5*/f32[8,128]{1,0:T(8,128)}) custom-call(s32[2]{0:T(128)} %pad_add_fusion.1.refs_0_, bf16[704,512]{1,0:T(8,128)(2,1)} %collective-permute-done.34.refs_1_, ...), custom_call_target="tpu_custom_call" | custom-call | flops 1 | bytes 1 | tf_op jit(solution)/shard_map/wave/pallas_call | solution.py:764
  364.3 5.2 collective-permute-done.31.refs_1_
  370.2 5.8 %wave.30 = (bf16[704,512]{1,0:T(8,128)(2,1)}, bf16[704,512]{1,0:T(8,128)(2,1)}, bf16[704,512]{1,0:T(8,128)(2,1)}, bf16[704,512]{1,0:T(8,128)(2,1)}, f32[4,704,1024]{2,1,0:T(8,128)}, /*index=5*/f32[8,128]{1,0:T(8,128)}) custom-call(s32[2]{0:T(128)} %pad_add_fusion.1.refs_0_, bf16[704,512]{1,0:T(8,128)(2,1)} %collective-permute-done.31.refs_1_, ...), custom_call_target="tpu_custom_call" | custom-call | flops 1 | bytes 1 | tf_op jit(solution)/shard_map/wave/pallas_call | solution.py:764
  386.0 5.7 %wave.31 = (bf16[704,512]{1,0:T(8,128)(2,1)}, bf16[704,512]{1,0:T(8,128)(2,1)}, bf16[704,512]{1,0:T(8,128)(2,1)}, bf16[704,512]{1,0:T(8,128)(2,1)}, f32[4,704,1024]{2,1,0:T(8,128)}, /*index=5*/f32[8,128]{1,0:T(8,128)}) custom-call(s32[2]{0:T(128)} %pad_add_fusion.1.refs_0_, ...), custom_call_target="tpu_custom_call", output_to_operand_aliasing={{4}: (10, {})} | custom-call | flops 1 | bytes 1 | tf_op jit(solution)/shard_map/wave/pallas_call | solution.py:764
  391.8 7.8 %collective-permute-start.49 = (bf16[704,512]{1,0:T(8,128)(2,1)}, bf16[704,512]{1,0:T(8,128)(2,1)S(1)}, u32[]{:S(2)}, u32[]{:S(2)}) collective-permute-start(bf16[704,512]{1,0:T(8,128)(2,1)} %get-tuple-element.243.refs_5_), channel_id=1, source_target_pairs={{0,8},{4,12},{8,0},{12,4},{16,24},{20,28},{24,16},{28,20},{1,9},{5... | collective-permute-start | bytes 2162696 | tf_op jit(solution)/shard_map/ppermute | solution.py:693
  401.5 5.7 %wave.32 = (bf16[704,512]{1,0:T(8,128)(2,1)}, bf16[704,512]{1,0:T(8,128)(2,1)}, bf16[704,512]{1,0:T(8,128)(2,1)}, bf16[704,512]{1,0:T(8,128)(2,1)}, f32[4,704,1024]{2,1,0:T(8,128)}, /*index=5*/f32[8,128]{1,0:T(8,128)}) custom-call(s32[2]{0:T(128)} %pad_add_fusion.1.refs_0_, bf16[704,512]{1,0:T(8,128)(2,1)} %copy-done.37, ...), custom_call_target="tpu_custom_call", output_to_operand_aliasing={{4}: (10, {})} | custom-call | flops 1 | bytes 1 | tf_op jit(solution)/shard_map/wave/pallas_call | solution.py:764
  407.4 6.2 %collective-permute-start.47 = (bf16[704,512]{1,0:T(8,128)(2,1)}, bf16[704,512]{1,0:T(8,128)(2,1)S(1)}, u32[]{:S(2)}, u32[]{:S(2)}) collective-permute-start(bf16[704,512]{1,0:T(8,128)(2,1)} %get-tuple-element.240.refs_5_), channel_id=1, source_target_pairs={{0,8},{4,12},{8,0},{12,4},{16,24},{20,28},{24,16},{28,20},{1,9},{5... | collective-permute-start | bytes 2162696 | tf_op jit(solution)/shard_map/ppermute | solution.py:693
  415.1 6.3 %combine.3 = (bf16[4,256,1024]{2,1,0:T(8,128)(2,1)}, f32[8,128]{1,0:T(8,128)}) custom-call(s32[1]{0:T(128)} %bitcast.19.me_ref, s32[4,256,128]{2,1,0:T(8,128)} %pad.17.pos_ref, bf16[4,576,1024]{2,1,0:T(8,128)(2,1)} %get-tuple-element.166.src_ref, f32[8,128]{1,0:T(8,128)} %get-tuple-element.237.refs_0_), custom_call_target="tpu_custom_call" | custom-call | flops 1 | bytes 1 | tf_op jit(solution)/shard_map/combine/pallas_call | solution.py:426
  427.7 5.5 wave.33
  437.0 5.5 wave.34
  452.7 5.1 wave.35
  468.2 5.1 wave.36
  492.4 6.5 %collective-permute-done.59.refs_1_ = bf16[704,512]{1,0:T(8,128)(2,1)S(1)} collective-permute-done((bf16[704,512]{1,0:T(8,128)(2,1)}, bf16[704,512]{1,0:T(8,128)(2,1)S(1)}, u32[]{:S(2)}, u32[]{:S(2)}) %collective-permute-start.59) | collective-permute-done | bytes 720928 | tf_op jit(solution)/shard_map/ppermute | solution.py:693
  508.0 6.4 %collective-permute-done.66.refs_1_ = bf16[704,512]{1,0:T(8,128)(2,1)S(1)} collective-permute-done((bf16[704,512]{1,0:T(8,128)(2,1)}, bf16[704,512]{1,0:T(8,128)(2,1)S(1)}, u32[]{:S(2)}, u32[]{:S(2)}) %collective-permute-start.66) | collective-permute-done | bytes 720928 | tf_op jit(solution)/shard_map/ppermute | solution.py:693
  519.8 9.5 %collective-permute-done.65.refs_1_ = bf16[704,512]{1,0:T(8,128)(2,1)S(1)} collective-permute-done((bf16[704,512]{1,0:T(8,128)(2,1)}, bf16[704,512]{1,0:T(8,128)(2,1)S(1)}, u32[]{:S(2)}, u32[]{:S(2)}) %collective-permute-start.65) | collective-permute-done | bytes 720928 | tf_op jit(solution)/shard_map/ppermute | solution.py:693
  (355 shorter events, 250.9 us)
Async XLA Ops:
  3.6 26.2 %collective-permute-start.2 = (bf16[128,4096]{1,0:T(8,128)(2,1)S(1)}, bf16[128,4096]{1,0:T(8,128)(2,1)S(1)}, u32[]{:S(2)}, u32[]{:S(2)}) collective-permute-start(bf16[128,4096]{1,0:T(8,128)(2,1)S(1)} %maximum_select_fusion), channel_id=1, source_target_pairs={{0,2},{1,3},{2,0},{3,1},{4,6},{5,7},{6,4},{7,5},{8,10},{9,11},{10,... | collective-permute-start | bytes 3145736 | tf_op jit(solution)/shard_map/ppermute | solution.py:783
  6.6 25.0 %collective-permute-start = (bf16[128,4096]{1,0:T(8,128)(2,1)S(1)}, bf16[128,4096]{1,0:T(8,128)(2,1)}, u32[]{:S(2)}, u32[]{:S(2)}) collective-permute-start(bf16[128,4096]{1,0:T(8,128)(2,1)S(1)} %maximum_select_fusion), channel_id=1, source_target_pairs={{0,1},{1,0},{2,3},{3,2},{4,5},{5,4},{6,7},{7,6},{8,9},{9,8},{10,11... | collective-permute-start | bytes 3145736 | tf_op jit(solution)/shard_map/ppermute | solution.py:783
  34.3 28.3 %collective-permute-start.3 = (bf16[128,4096]{1,0:T(8,128)(2,1)S(1)}, bf16[128,4096]{1,0:T(8,128)(2,1)}, u32[]{:S(2)}, u32[]{:S(2)}) collective-permute-start(bf16[128,4096]{1,0:T(8,128)(2,1)S(1)} %collective-permute-done.2.refs_10_), channel_id=1, source_target_pairs={{0,4},{4,0},{8,12},{12,8},{16,20},{20,16},{24,28},{28,24},{1,5},{5... | collective-permute-start | bytes 3145736 | tf_op jit(solution)/shard_map/ppermute | solution.py:779
  34.3 28.3 %collective-permute-start.1 = (bf16[128,4096]{1,0:T(8,128)(2,1)}, bf16[128,4096]{1,0:T(8,128)(2,1)}, u32[]{:S(2)}, u32[]{:S(2)}) collective-permute-start(bf16[128,4096]{1,0:T(8,128)(2,1)} %collective-permute-done.refs_8_), channel_id=1, source_target_pairs={{0,4},{4,0},{8,12},{12,8},{16,20},{20,16},{24,28},{28,24},{1,5},{5... | collective-permute-start | bytes 3145736 | tf_op jit(solution)/shard_map/ppermute | solution.py:779
  50.5 29.4 %collective-permute-start.9 = (bf16[256,1024]{1,0:T(8,128)(2,1)S(1)}, bf16[256,1024]{1,0:T(8,128)(2,1)S(1)}, u32[]{:S(2)}, u32[]{:S(2)}) collective-permute-start(bf16[256,1024]{1,0:T(8,128)(2,1)S(1)} %bitcast.88), channel_id=1, source_target_pairs={{0,2},{1,3},{2,0},{3,1},{4,6},{5,7},{6,4},{7,5},{8,10},{9,11},{10,... | collective-permute-start | bytes 1572872 | tf_op jit(solution)/shard_map/ppermute | solution.py:783
  52.5 27.4 %collective-permute-start.8 = (bf16[256,1024]{1,0:T(8,128)(2,1)S(1)}, bf16[256,1024]{1,0:T(8,128)(2,1)S(1)}, u32[]{:S(2)}, u32[]{:S(2)}) collective-permute-start(bf16[256,1024]{1,0:T(8,128)(2,1)S(1)} %bitcast.89), channel_id=1, source_target_pairs={{0,1},{1,0},{2,3},{3,2},{4,5},{5,4},{6,7},{7,6},{8,9},{9,8},{10,11... | collective-permute-start | bytes 1572872 | tf_op jit(solution)/shard_map/ppermute | solution.py:783
  145.2 46.3 %collective-permute-start.18 = (bf16[2,704,512]{2,1,0:T(8,128)(2,1)}, bf16[2,704,512]{2,1,0:T(8,128)(2,1)S(1)}, u32[]{:S(2)}, u32[]{:S(2)}) collective-permute-start(bf16[2,704,512]{2,1,0:T(8,128)(2,1)} %get-tuple-element.169), channel_id=1, source_target_pairs={{0,4},{4,0},{8,12},{12,8},{16,20},{20,16},{24,28},{28,24},{1,5},{5... | collective-permute-start | bytes 4325384 | tf_op jit(solution)/shard_map/ppermute | solution.py:779
  153.5 38.1 %collective-permute-start.19 = (bf16[704,512]{1,0:T(8,128)(2,1)}, bf16[704,512]{1,0:T(8,128)(2,1)S(1)}, u32[]{:S(2)}, u32[]{:S(2)}) collective-permute-start(bf16[704,512]{1,0:T(8,128)(2,1)} %get-tuple-element.171), channel_id=1, source_target_pairs={{0,8},{4,12},{8,0},{12,4},{16,24},{20,28},{24,16},{28,20},{1,9},{5... | collective-permute-start | bytes 2162696 | tf_op jit(solution)/shard_map/ppermute | solution.py:693
  155.0 76.7 %collective-permute-start.22 = (bf16[2,704,512]{2,1,0:T(8,128)(2,1)}, bf16[2,704,512]{2,1,0:T(8,128)(2,1)}, u32[]{:S(2)}, u32[]{:S(2)}) collective-permute-start(bf16[2,704,512]{2,1,0:T(8,128)(2,1)} %get-tuple-element.179), channel_id=1, source_target_pairs={{0,4},{4,0},{8,12},{12,8},{16,20},{20,16},{24,28},{28,24},{1,5},{5... | collective-permute-start | bytes 4325384 | tf_op jit(solution)/shard_map/ppermute | solution.py:779
  203.5 61.4 %all-to-all-start.1 = ((bf16[4,256,1152]{2,1,0:T(8,128)(2,1)}), bf16[4,256,1152]{2,1,0:T(8,128)(2,1)S(1)}, u32[]{:S(2)}, u32[]{:S(2)}) async-start(bf16[4,256,1152]{2,1,0:T(8,128)(2,1)} %get-tuple-element.194), calls=%async_computation.1 | async-start | bytes 4718592 | tf_op jit(solution)/shard_map/all_to_all | solution.py:816
  207.6 34.3 %collective-permute-start.23 = (bf16[704,512]{1,0:T(8,128)(2,1)}, bf16[704,512]{1,0:T(8,128)(2,1)}, u32[]{:S(2)}, u32[]{:S(2)}) collective-permute-start(bf16[704,512]{1,0:T(8,128)(2,1)} %get-tuple-element.180), channel_id=1, source_target_pairs={{0,8},{4,12},{8,0},{12,4},{16,24},{20,28},{24,16},{28,20},{1,9},{5... | collective-permute-start | bytes 2162696 | tf_op jit(solution)/shard_map/ppermute | solution.py:693
  209.2 32.7 %collective-permute-start.24 = (bf16[704,512]{1,0:T(8,128)(2,1)}, bf16[704,512]{1,0:T(8,128)(2,1)}, u32[]{:S(2)}, u32[]{:S(2)}) collective-permute-start(bf16[704,512]{1,0:T(8,128)(2,1)} %get-tuple-element.181.refs_2_), channel_id=1, source_target_pairs={{8,16},{12,20},{16,8},{20,12},{9,17},{13,21},{17,9},{21,13},{10,18... | collective-permute-start | bytes 2162696 | tf_op jit(solution)/shard_map/ppermute | solution.py:696
  210.7 77.5 %collective-permute-start.27 = (bf16[2,704,512]{2,1,0:T(8,128)(2,1)}, bf16[2,704,512]{2,1,0:T(8,128)(2,1)}, u32[]{:S(2)}, u32[]{:S(2)}) collective-permute-start(bf16[2,704,512]{2,1,0:T(8,128)(2,1)} %get-tuple-element.189), channel_id=1, source_target_pairs={{0,4},{4,0},{8,12},{12,8},{16,20},{20,16},{24,28},{28,24},{1,5},{5... | collective-permute-start | bytes 4325384 | tf_op jit(solution)/shard_map/ppermute | solution.py:779
  231.2 26.0 %collective-permute-start.20 = (bf16[704,512]{1,0:T(8,128)(2,1)}, bf16[704,512]{1,0:T(8,128)(2,1)S(1)}, u32[]{:S(2)}, u32[]{:S(2)}) collective-permute-start(bf16[704,512]{1,0:T(8,128)(2,1)} %get-tuple-element.176), channel_id=1, source_target_pairs={{0,8},{4,12},{8,0},{12,4},{16,24},{20,28},{24,16},{28,20},{1,9},{5... | collective-permute-start | bytes 2162696 | tf_op jit(solution)/shard_map/ppermute | solution.py:693
  231.7 25.5 %collective-permute-start.21 = (bf16[704,512]{1,0:T(8,128)(2,1)}, bf16[704,512]{1,0:T(8,128)(2,1)}, u32[]{:S(2)}, u32[]{:S(2)}) collective-permute-start(bf16[704,512]{1,0:T(8,128)(2,1)} %get-tuple-element.177.refs_2_), channel_id=1, source_target_pairs={{8,16},{12,20},{16,8},{20,12},{9,17},{13,21},{17,9},{21,13},{10,18... | collective-permute-start | bytes 2162696 | tf_op jit(solution)/shard_map/ppermute | solution.py:696
  246.2 42.1 %collective-permute-start.28 = (bf16[704,512]{1,0:T(8,128)(2,1)}, bf16[704,512]{1,0:T(8,128)(2,1)}, u32[]{:S(2)}, u32[]{:S(2)}) collective-permute-start(bf16[704,512]{1,0:T(8,128)(2,1)} %get-tuple-element.190.refs_5_), channel_id=1, source_target_pairs={{0,8},{4,12},{8,0},{12,4},{16,24},{20,28},{24,16},{28,20},{1,9},{5... | collective-permute-start | bytes 2162696 | tf_op jit(solution)/shard_map/ppermute | solution.py:693
  246.7 41.6 %collective-permute-start.29 = (bf16[704,512]{1,0:T(8,128)(2,1)}, bf16[704,512]{1,0:T(8,128)(2,1)}, u32[]{:S(2)}, u32[]{:S(2)}) collective-permute-start(bf16[704,512]{1,0:T(8,128)(2,1)} %get-tuple-element.191.refs_2_), channel_id=1, source_target_pairs={{8,16},{12,20},{16,8},{20,12},{9,17},{13,21},{17,9},{21,13},{10,18... | collective-permute-start | bytes 2162696 | tf_op jit(solution)/shard_map/ppermute | solution.py:696
  262.4 31.8 %collective-permute-start.25 = (bf16[704,512]{1,0:T(8,128)(2,1)}, bf16[704,512]{1,0:T(8,128)(2,1)S(1)}, u32[]{:S(2)}, u32[]{:S(2)}) collective-permute-start(bf16[704,512]{1,0:T(8,128)(2,1)} %get-tuple-element.185.refs_5_), channel_id=1, source_target_pairs={{0,8},{4,12},{8,0},{12,4},{16,24},{20,28},{24,16},{28,20},{1,9},{5... | collective-permute-start | bytes 2162696 | tf_op jit(solution)/shard_map/ppermute | solution.py:693
  262.9 31.4 %collective-permute-start.26 = (bf16[704,512]{1,0:T(8,128)(2,1)}, bf16[704,512]{1,0:T(8,128)(2,1)}, u32[]{:S(2)}, u32[]{:S(2)}) collective-permute-start(bf16[704,512]{1,0:T(8,128)(2,1)} %get-tuple-element.186.refs_2_), channel_id=1, source_target_pairs={{8,16},{12,20},{16,8},{20,12},{9,17},{13,21},{17,9},{21,13},{10,18... | collective-permute-start | bytes 2162696 | tf_op jit(solution)/shard_map/ppermute | solution.py:696
  314.7 25.3 %collective-permute-start.33 = (bf16[2,704,512]{2,1,0:T(8,128)(2,1)}, bf16[2,704,512]{2,1,0:T(8,128)(2,1)S(1)}, u32[]{:S(2)}, u32[]{:S(2)}) collective-permute-start(bf16[2,704,512]{2,1,0:T(8,128)(2,1)} %get-tuple-element.204), channel_id=1, source_target_pairs={{0,4},{4,0},{8,12},{12,8},{16,20},{20,16},{24,28},{28,24},{1,5},{5... | collective-permute-start | bytes 4325384 | tf_op jit(solution)/shard_map/ppermute | solution.py:779
  328.0 93.3 %all-to-all-start.3 = ((bf16[4,1152,512]{2,1,0:T(8,128)(2,1)}), bf16[4,1152,512]{2,1,0:T(8,128)(2,1)}, u32[]{:S(2)}, u32[]{:S(2)}) async-start(bf16[4,1152,512]{2,1,0:T(8,128)(2,1)} %pad_maximum_fusion.refs_11_), calls=%async_computation.3 | async-start | bytes 9437184 | tf_op jit(solution)/shard_map/all_to_all | solution.py:816
  338.3 31.1 %collective-permute-start.31 = (bf16[704,512]{1,0:T(8,128)(2,1)S(1)}, bf16[704,512]{1,0:T(8,128)(2,1)}, u32[]{:S(2)}, u32[]{:S(2)}) collective-permute-start(bf16[704,512]{1,0:T(8,128)(2,1)S(1)} %copy-done.22), channel_id=1, source_target_pairs={{0,8},{4,12},{8,0},{12,4},{16,24},{20,28},{24,16},{28,20},{1,9},{5... | collective-permute-start | bytes 2162696 | tf_op jit(solution)/shard_map/ppermute | solution.py:693
  340.0 30.1 %collective-permute-start.32 = (bf16[704,512]{1,0:T(8,128)(2,1)S(1)}, bf16[704,512]{1,0:T(8,128)(2,1)}, u32[]{:S(2)}, u32[]{:S(2)}) collective-permute-start(bf16[704,512]{1,0:T(8,128)(2,1)S(1)} %copy-done.21), channel_id=1, source_target_pairs={{8,16},{12,20},{16,8},{20,12},{9,17},{13,21},{17,9},{21,13},{10,18... | collective-permute-start | bytes 2162696 | tf_op jit(solution)/shard_map/ppermute | solution.py:696
  360.3 24.6 %collective-permute-start.43 = (bf16[704,512]{1,0:T(8,128)(2,1)}, bf16[704,512]{1,0:T(8,128)(2,1)}, u32[]{:S(2)}, u32[]{:S(2)}) collective-permute-start(bf16[704,512]{1,0:T(8,128)(2,1)} %get-tuple-element.228.refs_5_), channel_id=1, source_target_pairs={{0,8},{4,12},{8,0},{12,4},{16,24},{20,28},{24,16},{28,20},{1,9},{5... | collective-permute-start | bytes 2162696 | tf_op jit(solution)/shard_map/ppermute | solution.py:693
  376.0 24.4 %collective-permute-start.40 = (bf16[704,512]{1,0:T(8,128)(2,1)}, bf16[704,512]{1,0:T(8,128)(2,1)S(1)}, u32[]{:S(2)}, u32[]{:S(2)}) collective-permute-start(bf16[704,512]{1,0:T(8,128)(2,1)} %get-tuple-element.224.refs_5_), channel_id=1, source_target_pairs={{0,8},{4,12},{8,0},{12,4},{16,24},{20,28},{24,16},{28,20},{1,9},{5... | collective-permute-start | bytes 2162696 | tf_op jit(solution)/shard_map/ppermute | solution.py:693
  391.8 34.7 %collective-permute-start.49 = (bf16[704,512]{1,0:T(8,128)(2,1)}, bf16[704,512]{1,0:T(8,128)(2,1)S(1)}, u32[]{:S(2)}, u32[]{:S(2)}) collective-permute-start(bf16[704,512]{1,0:T(8,128)(2,1)} %get-tuple-element.243.refs_5_), channel_id=1, source_target_pairs={{0,8},{4,12},{8,0},{12,4},{16,24},{20,28},{24,16},{28,20},{1,9},{5... | collective-permute-start | bytes 2162696 | tf_op jit(solution)/shard_map/ppermute | solution.py:693
  399.7 26.9 %collective-permute-start.50 = (bf16[704,512]{1,0:T(8,128)(2,1)}, bf16[704,512]{1,0:T(8,128)(2,1)S(1)}, u32[]{:S(2)}, u32[]{:S(2)}) collective-permute-start(bf16[704,512]{1,0:T(8,128)(2,1)} %get-tuple-element.244.refs_2_), channel_id=1, source_target_pairs={{8,16},{12,20},{16,8},{20,12},{9,17},{13,21},{17,9},{21,13},{10,18... | collective-permute-start | bytes 2162696 | tf_op jit(solution)/shard_map/ppermute | solution.py:696
  407.4 28.4 %collective-permute-start.47 = (bf16[704,512]{1,0:T(8,128)(2,1)}, bf16[704,512]{1,0:T(8,128)(2,1)S(1)}, u32[]{:S(2)}, u32[]{:S(2)}) collective-permute-start(bf16[704,512]{1,0:T(8,128)(2,1)} %get-tuple-element.240.refs_5_), channel_id=1, source_target_pairs={{0,8},{4,12},{8,0},{12,4},{16,24},{20,28},{24,16},{28,20},{1,9},{5... | collective-permute-start | bytes 2162696 | tf_op jit(solution)/shard_map/ppermute | solution.py:693
  442.7 30.7 %all-to-all-start.2 = ((bf16[4,256,1024]{2,1,0:T(8,128)(2,1)}), bf16[4,256,1024]{2,1,0:T(8,128)(2,1)S(1)}, u32[]{:S(2)}, u32[]{:S(2)}) async-start(bf16[4,256,1024]{2,1,0:T(8,128)(2,1)} %get-tuple-element.238), calls=%async_computation.2 | async-start | bytes 4194304 | tf_op jit(solution)/shard_map/all_to_all | solution.py:816
  457.9 25.7 %collective-permute-start.61 = (bf16[704,512]{1,0:T(8,128)(2,1)}, bf16[704,512]{1,0:T(8,128)(2,1)}, u32[]{:S(2)}, u32[]{:S(2)}) collective-permute-start(bf16[704,512]{1,0:T(8,128)(2,1)} %get-tuple-element.266.refs_4_), channel_id=1, source_target_pairs={{0,8},{4,12},{8,0},{12,4},{16,24},{20,28},{24,16},{28,20},{1,9},{5... | collective-permute-start | bytes 2162696 | tf_op jit(solution)/shard_map/ppermute | solution.py:693
  488.4 26.0 %collective-permute-start.66 = (bf16[704,512]{1,0:T(8,128)(2,1)}, bf16[704,512]{1,0:T(8,128)(2,1)S(1)}, u32[]{:S(2)}, u32[]{:S(2)}) collective-permute-start(bf16[704,512]{1,0:T(8,128)(2,1)} %get-tuple-element.275.refs_2_), channel_id=1, source_target_pairs={{0,8},{4,12},{8,0},{12,4},{16,24},{20,28},{24,16},{28,20},{1,9},{5... | collective-permute-start | bytes 2162696 | tf_op jit(solution)/shard_map/ppermute | solution.py:693
  505.1 24.2 %collective-permute-start.65 = (bf16[704,512]{1,0:T(8,128)(2,1)}, bf16[704,512]{1,0:T(8,128)(2,1)S(1)}, u32[]{:S(2)}, u32[]{:S(2)}) collective-permute-start(bf16[704,512]{1,0:T(8,128)(2,1)} %get-tuple-element.274.refs_2_), channel_id=1, source_target_pairs={{0,8},{4,12},{8,0},{12,4},{16,24},{20,28},{24,16},{28,20},{1,9},{5... | collective-permute-start | bytes 2162696 | tf_op jit(solution)/shard_map/ppermute | solution.py:693
  (98 other events, 1073.3 us)

commit v3 on v2

--- a/solution.py
+++ b/solution.py
@@ -72,33 +72,6 @@
     return pl.BlockSpec(memory_space=pltpu.SMEM)
 
 
-def bias_kernel(len_ref, base_ref, out_ref):
-    n = base_ref.shape[2]
-    rows = lax.broadcasted_iota(jnp.int32, (n, n), 0)
-    cols = lax.broadcasted_iota(jnp.int32, (n, n), 1)
-    allowed = (cols <= rows) & (cols < len_ref[0])
-    for h in range(2):
-        row = jnp.broadcast_to(base_ref[0, h : h + 1, :], (n, n))
-        bias = pltpu.roll(row, 0, 1, stride=1, stride_axis=0)
-        out_ref[h] = jnp.where(allowed, bias, -1000000000.0).astype(bf16)
-
-
-def bias_of(length, base):
-    pairs, _, n = base.shape
-    return pl.pallas_call(
-        bias_kernel,
-        grid_spec=pltpu.PrefetchScalarGridSpec(
-            num_scalar_prefetch=1,
-            grid=(pairs,),
-            in_specs=[pl.BlockSpec((1, 2, n), lambda i, l: (i, 0, 0))],
-            out_specs=pl.BlockSpec((2, n, n), lambda i, l: (i, 0, 0)),
-        ),
-        out_shape=jax.ShapeDtypeStruct((2 * pairs, n, n), bf16),
-        compiler_params=params(60),
-        name="bias",
-    )(length, base)
-
-
 def softmax_of(q, k, bias):
     s = dot_nt(q, k) * 0.125 + bias.astype(f32)
     e = jnp.exp(s - jnp.max(s, axis=-1, keepdims=True))
@@ -106,22 +79,39 @@
 
 
 def attn_fwd_kernel(N, *refs):
-    off_ref, x_ref, gain_ref, bias_ref = refs[:4]
-    own, pieces = refs[4:8], refs[8 : 8 + N]
-    h_ref, qkv_ref, c_ref, wout_ref, w_s, sem = refs[8 + N :]
-    width = x_ref.shape[1]
+    off_ref, len_ref, x_ref, gain_ref, gain2_ref, base_ref = refs[:6]
+    own, pieces = refs[6:10], refs[10 : 10 + N]
+    h_ref, qkv_ref, c_ref, mid_ref, h2_ref, wout_ref, bias_hbm, w_s, bias_ref, sem, sems = refs[10 + N :]
+    n, width = x_ref.shape
     unit = min(piece.shape[0] for piece in pieces)
+    copies = []
     first = pl.multiple_of(off_ref[N] * unit, unit)
     for j in range(4):
-        w_s[pl.ds(first, own[j].shape[0]), j * width : (j + 1) * width] = own[j][...]
+        dest = w_s.at[pl.ds(first, own[j].shape[0]), pl.ds(j * width, width)]
+        copies.append(pltpu.make_async_copy(own[j], dest, sems.at[N + j]))
     for p, piece in enumerate(pieces):
         start = pl.multiple_of(off_ref[p] * unit, unit)
-        w_s[pl.ds(start, piece.shape[0]), :] = piece[...]
-    out = pltpu.make_async_copy(w_s, wout_ref, sem)
-    out.start()
+        copies.append(
+            pltpu.make_async_copy(piece, w_s.at[pl.ds(start, piece.shape[0])], sems.at[p])
+        )
+    for copy in copies:
+        copy.start()
     x = x_ref[...].astype(f32)
     scale = lax.rsqrt(jnp.mean(x * x, axis=-1, keepdims=True) + eps)
     h_ref[...] = (x * scale * gain_ref[...]).astype(bf16)
+    rows = lax.broadcasted_iota(jnp.int32, (n, n), 0)
+    cols = lax.broadcasted_iota(jnp.int32, (n, n), 1)
+    allowed = (cols <= rows) & (cols < len_ref[0])
+    for h in range(HEADS):
+        row = jnp.broadcast_to(base_ref[h : h + 1, :], (n, n))
+        turned = pltpu.roll(row, 0, 1, stride=1, stride_axis=0)
+        bias_ref[h] = jnp.where(allowed, turned, -1000000000.0).astype(bf16)
+    outs = [pltpu.make_async_copy(bias_ref, bias_hbm, sem.at[0])]
+    outs.append(pltpu.make_async_copy(w_s, wout_ref, sem.at[1]))
+    outs[0].start()
+    for copy in copies:
+        copy.wait()
+    outs[1].start()
     step = width // 2
 
     def project(i, carry):
@@ -131,113 +121,100 @@
 
     lax.fori_loop(0, 3 * width // step, project, 0)
 
-    def pair(i, carry):
+    def some_heads(i, carry):
         def at(j):
-            return pl.ds(pl.multiple_of(j * width + i * LANES, LANES), LANES)
-
-        q2, k2, v2 = qkv_ref[:, at(0)], qkv_ref[:, at(1)], qkv_ref[:, at(2)]
+            return pl.ds(pl.multiple_of(j * width + i * 2 * LANES, LANES), 2 * LANES)
+
+        q, k, v = qkv_ref[:, at(0)], qkv_ref[:, at(1)], qkv_ref[:, at(2)]
         heads = []
-        for h in range(2):
+        for h in range(4):
             cut = slice(h * HEAD_DIM, (h + 1) * HEAD_DIM)
-            p = softmax_of(q2[:, cut], k2[:, cut], bias_ref[2 * i + h]).astype(bf16)
-            heads.append(dot_nn(p, v2[:, cut]).astype(bf16))
+            p = softmax_of(q[:, cut], k[:, cut], bias_ref[4 * i + h]).astype(bf16)
+            heads.append(dot_nn(p, v[:, cut]).astype(bf16))
         c_ref[:, at(0)] = jnp.concatenate(heads, axis=1)
         return carry
 
-    lax.fori_loop(0, HEADS // 2, pair, 0)
-    out.wait()
-
-
-def attn_fwd(offsets, x, gain, bias, own, pieces):
+    lax.fori_loop(0, HEADS // 4, some_heads, 0)
+    mid = x_ref[...].astype(f32) + dot_nn(c_ref[...], w_s[:, 3 * width :])
+    scale = lax.rsqrt(jnp.mean(mid * mid, axis=-1, keepdims=True) + eps)
+    mid_ref[...] = mid
+    h2_ref[...] = (mid * scale * gain2_ref[...]).astype(bf16)
+    for copy in outs:
+        copy.wait()
+
+
+def attn_fwd(offsets, length, x, gain, gain_two, base, own, pieces):
     n, width = x.shape
     N = len(pieces)
     full = jax.ShapeDtypeStruct((n, width), bf16)
     return pl.pallas_call(
         functools.partial(attn_fwd_kernel, N),
-        in_specs=[smem(), vmem(), vmem(), vmem()] + [vmem()] * (4 + N),
-        out_specs=[vmem(), vmem(), vmem(), hbm()],
+        in_specs=[smem(), smem(), vmem(), vmem(), vmem(), vmem()] + [anywhere()] * (4 + N),
+        out_specs=[vmem()] * 5 + [hbm()] * 2,
         out_shape=[
             full,
             jax.ShapeDtypeStruct((n, 3 * width), bf16),
             full,
+            jax.ShapeDtypeStruct((n, width), f32),
+            full,
             pltpu.HBM((width, 4 * width), bf16),
+            pltpu.HBM((HEADS, n, n), bf16),
         ],
-        scratch_shapes=[pltpu.VMEM((width, 4 * width), bf16), pltpu.SemaphoreType.DMA],
+        scratch_shapes=[
+            pltpu.VMEM((width, 4 * width), bf16),
+            pltpu.VMEM((HEADS, n, n), bf16),
+            pltpu.SemaphoreType.DMA((2,)),
+            pltpu.SemaphoreType.DMA((N + 4,)),
+        ],
         compiler_params=params(60),
         cost_estimate=short(),
         name="attn_fwd",
-    )(offsets, x, gain, bias, *own, *pieces)
-
-
-def mid_kernel(x_ref, gain_ref, c_ref, w_hbm, *refs):
-    mid_ref, h_ref, w_s, sem = refs[-4:]
-    width = x_ref.shape[1]
-    load = pltpu.make_async_copy(w_hbm.at[:, pl.ds(3 * width, width)], w_s, sem)
-    load.start()
-    load.wait()
-    mid = x_ref[...].astype(f32) + dot_nn(c_ref[...], w_s[...])
-    scale = lax.rsqrt(jnp.mean(mid * mid, axis=-1, keepdims=True) + eps)
-    mid_ref[...] = mid
-    h_ref[...] = (mid * scale * gain_ref[...]).astype(bf16)
-
-
-def mid_of(x, gain, context, weights, tokens):
-    n, width = x.shape
-    return pl.pallas_call(
-        mid_kernel,
-        in_specs=[vmem(), vmem(), vmem(), hbm()] + [anywhere()] * len(tokens),
-        out_specs=[vmem(), vmem()],
-        out_shape=[
-            jax.ShapeDtypeStruct((n, width), f32),
-            jax.ShapeDtypeStruct((n, width), bf16),
-        ],
-        scratch_shapes=[pltpu.VMEM((width, width), bf16), pltpu.SemaphoreType.DMA],
-        compiler_params=params(60),
-        cost_estimate=short(),
-        name="middle",
-    )(x, gain, context, weights, *tokens)
+    )(offsets, length, x, gain, gain_two, base, *own, *pieces)
 
 
 def attn_bwd_kernel(q_ref, k_ref, v_ref, bias_ref, dc_ref, *refs):
-    dq_ref, dk_ref, dv_ref, diag_ref, token = refs[-5:]
+    d_ref, diag_ref, token = refs[-3:]
     give(token)
     n = q_ref.shape[0]
     rows = lax.broadcasted_iota(jnp.int32, (n, n), 0)
     cols = lax.broadcasted_iota(jnp.int32, (n, n), 1)
     reverse = (rows + cols == n - 1).astype(bf16)
-    for h in range(2):
+    for h in range(4):
         cut = slice(h * HEAD_DIM, (h + 1) * HEAD_DIM)
         q, k, v, dc = q_ref[:, cut], k_ref[:, cut], v_ref[:, cut], dc_ref[:, cut]
         p = softmax_of(q, k, bias_ref[h])
         dp = dot_nt(dc, v)
         ds = p * (dp - jnp.sum(p * dp, axis=-1, keepdims=True))
         low = ds.astype(bf16)
-        dq_ref[:, cut] = (dot_nn(low, k) * 0.125).astype(bf16)
-        dk_ref[:, cut] = (dot_tn(low, q) * 0.125).astype(bf16)
-        dv_ref[:, cut] = dot_tn(p.astype(bf16), dc).astype(bf16)
+        d_ref[0, :, cut] = (dot_nn(low, k) * 0.125).astype(bf16)
+        d_ref[1, :, cut] = (dot_tn(low, q) * 0.125).astype(bf16)
+        d_ref[2, :, cut] = dot_tn(p.astype(bf16), dc).astype(bf16)
         turned = pltpu.roll(dot_nn(reverse, low), 1, 1, stride=1, stride_axis=0)
         diag_ref[0, h : h + 1, :] = jnp.sum(turned, axis=0, keepdims=True)
 
 
 def attn_bwd(qkv, bias, dc, tokens):
     n = qkv.shape[0]
-    pairs = HEADS // 2
-    blk = pl.BlockSpec((n, LANES), lambda i: (0, i))
-    row = pl.BlockSpec((1, 2, n), lambda i: (i, 0, 0))
-    full = jax.ShapeDtypeStruct((n, HEADS * HEAD_DIM), bf16)
+    steps = HEADS // 4
+    blk = pl.BlockSpec((n, 2 * LANES), lambda i: (0, i))
+    row = pl.BlockSpec((1, 4, n), lambda i: (i, 0, 0))
     return pl.pallas_call(
         attn_bwd_kernel,
-        grid=(pairs,),
+        grid=(steps,),
         in_specs=[
             blk,
-            pl.BlockSpec((n, LANES), lambda i: (0, pairs + i)),
-            pl.BlockSpec((n, LANES), lambda i: (0, 2 * pairs + i)),
-            pl.BlockSpec((2, n, n), lambda i: (i, 0, 0)),
+            pl.BlockSpec((n, 2 * LANES), lambda i: (0, steps + i)),
+            pl.BlockSpec((n, 2 * LANES), lambda i: (0, 2 * steps + i)),
+            pl.BlockSpec((4, n, n), lambda i: (i, 0, 0)),
             blk,
         ]
         + [anywhere()] * len(tokens),
-        out_specs=[blk, blk, blk, row, token_spec()],
-        out_shape=[full, full, full, jax.ShapeDtypeStruct((pairs, 2, n), f32), TOKEN],
+        out_specs=[pl.BlockSpec((3, n, 2 * LANES), lambda i: (0, 0, i)), row, token_spec()],
+        out_shape=[
+            jax.ShapeDtypeStruct((3, n, HEADS * HEAD_DIM), bf16),
+            jax.ShapeDtypeStruct((steps, 4, n), f32),
+            TOKEN,
+        ],
         compiler_params=params(60),
         cost_estimate=short(),
         name="attn_bwd",
@@ -272,7 +249,7 @@
         prob_ref, refs = refs[0], refs[1:]
     else:
         prob_ref = aux_ref
-    w_v, x_s, c_s, gate_s, a_s, u_s, d_s, hid_s, da_s, du_s, o_s, eo_s, dx_s, sem_l, sem_s = refs
+    w_v, x_s, c_s, gate_s, hid_s, da_s, du_s, o_s, eo_s, dx_s, sem_l, sem_s = refs
     n, width = pos_ref.shape[2], x_s.shape[1]
     loads = [[] for _ in experts]
     for i, e in enumerate(experts):
@@ -281,7 +258,7 @@
             copy.start()
             loads[i].append(copy)
     lanes = lax.broadcasted_iota(jnp.int32, (n, LANES), 1)
-    slot_lanes = lax.broadcasted_iota(jnp.int32, (CAP, LANES), 1)
+    slot_lanes = lax.broadcasted_iota(jnp.int32, (S * CAP, LANES), 1)
     slots = lax.broadcasted_iota(jnp.int32, (CAP, n), 0)
     if first:
         for s in range(S):
@@ -318,27 +295,27 @@
             gate_s[rows, :] = jnp.broadcast_to(
                 picked[:, e : e + 1] + picked[:, EXPERTS + e : EXPERTS + e + 1], (CAP, LANES)
             )
-        loads[i][0].wait()
-        a_s[...] = dot_nt(x_s[...], wg[...])
-        loads[i][1].wait()
-        u_s[...] = dot_nt(x_s[...], wu[...])
-        loads[i][2].wait()
-        d_s[...] = dot_nt(c_s[...], wd[...])
+        for copy in loads[i]:
+            copy.wait()
         settle("dx")
-        for s in range(S):
-            rows = slice(s * CAP, (s + 1) * CAP)
-            a, u, d0, gate = a_s[rows, :], u_s[rows, :], d_s[rows, :], gate_s[rows, 0:1]
+        cols, gate = hid_s.shape[1], gate_s[:, 0:1]
+        dg = jnp.zeros(gate.shape, f32)
+        for f in range(0, cols, 256):
+            cut = slice(f, min(f + 256, cols))
+            a = dot_nt(x_s[...], wg[cut, :])
+            u = dot_nt(x_s[...], wu[cut, :])
+            d0 = dot_nt(c_s[...], wd[cut, :])
             t = jnp.tanh(const * (a + 0.044715 * a * a * a))
             half = 0.5 * (1.0 + t)
             act = a * half
             slope = half + 0.5 * a * (1.0 - t * t) * (const * (1.0 + 3 * 0.044715 * a * a))
             hid = act * u
-            dg = jnp.sum(hid * d0, axis=-1, keepdims=True)
-            hid_s[rows, :] = (gate * hid).astype(bf16)
+            dg = dg + jnp.sum(hid * d0, axis=-1, keepdims=True)
+            hid_s[:, cut] = (gate * hid).astype(bf16)
             dh = gate * d0
-            da_s[rows, :] = (dh * u * slope).astype(bf16)
-            du_s[rows, :] = (dh * act).astype(bf16)
-            dx_s[rows, width:] = jnp.where(slot_lanes == e, dg, 0.0).astype(bf16)
+            da_s[:, cut] = (dh * u * slope).astype(bf16)
+            du_s[:, cut] = (dh * act).astype(bf16)
+        dx_s[:, width:] = jnp.where(slot_lanes == e, dg, 0.0).astype(bf16)
         for j, (left, right) in enumerate(((hid_s, c_s), (da_s, x_s), (du_s, x_s))):
             settle(j)
             o_s[j] = dot_tn(left[...], right[...]).astype(bf16)
@@ -389,7 +366,6 @@
         scratch_shapes=[pltpu.VMEM((N, 3, cols, width), bf16)]
         + [pltpu.VMEM((rows, width), bf16)] * 2
         + [pltpu.VMEM((rows, LANES), f32)]
-        + [pltpu.VMEM((rows, cols), f32)] * 3
         + [pltpu.VMEM((rows, cols), bf16)] * 3
         + [pltpu.VMEM((3, cols, width), bf16)]
         + [pltpu.VMEM((rows, width), bf16), pltpu.VMEM((rows, width + LANES), bf16)]
@@ -449,23 +425,9 @@
 PANEL = 512
 
 
-def split_rows(src, core, S, keep, send, sems):
-    half, panels = src.shape[0] // (2 * S), src.shape[1] // PANEL
-    copies = []
-    for m in range(S):
-        for c, dest in enumerate((keep, send)):
-            who = core if c == 0 else 1 - core
-            start = pl.multiple_of((2 * m + who) * half, half)
-            for p in range(panels):
-                copies.append(
-                    pltpu.make_async_copy(
-                        src.at[pl.ds(start, half), pl.ds(p * PANEL, PANEL)],
-                        dest.at[m, pl.ds(p * half, half)],
-                        sems.at[(2 * m + c) * panels + p],
-                    )
-                )
-                copies[-1].start()
-    return copies
+def core_columns(ref, core, s, half):
+    low = ref[:, 2 * s * half : (2 * s + 1) * half]
+    return jnp.where(core == 0, low, ref[:, (2 * s + 1) * half : (2 * s + 2) * half])
 
 
 def hi_lo(x):
@@ -480,9 +442,9 @@
 
 
 def back_mid_kernel(S, *refs):
-    core_ref, mid_ref, ct_ref, gain_ref, h2_ref, wr_ref, c_ref, wo_hbm = refs[:8]
-    parts_ref = refs[8]
-    dmid_ref, dc_ref, extra_ref, keep, send, token, wo, go_s, sem_w, sems = refs[-10:]
+    mid_ref, ct_ref, gain_ref, h2_ref, wr_ref, wo_hbm = refs[:6]
+    parts_ref = refs[6]
+    dmid_ref, low_ref, dc_ref, extra_ref, token, wo, sem_w = refs[-7:]
     give(token)
     n, width = mid_ref.shape
     load = pltpu.make_async_copy(wo_hbm.at[:, pl.ds(3 * width, width)], wo, sem_w)
@@ -509,70 +471,41 @@
     dmid = ct_ref[...].astype(f32) + dz
     dmid_ref[...] = dmid
     low = dmid.astype(bf16)
-    go_s[...] = dot_tn(c_ref[...], low).astype(bf16)
-    copies = split_rows(go_s, core_ref[0], S, keep, send, sems)
+    low_ref[...] = low
     load.wait()
     dc_ref[...] = dot_nt(low, wo[...]).astype(bf16)
     wide = lax.broadcasted_iota(jnp.int32, (width, LANES), 1)
     gain_column = sum_columns(dh2 * mid * scale)
     extra_ref[...] = jnp.where(wide == 1, gain_column, pltpu.roll(grad_router, 2, 1))
-    for copy in copies:
-        copy.wait()
-
-
-def back_mid(core, S, mid, ct, gain, h2, router_w, context, out_w, parts, tokens):
+
+
+def back_mid(S, mid, ct, gain, h2, router_w, dense_w, parts, tokens):
     n, width = mid.shape
-    panels = width // PANEL
-    part = pltpu.HBM((S, panels * width // (2 * S), PANEL), bf16)
+    low = jax.ShapeDtypeStruct((n, width), bf16)
     return pl.pallas_call(
         functools.partial(back_mid_kernel, S),
-        in_specs=[smem()]
-        + [vmem()] * 6
-        + [hbm()]
-        + [vmem()]
-        + [anywhere()] * len(tokens),
-        out_specs=[vmem(), vmem(), vmem(), hbm(), hbm(), vmem()],
+        in_specs=[vmem()] * 5 + [hbm(), vmem()] + [anywhere()] * len(tokens),
+        out_specs=[vmem()] * 5,
         out_shape=[
             jax.ShapeDtypeStruct((n, width), f32),
-            jax.ShapeDtypeStruct((n, width), bf16),
+            low,
+            low,
             jax.ShapeDtypeStruct((width, LANES), f32),
-            part,
-            part,
             TOKEN,
         ],
-        scratch_shapes=[
-            pltpu.VMEM((width, width), bf16),
-            pltpu.VMEM((width, width), bf16),
-            pltpu.SemaphoreType.DMA,
-            pltpu.SemaphoreType.DMA((2 * S * panels,)),
-        ],
+        scratch_shapes=[pltpu.VMEM((width, width), bf16), pltpu.SemaphoreType.DMA],
         compiler_params=params(60),
         cost_estimate=short(),
         name="back_mid",
-    )(core, mid, ct, gain, h2, router_w, context, out_w, parts, *tokens)
-
-
-def back_in_kernel(S, *refs):
-    core_ref, x_ref, gain_ref, h_ref, dq_ref, dk_ref, dv_ref, diag_ref, hot_ref = refs[:9]
-    extra_ref, dmid_ref, w_hbm = refs[9:12]
-    dx_ref, keep, send, token, w_s, g_s, sem_w, sems = refs[-8:]
+    )(mid, ct, gain, h2, router_w, dense_w, parts, *tokens)
+
+
+def back_in_kernel(S, x_ref, gain_ref, d_ref, diag_ref, hot_ref, extra_ref, dmid_ref, w_hbm, *refs):
+    dx_ref, small_ref, token, w_s, sem = refs[-5:]
     give(token)
     n, width = x_ref.shape
-    load = pltpu.make_async_copy(w_hbm.at[:, pl.ds(0, 3 * width)], w_s, sem_w)
+    load = pltpu.make_async_copy(w_hbm.at[:, pl.ds(0, 3 * width)], w_s, sem)
     load.start()
-    for j, d_ref in enumerate((dq_ref, dk_ref, dv_ref)):
-        g_s[:, j * width : (j + 1) * width] = dot_tn(h_ref[...], d_ref[...]).astype(bf16)
-    load.wait()
-    dh = dot_nt(dq_ref[...], w_s[:, :width])
-    dh = dh + dot_nt(dk_ref[...], w_s[:, width : 2 * width])
-    dh = dh + dot_nt(dv_ref[...], w_s[:, 2 * width :])
-    x = x_ref[...].astype(f32)
-    scale = lax.rsqrt(jnp.mean(x * x, axis=-1, keepdims=True) + eps)
-    wide = lax.broadcasted_iota(jnp.int32, (width, LANES), 1)
-    extra = jnp.where(wide == 0, sum_columns(dh * x * scale), extra_ref[...])
-    end = 3 * width + LANES
-    g_s[:, 3 * width : end] = jnp.where(wide < 2 + EXPERTS, extra, 0.0).astype(bf16)
-    g_s[:, end:] = jnp.zeros((width, PANEL - LANES), bf16)
     diag = jnp.concatenate(
         [jnp.zeros((8, n), f32), diag_ref[...], jnp.zeros((LANES - 8 - HEADS, n), f32)], axis=0
     )
@@ -582,41 +515,98 @@
     places = lax.broadcasted_iota(jnp.int32, (16, BUCKETS), 0)
     buckets = lax.broadcasted_iota(jnp.int32, (16, BUCKETS), 1)
     high, rest = hi_lo(table)
+    x = x_ref[...].astype(f32)
+    scale = lax.rsqrt(jnp.mean(x * x, axis=-1, keepdims=True) + eps)
+    load.wait()
+    dh = dot_nt(d_ref[0], w_s[:, :width])
+    dh = dh + dot_nt(d_ref[1], w_s[:, width : 2 * width])
+    dh = dh + dot_nt(d_ref[2], w_s[:, 2 * width :])
+    wide = lax.broadcasted_iota(jnp.int32, (width, LANES), 1)
+    extra = jnp.where(wide == 0, sum_columns(dh * x * scale), extra_ref[...])
+    small_ref[...] = jnp.where(wide < 2 + EXPERTS, extra, 0.0).astype(bf16)
     for s in range(S):
         pick = ((places < count) & (buckets == places + s * count)).astype(bf16)
-        rows = dot_nn(pick, high) + dot_nn(pick, rest)
-        rows = rows + g_s[s * part : s * part + 16, 3 * width : end].astype(f32)
-        g_s[s * part : s * part + 16, 3 * width : end] = rows.astype(bf16)
-    copies = split_rows(g_s, core_ref[0], S, keep, send, sems)
+        cut = slice(s * part, s * part + 16)
+        rows = dot_nn(pick, high) + dot_nn(pick, rest) + small_ref[cut, :].astype(f32)
+        small_ref[cut, :] = rows.astype(bf16)
     weighted = dh * gain_ref[...]
     dz = scale * weighted - x * (scale * scale * scale) * jnp.mean(
         x * weighted, axis=-1, keepdims=True
     )
     dx_ref[...] = (dz + dmid_ref[...]).astype(bf16)
-    for copy in copies:
-        copy.wait()
-
-
-def back_in(core, S, x, gain, h1, dq, dk, dv, diag, hot, extra, dmid, qkv_w, tokens):
+
+
+def back_in(S, x, gain, d3, diag, hot, extra, dmid, dense_w, tokens):
     n, width = x.shape
-    cols = 3 * width + PANEL
-    panels = cols // PANEL
-    part = pltpu.HBM((S, panels * width // (2 * S), PANEL), bf16)
     return pl.pallas_call(
         functools.partial(back_in_kernel, S),
-        in_specs=[smem()] + [vmem()] * 10 + [hbm()] + [anywhere()] * len(tokens),
-        out_specs=[vmem(), hbm(), hbm(), vmem()],
-        out_shape=[jax.ShapeDtypeStruct((n, width), bf16), part, part, TOKEN],
-        scratch_shapes=[
-            pltpu.VMEM((width, 3 * width), bf16),
-            pltpu.VMEM((width, cols), bf16),
-            pltpu.SemaphoreType.DMA,
-            pltpu.SemaphoreType.DMA((2 * S * panels,)),
+        in_specs=[vmem()] * 7 + [hbm()] + [anywhere()] * len(tokens),
+        out_specs=[vmem()] * 3,
+        out_shape=[
+            jax.ShapeDtypeStruct((n, width), bf16),
+            jax.ShapeDtypeStruct((width, LANES), bf16),
+            TOKEN,
         ],
+        scratch_shapes=[pltpu.VMEM((width, 3 * width), bf16), pltpu.SemaphoreType.DMA],
         compiler_params=params(60),
         cost_estimate=short(),
         name="back_in",
-    )(core, x, gain, h1, dq, dk, dv, diag, hot, extra, dmid, qkv_w, *tokens)
+    )(x, gain, d3, diag, hot, extra, dmid, dense_w, *tokens)
+
+
+def dense_kernel(S, N, with_small, core_ref, *refs):
+    left, left_o, *refs = refs
+    right, refs = refs[: 2 * N], refs[2 * N :]
+    out, token = refs[-2:]
+    give(token)
+    core = core_ref[0]
+    width = left.shape[1]
+    half, many = width // (2 * S), width // PANEL
+    for s in range(S):
+        a, b = core_columns(left, core, s, half), core_columns(left_o, core, s, half)
+        for j in range(N):
+            total = (dot_tn(a, right[j][...]) + dot_tn(b, right[N + j][...])).astype(bf16)
+            for p in range(many):
+                rows = slice((j * many + p) * half, (j * many + p + 1) * half)
+                out[s, rows, :] = total[:, p * PANEL : (p + 1) * PANEL]
+        if with_small:
+            low, high = slice(2 * s * half, (2 * s + 1) * half), slice((2 * s + 1) * half, (2 * s + 2) * half)
+            total = [
+                jnp.where(core == 0, r[low, :], r[high, :]).astype(f32) for r in refs[:2]
+            ]
+            rows = slice(N * many * half, (N * many + 1) * half)
+            out[s, rows, :LANES] = (total[0] + total[1]).astype(bf16)
+            out[s, rows, LANES:] = jnp.zeros((half, PANEL - LANES), bf16)
+
+
+def dense_grads_of(S, core, left, left_o, right, right_o, small, tokens):
+    n, width = left.shape
+    if isinstance(right, list):
+        N, arrays = len(right), right + right_o
+        specs = [vmem()] * (2 * N)
+    else:
+        N, arrays = 3, [right] * 3 + [right_o] * 3
+        specs = [pl.BlockSpec((None, n, width), lambda i, j=j: (j, 0, 0)) for j in range(3)] * 2
+    panels = N * (width // PANEL) + (1 if small else 0)
+    shape = (S, panels * width // (2 * S), PANEL)
+
+    def whole(x):
+        return pl.BlockSpec(x.shape, lambda i: (0,) * x.ndim)
+
+    out, token = pl.pallas_call(
+        functools.partial(dense_kernel, S, N, bool(small)),
+        grid=(1,),
+        in_specs=[smem(), whole(left), whole(left_o)]
+        + ([whole(x) for x in arrays] if isinstance(right, list) else specs)
+        + [whole(x) for x in small]
+        + [anywhere()] * len(tokens),
+        out_specs=[pl.BlockSpec(shape, lambda i: (0, 0, 0)), token_spec()],
+        out_shape=[jax.ShapeDtypeStruct(shape, bf16), TOKEN],
+        compiler_params=params(60),
+        cost_estimate=short(),
+        name="dense",
+    )(core, left, left_o, *arrays, *small, *tokens)
+    return out, [token]
 
 
 def wave_kernel(shapes_in, shapes_out, *refs):
@@ -661,6 +651,7 @@
         self.ids = [{}, {}]
         self.turn = 0
         self.added = 0
+        self.dense = {}
         self.final = None
         self.targets = {}
         self.last = []
@@ -680,6 +671,38 @@
 
     def busy(self):
         return any(self.queues) or any(self.state) or self.final is not None
+
+    def begin(self):
+        items = [queue.pop(0) for queue in self.queues]
+        rows, cols = items[0][0].shape[1:]
+        steps = max(g for g in (1, 2, 4) if rows % (16 * g) == 0)
+
+        def block(k):
+            return pl.BlockSpec((None, rows // steps, cols), lambda r: (k, r, 0))
+
+        def kernel(*refs):
+            give(refs[-1])
+            outs = refs[-3:-1]
+            for i in range(2):
+                total = refs[2 * i][...].astype(f32) + refs[2 * i + 1][...].astype(f32)
+                outs[i][...] = total.astype(bf16)
+
+        spec = pl.BlockSpec((rows // steps, cols), lambda r: (r, 0))
+        *sums, token = pl.pallas_call(
+            kernel,
+            grid=(steps,),
+            in_specs=[block(k) for item in items for k in (item[1], item[3])]
+            + [anywhere()] * len(self.last),
+            out_specs=[spec, spec, token_spec()],
+            out_shape=[pltpu.HBM((rows, cols), bf16)] * 2 + [TOKEN],
+            compiler_params=params(60),
+            cost_estimate=short(),
+            name="begin",
+        )(*[pin(x) for item in items for x in (item[0], item[2])], *self.last)
+        self.last = [token]
+        for i, item in enumerate(items):
+            self.state[i] = {"s0": sums[i], "pair": sums[i]}
+            self.ids[i] = {"in": (item[4], item[5])}
 
     def step(self, more=()):
         self.last = self.last + list(more)
@@ -724,7 +747,12 @@
         result = self.kernel(ins, outs, self.final[1] if self.final is not None else None)
         if self.final is not None:
             self.targets[self.final[1][0]] = result["final"]
-        self.final = (result["core"], ids["out"]) if "core" in outs else None
+        self.final = None
+        if "core" in outs:
+            if ids["out"][1] is None:
+                self.dense[ids["out"][0]] = result["core"]
+            else:
+                self.final = (result["core"], ids["out"])
         self.last = [result["token"]]
         self.state[stream] = {key: result[key] for key in ("s0", "mid", "pair") if key in outs}
         self.ids[stream] = new_ids
@@ -743,7 +771,7 @@
                     pl.BlockSpec((None, rows // steps, cols), lambda r, k=x[1]: (k, r, 0))
                 )
             else:
-                arrays.append(pin(x))
+                arrays.append(x)
                 specs.append(spec)
         shape = pltpu.HBM((rows, cols), bf16)
         out_specs, out_shapes, extra, aliases = [], [], [], {}
@@ -753,8 +781,7 @@
                 out_specs.append(
                     pl.BlockSpec((None, rows // steps, 2 * cols), lambda r: (expert, r, 0))
                 )
-                count = EXPERTS if name in ("gate", "up", "down") else 1
-                out_shapes.append(pltpu.HBM((count, rows, 2 * cols), f32))
+                out_shapes.append(pltpu.HBM((EXPERTS, rows, 2 * cols), f32))
                 if name in self.targets:
                     extra.append(pin(self.targets[name]))
                     aliases[1 + len(arrays)] = i
@@ -773,6 +800,44 @@
             name="wave",
         )(self.place, *arrays, *extra, *self.last)
         return dict(zip(tuple(outs) + ("token",), values))
+
+
+def assemble_kernel(half, many, place_ref, *refs):
+    mine, other, outs = refs[:2], refs[2:4], refs[4:]
+    core = place_ref[1]
+
+    def rows(parts, first):
+        cut = parts[0].shape[0]
+        if first + half <= cut:
+            return parts[0][first : first + half, :]
+        if first >= cut:
+            return parts[1][first - cut : first - cut + half, :]
+        return jnp.concatenate([parts[0][first:, :], parts[1][: first + half - cut, :]], axis=0)
+
+    def put(out, column, p, width):
+        a = rows(mine, p * half)[:, :width].astype(f32)
+        b = rows(other, p * half)[:, :width].astype(f32)
+        out[:half, column : column + width] = jnp.where(core == 0, a, b)
+        out[half:, column : column + width] = jnp.where(core == 0, b, a)
+
+    for j in range(4):
+        for q in range(many):
+            put(outs[j], q * PANEL, j * many + q + (1 if j == 3 else 0), PANEL)
+    put(outs[4], 0, 3 * many, LANES)
+
+
+def assemble(place, half, width, mine, other):
+    shapes = [jax.ShapeDtypeStruct((2 * half, width), f32)] * 4
+    shapes.append(jax.ShapeDtypeStruct((2 * half, LANES), f32))
+    return pl.pallas_call(
+        functools.partial(assemble_kernel, half, width // PANEL),
+        in_specs=[smem()] + [vmem()] * 4,
+        out_specs=[vmem()] * 5,
+        out_shape=shapes,
+        compiler_params=params(60),
+        cost_estimate=short(),
+        name="assemble",
+    )(place, *mine, *other)
 
 
 def swap_core(x, size):
@@ -898,7 +963,7 @@
     small = jnp.pad(small, ((0, n - part), (0, 0)))
     plan = jnp.concatenate([routes[0], fill_order[0][:, None]], axis=1).astype(bf16)
     small = jnp.concatenate([small, plan], axis=1)
-    small = after(small, blocks[1][0])
+    small = after(small, stack)
     small_all = deal_out(jnp.broadcast_to(small[None], (S,) + small.shape))
     plan_all = small_all[:, :, 3 + EXPERTS :]
     small_all = small_all[:, :part]
@@ -911,12 +976,11 @@
 
     turned = jnp.arange(n, dtype=jnp.int32)
     hot = (bucket_of((n - turned) % n)[None, :] == jnp.arange(BUCKETS)[:, None]).astype(bf16)
-    base = dot_tn(bias_table, hot).reshape(HEADS // 2, 2, n)
-
-    bias = bias_of(length, base)
-    normed_low, qkv, context, dense_w = attn_fwd(offsets, x_low, gain_one[None], bias, dense, pieces)
-    ct_tokens = [ct_all[m][0] for m in range(1, 3)]
-    middle, ffn_in = mid_of(x_low, gain_two[None], context, dense_w, ct_tokens)
+    base = dot_tn(bias_table, hot)
+
+    normed_low, qkv, context, middle, ffn_in, dense_w, bias = attn_fwd(
+        offsets, length, x_low, gain_one[None], gain_two[None], base, dense, pieces
+    )
 
     plan_all = after(plan_all, ffn_in).astype(jnp.int32)
     deal = sequence_deal[0]
@@ -933,9 +997,11 @@
     where = jnp.stack([me, core]).astype(jnp.int32)
     weights = [pin(w) for w in (jnp.swapaxes(w_gate, 1, 2), jnp.swapaxes(w_up, 1, 2), w_down)]
     sums = Sums(R, place)
+    h1_other, context_other = swap_core(normed_low, R), swap_core(context, R)
     chain, aux = (), router_pad
     for experts, groups in (((0, 1), (2, 2, 2)), ((2, 3), (2, 2, 2))):
-        got = ffn(experts, groups, where, pos, aux, h2_all, ct_all, weights, chain, sums.last)
+        first = sums.last if experts[0] == 0 else sums.last + [h1_other, context_other]
+        got = ffn(experts, groups, where, pos, aux, h2_all, ct_all, weights, chain, first)
         M = 1 + len(groups)
         keep, sends, chain = got[0], got[1:M], got[M : M + 2]
         sums.last = [got[M + 2]]
@@ -948,81 +1014,70 @@
                 g, k = where_to[3 * i + j]
                 sums.add(keep, 3 * i + j, recvs[g], k, name, e)
         if experts[0] == 0 and sums.line:
-            sums.step()
-            sums.step()
+            sums.begin()
 
     def run(steps, more=()):
         for _ in range(steps):
             if sums.line and sums.busy():
                 sums.step(more)
 
-    run(1)
     flat = jnp.arange(EXPERTS, dtype=jnp.int32) * CAP
     pos_col = jnp.swapaxes(jnp.where(pos < 0, -1, pos + flat[None, :, None]), 1, 2)
     pos_col = jnp.pad(pos_col, ((0, 0), (0, 0), (0, LANES - EXPERTS)))
+    run(2)
     d_parts, sums.last = combine(me_one, pos_col, chain[1], sums.last)
     d_parts = deal_out(d_parts)
-    run(3)
-
-    dmid, dc, extra, keep, send, token = back_mid(
-        core_one, S, middle, ct_low, gain_two[None], ffn_in, router_pad, context, dense_w, d_parts, sums.last
-    )
-    recv = swap_core(send, R)
-    dq, dk, dv, diag, token = attn_bwd(qkv, bias, dc, [token])
+    run(1)
+    run(1, recvs)
+
+    dmid, dm, dc, extra, token = back_mid(
+        S, middle, ct_low, gain_two[None], ffn_in, router_pad, dense_w, d_parts, sums.last
+    )
+    sums.last = [token]
+    run(0)
+    d3, diag, token = attn_bwd(qkv, bias, dc, sums.last)
     sums.last = [token]
     run(2)
-    grad_x, keep_in, send, token = back_in(
-        core_one, S, x_low, gain_one[None], normed_low, dq, dk, dv, diag.reshape(HEADS, n), hot, extra, dmid, dense_w, sums.last
+    out_grads, sums.last = dense_grads_of(
+        S, core_one, context, context_other, [dm], [swap_core(dm, R)], [], sums.last
+    )
+    out_grads = deal_out(out_grads)
+    run(0)
+    grad_x, extra, token = back_in(
+        S, x_low, gain_one[None], d3, diag.reshape(HEADS, n), hot, extra, dmid, dense_w, sums.last
     )
     sums.last = [token]
-
-    recv_in = swap_core(send, R)
     run(1)
-    halves = jnp.concatenate(
-        [
-            (keep_in.astype(f32) + recv_in.astype(f32)).astype(bf16),
-            (keep.astype(f32) + recv.astype(f32)).astype(bf16),
-        ],
-        axis=1,
-    )
-    run(1, [halves])
-    owned = jnp.sum(deal_out(halves).astype(f32), axis=0).astype(bf16)
+    in_grads, sums.last = dense_grads_of(
+        S, core_one, normed_low, h1_other, d3, swap_core(d3, R), [extra, swap_core(extra, R)], sums.last
+    )
+    in_grads = deal_out(in_grads)
+    run(5)
+
+    owned = [jnp.sum(x.astype(f32), axis=0).astype(bf16) for x in (in_grads, out_grads)]
+    owned = jnp.concatenate(owned, axis=0)
     rows, cut = owned.shape[0], weights[0].shape[1]
-    if sums.line:
+    if sums.line and rows <= 2 * cut:
         owned = jnp.pad(owned, ((0, 2 * cut - rows), (0, 0)))[None]
+        sums.add(owned[:, :cut], 0, None, 0, "top", None)
+        sums.add(owned[:, cut:], 0, None, 0, "bottom", None)
         run(1)
-        sums.add(owned[:, :cut], 0, None, 0, "dense0", 0)
-        sums.add(owned[:, cut:], 0, None, 0, "dense1", 0)
     else:
         owned = line_sum(owned, R)
-        other = swap_core(owned, R)
-        owned = jnp.concatenate(
-            [jnp.where(core == 0, owned, other), jnp.where(core == 0, other, owned)], axis=1
-        ).astype(f32)
-    run(1)
+        sums.dense = {"top": owned[: rows // 2], "bottom": owned[rows // 2 :]}
     out_parts, sums.last = combine(me_one, pos_col, chain[0], sums.last)
     out_parts = deal_out(out_parts)
     run(4)
     result = (middle + jnp.sum(out_parts.astype(f32), axis=0)).astype(bf16)
     run(1, [result])
     run(100)
-    if sums.line:
-        owned = jnp.concatenate([sums.targets["dense0"][0], sums.targets["dense1"][0]], axis=0)
-
-    def matrix(first, count):
-        x = owned[first * half : (first + count) * half].reshape(count, half, 2, PANEL)
-        return jnp.transpose(x, (2, 1, 0, 3)).reshape(part, count * PANEL)
-
-    many = width // PANEL
-    small = matrix(3 * many, 1)
-    grad_in_w = [matrix(j * many, many) for j in range(3)]
-    grad_out_w = matrix(3 * many + 1, many)
+    mine = [sums.dense["top"], sums.dense["bottom"]]
+    *dense_grads, small = assemble(place, half, width, mine, [swap_core(x, R) for x in mine])
     return (
         result[None],
         grad_x[None],
         small[:, 0],
-        *grad_in_w,
-        grad_out_w,
+        *dense_grads,
         small[: BUCKETS // S, 8 : 8 + HEADS],
         small[:, 1],
         small[:, 2 : 2 + EXPERTS],

time: 573 us -> 499 us (0.87)
  waiting for transfers between devices: 139 us -> 96.8 us
  local copies, waits for them, and re-layouts: 60.2 us -> 36.1 us
  Pallas kernels: 240 us -> 231 us
  starting transfers between devices: 107 us -> 114 us
  other arithmetic: 17.7 us -> 11.2 us
    ppermute x18, waiting for transfers between devices: 86.8 us -> 49.1 us  [step(): ins['got_pair'] = lax.ppermute(state['pair'], rep_axis, pairs)]
    reshape x5 -> x0, local copies, waits for them, and re-layouts: 6.5 us -> none  [matrix(): owned[first * half:(first + count) * half].reshape(count, half, 2, PANEL)]
    pallas_call x21 -> x20, Pallas kernels: 101 us -> 94.9 us  [kernel(): pl.pallas_call(functools.partial(wave_kernel, tuple(ins), tuple(outs) + (...]
    slice x5 -> x2, local copies, waits for them, and re-layouts: 7.17 us -> 1.22 us  [the longest x1 1.21 us: shards(): sums.add(owned[:, cut:], 0, None, 0, 'bottom', None)]
    unnamed x119 -> x124, local copies, waits for them, and re-layouts: 24.1 us -> 19 us
    all_to_all x4 -> x5, starting transfers between devices: 16.6 us -> 21.3 us  [deal_out(): return lax.all_to_all(x, 'shard', 0, 0, tiled=True)]
    pallas_call x6 -> x8, Pallas kernels: 61.4 us -> 62.2 us  [the longest x1 16.9 us: attn_fwd(): pl.pallas_call(functools.partial(attn_fwd_kernel, N), in_specs=[smem(), s...]
  transfers between devices with their start and end apart: 74 -> 78, of which waited for: 21 -> 20; matrix products, arithmetic and copies ran while one was open for 7% -> 5% of each run, Pallas kernels for 31% -> 40%
where the time goes in v3:
time: 499 us; the launch traced here: 492 us
  Pallas kernels  231 us (46%)
  starting transfers between devices  114 us (23%)
  waiting for transfers between devices  96.8 us (19%)
  local copies, waits for them, and re-layouts  36.1 us (7%)
  other arithmetic  11.2 us (2%)
    pallas_call x20, Pallas kernels, kernel(): pl.pallas_call(functools.partial(wave_kernel, tuple(ins), tuple(outs) + (...  94.9 us
    pallas_call x2, Pallas kernels, ffn(): pl.pallas_call(functools.partial(ffn_kernel, shape, experts, groups, len(...  61 us
    ppermute x18, starting transfers between devices, step(): ins['got_pair'] = lax.ppermute(state['pair'], rep_axis, pairs)  52.5 us
    ppermute x18, waiting for transfers between devices, step(): ins['got_pair'] = lax.ppermute(state['pair'], rep_axis, pairs)  49.1 us
    ppermute x12, waiting for transfers between devices, swap_shard(): return lax.ppermute(x, 'shard', [(i, i ^ mask) for i in range(size)])  39.1 us
    all_to_all x5, starting transfers between devices, deal_out(): return lax.all_to_all(x, 'shard', 0, 0, tiled=True)  21.3 us
    unnamed x124, local copies, waits for them, and re-layouts  19 us
    ppermute x14, starting transfers between devices, step(): lax.ppermute(state['mid'], rep_axis, line_perm([(1, 2), (2, 1)]))  18.5 us
  transfers between devices with their start and end apart: 78, of which 20 were waited for; matrix products, arithmetic and copies ran while one was open for 5% of the time, Pallas kernels for 40%

profile of v3, /device:TPU:0, one launch (start us, length us, event | category | flops | bytes accessed | tf_op | source)
XLA Modules:
  0.0 492.0 jit_solution(15562943142430798740)
XLA Ops:
  12.8 16.1 %collective-permute-done.2.refs_12_ = bf16[128,4096]{1,0:T(8,128)(2,1)S(1)} collective-permute-done((bf16[128,4096]{1,0:T(8,128)(2,1)S(1)}, bf16[128,4096]{1,0:T(8,128)(2,1)S(1)}, u32[]{:S(2)}, u32[]{:S(2)}) %collective-permute-start.2) | collective-permute-done | bytes 1048608 | tf_op jit(solution)/shard_map/ppermute | solution.py:848
  34.0 8.1 %collective-permute-done.5.refs_15_ = bf16[64,4096]{1,0:T(8,128)(2,1)S(1)} collective-permute-done((bf16[64,4096]{1,0:T(8,128)(2,1)S(1)}, bf16[64,4096]{1,0:T(8,128)(2,1)S(1)}, u32[]{:S(2)}, u32[]{:S(2)}) %collective-permute-start.5) | collective-permute-done | bytes 524320 | tf_op jit(solution)/shard_map/ppermute | solution.py:848
  50.9 16.9 %attn_fwd.1 = (bf16[256,1024]{1,0:T(8,128)(2,1)}, bf16[256,3072]{1,0:T(8,128)(2,1)}, bf16[256,1024]{1,0:T(8,128)(2,1)}, f32[256,1024]{1,0:T(8,128)}, bf16[256,10...) custom-call(s32[9]{0:T(128)} %stack.53.refs_0_, s32[1]{0:T(128)} %bitcast.9.refs_1_, ...), custom_call_target="tpu_custom_call" | custom-call | flops 1 | bytes 1 | tf_op jit(solution)/shard_map/attn_fwd/pallas_call | solution.py:150
  75.4 7.5 %collective-permute-done.9.refs_5_ = bf16[256,1024]{1,0:T(8,128)(2,1)S(1)} collective-permute-done((bf16[256,1024]{1,0:T(8,128)(2,1)}, bf16[256,1024]{1,0:T(8,128)(2,1)S(1)}, u32[]{:S(2)}, u32[]{:S(2)}) %collective-permute-start.9) | collective-permute-done | bytes 524320 | tf_op jit(solution)/shard_map/ppermute | solution.py:848
  89.0 4.9 collective-permute-done.11.refs_7_
  94.8 30.7 %ffn0.1 = (bf16[6,704,512]{2,1,0:T(8,128)(2,1)}, bf16[2,704,512]{2,1,0:T(8,128)(2,1)}, bf16[2,704,512]{2,1,0:T(8,128)(2,1)}, bf16[2,704,512]{2,1,0:T(8,128)(2,1)...) custom-call(s32[2]{0:T(128)} %pad_add_fusion.refs_0_, ...), custom_call_target="tpu_custom_call" | custom-call | flops 1 | bytes 1 | tf_op jit(solution)/shard_map/ffn0/pallas_call | solution.py:356
  138.7 30.3 %ffn2.1 = (bf16[6,704,512]{2,1,0:T(8,128)(2,1)}, bf16[2,704,512]{2,1,0:T(8,128)(2,1)}, bf16[2,704,512]{2,1,0:T(8,128)(2,1)}, bf16[2,704,512]{2,1,0:T(8,128)(2,1)...) custom-call(s32[2]{0:T(128)} %pad_add_fusion.refs_0_, ...), custom_call_target="tpu_custom_call", output_to_operand_aliasing={{4}: (19, {}), {5}: (20, {})} | custom-call | flops 1 | bytes 1 | tf_op jit(solution)/shard_map/ffn2/pallas_call | solution.py:356
  182.2 6.6 %combine.2 = (bf16[4,256,1152]{2,1,0:T(8,128)(2,1)}, f32[8,128]{1,0:T(8,128)}) custom-call(s32[1]{0:T(128)} %bitcast.15.me_ref, s32[4,256,128]{2,1,0:T(8,128)} %pad.17.pos_ref, bf16[4,576,1152]{2,1,0:T(8,128)(2,1)} %get-tuple-element.175.src_ref, f32[8,128]{1,0:T(8,128)} %get-tuple-element.178.refs_0_), custom_call_target="tpu_custom_call" | custom-call | flops 1 | bytes 1 | tf_op jit(solution)/shard_map/combine/pallas_call | solution.py:402
  188.8 4.6 all-to-all-start.1
  203.5 11.2 %collective-permute-done.28.refs_1_ = bf16[704,512]{1,0:T(8,128)(2,1)} collective-permute-done((bf16[704,512]{1,0:T(8,128)(2,1)}, bf16[704,512]{1,0:T(8,128)(2,1)}, u32[]{:S(2)}, u32[]{:S(2)}) %collective-permute-start.28) | collective-permute-done | bytes 720928 | tf_op jit(solution)/shard_map/ppermute | solution.py:716
  228.3 6.0 %back_mid.1 = (f32[256,1024]{1,0:T(8,128)}, bf16[256,1024]{1,0:T(8,128)(2,1)}, bf16[256,1024]{1,0:T(8,128)(2,1)}, f32[1024,128]{1,0:T(8,128)}, f32[8,128]{1,0:T(8,128)}) custom-call(f32[256,1024]{1,0:T(8,128)} %get-tuple-element.154.refs_0_, bf16[256,1024]{1,0:T(8,128)(2,1)} %bitcast.53, f32[1,1024]{1,0:T(1,128)} %convert.14.refs_4_.refs_2_, ...), custom_call_target="tpu_custom_call" | custom-call | flops 1 | bytes 1 | tf_op jit(solution)/shard_map/back_mid/pallas_call | solution.py:485
  234.3 13.8 %attn_bwd.1 = (bf16[3,256,1024]{2,1,0:T(8,128)(2,1)}, f32[4,4,256]{2,1,0:T(4,128)}, f32[8,128]{1,0:T(8,128)}) custom-call(bf16[256,3072]{1,0:T(8,128)(2,1)} %get-tuple-element.185.q_ref.k_ref.v_ref, bf16[256,3072]{1,0:T(8,128)(2,1)} %get-tuple-element.185.q_ref.k_ref.v_ref, bf16[256,3072]{1,0:T(8,128)(2,1)} %get-tuple-element.185.q_ref.k_ref.v_ref, ...), custom_call_target="tpu_custom_call" | custom-call | flops 1 | bytes 1 | tf_op jit(solution)/shard_map/attn_bwd/pallas_call | solution.py:201
  249.0 4.7 wave.24
  257.6 5.7 %wave.25 = (bf16[704,512]{1,0:T(8,128)(2,1)}, bf16[704,512]{1,0:T(8,128)(2,1)}, bf16[704,512]{1,0:T(8,128)(2,1)}, bf16[704,512]{1,0:T(8,128)(2,1)}, f32[4,704,1024]{2,1,0:T(8,128)}, /*index=5*/f32[8,128]{1,0:T(8,128)}) custom-call(s32[2]{0:T(128)} %pad_add_fusion.1.refs_0_.place_ref, bf16[704,512]{1,0:T(8,128)(2,1)} %collective-permute-done.34.refs_1_, ...), custom_call_target="tpu_custom_call" | custom-call | flops 1 | bytes 1 | tf_op jit(solution)/shard_map/wave/pallas_call | solution.py:791
  271.9 8.3 %back_in.1 = (bf16[256,1024]{1,0:T(8,128)(2,1)}, bf16[1024,128]{1,0:T(8,128)(2,1)}, f32[8,128]{1,0:T(8,128)}) custom-call(bf16[256,1024]{1,0:T(8,128)(2,1)} %bitcast.58, f32[1,1024]{1,0:T(1,128)} %convert.15.refs_3_.gain_ref, bf16[3,256,1024]{2,1,0:T(8,128)(2,1)} %get-tuple-element.208.d_ref.refs_2_.refs_3_.refs_4_, f32[16,256]{1,0:T(8,128)} %reshape.171.diag_ref, ...), custom_call_target="tpu_custom_call" | custom-call | flops 1 | bytes 1 | tf_op jit(solution)/shard_map/back_in/pallas_call | solution.py:541
  281.8 5.7 %wave.26 = (bf16[704,512]{1,0:T(8,128)(2,1)}, bf16[704,512]{1,0:T(8,128)(2,1)}, bf16[704,512]{1,0:T(8,128)(2,1)}, bf16[704,512]{1,0:T(8,128)(2,1)}, f32[4,704,1024]{2,1,0:T(8,128)}, /*index=5*/f32[8,128]{1,0:T(8,128)}) custom-call(s32[2]{0:T(128)} %pad_add_fusion.1.refs_0_.place_ref, bf16[704,512]{1,0:T(8,128)(2,1)} %collective-permute-done.32.refs_1_, ...), custom_call_target="tpu_custom_call" | custom-call | flops 1 | bytes 1 | tf_op jit(solution)/shard_map/wave/pallas_call | solution.py:791
  295.9 6.0 %dense.3 = (bf16[4,896,512]{2,1,0:T(8,128)(2,1)}, f32[8,128]{1,0:T(8,128)}) custom-call(s32[1]{0:T(128)} %bitcast.21.core_ref, bf16[256,1024]{1,0:T(8,128)(2,1)} %get-tuple-element.163.refs_0_, bf16[256,1024]{1,0:T(8,128)(2,1)} %copy-done.15, bf16[3,256,1024]{2,1,0:T(8,128)(2,1)} %get-tuple-element.208.d_ref.refs_2_.refs_3_.refs_4_, ...), custom_call_target="tpu_custom_call" | custom-call | flops 1 | bytes 1 | tf_op jit(solution)/shard_map/dense/pallas_call | solution.py:596
  301.9 5.8 %wave.27 = (bf16[704,512]{1,0:T(8,128)(2,1)}, bf16[704,512]{1,0:T(8,128)(2,1)}, bf16[704,512]{1,0:T(8,128)(2,1)}, bf16[704,512]{1,0:T(8,128)(2,1)}, f32[4,704,1024]{2,1,0:T(8,128)}, /*index=5*/f32[8,128]{1,0:T(8,128)}) custom-call(s32[2]{0:T(128)} %pad_add_fusion.1.refs_0_.place_ref, bf16[704,512]{1,0:T(8,128)(2,1)} %collective-permute-done.41.refs_1_, ...), custom_call_target="tpu_custom_call" | custom-call | flops 1 | bytes 1 | tf_op jit(solution)/shard_map/wave/pallas_call | solution.py:791
  307.8 4.9 all-to-all-start.2
  317.7 5.7 %wave.28 = (bf16[704,512]{1,0:T(8,128)(2,1)}, bf16[704,512]{1,0:T(8,128)(2,1)}, bf16[704,512]{1,0:T(8,128)(2,1)}, bf16[704,512]{1,0:T(8,128)(2,1)}, f32[4,704,1024]{2,1,0:T(8,128)}, /*index=5*/f32[8,128]{1,0:T(8,128)}) custom-call(s32[2]{0:T(128)} %pad_add_fusion.1.refs_0_.place_ref, ...), custom_call_target="tpu_custom_call", output_to_operand_aliasing={{4}: (10, {})} | custom-call | flops 1 | bytes 1 | tf_op jit(solution)/shard_map/wave/pallas_call | solution.py:791
  326.0 6.2 %collective-permute-done.49.refs_1_ = bf16[704,512]{1,0:T(8,128)(2,1)S(1)} collective-permute-done((bf16[704,512]{1,0:T(8,128)(2,1)S(1)}, bf16[704,512]{1,0:T(8,128)(2,1)S(1)}, u32[]{:S(2)}, u32[]{:S(2)}) %collective-permute-start.49) | collective-permute-done | bytes 720928 | tf_op jit(solution)/shard_map/ppermute | solution.py:716
  333.1 5.7 %wave.29 = (bf16[704,512]{1,0:T(8,128)(2,1)}, bf16[704,512]{1,0:T(8,128)(2,1)}, bf16[704,512]{1,0:T(8,128)(2,1)}, bf16[704,512]{1,0:T(8,128)(2,1)}, f32[4,704,1024]{2,1,0:T(8,128)}, /*index=5*/f32[8,128]{1,0:T(8,128)}) custom-call(s32[2]{0:T(128)} %pad_add_fusion.1.refs_0_.place_ref, bf16[704,512]{1,0:T(8,128)(2,1)} %copy-done.47, ...), custom_call_target="tpu_custom_call", output_to_operand_aliasing={{4}: (10, {})} | custom-call | flops 1 | bytes 1 | tf_op jit(solution)/shard_map/wave/pallas_call | solution.py:791
  349.0 5.1 %wave.30 = (bf16[704,512]{1,0:T(8,128)(2,1)}, bf16[704,512]{1,0:T(8,128)(2,1)}, bf16[704,512]{1,0:T(8,128)(2,1)}, f32[4,704,1024]{2,1,0:T(8,128)}, f32[8,128]{1,0:T(8,128)}) custom-call(s32[2]{0:T(128)} %pad_add_fusion.1.refs_0_.place_ref, bf16[704,512]{1,0:T(8,128)(2,1)} %copy-done.30, ...), custom_call_target="tpu_custom_call", output_to_operand_aliasing={{3}: (8, {})} | custom-call | flops 1 | bytes 1 | tf_op jit(solution)/shard_map/wave/pallas_call | solution.py:791
  364.2 5.1 %wave.31 = (bf16[704,512]{1,0:T(8,128)(2,1)}, bf16[704,512]{1,0:T(8,128)(2,1)}, bf16[704,512]{1,0:T(8,128)(2,1)}, f32[4,704,1024]{2,1,0:T(8,128)}, f32[8,128]{1,0:T(8,128)}) custom-call(s32[2]{0:T(128)} %pad_add_fusion.1.refs_0_.place_ref, bf16[704,512]{1,0:T(8,128)(2,1)} %copy-done.32, ...), custom_call_target="tpu_custom_call", output_to_operand_aliasing={{3}: (8, {})} | custom-call | flops 1 | bytes 1 | tf_op jit(solution)/shard_map/wave/pallas_call | solution.py:791
  381.9 5.1 %wave.32 = (bf16[704,512]{1,0:T(8,128)(2,1)}, bf16[704,512]{1,0:T(8,128)(2,1)}, bf16[704,512]{1,0:T(8,128)(2,1)}, f32[4,704,1024]{2,1,0:T(8,128)}, f32[8,128]{1,0:T(8,128)}) custom-call(s32[2]{0:T(128)} %pad_add_fusion.1.refs_0_.place_ref, bf16[704,512]{1,0:T(8,128)(2,1)} %copy-done.26, ...), custom_call_target="tpu_custom_call", output_to_operand_aliasing={{3}: (8, {})} | custom-call | flops 1 | bytes 1 | tf_op jit(solution)/shard_map/wave/pallas_call | solution.py:791
  389.5 6.3 %combine.3 = (bf16[4,256,1024]{2,1,0:T(8,128)(2,1)}, f32[8,128]{1,0:T(8,128)}) custom-call(s32[1]{0:T(128)} %bitcast.15.me_ref, s32[4,256,128]{2,1,0:T(8,128)} %pad.17.pos_ref, bf16[4,576,1024]{2,1,0:T(8,128)(2,1)} %get-tuple-element.167.src_ref, f32[8,128]{1,0:T(8,128)} %get-tuple-element.254.refs_0_), custom_call_target="tpu_custom_call" | custom-call | flops 1 | bytes 1 | tf_op jit(solution)/shard_map/combine/pallas_call | solution.py:402
  397.3 5.1 %wave.33 = (bf16[704,512]{1,0:T(8,128)(2,1)}, bf16[704,512]{1,0:T(8,128)(2,1)}, bf16[704,512]{1,0:T(8,128)(2,1)}, f32[4,704,1024]{2,1,0:T(8,128)}, f32[8,128]{1,0:T(8,128)}) custom-call(s32[2]{0:T(128)} %pad_add_fusion.1.refs_0_.place_ref, bf16[704,512]{1,0:T(8,128)(2,1)} %copy-done.28, ...), custom_call_target="tpu_custom_call", output_to_operand_aliasing={{3}: (8, {})} | custom-call | flops 1 | bytes 1 | tf_op jit(solution)/shard_map/wave/pallas_call | solution.py:791
  411.6 4.6 wave.34
  417.8 9.3 %collective-permute-done.65.refs_1_ = bf16[704,512]{1,0:T(8,128)(2,1)S(1)} collective-permute-done((bf16[704,512]{1,0:T(8,128)(2,1)S(1)}, bf16[704,512]{1,0:T(8,128)(2,1)S(1)}, u32[]{:S(2)}, u32[]{:S(2)}) %collective-permute-start.65) | collective-permute-done | bytes 720928 | tf_op jit(solution)/shard_map/ppermute | solution.py:716
  427.9 4.6 wave.35
  447.0 11.6 %collective-permute-start.70 = (bf16[704,512]{1,0:T(8,128)(2,1)}, bf16[704,512]{1,0:T(8,128)(2,1)S(1)}, u32[]{:S(2)}, u32[]{:S(2)}) collective-permute-start(bf16[704,512]{1,0:T(8,128)(2,1)} %get-tuple-element.281.refs_2_), channel_id=1, source_target_pairs={{0,8},{4,12},{8,0},{12,4},{16,24},{20,28},{24,16},{28,20},{1,9},{5... | collective-permute-start | bytes 2162696 | tf_op jit(solution)/shard_map/ppermute | solution.py:716
  464.9 10.6 %collective-permute-done.70.refs_1_ = bf16[704,512]{1,0:T(8,128)(2,1)S(1)} collective-permute-done((bf16[704,512]{1,0:T(8,128)(2,1)}, bf16[704,512]{1,0:T(8,128)(2,1)S(1)}, u32[]{:S(2)}, u32[]{:S(2)}) %collective-permute-start.70) | collective-permute-done | bytes 720928 | tf_op jit(solution)/shard_map/ppermute | solution.py:716
  (351 shorter events, 207.0 us)
Async XLA Ops:
  2.6 26.3 %collective-permute-start.2 = (bf16[128,4096]{1,0:T(8,128)(2,1)S(1)}, bf16[128,4096]{1,0:T(8,128)(2,1)S(1)}, u32[]{:S(2)}, u32[]{:S(2)}) collective-permute-start(bf16[128,4096]{1,0:T(8,128)(2,1)S(1)} %maximum_select_fusion), channel_id=1, source_target_pairs={{0,2},{1,3},{2,0},{3,1},{4,6},{5,7},{6,4},{7,5},{8,10},{9,11},{10,... | collective-permute-start | bytes 3145736 | tf_op jit(solution)/shard_map/ppermute | solution.py:848
  5.7 25.2 %collective-permute-start = (bf16[128,4096]{1,0:T(8,128)(2,1)S(1)}, bf16[128,4096]{1,0:T(8,128)(2,1)}, u32[]{:S(2)}, u32[]{:S(2)}) collective-permute-start(bf16[128,4096]{1,0:T(8,128)(2,1)S(1)} %maximum_select_fusion), channel_id=1, source_target_pairs={{0,1},{1,0},{2,3},{3,2},{4,5},{5,4},{6,7},{7,6},{8,9},{9,8},{10,11... | collective-permute-start | bytes 3145736 | tf_op jit(solution)/shard_map/ppermute | solution.py:848
  8.1 39.7 %all-to-all-start = ((bf16[4,256,10]{1,2,0:T(8,128)(2,1)}), bf16[4,256,10]{1,2,0:T(8,128)(2,1)S(1)}, u32[]{:S(2)}, u32[]{:S(2)}) async-start(bf16[4,256,10]{1,2,0:T(8,128)(2,1)} %broadcast_in_dim.68), calls=%async_computation | async-start | bytes 65536 | tf_op jit(solution)/shard_map/all_to_all | solution.py:881
  45.3 24.2 %collective-permute-start.13 = (bf16[256,1024]{1,0:T(8,128)(2,1)S(1)}, bf16[256,1024]{1,0:T(8,128)(2,1)S(1)}, u32[]{:S(2)}, u32[]{:S(2)}) collective-permute-start(bf16[256,1024]{1,0:T(8,128)(2,1)S(1)} %bitcast.54), channel_id=1, source_target_pairs={{0,2},{1,3},{2,0},{3,1},{4,6},{5,7},{6,4},{7,5},{8,10},{9,11},{10,... | collective-permute-start | bytes 1572872 | tf_op jit(solution)/shard_map/ppermute | solution.py:848
  46.8 24.5 %collective-permute-start.12 = (bf16[256,1024]{1,0:T(8,128)(2,1)S(1)}, bf16[256,1024]{1,0:T(8,128)(2,1)S(1)}, u32[]{:S(2)}, u32[]{:S(2)}) collective-permute-start(bf16[256,1024]{1,0:T(8,128)(2,1)S(1)} %bitcast.55), channel_id=1, source_target_pairs={{0,1},{1,0},{2,3},{3,2},{4,5},{5,4},{6,7},{7,6},{8,9},{9,8},{10,11... | collective-permute-start | bytes 1572872 | tf_op jit(solution)/shard_map/ppermute | solution.py:848
  125.6 43.4 %collective-permute-start.20 = (bf16[2,704,512]{2,1,0:T(8,128)(2,1)}, bf16[2,704,512]{2,1,0:T(8,128)(2,1)S(1)}, u32[]{:S(2)}, u32[]{:S(2)}) collective-permute-start(bf16[2,704,512]{2,1,0:T(8,128)(2,1)} %get-tuple-element.169), channel_id=1, source_target_pairs={{0,4},{4,0},{8,12},{12,8},{16,20},{20,16},{24,28},{28,24},{1,5},{5... | collective-permute-start | bytes 4325384 | tf_op jit(solution)/shard_map/ppermute | solution.py:844
  126.2 67.8 %collective-permute-start.23 = (bf16[2,704,512]{2,1,0:T(8,128)(2,1)}, bf16[2,704,512]{2,1,0:T(8,128)(2,1)}, u32[]{:S(2)}, u32[]{:S(2)}) collective-permute-start(bf16[2,704,512]{2,1,0:T(8,128)(2,1)} %get-tuple-element.174), channel_id=1, source_target_pairs={{0,4},{4,0},{8,12},{12,8},{16,20},{20,16},{24,28},{28,24},{1,5},{5... | collective-permute-start | bytes 4325384 | tf_op jit(solution)/shard_map/ppermute | solution.py:844
  134.2 34.9 %collective-permute-start.19 = (bf16[704,512]{1,0:T(8,128)(2,1)}, bf16[704,512]{1,0:T(8,128)(2,1)}, u32[]{:S(2)}, u32[]{:S(2)}) collective-permute-start(bf16[704,512]{1,0:T(8,128)(2,1)} %get-tuple-element.168.refs_2_), channel_id=1, source_target_pairs={{0,8},{4,12},{8,0},{12,4},{16,24},{20,28},{24,16},{28,20},{1,9},{5... | collective-permute-start | bytes 2162696 | tf_op jit(solution)/shard_map/ppermute | solution.py:716
  135.8 41.4 %collective-permute-start.24 = (bf16[704,512]{1,0:T(8,128)(2,1)}, bf16[704,512]{1,0:T(8,128)(2,1)S(1)}, u32[]{:S(2)}, u32[]{:S(2)}) collective-permute-start(bf16[704,512]{1,0:T(8,128)(2,1)} %get-tuple-element.176.refs_2_), channel_id=1, source_target_pairs={{0,8},{4,12},{8,0},{12,4},{16,24},{20,28},{24,16},{28,20},{1,9},{5... | collective-permute-start | bytes 2162696 | tf_op jit(solution)/shard_map/ppermute | solution.py:716
  174.9 22.8 %collective-permute-start.22 = (bf16[704,512]{1,0:T(8,128)(2,1)}, bf16[704,512]{1,0:T(8,128)(2,1)}, u32[]{:S(2)}, u32[]{:S(2)}) collective-permute-start(bf16[704,512]{1,0:T(8,128)(2,1)} %get-tuple-element.172.refs_2_), channel_id=1, source_target_pairs={{8,16},{12,20},{16,8},{20,12},{9,17},{13,21},{17,9},{21,13},{10,18... | collective-permute-start | bytes 2162696 | tf_op jit(solution)/shard_map/ppermute | solution.py:719
  188.8 39.5 %all-to-all-start.1 = ((bf16[4,256,1152]{2,1,0:T(8,128)(2,1)}), bf16[4,256,1152]{2,1,0:T(8,128)(2,1)}, u32[]{:S(2)}, u32[]{:S(2)}) async-start(bf16[4,256,1152]{2,1,0:T(8,128)(2,1)} %get-tuple-element.188), calls=%async_computation.1 | async-start | bytes 4718592 | tf_op jit(solution)/shard_map/all_to_all | solution.py:881
  193.4 23.7 %collective-permute-start.27 = (bf16[2,704,512]{2,1,0:T(8,128)(2,1)}, bf16[2,704,512]{2,1,0:T(8,128)(2,1)S(1)}, u32[]{:S(2)}, u32[]{:S(2)}) collective-permute-start(bf16[2,704,512]{2,1,0:T(8,128)(2,1)} %get-tuple-element.184), channel_id=1, source_target_pairs={{0,4},{4,0},{8,12},{12,8},{16,20},{20,16},{24,28},{28,24},{1,5},{5... | collective-permute-start | bytes 4325384 | tf_op jit(solution)/shard_map/ppermute | solution.py:844
  193.5 23.7 %collective-permute-start.30 = (bf16[2,704,512]{2,1,0:T(8,128)(2,1)}, bf16[2,704,512]{2,1,0:T(8,128)(2,1)S(1)}, u32[]{:S(2)}, u32[]{:S(2)}) collective-permute-start(bf16[2,704,512]{2,1,0:T(8,128)(2,1)} %get-tuple-element.193), channel_id=1, source_target_pairs={{0,4},{4,0},{8,12},{12,8},{16,20},{20,16},{24,28},{28,24},{1,5},{5... | collective-permute-start | bytes 4325384 | tf_op jit(solution)/shard_map/ppermute | solution.py:844
  194.0 23.2 %collective-permute-start.31 = (bf16[2,704,512]{2,1,0:T(8,128)(2,1)}, bf16[2,704,512]{2,1,0:T(8,128)(2,1)}, u32[]{:S(2)}, u32[]{:S(2)}) collective-permute-start(bf16[2,704,512]{2,1,0:T(8,128)(2,1)} %get-tuple-element.194), channel_id=1, source_target_pairs={{0,4},{4,0},{8,12},{12,8},{16,20},{20,16},{24,28},{28,24},{1,5},{5... | collective-permute-start | bytes 4325384 | tf_op jit(solution)/shard_map/ppermute | solution.py:844
  214.7 33.4 %collective-permute-start.25 = (bf16[704,512]{1,0:T(8,128)(2,1)}, bf16[704,512]{1,0:T(8,128)(2,1)}, u32[]{:S(2)}, u32[]{:S(2)}) collective-permute-start(bf16[704,512]{1,0:T(8,128)(2,1)} %get-tuple-element.180.refs_5_), channel_id=1, source_target_pairs={{0,8},{4,12},{8,0},{12,4},{16,24},{20,28},{24,16},{28,20},{1,9},{5... | collective-permute-start | bytes 2162696 | tf_op jit(solution)/shard_map/ppermute | solution.py:716
  216.5 31.7 %collective-permute-start.26 = (bf16[704,512]{1,0:T(8,128)(2,1)}, bf16[704,512]{1,0:T(8,128)(2,1)S(1)}, u32[]{:S(2)}, u32[]{:S(2)}) collective-permute-start(bf16[704,512]{1,0:T(8,128)(2,1)} %get-tuple-element.181.refs_2_), channel_id=1, source_target_pairs={{8,16},{12,20},{16,8},{20,12},{9,17},{13,21},{17,9},{21,13},{10,18... | collective-permute-start | bytes 2162696 | tf_op jit(solution)/shard_map/ppermute | solution.py:719
  223.2 32.9 %collective-permute-start.34 = (bf16[704,512]{1,0:T(8,128)(2,1)}, bf16[704,512]{1,0:T(8,128)(2,1)}, u32[]{:S(2)}, u32[]{:S(2)}) collective-permute-start(bf16[704,512]{1,0:T(8,128)(2,1)} %get-tuple-element.202.refs_5_), channel_id=1, source_target_pairs={{0,8},{4,12},{8,0},{12,4},{16,24},{20,28},{24,16},{28,20},{1,9},{5... | collective-permute-start | bytes 2162696 | tf_op jit(solution)/shard_map/ppermute | solution.py:716
  226.8 30.8 %collective-permute-start.35 = (bf16[704,512]{1,0:T(8,128)(2,1)}, bf16[704,512]{1,0:T(8,128)(2,1)}, u32[]{:S(2)}, u32[]{:S(2)}) collective-permute-start(bf16[704,512]{1,0:T(8,128)(2,1)} %get-tuple-element.203.refs_2_), channel_id=1, source_target_pairs={{8,16},{12,20},{16,8},{20,12},{9,17},{13,21},{17,9},{21,13},{10,18... | collective-permute-start | bytes 2162696 | tf_op jit(solution)/shard_map/ppermute | solution.py:719
  253.8 40.9 %collective-permute-start.44 = (bf16[3,256,1024]{2,1,0:T(8,128)(2,1)S(1)}, bf16[3,256,1024]{2,1,0:T(8,128)(2,1)S(1)}, u32[]{:S(2)}, u32[]{:S(2)}) collective-permute-start(bf16[3,256,1024]{2,1,0:T(8,128)(2,1)S(1)} %copy-done.2), channel_id=1, source_target_pairs={{0,4},{4,0},{8,12},{12,8},{16,20},{20,16},{24,28},{28,24},{1,5},{5... | collective-permute-start | bytes 4718600 | tf_op jit(solution)/shard_map/ppermute | solution.py:844
  254.3 25.9 %collective-permute-start.32 = (bf16[704,512]{1,0:T(8,128)(2,1)}, bf16[704,512]{1,0:T(8,128)(2,1)}, u32[]{:S(2)}, u32[]{:S(2)}) collective-permute-start(bf16[704,512]{1,0:T(8,128)(2,1)} %get-tuple-element.199.refs_5_), channel_id=1, source_target_pairs={{0,8},{4,12},{8,0},{12,4},{16,24},{20,28},{24,16},{28,20},{1,9},{5... | collective-permute-start | bytes 2162696 | tf_op jit(solution)/shard_map/ppermute | solution.py:716
  256.1 25.7 %collective-permute-start.33 = (bf16[704,512]{1,0:T(8,128)(2,1)}, bf16[704,512]{1,0:T(8,128)(2,1)}, u32[]{:S(2)}, u32[]{:S(2)}) collective-permute-start(bf16[704,512]{1,0:T(8,128)(2,1)} %get-tuple-element.200.refs_2_), channel_id=1, source_target_pairs={{8,16},{12,20},{16,8},{20,12},{9,17},{13,21},{17,9},{21,13},{10,18... | collective-permute-start | bytes 2162696 | tf_op jit(solution)/shard_map/ppermute | solution.py:719
  266.7 35.2 %collective-permute-start.41 = (bf16[704,512]{1,0:T(8,128)(2,1)}, bf16[704,512]{1,0:T(8,128)(2,1)}, u32[]{:S(2)}, u32[]{:S(2)}) collective-permute-start(bf16[704,512]{1,0:T(8,128)(2,1)} %get-tuple-element.219.refs_5_), channel_id=1, source_target_pairs={{0,8},{4,12},{8,0},{12,4},{16,24},{20,28},{24,16},{28,20},{1,9},{5... | collective-permute-start | bytes 2162696 | tf_op jit(solution)/shard_map/ppermute | solution.py:716
  293.6 23.2 %collective-permute-start.39 = (bf16[704,512]{1,0:T(8,128)(2,1)}, bf16[704,512]{1,0:T(8,128)(2,1)}, u32[]{:S(2)}, u32[]{:S(2)}) collective-permute-start(bf16[704,512]{1,0:T(8,128)(2,1)} %get-tuple-element.216.refs_5_), channel_id=1, source_target_pairs={{0,8},{4,12},{8,0},{12,4},{16,24},{20,28},{24,16},{28,20},{1,9},{5... | collective-permute-start | bytes 2162696 | tf_op jit(solution)/shard_map/ppermute | solution.py:716
  307.8 63.1 %all-to-all-start.2 = ((bf16[4,896,512]{2,1,0:T(8,128)(2,1)}), bf16[4,896,512]{2,1,0:T(8,128)(2,1)}, u32[]{:S(2)}, u32[]{:S(2)}) async-start(bf16[4,896,512]{2,1,0:T(8,128)(2,1)} %get-tuple-element.243), calls=%async_computation.2 | async-start | bytes 7340032 | tf_op jit(solution)/shard_map/all_to_all | solution.py:881
  323.7 24.0 %collective-permute-start.47 = (bf16[704,512]{1,0:T(8,128)(2,1)}, bf16[704,512]{1,0:T(8,128)(2,1)S(1)}, u32[]{:S(2)}, u32[]{:S(2)}) collective-permute-start(bf16[704,512]{1,0:T(8,128)(2,1)} %get-tuple-element.229.refs_5_), channel_id=1, source_target_pairs={{0,8},{4,12},{8,0},{12,4},{16,24},{20,28},{24,16},{28,20},{1,9},{5... | collective-permute-start | bytes 2162696 | tf_op jit(solution)/shard_map/ppermute | solution.py:716
  325.3 22.3 %collective-permute-start.48 = (bf16[704,512]{1,0:T(8,128)(2,1)}, bf16[704,512]{1,0:T(8,128)(2,1)S(1)}, u32[]{:S(2)}, u32[]{:S(2)}) collective-permute-start(bf16[704,512]{1,0:T(8,128)(2,1)} %get-tuple-element.230.refs_2_), channel_id=1, source_target_pairs={{8,16},{12,20},{16,8},{20,12},{9,17},{13,21},{17,9},{21,13},{10,18... | collective-permute-start | bytes 2162696 | tf_op jit(solution)/shard_map/ppermute | solution.py:719
  338.9 24.2 %collective-permute-start.55 = (bf16[704,512]{1,0:T(8,128)(2,1)}, bf16[704,512]{1,0:T(8,128)(2,1)S(1)}, u32[]{:S(2)}, u32[]{:S(2)}) collective-permute-start(bf16[704,512]{1,0:T(8,128)(2,1)} %get-tuple-element.245.refs_5_), channel_id=1, source_target_pairs={{0,8},{4,12},{8,0},{12,4},{16,24},{20,28},{24,16},{28,20},{1,9},{5... | collective-permute-start | bytes 2162696 | tf_op jit(solution)/shard_map/ppermute | solution.py:716
  354.2 26.6 %collective-permute-start.53 = (bf16[704,512]{1,0:T(8,128)(2,1)}, bf16[704,512]{1,0:T(8,128)(2,1)S(1)}, u32[]{:S(2)}, u32[]{:S(2)}) collective-permute-start(bf16[704,512]{1,0:T(8,128)(2,1)} %get-tuple-element.241.refs_4_), channel_id=1, source_target_pairs={{0,8},{4,12},{8,0},{12,4},{16,24},{20,28},{24,16},{28,20},{1,9},{5... | collective-permute-start | bytes 2162696 | tf_op jit(solution)/shard_map/ppermute | solution.py:716
  357.9 22.9 %collective-permute-start.54 = (bf16[704,512]{1,0:T(8,128)(2,1)}, bf16[704,512]{1,0:T(8,128)(2,1)S(1)}, u32[]{:S(2)}, u32[]{:S(2)}) collective-permute-start(bf16[704,512]{1,0:T(8,128)(2,1)} %get-tuple-element.242.refs_2_), channel_id=1, source_target_pairs={{8,16},{12,20},{16,8},{20,12},{9,17},{13,21},{17,9},{21,13},{10,18... | collective-permute-start | bytes 2162696 | tf_op jit(solution)/shard_map/ppermute | solution.py:719
  387.3 24.3 %collective-permute-start.59 = (bf16[704,512]{1,0:T(8,128)(2,1)}, bf16[704,512]{1,0:T(8,128)(2,1)}, u32[]{:S(2)}, u32[]{:S(2)}) collective-permute-start(bf16[704,512]{1,0:T(8,128)(2,1)} %get-tuple-element.257.refs_3_), channel_id=1, source_target_pairs={{0,8},{4,12},{8,0},{12,4},{16,24},{20,28},{24,16},{28,20},{1,9},{5... | collective-permute-start | bytes 2162696 | tf_op jit(solution)/shard_map/ppermute | solution.py:716
  402.5 31.8 %all-to-all-start.4 = ((bf16[4,256,1024]{2,1,0:T(8,128)(2,1)}), bf16[4,256,1024]{2,1,0:T(8,128)(2,1)S(1)}, u32[]{:S(2)}, u32[]{:S(2)}) async-start(bf16[4,256,1024]{2,1,0:T(8,128)(2,1)} %get-tuple-element.255), calls=%async_computation.4 | async-start | bytes 4194304 | tf_op jit(solution)/shard_map/all_to_all | solution.py:881
  447.0 28.5 %collective-permute-start.70 = (bf16[704,512]{1,0:T(8,128)(2,1)}, bf16[704,512]{1,0:T(8,128)(2,1)S(1)}, u32[]{:S(2)}, u32[]{:S(2)}) collective-permute-start(bf16[704,512]{1,0:T(8,128)(2,1)} %get-tuple-element.281.refs_2_), channel_id=1, source_target_pairs={{0,8},{4,12},{8,0},{12,4},{16,24},{20,28},{24,16},{28,20},{1,9},{5... | collective-permute-start | bytes 2162696 | tf_op jit(solution)/shard_map/ppermute | solution.py:716
  (107 other events, 902.3 us)

commit v4 on v3

--- a/solution.py
+++ b/solution.py
@@ -823,16 +823,21 @@
     for j in range(4):
         for q in range(many):
             put(outs[j], q * PANEL, j * many + q + (1 if j == 3 else 0), PANEL)
-    put(outs[4], 0, 3 * many, LANES)
+    small = outs[6]
+    put(small, 0, 3 * many, LANES)
+    outs[4][...] = small[:, 2 : 2 + EXPERTS]
+    outs[5][...] = small[: outs[5].shape[0], 8 : 8 + HEADS]
 
 
 def assemble(place, half, width, mine, other):
     shapes = [jax.ShapeDtypeStruct((2 * half, width), f32)] * 4
+    shapes.append(jax.ShapeDtypeStruct((2 * half, EXPERTS), f32))
+    shapes.append(jax.ShapeDtypeStruct((BUCKETS * 2 * half // width, HEADS), f32))
     shapes.append(jax.ShapeDtypeStruct((2 * half, LANES), f32))
     return pl.pallas_call(
         functools.partial(assemble_kernel, half, width // PANEL),
         in_specs=[smem()] + [vmem()] * 4,
-        out_specs=[vmem()] * 5,
+        out_specs=[vmem()] * 7,
         out_shape=shapes,
         compiler_params=params(60),
         cost_estimate=short(),
@@ -856,7 +861,17 @@
     return lax.optimization_barrier((x,) + others)[0]
 
 
-def relay_gather(x, S):
+def relay_gather(top, bottom, S):
+    if S != 4:
+        x = jnp.concatenate([top, bottom], axis=0)
+        return [[x]] + [[swap_shard(x, S, m)] for m in range(1, S)]
+    one_top, two_bottom = swap_shard(top, S, 1), swap_shard(bottom, S, 2)
+    one = [one_top, swap_shard(bottom, S, 1)]
+    two = [swap_shard(top, S, 2), two_bottom]
+    return [[top, bottom], one, two, [swap_shard(one_top, S, 2), swap_shard(two_bottom, S, 1)]]
+
+
+def relay_whole(x, S):
     if S != 4:
         return [[x]] + [[swap_shard(x, S, m)] for m in range(1, S)]
     cut = x.shape[0] // 2
@@ -937,12 +952,17 @@
     group = jnp.arange(S, dtype=jnp.int32)
 
     dense = (w_query, w_key, w_value, w_out)
-    stack = jnp.where(
-        core == 0,
-        jnp.concatenate([w[:half] for w in dense], axis=1),
-        jnp.concatenate([w[half:] for w in dense], axis=1),
-    )
-    blocks = relay_gather(stack, S)
+    cut = half // 2
+
+    def rows_for_core(first):
+        return jnp.where(
+            core == 0,
+            jnp.concatenate([w[first : first + cut] for w in dense], axis=1),
+            jnp.concatenate([w[half + first : half + first + cut] for w in dense], axis=1),
+        )
+
+    stack = rows_for_core(0)
+    blocks = relay_gather(stack, rows_for_core(cut), S)
     count = len(blocks[-1])
     pieces, places = [], []
     for m in range(1, S):
@@ -954,7 +974,7 @@
             pieces.append(swap_core(block, R))
             places.append(place + count * (1 - core) + j * each)
     offsets = jnp.stack(places + [2 * count * me]).astype(jnp.int32)
-    ct_all = relay_gather(after(ct_low, *blocks[-1]), S)
+    ct_all = relay_whole(after(ct_low, *blocks[-1]), S)
 
     bias_flat = jnp.pad(rel_bias.reshape(-1), (0, part - rel_bias.size))
     small = jnp.concatenate(
@@ -989,7 +1009,7 @@
     plans = jnp.take(plan_all, jnp.take(row_of, homes), axis=0)
     pos = slot_positions(plans[:, :, :2], plans[:, :, 2], jnp.take(lengths[0], homes))
 
-    h2_all = relay_gather(ffn_in, S)
+    h2_all = relay_whole(ffn_in, S)
     router_pad = jnp.pad(router_w, ((0, 0), (0, LANES - EXPERTS)))
     core_one = core.reshape(1).astype(jnp.int32)
     place = jnp.stack([line, core]).astype(jnp.int32)
@@ -1072,15 +1092,15 @@
     run(1, [result])
     run(100)
     mine = [sums.dense["top"], sums.dense["bottom"]]
-    *dense_grads, small = assemble(place, half, width, mine, [swap_core(x, R) for x in mine])
+    *dense_grads, grad_router_w, grad_table, small = assemble(place, half, width, mine, [swap_core(x, R) for x in mine])
     return (
         result[None],
         grad_x[None],
         small[:, 0],
         *dense_grads,
-        small[: BUCKETS // S, 8 : 8 + HEADS],
+        grad_table,
         small[:, 1],
-        small[:, 2 : 2 + EXPERTS],
+        grad_router_w,
         jnp.swapaxes(sums.targets["gate"], 1, 2),
         jnp.swapaxes(sums.targets["up"], 1, 2),
         sums.targets["down"],

time: 499 us -> 499 us (level)
    unnamed x124 -> x122, local copies, waits for them, and re-layouts: 19 us -> 20.4 us
    ppermute x12 -> x14, waiting for transfers between devices: 39.1 us -> 38.5 us  [swap_shard(): return lax.ppermute(x, 'shard', [(i, i ^ mask) for i in range(size)])]
    ppermute x12 -> x14, starting transfers between devices: 16.7 us -> 16.7 us  [swap_shard(): return lax.ppermute(x, 'shard', [(i, i ^ mask) for i in range(size)])]
  transfers between devices with their start and end apart: 78 -> 82, of which waited for: 20 -> 23; matrix products, arithmetic and copies ran while one was open for 5% -> 5% of each run, Pallas kernels for 40% -> 40%
where the time goes in v4:
time: 499 us; the launch traced here: 492 us
  Pallas kernels  231 us (46%)
  starting transfers between devices  115 us (23%)
  waiting for transfers between devices  95.6 us (19%)
  local copies, waits for them, and re-layouts  35.4 us (7%)
  other arithmetic  11.3 us (2%)
    pallas_call x20, Pallas kernels, kernel(): pl.pallas_call(functools.partial(wave_kernel, tuple(ins), tuple(outs) + (...  94.8 us
    pallas_call x2, Pallas kernels, ffn(): pl.pallas_call(functools.partial(ffn_kernel, shape, experts, groups, len(...  61 us
    ppermute x18, starting transfers between devices, step(): ins['got_pair'] = lax.ppermute(state['pair'], rep_axis, pairs)  53.2 us
    ppermute x18, waiting for transfers between devices, step(): ins['got_pair'] = lax.ppermute(state['pair'], rep_axis, pairs)  48.5 us
    ppermute x14, waiting for transfers between devices, swap_shard(): return lax.ppermute(x, 'shard', [(i, i ^ mask) for i in range(size)])  38.5 us
    all_to_all x5, starting transfers between devices, deal_out(): return lax.all_to_all(x, 'shard', 0, 0, tiled=True)  22.2 us
    unnamed x122, local copies, waits for them, and re-layouts  20.4 us
    ppermute x14, starting transfers between devices, step(): lax.ppermute(state['mid'], rep_axis, line_perm([(1, 2), (2, 1)]))  17.8 us
  transfers between devices with their start and end apart: 82, of which 23 were waited for; matrix products, arithmetic and copies ran while one was open for 5% of the time, Pallas kernels for 40%

profile of v4, /device:TPU:0, one launch (start us, length us, event | category | flops | bytes accessed | tf_op | source)
XLA Modules:
  0.0 491.7 jit_solution(6455449718561141581)
XLA Ops:
  22.1 7.9 %collective-permute-done.4.refs_14_ = bf16[64,4096]{1,0:T(8,128)(2,1)S(1)} collective-permute-done((bf16[64,4096]{1,0:T(8,128)(2,1)S(1)}, bf16[64,4096]{1,0:T(8,128)(2,1)S(1)}, u32[]{:S(2)}, u32[]{:S(2)}) %collective-permute-start.4) | collective-permute-done | bytes 524320 | tf_op jit(solution)/shard_map/ppermute | solution.py:853
  35.1 8.0 %collective-permute-done.9.refs_19_ = bf16[64,4096]{1,0:T(8,128)(2,1)} collective-permute-done((bf16[64,4096]{1,0:T(8,128)(2,1)S(1)}, bf16[64,4096]{1,0:T(8,128)(2,1)}, u32[]{:S(2)}, u32[]{:S(2)}) %collective-permute-start.9) | collective-permute-done | bytes 524320 | tf_op jit(solution)/shard_map/ppermute | solution.py:853
  52.3 17.0 %attn_fwd.1 = (bf16[256,1024]{1,0:T(8,128)(2,1)}, bf16[256,3072]{1,0:T(8,128)(2,1)}, bf16[256,1024]{1,0:T(8,128)(2,1)}, f32[256,1024]{1,0:T(8,128)}, bf16[256,10...) custom-call(s32[13]{0:T(128)} %stack.69.refs_0_, s32[1]{0:T(128)} %bitcast.13.refs_1_, ...), custom_call_target="tpu_custom_call" | custom-call | flops 1 | bytes 1 | tf_op jit(solution)/shard_map/attn_fwd/pallas_call | solution.py:150
  76.8 7.6 %collective-permute-done.13.refs_5_ = bf16[256,1024]{1,0:T(8,128)(2,1)S(1)} collective-permute-done((bf16[256,1024]{1,0:T(8,128)(2,1)}, bf16[256,1024]{1,0:T(8,128)(2,1)S(1)}, u32[]{:S(2)}, u32[]{:S(2)}) %collective-permute-start.13) | collective-permute-done | bytes 524320 | tf_op jit(solution)/shard_map/ppermute | solution.py:853
  95.7 30.7 %ffn0.1 = (bf16[6,704,512]{2,1,0:T(8,128)(2,1)}, bf16[2,704,512]{2,1,0:T(8,128)(2,1)}, bf16[2,704,512]{2,1,0:T(8,128)(2,1)}, bf16[2,704,512]{2,1,0:T(8,128)(2,1)...) custom-call(s32[2]{0:T(128)} %pad_add_fusion.refs_0_, ...), custom_call_target="tpu_custom_call" | custom-call | flops 1 | bytes 1 | tf_op jit(solution)/shard_map/ffn0/pallas_call | solution.py:356
  139.7 30.3 %ffn2.1 = (bf16[6,704,512]{2,1,0:T(8,128)(2,1)}, bf16[2,704,512]{2,1,0:T(8,128)(2,1)}, bf16[2,704,512]{2,1,0:T(8,128)(2,1)}, bf16[2,704,512]{2,1,0:T(8,128)(2,1)...) custom-call(s32[2]{0:T(128)} %pad_add_fusion.refs_0_, ...), custom_call_target="tpu_custom_call", output_to_operand_aliasing={{4}: (19, {}), {5}: (20, {})} | custom-call | flops 1 | bytes 1 | tf_op jit(solution)/shard_map/ffn2/pallas_call | solution.py:356
  183.2 6.6 %combine.2 = (bf16[4,256,1152]{2,1,0:T(8,128)(2,1)}, f32[8,128]{1,0:T(8,128)}) custom-call(s32[1]{0:T(128)} %bitcast.19.me_ref, s32[4,256,128]{2,1,0:T(8,128)} %pad.17.pos_ref, bf16[4,576,1152]{2,1,0:T(8,128)(2,1)} %get-tuple-element.177.src_ref, f32[8,128]{1,0:T(8,128)} %get-tuple-element.180.refs_0_), custom_call_target="tpu_custom_call" | custom-call | flops 1 | bytes 1 | tf_op jit(solution)/shard_map/combine/pallas_call | solution.py:402
  189.8 4.6 all-to-all-start.1
  204.5 11.2 %collective-permute-done.32.refs_1_ = bf16[704,512]{1,0:T(8,128)(2,1)} collective-permute-done((bf16[704,512]{1,0:T(8,128)(2,1)}, bf16[704,512]{1,0:T(8,128)(2,1)}, u32[]{:S(2)}, u32[]{:S(2)}) %collective-permute-start.32) | collective-permute-done | bytes 720928 | tf_op jit(solution)/shard_map/ppermute | solution.py:716
  229.3 6.0 %back_mid.1 = (f32[256,1024]{1,0:T(8,128)}, bf16[256,1024]{1,0:T(8,128)(2,1)}, bf16[256,1024]{1,0:T(8,128)(2,1)}, f32[1024,128]{1,0:T(8,128)}, f32[8,128]{1,0:T(8,128)}) custom-call(f32[256,1024]{1,0:T(8,128)} %get-tuple-element.156.refs_0_, bf16[256,1024]{1,0:T(8,128)(2,1)} %bitcast.57, f32[1,1024]{1,0:T(1,128)} %convert.14.refs_4_.refs_2_, ...), custom_call_target="tpu_custom_call" | custom-call | flops 1 | bytes 1 | tf_op jit(solution)/shard_map/back_mid/pallas_call | solution.py:485
  235.3 13.8 %attn_bwd.1 = (bf16[3,256,1024]{2,1,0:T(8,128)(2,1)}, f32[4,4,256]{2,1,0:T(4,128)}, f32[8,128]{1,0:T(8,128)}) custom-call(bf16[256,3072]{1,0:T(8,128)(2,1)} %get-tuple-element.187.q_ref.k_ref.v_ref, bf16[256,3072]{1,0:T(8,128)(2,1)} %get-tuple-element.187.q_ref.k_ref.v_ref, bf16[256,3072]{1,0:T(8,128)(2,1)} %get-tuple-element.187.q_ref.k_ref.v_ref, ...), custom_call_target="tpu_custom_call" | custom-call | flops 1 | bytes 1 | tf_op jit(solution)/shard_map/attn_bwd/pallas_call | solution.py:201
  250.0 4.7 wave.24
  258.6 5.7 %wave.25 = (bf16[704,512]{1,0:T(8,128)(2,1)}, bf16[704,512]{1,0:T(8,128)(2,1)}, bf16[704,512]{1,0:T(8,128)(2,1)}, bf16[704,512]{1,0:T(8,128)(2,1)}, f32[4,704,1024]{2,1,0:T(8,128)}, /*index=5*/f32[8,128]{1,0:T(8,128)}) custom-call(s32[2]{0:T(128)} %pad_add_fusion.1.refs_0_.place_ref, bf16[704,512]{1,0:T(8,128)(2,1)} %collective-permute-done.38.refs_1_, ...), custom_call_target="tpu_custom_call" | custom-call | flops 1 | bytes 1 | tf_op jit(solution)/shard_map/wave/pallas_call | solution.py:791
  273.0 8.3 %back_in.1 = (bf16[256,1024]{1,0:T(8,128)(2,1)}, bf16[1024,128]{1,0:T(8,128)(2,1)}, f32[8,128]{1,0:T(8,128)}) custom-call(bf16[256,1024]{1,0:T(8,128)(2,1)} %bitcast.62, f32[1,1024]{1,0:T(1,128)} %convert.15.refs_3_.gain_ref, bf16[3,256,1024]{2,1,0:T(8,128)(2,1)} %get-tuple-element.210.d_ref.refs_2_.refs_3_.refs_4_, f32[16,256]{1,0:T(8,128)} %reshape.171.diag_ref, ...), custom_call_target="tpu_custom_call" | custom-call | flops 1 | bytes 1 | tf_op jit(solution)/shard_map/back_in/pallas_call | solution.py:541
  282.9 5.8 %wave.26 = (bf16[704,512]{1,0:T(8,128)(2,1)}, bf16[704,512]{1,0:T(8,128)(2,1)}, bf16[704,512]{1,0:T(8,128)(2,1)}, bf16[704,512]{1,0:T(8,128)(2,1)}, f32[4,704,1024]{2,1,0:T(8,128)}, /*index=5*/f32[8,128]{1,0:T(8,128)}) custom-call(s32[2]{0:T(128)} %pad_add_fusion.1.refs_0_.place_ref, bf16[704,512]{1,0:T(8,128)(2,1)} %collective-permute-done.36.refs_1_, ...), custom_call_target="tpu_custom_call" | custom-call | flops 1 | bytes 1 | tf_op jit(solution)/shard_map/wave/pallas_call | solution.py:791
  296.9 6.0 %dense.3 = (bf16[4,896,512]{2,1,0:T(8,128)(2,1)}, f32[8,128]{1,0:T(8,128)}) custom-call(s32[1]{0:T(128)} %bitcast.25.core_ref, bf16[256,1024]{1,0:T(8,128)(2,1)} %get-tuple-element.165.refs_0_, bf16[256,1024]{1,0:T(8,128)(2,1)} %copy-done.14, bf16[3,256,1024]{2,1,0:T(8,128)(2,1)} %get-tuple-element.210.d_ref.refs_2_.refs_3_.refs_4_, ...), custom_call_target="tpu_custom_call" | custom-call | flops 1 | bytes 1 | tf_op jit(solution)/shard_map/dense/pallas_call | solution.py:596
  303.0 5.8 %wave.27 = (bf16[704,512]{1,0:T(8,128)(2,1)}, bf16[704,512]{1,0:T(8,128)(2,1)}, bf16[704,512]{1,0:T(8,128)(2,1)}, bf16[704,512]{1,0:T(8,128)(2,1)}, f32[4,704,1024]{2,1,0:T(8,128)}, /*index=5*/f32[8,128]{1,0:T(8,128)}) custom-call(s32[2]{0:T(128)} %pad_add_fusion.1.refs_0_.place_ref, bf16[704,512]{1,0:T(8,128)(2,1)} %collective-permute-done.45.refs_1_, ...), custom_call_target="tpu_custom_call" | custom-call | flops 1 | bytes 1 | tf_op jit(solution)/shard_map/wave/pallas_call | solution.py:791
  308.9 4.9 all-to-all-start.2
  318.7 5.7 %wave.28 = (bf16[704,512]{1,0:T(8,128)(2,1)}, bf16[704,512]{1,0:T(8,128)(2,1)}, bf16[704,512]{1,0:T(8,128)(2,1)}, bf16[704,512]{1,0:T(8,128)(2,1)}, f32[4,704,1024]{2,1,0:T(8,128)}, /*index=5*/f32[8,128]{1,0:T(8,128)}) custom-call(s32[2]{0:T(128)} %pad_add_fusion.1.refs_0_.place_ref, ...), custom_call_target="tpu_custom_call", output_to_operand_aliasing={{4}: (10, {})} | custom-call | flops 1 | bytes 1 | tf_op jit(solution)/shard_map/wave/pallas_call | solution.py:791
  327.1 6.1 %collective-permute-done.53.refs_1_ = bf16[704,512]{1,0:T(8,128)(2,1)S(1)} collective-permute-done((bf16[704,512]{1,0:T(8,128)(2,1)S(1)}, bf16[704,512]{1,0:T(8,128)(2,1)S(1)}, u32[]{:S(2)}, u32[]{:S(2)}) %collective-permute-start.53) | collective-permute-done | bytes 720928 | tf_op jit(solution)/shard_map/ppermute | solution.py:716
  334.1 5.7 %wave.29 = (bf16[704,512]{1,0:T(8,128)(2,1)}, bf16[704,512]{1,0:T(8,128)(2,1)}, bf16[704,512]{1,0:T(8,128)(2,1)}, bf16[704,512]{1,0:T(8,128)(2,1)}, f32[4,704,1024]{2,1,0:T(8,128)}, /*index=5*/f32[8,128]{1,0:T(8,128)}) custom-call(s32[2]{0:T(128)} %pad_add_fusion.1.refs_0_.place_ref, bf16[704,512]{1,0:T(8,128)(2,1)} %copy-done.44, ...), custom_call_target="tpu_custom_call", output_to_operand_aliasing={{4}: (10, {})} | custom-call | flops 1 | bytes 1 | tf_op jit(solution)/shard_map/wave/pallas_call | solution.py:791
  343.8 4.9 collective-permute-done.51.refs_1_
  350.0 5.1 %wave.30 = (bf16[704,512]{1,0:T(8,128)(2,1)}, bf16[704,512]{1,0:T(8,128)(2,1)}, bf16[704,512]{1,0:T(8,128)(2,1)}, f32[4,704,1024]{2,1,0:T(8,128)}, f32[8,128]{1,0:T(8,128)}) custom-call(s32[2]{0:T(128)} %pad_add_fusion.1.refs_0_.place_ref, bf16[704,512]{1,0:T(8,128)(2,1)} %copy-done.25, ...), custom_call_target="tpu_custom_call", output_to_operand_aliasing={{3}: (8, {})} | custom-call | flops 1 | bytes 1 | tf_op jit(solution)/shard_map/wave/pallas_call | solution.py:791
  365.5 5.1 %wave.31 = (bf16[704,512]{1,0:T(8,128)(2,1)}, bf16[704,512]{1,0:T(8,128)(2,1)}, bf16[704,512]{1,0:T(8,128)(2,1)}, f32[4,704,1024]{2,1,0:T(8,128)}, f32[8,128]{1,0:T(8,128)}) custom-call(s32[2]{0:T(128)} %pad_add_fusion.1.refs_0_.place_ref, bf16[704,512]{1,0:T(8,128)(2,1)} %copy-done.29, ...), custom_call_target="tpu_custom_call", output_to_operand_aliasing={{3}: (8, {})} | custom-call | flops 1 | bytes 1 | tf_op jit(solution)/shard_map/wave/pallas_call | solution.py:791
  381.9 5.1 %wave.32 = (bf16[704,512]{1,0:T(8,128)(2,1)}, bf16[704,512]{1,0:T(8,128)(2,1)}, bf16[704,512]{1,0:T(8,128)(2,1)}, f32[4,704,1024]{2,1,0:T(8,128)}, f32[8,128]{1,0:T(8,128)}) custom-call(s32[2]{0:T(128)} %pad_add_fusion.1.refs_0_.place_ref, bf16[704,512]{1,0:T(8,128)(2,1)} %copy-done.22, ...), custom_call_target="tpu_custom_call", output_to_operand_aliasing={{3}: (8, {})} | custom-call | flops 1 | bytes 1 | tf_op jit(solution)/shard_map/wave/pallas_call | solution.py:791
  390.3 6.3 %combine.3 = (bf16[4,256,1024]{2,1,0:T(8,128)(2,1)}, f32[8,128]{1,0:T(8,128)}) custom-call(s32[1]{0:T(128)} %bitcast.19.me_ref, s32[4,256,128]{2,1,0:T(8,128)} %pad.17.pos_ref, bf16[4,576,1024]{2,1,0:T(8,128)(2,1)} %get-tuple-element.169.src_ref, f32[8,128]{1,0:T(8,128)} %get-tuple-element.256.refs_0_), custom_call_target="tpu_custom_call" | custom-call | flops 1 | bytes 1 | tf_op jit(solution)/shard_map/combine/pallas_call | solution.py:402
  398.4 5.1 %wave.33 = (bf16[704,512]{1,0:T(8,128)(2,1)}, bf16[704,512]{1,0:T(8,128)(2,1)}, bf16[704,512]{1,0:T(8,128)(2,1)}, f32[4,704,1024]{2,1,0:T(8,128)}, f32[8,128]{1,0:T(8,128)}) custom-call(s32[2]{0:T(128)} %pad_add_fusion.1.refs_0_.place_ref, bf16[704,512]{1,0:T(8,128)(2,1)} %copy-done.23, ...), custom_call_target="tpu_custom_call", output_to_operand_aliasing={{3}: (8, {})} | custom-call | flops 1 | bytes 1 | tf_op jit(solution)/shard_map/wave/pallas_call | solution.py:791
  413.4 4.6 wave.34
  419.6 8.5 %collective-permute-done.69.refs_1_ = bf16[704,512]{1,0:T(8,128)(2,1)} collective-permute-done((bf16[704,512]{1,0:T(8,128)(2,1)S(1)}, bf16[704,512]{1,0:T(8,128)(2,1)}, u32[]{:S(2)}, u32[]{:S(2)}) %collective-permute-start.69) | collective-permute-done | bytes 720928 | tf_op jit(solution)/shard_map/ppermute | solution.py:716
  428.9 4.6 wave.35
  448.4 11.3 %collective-permute-start.74 = (bf16[704,512]{1,0:T(8,128)(2,1)}, bf16[704,512]{1,0:T(8,128)(2,1)S(1)}, u32[]{:S(2)}, u32[]{:S(2)}) collective-permute-start(bf16[704,512]{1,0:T(8,128)(2,1)} %get-tuple-element.283.refs_2_), channel_id=1, source_target_pairs={{0,8},{4,12},{8,0},{12,4},{16,24},{20,28},{24,16},{28,20},{1,9},{5... | collective-permute-start | bytes 2162696 | tf_op jit(solution)/shard_map/ppermute | solution.py:716
  466.2 10.4 %collective-permute-done.74.refs_1_ = bf16[704,512]{1,0:T(8,128)(2,1)S(1)} collective-permute-done((bf16[704,512]{1,0:T(8,128)(2,1)}, bf16[704,512]{1,0:T(8,128)(2,1)S(1)}, u32[]{:S(2)}, u32[]{:S(2)}) %collective-permute-start.74) | collective-permute-done | bytes 720928 | tf_op jit(solution)/shard_map/ppermute | solution.py:716
  (354 shorter events, 216.2 us)
Async XLA Ops:
  8.9 24.0 %collective-permute-start = (bf16[64,4096]{1,0:T(8,128)(2,1)S(1)}, bf16[64,4096]{1,0:T(8,128)(2,1)}, u32[]{:S(2)}, u32[]{:S(2)}) collective-permute-start(bf16[64,4096]{1,0:T(8,128)(2,1)S(1)} %maximum_select_fusion), channel_id=1, source_target_pairs={{0,1},{1,0},{2,3},{3,2},{4,5},{5,4},{6,7},{7,6},{8,9},{9,8},{10,11... | collective-permute-start | bytes 1572872 | tf_op jit(solution)/shard_map/ppermute | solution.py:853
  10.0 39.2 %all-to-all-start = ((bf16[4,256,10]{1,2,0:T(8,128)(2,1)}), bf16[4,256,10]{1,2,0:T(8,128)(2,1)S(1)}, u32[]{:S(2)}, u32[]{:S(2)}) async-start(bf16[4,256,10]{1,2,0:T(8,128)(2,1)} %broadcast_in_dim.68), calls=%async_computation | async-start | bytes 65536 | tf_op jit(solution)/shard_map/all_to_all | solution.py:896
  19.5 23.6 %collective-permute-start.9 = (bf16[64,4096]{1,0:T(8,128)(2,1)S(1)}, bf16[64,4096]{1,0:T(8,128)(2,1)}, u32[]{:S(2)}, u32[]{:S(2)}) collective-permute-start(bf16[64,4096]{1,0:T(8,128)(2,1)S(1)} %collective-permute-done.5.refs_15_), channel_id=1, source_target_pairs={{0,1},{1,0},{2,3},{3,2},{4,5},{5,4},{6,7},{7,6},{8,9},{9,8},{10,11... | collective-permute-start | bytes 1572872 | tf_op jit(solution)/shard_map/ppermute | solution.py:853
  21.5 25.6 %collective-permute-start.7 = (bf16[64,4096]{1,0:T(8,128)(2,1)S(1)}, bf16[64,4096]{1,0:T(8,128)(2,1)}, u32[]{:S(2)}, u32[]{:S(2)}) collective-permute-start(bf16[64,4096]{1,0:T(8,128)(2,1)S(1)} %collective-permute-done.5.refs_15_), channel_id=1, source_target_pairs={{0,4},{4,0},{8,12},{12,8},{16,20},{20,16},{24,28},{28,24},{1,5},{5... | collective-permute-start | bytes 1572872 | tf_op jit(solution)/shard_map/ppermute | solution.py:849
  21.6 27.1 %collective-permute-start.3 = (bf16[64,4096]{1,0:T(8,128)(2,1)S(1)}, bf16[64,4096]{1,0:T(8,128)(2,1)}, u32[]{:S(2)}, u32[]{:S(2)}) collective-permute-start(bf16[64,4096]{1,0:T(8,128)(2,1)S(1)} %collective-permute-done.1.refs_11_), channel_id=1, source_target_pairs={{0,4},{4,0},{8,12},{12,8},{16,20},{20,16},{24,28},{28,24},{1,5},{5... | collective-permute-start | bytes 1572872 | tf_op jit(solution)/shard_map/ppermute | solution.py:849
  45.4 24.8 %collective-permute-start.17 = (bf16[256,1024]{1,0:T(8,128)(2,1)S(1)}, bf16[256,1024]{1,0:T(8,128)(2,1)S(1)}, u32[]{:S(2)}, u32[]{:S(2)}) collective-permute-start(bf16[256,1024]{1,0:T(8,128)(2,1)S(1)} %bitcast.58), channel_id=1, source_target_pairs={{0,2},{1,3},{2,0},{3,1},{4,6},{5,7},{6,4},{7,5},{8,10},{9,11},{10,... | collective-permute-start | bytes 1572872 | tf_op jit(solution)/shard_map/ppermute | solution.py:853
  47.2 25.5 %collective-permute-start.16 = (bf16[256,1024]{1,0:T(8,128)(2,1)S(1)}, bf16[256,1024]{1,0:T(8,128)(2,1)S(1)}, u32[]{:S(2)}, u32[]{:S(2)}) collective-permute-start(bf16[256,1024]{1,0:T(8,128)(2,1)S(1)} %bitcast.59), channel_id=1, source_target_pairs={{0,1},{1,0},{2,3},{3,2},{4,5},{5,4},{6,7},{7,6},{8,9},{9,8},{10,11... | collective-permute-start | bytes 1572872 | tf_op jit(solution)/shard_map/ppermute | solution.py:853
  126.6 43.4 %collective-permute-start.24 = (bf16[2,704,512]{2,1,0:T(8,128)(2,1)}, bf16[2,704,512]{2,1,0:T(8,128)(2,1)S(1)}, u32[]{:S(2)}, u32[]{:S(2)}) collective-permute-start(bf16[2,704,512]{2,1,0:T(8,128)(2,1)} %get-tuple-element.171), channel_id=1, source_target_pairs={{0,4},{4,0},{8,12},{12,8},{16,20},{20,16},{24,28},{28,24},{1,5},{5... | collective-permute-start | bytes 4325384 | tf_op jit(solution)/shard_map/ppermute | solution.py:849
  127.1 67.9 %collective-permute-start.27 = (bf16[2,704,512]{2,1,0:T(8,128)(2,1)}, bf16[2,704,512]{2,1,0:T(8,128)(2,1)}, u32[]{:S(2)}, u32[]{:S(2)}) collective-permute-start(bf16[2,704,512]{2,1,0:T(8,128)(2,1)} %get-tuple-element.176), channel_id=1, source_target_pairs={{0,4},{4,0},{8,12},{12,8},{16,20},{20,16},{24,28},{28,24},{1,5},{5... | collective-permute-start | bytes 4325384 | tf_op jit(solution)/shard_map/ppermute | solution.py:849
  135.1 34.9 %collective-permute-start.23 = (bf16[704,512]{1,0:T(8,128)(2,1)}, bf16[704,512]{1,0:T(8,128)(2,1)}, u32[]{:S(2)}, u32[]{:S(2)}) collective-permute-start(bf16[704,512]{1,0:T(8,128)(2,1)} %get-tuple-element.170.refs_2_), channel_id=1, source_target_pairs={{0,8},{4,12},{8,0},{12,4},{16,24},{20,28},{24,16},{28,20},{1,9},{5... | collective-permute-start | bytes 2162696 | tf_op jit(solution)/shard_map/ppermute | solution.py:716
  136.8 41.5 %collective-permute-start.28 = (bf16[704,512]{1,0:T(8,128)(2,1)}, bf16[704,512]{1,0:T(8,128)(2,1)S(1)}, u32[]{:S(2)}, u32[]{:S(2)}) collective-permute-start(bf16[704,512]{1,0:T(8,128)(2,1)} %get-tuple-element.178.refs_2_), channel_id=1, source_target_pairs={{0,8},{4,12},{8,0},{12,4},{16,24},{20,28},{24,16},{28,20},{1,9},{5... | collective-permute-start | bytes 2162696 | tf_op jit(solution)/shard_map/ppermute | solution.py:716
  175.9 22.8 %collective-permute-start.26 = (bf16[704,512]{1,0:T(8,128)(2,1)}, bf16[704,512]{1,0:T(8,128)(2,1)}, u32[]{:S(2)}, u32[]{:S(2)}) collective-permute-start(bf16[704,512]{1,0:T(8,128)(2,1)} %get-tuple-element.174.refs_2_), channel_id=1, source_target_pairs={{8,16},{12,20},{16,8},{20,12},{9,17},{13,21},{17,9},{21,13},{10,18... | collective-permute-start | bytes 2162696 | tf_op jit(solution)/shard_map/ppermute | solution.py:719
  189.8 39.5 %all-to-all-start.1 = ((bf16[4,256,1152]{2,1,0:T(8,128)(2,1)}), bf16[4,256,1152]{2,1,0:T(8,128)(2,1)}, u32[]{:S(2)}, u32[]{:S(2)}) async-start(bf16[4,256,1152]{2,1,0:T(8,128)(2,1)} %get-tuple-element.190), calls=%async_computation.1 | async-start | bytes 4718592 | tf_op jit(solution)/shard_map/all_to_all | solution.py:896
  194.4 23.7 %collective-permute-start.31 = (bf16[2,704,512]{2,1,0:T(8,128)(2,1)}, bf16[2,704,512]{2,1,0:T(8,128)(2,1)S(1)}, u32[]{:S(2)}, u32[]{:S(2)}) collective-permute-start(bf16[2,704,512]{2,1,0:T(8,128)(2,1)} %get-tuple-element.186), channel_id=1, source_target_pairs={{0,4},{4,0},{8,12},{12,8},{16,20},{20,16},{24,28},{28,24},{1,5},{5... | collective-permute-start | bytes 4325384 | tf_op jit(solution)/shard_map/ppermute | solution.py:849
  194.5 23.7 %collective-permute-start.34 = (bf16[2,704,512]{2,1,0:T(8,128)(2,1)}, bf16[2,704,512]{2,1,0:T(8,128)(2,1)S(1)}, u32[]{:S(2)}, u32[]{:S(2)}) collective-permute-start(bf16[2,704,512]{2,1,0:T(8,128)(2,1)} %get-tuple-element.195), channel_id=1, source_target_pairs={{0,4},{4,0},{8,12},{12,8},{16,20},{20,16},{24,28},{28,24},{1,5},{5... | collective-permute-start | bytes 4325384 | tf_op jit(solution)/shard_map/ppermute | solution.py:849
  195.0 23.2 %collective-permute-start.35 = (bf16[2,704,512]{2,1,0:T(8,128)(2,1)}, bf16[2,704,512]{2,1,0:T(8,128)(2,1)}, u32[]{:S(2)}, u32[]{:S(2)}) collective-permute-start(bf16[2,704,512]{2,1,0:T(8,128)(2,1)} %get-tuple-element.196), channel_id=1, source_target_pairs={{0,4},{4,0},{8,12},{12,8},{16,20},{20,16},{24,28},{28,24},{1,5},{5... | collective-permute-start | bytes 4325384 | tf_op jit(solution)/shard_map/ppermute | solution.py:849
  215.7 33.4 %collective-permute-start.29 = (bf16[704,512]{1,0:T(8,128)(2,1)}, bf16[704,512]{1,0:T(8,128)(2,1)}, u32[]{:S(2)}, u32[]{:S(2)}) collective-permute-start(bf16[704,512]{1,0:T(8,128)(2,1)} %get-tuple-element.182.refs_5_), channel_id=1, source_target_pairs={{0,8},{4,12},{8,0},{12,4},{16,24},{20,28},{24,16},{28,20},{1,9},{5... | collective-permute-start | bytes 2162696 | tf_op jit(solution)/shard_map/ppermute | solution.py:716
  217.5 31.7 %collective-permute-start.30 = (bf16[704,512]{1,0:T(8,128)(2,1)}, bf16[704,512]{1,0:T(8,128)(2,1)S(1)}, u32[]{:S(2)}, u32[]{:S(2)}) collective-permute-start(bf16[704,512]{1,0:T(8,128)(2,1)} %get-tuple-element.183.refs_2_), channel_id=1, source_target_pairs={{8,16},{12,20},{16,8},{20,12},{9,17},{13,21},{17,9},{21,13},{10,18... | collective-permute-start | bytes 2162696 | tf_op jit(solution)/shard_map/ppermute | solution.py:719
  224.2 32.9 %collective-permute-start.38 = (bf16[704,512]{1,0:T(8,128)(2,1)}, bf16[704,512]{1,0:T(8,128)(2,1)}, u32[]{:S(2)}, u32[]{:S(2)}) collective-permute-start(bf16[704,512]{1,0:T(8,128)(2,1)} %get-tuple-element.204.refs_5_), channel_id=1, source_target_pairs={{0,8},{4,12},{8,0},{12,4},{16,24},{20,28},{24,16},{28,20},{1,9},{5... | collective-permute-start | bytes 2162696 | tf_op jit(solution)/shard_map/ppermute | solution.py:716
  227.8 30.8 %collective-permute-start.39 = (bf16[704,512]{1,0:T(8,128)(2,1)}, bf16[704,512]{1,0:T(8,128)(2,1)}, u32[]{:S(2)}, u32[]{:S(2)}) collective-permute-start(bf16[704,512]{1,0:T(8,128)(2,1)} %get-tuple-element.205.refs_2_), channel_id=1, source_target_pairs={{8,16},{12,20},{16,8},{20,12},{9,17},{13,21},{17,9},{21,13},{10,18... | collective-permute-start | bytes 2162696 | tf_op jit(solution)/shard_map/ppermute | solution.py:719
  254.8 41.0 %collective-permute-start.48 = (bf16[3,256,1024]{2,1,0:T(8,128)(2,1)S(1)}, bf16[3,256,1024]{2,1,0:T(8,128)(2,1)S(1)}, u32[]{:S(2)}, u32[]{:S(2)}) collective-permute-start(bf16[3,256,1024]{2,1,0:T(8,128)(2,1)S(1)} %copy-done.2), channel_id=1, source_target_pairs={{0,4},{4,0},{8,12},{12,8},{16,20},{20,16},{24,28},{28,24},{1,5},{5... | collective-permute-start | bytes 4718600 | tf_op jit(solution)/shard_map/ppermute | solution.py:849
  255.3 25.9 %collective-permute-start.36 = (bf16[704,512]{1,0:T(8,128)(2,1)}, bf16[704,512]{1,0:T(8,128)(2,1)}, u32[]{:S(2)}, u32[]{:S(2)}) collective-permute-start(bf16[704,512]{1,0:T(8,128)(2,1)} %get-tuple-element.201.refs_5_), channel_id=1, source_target_pairs={{0,8},{4,12},{8,0},{12,4},{16,24},{20,28},{24,16},{28,20},{1,9},{5... | collective-permute-start | bytes 2162696 | tf_op jit(solution)/shard_map/ppermute | solution.py:716
  257.1 25.8 %collective-permute-start.37 = (bf16[704,512]{1,0:T(8,128)(2,1)}, bf16[704,512]{1,0:T(8,128)(2,1)}, u32[]{:S(2)}, u32[]{:S(2)}) collective-permute-start(bf16[704,512]{1,0:T(8,128)(2,1)} %get-tuple-element.202.refs_2_), channel_id=1, source_target_pairs={{8,16},{12,20},{16,8},{20,12},{9,17},{13,21},{17,9},{21,13},{10,18... | collective-permute-start | bytes 2162696 | tf_op jit(solution)/shard_map/ppermute | solution.py:719
  267.7 35.2 %collective-permute-start.45 = (bf16[704,512]{1,0:T(8,128)(2,1)}, bf16[704,512]{1,0:T(8,128)(2,1)}, u32[]{:S(2)}, u32[]{:S(2)}) collective-permute-start(bf16[704,512]{1,0:T(8,128)(2,1)} %get-tuple-element.221.refs_5_), channel_id=1, source_target_pairs={{0,8},{4,12},{8,0},{12,4},{16,24},{20,28},{24,16},{28,20},{1,9},{5... | collective-permute-start | bytes 2162696 | tf_op jit(solution)/shard_map/ppermute | solution.py:716
  294.7 23.2 %collective-permute-start.43 = (bf16[704,512]{1,0:T(8,128)(2,1)}, bf16[704,512]{1,0:T(8,128)(2,1)}, u32[]{:S(2)}, u32[]{:S(2)}) collective-permute-start(bf16[704,512]{1,0:T(8,128)(2,1)} %get-tuple-element.218.refs_5_), channel_id=1, source_target_pairs={{0,8},{4,12},{8,0},{12,4},{16,24},{20,28},{24,16},{28,20},{1,9},{5... | collective-permute-start | bytes 2162696 | tf_op jit(solution)/shard_map/ppermute | solution.py:716
  308.9 63.3 %all-to-all-start.2 = ((bf16[4,896,512]{2,1,0:T(8,128)(2,1)}), bf16[4,896,512]{2,1,0:T(8,128)(2,1)}, u32[]{:S(2)}, u32[]{:S(2)}) async-start(bf16[4,896,512]{2,1,0:T(8,128)(2,1)} %get-tuple-element.245), calls=%async_computation.2 | async-start | bytes 7340032 | tf_op jit(solution)/shard_map/all_to_all | solution.py:896
  324.7 24.0 %collective-permute-start.51 = (bf16[704,512]{1,0:T(8,128)(2,1)}, bf16[704,512]{1,0:T(8,128)(2,1)S(1)}, u32[]{:S(2)}, u32[]{:S(2)}) collective-permute-start(bf16[704,512]{1,0:T(8,128)(2,1)} %get-tuple-element.231.refs_5_), channel_id=1, source_target_pairs={{0,8},{4,12},{8,0},{12,4},{16,24},{20,28},{24,16},{28,20},{1,9},{5... | collective-permute-start | bytes 2162696 | tf_op jit(solution)/shard_map/ppermute | solution.py:716
  339.9 24.2 %collective-permute-start.59 = (bf16[704,512]{1,0:T(8,128)(2,1)}, bf16[704,512]{1,0:T(8,128)(2,1)S(1)}, u32[]{:S(2)}, u32[]{:S(2)}) collective-permute-start(bf16[704,512]{1,0:T(8,128)(2,1)} %get-tuple-element.247.refs_5_), channel_id=1, source_target_pairs={{0,8},{4,12},{8,0},{12,4},{16,24},{20,28},{24,16},{28,20},{1,9},{5... | collective-permute-start | bytes 2162696 | tf_op jit(solution)/shard_map/ppermute | solution.py:716
  355.3 25.7 %collective-permute-start.57 = (bf16[704,512]{1,0:T(8,128)(2,1)}, bf16[704,512]{1,0:T(8,128)(2,1)S(1)}, u32[]{:S(2)}, u32[]{:S(2)}) collective-permute-start(bf16[704,512]{1,0:T(8,128)(2,1)} %get-tuple-element.243.refs_4_), channel_id=1, source_target_pairs={{0,8},{4,12},{8,0},{12,4},{16,24},{20,28},{24,16},{28,20},{1,9},{5... | collective-permute-start | bytes 2162696 | tf_op jit(solution)/shard_map/ppermute | solution.py:716
  387.2 25.3 %collective-permute-start.63 = (bf16[704,512]{1,0:T(8,128)(2,1)}, bf16[704,512]{1,0:T(8,128)(2,1)S(1)}, u32[]{:S(2)}, u32[]{:S(2)}) collective-permute-start(bf16[704,512]{1,0:T(8,128)(2,1)} %get-tuple-element.259.refs_3_), channel_id=1, source_target_pairs={{0,8},{4,12},{8,0},{12,4},{16,24},{20,28},{24,16},{28,20},{1,9},{5... | collective-permute-start | bytes 2162696 | tf_op jit(solution)/shard_map/ppermute | solution.py:716
  403.6 31.8 %all-to-all-start.4 = ((bf16[4,256,1024]{2,1,0:T(8,128)(2,1)}), bf16[4,256,1024]{2,1,0:T(8,128)(2,1)S(1)}, u32[]{:S(2)}, u32[]{:S(2)}) async-start(bf16[4,256,1024]{2,1,0:T(8,128)(2,1)} %get-tuple-element.257), calls=%async_computation.4 | async-start | bytes 4194304 | tf_op jit(solution)/shard_map/all_to_all | solution.py:896
  448.4 28.2 %collective-permute-start.74 = (bf16[704,512]{1,0:T(8,128)(2,1)}, bf16[704,512]{1,0:T(8,128)(2,1)S(1)}, u32[]{:S(2)}, u32[]{:S(2)}) collective-permute-start(bf16[704,512]{1,0:T(8,128)(2,1)} %get-tuple-element.283.refs_2_), channel_id=1, source_target_pairs={{0,8},{4,12},{8,0},{12,4},{16,24},{20,28},{24,16},{28,20},{1,9},{5... | collective-permute-start | bytes 2162696 | tf_op jit(solution)/shard_map/ppermute | solution.py:716
  (110 other events, 1084.9 us)

commit v5 on v4

--- a/solution.py
+++ b/solution.py
@@ -1072,7 +1072,10 @@
         S, core_one, normed_low, h1_other, d3, swap_core(d3, R), [extra, swap_core(extra, R)], sums.last
     )
     in_grads = deal_out(in_grads)
-    run(5)
+    run(3)
+    out_parts, sums.last = combine(me_one, pos_col, chain[0], sums.last)
+    out_parts = deal_out(out_parts)
+    run(2)
 
     owned = [jnp.sum(x.astype(f32), axis=0).astype(bf16) for x in (in_grads, out_grads)]
     owned = jnp.concatenate(owned, axis=0)
@@ -1085,8 +1088,6 @@
     else:
         owned = line_sum(owned, R)
         sums.dense = {"top": owned[: rows // 2], "bottom": owned[rows // 2 :]}
-    out_parts, sums.last = combine(me_one, pos_col, chain[0], sums.last)
-    out_parts = deal_out(out_parts)
     run(4)
     result = (middle + jnp.sum(out_parts.astype(f32), axis=0)).astype(bf16)
     run(1, [result])

time: 499 us -> 498 us (level)
  transfers between devices with their start and end apart: 82 -> 82, of which waited for: 23 -> 22; matrix products, arithmetic and copies ran while one was open for 5% -> 5% of each run, Pallas kernels for 40% -> 40%
where the time goes in v5:
time: 498 us; the launch traced here: 492 us
  Pallas kernels  231 us (46%)
  starting transfers between devices  114 us (23%)
  waiting for transfers between devices  96.8 us (19%)
  local copies, waits for them, and re-layouts  35.4 us (7%)
  other arithmetic  11.3 us (2%)
    pallas_call x20, Pallas kernels, kernel(): pl.pallas_call(functools.partial(wave_kernel, tuple(ins), tuple(outs) + (...  94.7 us
    pallas_call x2, Pallas kernels, ffn(): pl.pallas_call(functools.partial(ffn_kernel, shape, experts, groups, len(...  61 us
    ppermute x18, starting transfers between devices, step(): ins['got_pair'] = lax.ppermute(state['pair'], rep_axis, pairs)  52 us
    ppermute x18, waiting for transfers between devices, step(): ins['got_pair'] = lax.ppermute(state['pair'], rep_axis, pairs)  49.7 us
    ppermute x14, waiting for transfers between devices, swap_shard(): return lax.ppermute(x, 'shard', [(i, i ^ mask) for i in range(size)])  38.5 us
    all_to_all x5, starting transfers between devices, deal_out(): return lax.all_to_all(x, 'shard', 0, 0, tiled=True)  22.1 us
    unnamed x122, local copies, waits for them, and re-layouts  20.4 us
    ppermute x14, starting transfers between devices, step(): lax.ppermute(state['mid'], rep_axis, line_perm([(1, 2), (2, 1)]))  17.3 us
  transfers between devices with their start and end apart: 82, of which 22 were waited for; matrix products, arithmetic and copies ran while one was open for 5% of the time, Pallas kernels for 40%

profile of v5, /device:TPU:0, one launch (start us, length us, event | category | flops | bytes accessed | tf_op | source)
XLA Modules:
  0.0 491.5 jit_solution(4394742285348422125)
XLA Ops:
  22.1 7.9 %collective-permute-done.4.refs_14_ = bf16[64,4096]{1,0:T(8,128)(2,1)S(1)} collective-permute-done((bf16[64,4096]{1,0:T(8,128)(2,1)S(1)}, bf16[64,4096]{1,0:T(8,128)(2,1)S(1)}, u32[]{:S(2)}, u32[]{:S(2)}) %collective-permute-start.4) | collective-permute-done | bytes 524320 | tf_op jit(solution)/shard_map/ppermute | solution.py:853
  35.1 8.0 %collective-permute-done.9.refs_19_ = bf16[64,4096]{1,0:T(8,128)(2,1)} collective-permute-done((bf16[64,4096]{1,0:T(8,128)(2,1)S(1)}, bf16[64,4096]{1,0:T(8,128)(2,1)}, u32[]{:S(2)}, u32[]{:S(2)}) %collective-permute-start.9) | collective-permute-done | bytes 524320 | tf_op jit(solution)/shard_map/ppermute | solution.py:853
  52.3 17.0 %attn_fwd.1 = (bf16[256,1024]{1,0:T(8,128)(2,1)}, bf16[256,3072]{1,0:T(8,128)(2,1)}, bf16[256,1024]{1,0:T(8,128)(2,1)}, f32[256,1024]{1,0:T(8,128)}, bf16[256,10...) custom-call(s32[13]{0:T(128)} %stack.69.refs_0_, s32[1]{0:T(128)} %bitcast.13.refs_1_, ...), custom_call_target="tpu_custom_call" | custom-call | flops 1 | bytes 1 | tf_op jit(solution)/shard_map/attn_fwd/pallas_call | solution.py:150
  76.8 7.6 %collective-permute-done.13.refs_5_ = bf16[256,1024]{1,0:T(8,128)(2,1)S(1)} collective-permute-done((bf16[256,1024]{1,0:T(8,128)(2,1)}, bf16[256,1024]{1,0:T(8,128)(2,1)S(1)}, u32[]{:S(2)}, u32[]{:S(2)}) %collective-permute-start.13) | collective-permute-done | bytes 524320 | tf_op jit(solution)/shard_map/ppermute | solution.py:853
  95.7 30.7 %ffn0.1 = (bf16[6,704,512]{2,1,0:T(8,128)(2,1)}, bf16[2,704,512]{2,1,0:T(8,128)(2,1)}, bf16[2,704,512]{2,1,0:T(8,128)(2,1)}, bf16[2,704,512]{2,1,0:T(8,128)(2,1)...) custom-call(s32[2]{0:T(128)} %pad_add_fusion.refs_0_, ...), custom_call_target="tpu_custom_call" | custom-call | flops 1 | bytes 1 | tf_op jit(solution)/shard_map/ffn0/pallas_call | solution.py:356
  139.7 30.3 %ffn2.1 = (bf16[6,704,512]{2,1,0:T(8,128)(2,1)}, bf16[2,704,512]{2,1,0:T(8,128)(2,1)}, bf16[2,704,512]{2,1,0:T(8,128)(2,1)}, bf16[2,704,512]{2,1,0:T(8,128)(2,1)...) custom-call(s32[2]{0:T(128)} %pad_add_fusion.refs_0_, ...), custom_call_target="tpu_custom_call", output_to_operand_aliasing={{4}: (19, {}), {5}: (20, {})} | custom-call | flops 1 | bytes 1 | tf_op jit(solution)/shard_map/ffn2/pallas_call | solution.py:356
  183.2 6.6 %combine.2 = (bf16[4,256,1152]{2,1,0:T(8,128)(2,1)}, f32[8,128]{1,0:T(8,128)}) custom-call(s32[1]{0:T(128)} %bitcast.19.me_ref, s32[4,256,128]{2,1,0:T(8,128)} %pad.17.pos_ref, bf16[4,576,1152]{2,1,0:T(8,128)(2,1)} %get-tuple-element.182.src_ref, f32[8,128]{1,0:T(8,128)} %get-tuple-element.183.refs_0_), custom_call_target="tpu_custom_call" | custom-call | flops 1 | bytes 1 | tf_op jit(solution)/shard_map/combine/pallas_call | solution.py:402
  189.8 4.6 all-to-all-start.1
  204.5 11.2 %collective-permute-done.26.refs_1_ = bf16[704,512]{1,0:T(8,128)(2,1)} collective-permute-done((bf16[704,512]{1,0:T(8,128)(2,1)}, bf16[704,512]{1,0:T(8,128)(2,1)}, u32[]{:S(2)}, u32[]{:S(2)}) %collective-permute-start.26) | collective-permute-done | bytes 720928 | tf_op jit(solution)/shard_map/ppermute | solution.py:716
  229.2 6.0 %back_mid.1 = (f32[256,1024]{1,0:T(8,128)}, bf16[256,1024]{1,0:T(8,128)(2,1)}, bf16[256,1024]{1,0:T(8,128)(2,1)}, f32[1024,128]{1,0:T(8,128)}, f32[8,128]{1,0:T(8,128)}) custom-call(f32[256,1024]{1,0:T(8,128)} %get-tuple-element.156.refs_0_, bf16[256,1024]{1,0:T(8,128)(2,1)} %bitcast.57, f32[1,1024]{1,0:T(1,128)} %convert.14.refs_4_.refs_2_, ...), custom_call_target="tpu_custom_call" | custom-call | flops 1 | bytes 1 | tf_op jit(solution)/shard_map/back_mid/pallas_call | solution.py:485
  235.2 13.8 %attn_bwd.1 = (bf16[3,256,1024]{2,1,0:T(8,128)(2,1)}, f32[4,4,256]{2,1,0:T(4,128)}, f32[8,128]{1,0:T(8,128)}) custom-call(bf16[256,3072]{1,0:T(8,128)(2,1)} %get-tuple-element.196.q_ref.k_ref.v_ref, bf16[256,3072]{1,0:T(8,128)(2,1)} %get-tuple-element.196.q_ref.k_ref.v_ref, bf16[256,3072]{1,0:T(8,128)(2,1)} %get-tuple-element.196.q_ref.k_ref.v_ref, ...), custom_call_target="tpu_custom_call" | custom-call | flops 1 | bytes 1 | tf_op jit(solution)/shard_map/attn_bwd/pallas_call | solution.py:201
  249.9 4.7 wave.24
  258.4 5.8 %wave.25 = (bf16[704,512]{1,0:T(8,128)(2,1)}, bf16[704,512]{1,0:T(8,128)(2,1)}, bf16[704,512]{1,0:T(8,128)(2,1)}, bf16[704,512]{1,0:T(8,128)(2,1)}, f32[4,704,1024]{2,1,0:T(8,128)}, /*index=5*/f32[8,128]{1,0:T(8,128)}) custom-call(s32[2]{0:T(128)} %pad_add_fusion.1.refs_0_.place_ref, bf16[704,512]{1,0:T(8,128)(2,1)} %collective-permute-done.34.refs_1_, ...), custom_call_target="tpu_custom_call" | custom-call | flops 1 | bytes 1 | tf_op jit(solution)/shard_map/wave/pallas_call | solution.py:791
  272.8 8.3 %back_in.1 = (bf16[256,1024]{1,0:T(8,128)(2,1)}, bf16[1024,128]{1,0:T(8,128)(2,1)}, f32[8,128]{1,0:T(8,128)}) custom-call(bf16[256,1024]{1,0:T(8,128)(2,1)} %bitcast.62, f32[1,1024]{1,0:T(1,128)} %convert.15.refs_3_.gain_ref, bf16[3,256,1024]{2,1,0:T(8,128)(2,1)} %get-tuple-element.213.d_ref.refs_2_.refs_3_.refs_4_, f32[16,256]{1,0:T(8,128)} %reshape.171.diag_ref, ...), custom_call_target="tpu_custom_call" | custom-call | flops 1 | bytes 1 | tf_op jit(solution)/shard_map/back_in/pallas_call | solution.py:541
  282.6 5.8 %wave.26 = (bf16[704,512]{1,0:T(8,128)(2,1)}, bf16[704,512]{1,0:T(8,128)(2,1)}, bf16[704,512]{1,0:T(8,128)(2,1)}, bf16[704,512]{1,0:T(8,128)(2,1)}, f32[4,704,1024]{2,1,0:T(8,128)}, /*index=5*/f32[8,128]{1,0:T(8,128)}) custom-call(s32[2]{0:T(128)} %pad_add_fusion.1.refs_0_.place_ref, bf16[704,512]{1,0:T(8,128)(2,1)} %collective-permute-done.41.refs_1_, ...), custom_call_target="tpu_custom_call" | custom-call | flops 1 | bytes 1 | tf_op jit(solution)/shard_map/wave/pallas_call | solution.py:791
  296.8 6.0 %dense.3 = (bf16[4,896,512]{2,1,0:T(8,128)(2,1)}, f32[8,128]{1,0:T(8,128)}) custom-call(s32[1]{0:T(128)} %bitcast.25.core_ref, bf16[256,1024]{1,0:T(8,128)(2,1)} %get-tuple-element.165.refs_0_, bf16[256,1024]{1,0:T(8,128)(2,1)} %copy-done.14, bf16[3,256,1024]{2,1,0:T(8,128)(2,1)} %get-tuple-element.213.d_ref.refs_2_.refs_3_.refs_4_, ...), custom_call_target="tpu_custom_call" | custom-call | flops 1 | bytes 1 | tf_op jit(solution)/shard_map/dense/pallas_call | solution.py:596
  302.8 5.8 %wave.27 = (bf16[704,512]{1,0:T(8,128)(2,1)}, bf16[704,512]{1,0:T(8,128)(2,1)}, bf16[704,512]{1,0:T(8,128)(2,1)}, bf16[704,512]{1,0:T(8,128)(2,1)}, f32[4,704,1024]{2,1,0:T(8,128)}, /*index=5*/f32[8,128]{1,0:T(8,128)}) custom-call(s32[2]{0:T(128)} %pad_add_fusion.1.refs_0_.place_ref, bf16[704,512]{1,0:T(8,128)(2,1)} %collective-permute-done.39.refs_1_, ...), custom_call_target="tpu_custom_call" | custom-call | flops 1 | bytes 1 | tf_op jit(solution)/shard_map/wave/pallas_call | solution.py:791
  308.7 4.9 all-to-all-start.3
  318.5 5.7 %wave.28 = (bf16[704,512]{1,0:T(8,128)(2,1)}, bf16[704,512]{1,0:T(8,128)(2,1)}, bf16[704,512]{1,0:T(8,128)(2,1)}, bf16[704,512]{1,0:T(8,128)(2,1)}, f32[4,704,1024]{2,1,0:T(8,128)}, /*index=5*/f32[8,128]{1,0:T(8,128)}) custom-call(s32[2]{0:T(128)} %pad_add_fusion.1.refs_0_.place_ref, ...), custom_call_target="tpu_custom_call", output_to_operand_aliasing={{4}: (10, {})} | custom-call | flops 1 | bytes 1 | tf_op jit(solution)/shard_map/wave/pallas_call | solution.py:791
  326.9 6.2 %collective-permute-done.48.refs_1_ = bf16[704,512]{1,0:T(8,128)(2,1)S(1)} collective-permute-done((bf16[704,512]{1,0:T(8,128)(2,1)S(1)}, bf16[704,512]{1,0:T(8,128)(2,1)S(1)}, u32[]{:S(2)}, u32[]{:S(2)}) %collective-permute-start.48) | collective-permute-done | bytes 720928 | tf_op jit(solution)/shard_map/ppermute | solution.py:716
  333.9 5.7 %wave.29 = (bf16[704,512]{1,0:T(8,128)(2,1)}, bf16[704,512]{1,0:T(8,128)(2,1)}, bf16[704,512]{1,0:T(8,128)(2,1)}, bf16[704,512]{1,0:T(8,128)(2,1)}, f32[4,704,1024]{2,1,0:T(8,128)}, /*index=5*/f32[8,128]{1,0:T(8,128)}) custom-call(s32[2]{0:T(128)} %pad_add_fusion.1.refs_0_.place_ref, bf16[704,512]{1,0:T(8,128)(2,1)} %copy-done.44, ...), custom_call_target="tpu_custom_call", output_to_operand_aliasing={{4}: (10, {})} | custom-call | flops 1 | bytes 1 | tf_op jit(solution)/shard_map/wave/pallas_call | solution.py:791
  343.6 6.5 %combine.3 = (bf16[4,256,1024]{2,1,0:T(8,128)(2,1)}, f32[8,128]{1,0:T(8,128)}) custom-call(s32[1]{0:T(128)} %bitcast.19.me_ref, s32[4,256,128]{2,1,0:T(8,128)} %pad.17.pos_ref, bf16[4,576,1024]{2,1,0:T(8,128)(2,1)} %get-tuple-element.169.src_ref, f32[8,128]{1,0:T(8,128)} %get-tuple-element.237.refs_0_), custom_call_target="tpu_custom_call" | custom-call | flops 1 | bytes 1 | tf_op jit(solution)/shard_map/combine/pallas_call | solution.py:402
  351.5 5.1 %wave.30 = (bf16[704,512]{1,0:T(8,128)(2,1)}, bf16[704,512]{1,0:T(8,128)(2,1)}, bf16[704,512]{1,0:T(8,128)(2,1)}, f32[4,704,1024]{2,1,0:T(8,128)}, f32[8,128]{1,0:T(8,128)}) custom-call(s32[2]{0:T(128)} %pad_add_fusion.1.refs_0_.place_ref, bf16[704,512]{1,0:T(8,128)(2,1)} %copy-done.23, ...), custom_call_target="tpu_custom_call", output_to_operand_aliasing={{3}: (8, {})} | custom-call | flops 1 | bytes 1 | tf_op jit(solution)/shard_map/wave/pallas_call | solution.py:791
  365.3 5.1 %wave.31 = (bf16[704,512]{1,0:T(8,128)(2,1)}, bf16[704,512]{1,0:T(8,128)(2,1)}, bf16[704,512]{1,0:T(8,128)(2,1)}, f32[4,704,1024]{2,1,0:T(8,128)}, f32[8,128]{1,0:T(8,128)}) custom-call(s32[2]{0:T(128)} %pad_add_fusion.1.refs_0_.place_ref, bf16[704,512]{1,0:T(8,128)(2,1)} %copy-done.25, ...), custom_call_target="tpu_custom_call", output_to_operand_aliasing={{3}: (8, {})} | custom-call | flops 1 | bytes 1 | tf_op jit(solution)/shard_map/wave/pallas_call | solution.py:791
  381.7 5.1 %wave.32 = (bf16[704,512]{1,0:T(8,128)(2,1)}, bf16[704,512]{1,0:T(8,128)(2,1)}, bf16[704,512]{1,0:T(8,128)(2,1)}, f32[4,704,1024]{2,1,0:T(8,128)}, f32[8,128]{1,0:T(8,128)}) custom-call(s32[2]{0:T(128)} %pad_add_fusion.1.refs_0_.place_ref, bf16[704,512]{1,0:T(8,128)(2,1)} %copy-done.22, ...), custom_call_target="tpu_custom_call", output_to_operand_aliasing={{3}: (8, {})} | custom-call | flops 1 | bytes 1 | tf_op jit(solution)/shard_map/wave/pallas_call | solution.py:791
  390.1 7.0 %collective-permute-done.64.refs_1_ = bf16[704,512]{1,0:T(8,128)(2,1)S(1)} collective-permute-done((bf16[704,512]{1,0:T(8,128)(2,1)S(1)}, bf16[704,512]{1,0:T(8,128)(2,1)S(1)}, u32[]{:S(2)}, u32[]{:S(2)}) %collective-permute-start.64) | collective-permute-done | bytes 720928 | tf_op jit(solution)/shard_map/ppermute | solution.py:716
  398.2 5.1 %wave.33 = (bf16[704,512]{1,0:T(8,128)(2,1)}, bf16[704,512]{1,0:T(8,128)(2,1)}, bf16[704,512]{1,0:T(8,128)(2,1)}, f32[4,704,1024]{2,1,0:T(8,128)}, f32[8,128]{1,0:T(8,128)}) custom-call(s32[2]{0:T(128)} %pad_add_fusion.1.refs_0_.place_ref, bf16[704,512]{1,0:T(8,128)(2,1)} %copy-done.28, ...), custom_call_target="tpu_custom_call", output_to_operand_aliasing={{3}: (8, {})} | custom-call | flops 1 | bytes 1 | tf_op jit(solution)/shard_map/wave/pallas_call | solution.py:791
  413.2 4.6 wave.34
  419.4 8.5 %collective-permute-done.69.refs_1_ = bf16[704,512]{1,0:T(8,128)(2,1)} collective-permute-done((bf16[704,512]{1,0:T(8,128)(2,1)S(1)}, bf16[704,512]{1,0:T(8,128)(2,1)}, u32[]{:S(2)}, u32[]{:S(2)}) %collective-permute-start.69) | collective-permute-done | bytes 720928 | tf_op jit(solution)/shard_map/ppermute | solution.py:716
  428.8 4.6 wave.35
  448.2 11.2 %collective-permute-start.74 = (bf16[704,512]{1,0:T(8,128)(2,1)}, bf16[704,512]{1,0:T(8,128)(2,1)S(1)}, u32[]{:S(2)}, u32[]{:S(2)}) collective-permute-start(bf16[704,512]{1,0:T(8,128)(2,1)} %get-tuple-element.283.refs_2_), channel_id=1, source_target_pairs={{0,8},{4,12},{8,0},{12,4},{16,24},{20,28},{24,16},{28,20},{1,9},{5... | collective-permute-start | bytes 2162696 | tf_op jit(solution)/shard_map/ppermute | solution.py:716
  466.0 10.3 %collective-permute-done.74.refs_1_ = bf16[704,512]{1,0:T(8,128)(2,1)S(1)} collective-permute-done((bf16[704,512]{1,0:T(8,128)(2,1)}, bf16[704,512]{1,0:T(8,128)(2,1)S(1)}, u32[]{:S(2)}, u32[]{:S(2)}) %collective-permute-start.74) | collective-permute-done | bytes 720928 | tf_op jit(solution)/shard_map/ppermute | solution.py:716
  (354 shorter events, 213.7 us)
Async XLA Ops:
  8.9 24.0 %collective-permute-start = (bf16[64,4096]{1,0:T(8,128)(2,1)S(1)}, bf16[64,4096]{1,0:T(8,128)(2,1)}, u32[]{:S(2)}, u32[]{:S(2)}) collective-permute-start(bf16[64,4096]{1,0:T(8,128)(2,1)S(1)} %maximum_select_fusion), channel_id=1, source_target_pairs={{0,1},{1,0},{2,3},{3,2},{4,5},{5,4},{6,7},{7,6},{8,9},{9,8},{10,11... | collective-permute-start | bytes 1572872 | tf_op jit(solution)/shard_map/ppermute | solution.py:853
  10.0 39.2 %all-to-all-start = ((bf16[4,256,10]{1,2,0:T(8,128)(2,1)}), bf16[4,256,10]{1,2,0:T(8,128)(2,1)S(1)}, u32[]{:S(2)}, u32[]{:S(2)}) async-start(bf16[4,256,10]{1,2,0:T(8,128)(2,1)} %broadcast_in_dim.68), calls=%async_computation | async-start | bytes 65536 | tf_op jit(solution)/shard_map/all_to_all | solution.py:896
  19.5 23.6 %collective-permute-start.9 = (bf16[64,4096]{1,0:T(8,128)(2,1)S(1)}, bf16[64,4096]{1,0:T(8,128)(2,1)}, u32[]{:S(2)}, u32[]{:S(2)}) collective-permute-start(bf16[64,4096]{1,0:T(8,128)(2,1)S(1)} %collective-permute-done.5.refs_15_), channel_id=1, source_target_pairs={{0,1},{1,0},{2,3},{3,2},{4,5},{5,4},{6,7},{7,6},{8,9},{9,8},{10,11... | collective-permute-start | bytes 1572872 | tf_op jit(solution)/shard_map/ppermute | solution.py:853
  21.5 25.6 %collective-permute-start.7 = (bf16[64,4096]{1,0:T(8,128)(2,1)S(1)}, bf16[64,4096]{1,0:T(8,128)(2,1)}, u32[]{:S(2)}, u32[]{:S(2)}) collective-permute-start(bf16[64,4096]{1,0:T(8,128)(2,1)S(1)} %collective-permute-done.5.refs_15_), channel_id=1, source_target_pairs={{0,4},{4,0},{8,12},{12,8},{16,20},{20,16},{24,28},{28,24},{1,5},{5... | collective-permute-start | bytes 1572872 | tf_op jit(solution)/shard_map/ppermute | solution.py:849
  21.6 27.1 %collective-permute-start.3 = (bf16[64,4096]{1,0:T(8,128)(2,1)S(1)}, bf16[64,4096]{1,0:T(8,128)(2,1)}, u32[]{:S(2)}, u32[]{:S(2)}) collective-permute-start(bf16[64,4096]{1,0:T(8,128)(2,1)S(1)} %collective-permute-done.1.refs_11_), channel_id=1, source_target_pairs={{0,4},{4,0},{8,12},{12,8},{16,20},{20,16},{24,28},{28,24},{1,5},{5... | collective-permute-start | bytes 1572872 | tf_op jit(solution)/shard_map/ppermute | solution.py:849
  45.4 24.8 %collective-permute-start.17 = (bf16[256,1024]{1,0:T(8,128)(2,1)S(1)}, bf16[256,1024]{1,0:T(8,128)(2,1)S(1)}, u32[]{:S(2)}, u32[]{:S(2)}) collective-permute-start(bf16[256,1024]{1,0:T(8,128)(2,1)S(1)} %bitcast.58), channel_id=1, source_target_pairs={{0,2},{1,3},{2,0},{3,1},{4,6},{5,7},{6,4},{7,5},{8,10},{9,11},{10,... | collective-permute-start | bytes 1572872 | tf_op jit(solution)/shard_map/ppermute | solution.py:853
  47.2 25.5 %collective-permute-start.16 = (bf16[256,1024]{1,0:T(8,128)(2,1)S(1)}, bf16[256,1024]{1,0:T(8,128)(2,1)S(1)}, u32[]{:S(2)}, u32[]{:S(2)}) collective-permute-start(bf16[256,1024]{1,0:T(8,128)(2,1)S(1)} %bitcast.59), channel_id=1, source_target_pairs={{0,1},{1,0},{2,3},{3,2},{4,5},{5,4},{6,7},{7,6},{8,9},{9,8},{10,11... | collective-permute-start | bytes 1572872 | tf_op jit(solution)/shard_map/ppermute | solution.py:853
  126.6 43.4 %collective-permute-start.24 = (bf16[2,704,512]{2,1,0:T(8,128)(2,1)}, bf16[2,704,512]{2,1,0:T(8,128)(2,1)S(1)}, u32[]{:S(2)}, u32[]{:S(2)}) collective-permute-start(bf16[2,704,512]{2,1,0:T(8,128)(2,1)} %get-tuple-element.171), channel_id=1, source_target_pairs={{0,4},{4,0},{8,12},{12,8},{16,20},{20,16},{24,28},{28,24},{1,5},{5... | collective-permute-start | bytes 4325384 | tf_op jit(solution)/shard_map/ppermute | solution.py:849
  127.1 67.9 %collective-permute-start.28 = (bf16[2,704,512]{2,1,0:T(8,128)(2,1)}, bf16[2,704,512]{2,1,0:T(8,128)(2,1)}, u32[]{:S(2)}, u32[]{:S(2)}) collective-permute-start(bf16[2,704,512]{2,1,0:T(8,128)(2,1)} %get-tuple-element.178), channel_id=1, source_target_pairs={{0,4},{4,0},{8,12},{12,8},{16,20},{20,16},{24,28},{28,24},{1,5},{5... | collective-permute-start | bytes 4325384 | tf_op jit(solution)/shard_map/ppermute | solution.py:849
  135.1 34.9 %collective-permute-start.25 = (bf16[704,512]{1,0:T(8,128)(2,1)}, bf16[704,512]{1,0:T(8,128)(2,1)}, u32[]{:S(2)}, u32[]{:S(2)}) collective-permute-start(bf16[704,512]{1,0:T(8,128)(2,1)} %get-tuple-element.172.refs_2_), channel_id=1, source_target_pairs={{0,8},{4,12},{8,0},{12,4},{16,24},{20,28},{24,16},{28,20},{1,9},{5... | collective-permute-start | bytes 2162696 | tf_op jit(solution)/shard_map/ppermute | solution.py:716
  136.8 41.5 %collective-permute-start.23 = (bf16[704,512]{1,0:T(8,128)(2,1)}, bf16[704,512]{1,0:T(8,128)(2,1)S(1)}, u32[]{:S(2)}, u32[]{:S(2)}) collective-permute-start(bf16[704,512]{1,0:T(8,128)(2,1)} %get-tuple-element.170.refs_2_), channel_id=1, source_target_pairs={{0,8},{4,12},{8,0},{12,4},{16,24},{20,28},{24,16},{28,20},{1,9},{5... | collective-permute-start | bytes 2162696 | tf_op jit(solution)/shard_map/ppermute | solution.py:716
  189.8 39.4 %all-to-all-start.1 = ((bf16[4,256,1152]{2,1,0:T(8,128)(2,1)}), bf16[4,256,1152]{2,1,0:T(8,128)(2,1)}, u32[]{:S(2)}, u32[]{:S(2)}) async-start(bf16[4,256,1152]{2,1,0:T(8,128)(2,1)} %get-tuple-element.199), calls=%async_computation.1 | async-start | bytes 4718592 | tf_op jit(solution)/shard_map/all_to_all | solution.py:896
  194.4 23.7 %collective-permute-start.31 = (bf16[2,704,512]{2,1,0:T(8,128)(2,1)}, bf16[2,704,512]{2,1,0:T(8,128)(2,1)S(1)}, u32[]{:S(2)}, u32[]{:S(2)}) collective-permute-start(bf16[2,704,512]{2,1,0:T(8,128)(2,1)} %get-tuple-element.186), channel_id=1, source_target_pairs={{0,4},{4,0},{8,12},{12,8},{16,20},{20,16},{24,28},{28,24},{1,5},{5... | collective-permute-start | bytes 4325384 | tf_op jit(solution)/shard_map/ppermute | solution.py:849
  194.5 23.7 %collective-permute-start.32 = (bf16[2,704,512]{2,1,0:T(8,128)(2,1)}, bf16[2,704,512]{2,1,0:T(8,128)(2,1)S(1)}, u32[]{:S(2)}, u32[]{:S(2)}) collective-permute-start(bf16[2,704,512]{2,1,0:T(8,128)(2,1)} %get-tuple-element.187), channel_id=1, source_target_pairs={{0,4},{4,0},{8,12},{12,8},{16,20},{20,16},{24,28},{28,24},{1,5},{5... | collective-permute-start | bytes 4325384 | tf_op jit(solution)/shard_map/ppermute | solution.py:849
  195.0 23.2 %collective-permute-start.33 = (bf16[2,704,512]{2,1,0:T(8,128)(2,1)}, bf16[2,704,512]{2,1,0:T(8,128)(2,1)}, u32[]{:S(2)}, u32[]{:S(2)}) collective-permute-start(bf16[2,704,512]{2,1,0:T(8,128)(2,1)} %get-tuple-element.188), channel_id=1, source_target_pairs={{0,4},{4,0},{8,12},{12,8},{16,20},{20,16},{24,28},{28,24},{1,5},{5... | collective-permute-start | bytes 4325384 | tf_op jit(solution)/shard_map/ppermute | solution.py:849
  215.7 33.4 %collective-permute-start.36 = (bf16[704,512]{1,0:T(8,128)(2,1)}, bf16[704,512]{1,0:T(8,128)(2,1)}, u32[]{:S(2)}, u32[]{:S(2)}) collective-permute-start(bf16[704,512]{1,0:T(8,128)(2,1)} %get-tuple-element.193.refs_5_), channel_id=1, source_target_pairs={{0,8},{4,12},{8,0},{12,4},{16,24},{20,28},{24,16},{28,20},{1,9},{5... | collective-permute-start | bytes 2162696 | tf_op jit(solution)/shard_map/ppermute | solution.py:716
  217.4 31.6 %collective-permute-start.37 = (bf16[704,512]{1,0:T(8,128)(2,1)}, bf16[704,512]{1,0:T(8,128)(2,1)S(1)}, u32[]{:S(2)}, u32[]{:S(2)}) collective-permute-start(bf16[704,512]{1,0:T(8,128)(2,1)} %get-tuple-element.194.refs_2_), channel_id=1, source_target_pairs={{8,16},{12,20},{16,8},{20,12},{9,17},{13,21},{17,9},{21,13},{10,18... | collective-permute-start | bytes 2162696 | tf_op jit(solution)/shard_map/ppermute | solution.py:719
  224.1 32.9 %collective-permute-start.34 = (bf16[704,512]{1,0:T(8,128)(2,1)}, bf16[704,512]{1,0:T(8,128)(2,1)}, u32[]{:S(2)}, u32[]{:S(2)}) collective-permute-start(bf16[704,512]{1,0:T(8,128)(2,1)} %get-tuple-element.189.refs_5_), channel_id=1, source_target_pairs={{0,8},{4,12},{8,0},{12,4},{16,24},{20,28},{24,16},{28,20},{1,9},{5... | collective-permute-start | bytes 2162696 | tf_op jit(solution)/shard_map/ppermute | solution.py:716
  227.7 30.7 %collective-permute-start.35 = (bf16[704,512]{1,0:T(8,128)(2,1)}, bf16[704,512]{1,0:T(8,128)(2,1)}, u32[]{:S(2)}, u32[]{:S(2)}) collective-permute-start(bf16[704,512]{1,0:T(8,128)(2,1)} %get-tuple-element.190.refs_2_), channel_id=1, source_target_pairs={{8,16},{12,20},{16,8},{20,12},{9,17},{13,21},{17,9},{21,13},{10,18... | collective-permute-start | bytes 2162696 | tf_op jit(solution)/shard_map/ppermute | solution.py:719
  254.7 40.9 %collective-permute-start.46 = (bf16[3,256,1024]{2,1,0:T(8,128)(2,1)S(1)}, bf16[3,256,1024]{2,1,0:T(8,128)(2,1)S(1)}, u32[]{:S(2)}, u32[]{:S(2)}) collective-permute-start(bf16[3,256,1024]{2,1,0:T(8,128)(2,1)S(1)} %copy-done.2), channel_id=1, source_target_pairs={{0,4},{4,0},{8,12},{12,8},{16,20},{20,16},{24,28},{28,24},{1,5},{5... | collective-permute-start | bytes 4718600 | tf_op jit(solution)/shard_map/ppermute | solution.py:849
  255.2 25.9 %collective-permute-start.41 = (bf16[704,512]{1,0:T(8,128)(2,1)}, bf16[704,512]{1,0:T(8,128)(2,1)}, u32[]{:S(2)}, u32[]{:S(2)}) collective-permute-start(bf16[704,512]{1,0:T(8,128)(2,1)} %get-tuple-element.209.refs_5_), channel_id=1, source_target_pairs={{0,8},{4,12},{8,0},{12,4},{16,24},{20,28},{24,16},{28,20},{1,9},{5... | collective-permute-start | bytes 2162696 | tf_op jit(solution)/shard_map/ppermute | solution.py:716
  256.9 25.7 %collective-permute-start.42 = (bf16[704,512]{1,0:T(8,128)(2,1)}, bf16[704,512]{1,0:T(8,128)(2,1)}, u32[]{:S(2)}, u32[]{:S(2)}) collective-permute-start(bf16[704,512]{1,0:T(8,128)(2,1)} %get-tuple-element.210.refs_2_), channel_id=1, source_target_pairs={{8,16},{12,20},{16,8},{20,12},{9,17},{13,21},{17,9},{21,13},{10,18... | collective-permute-start | bytes 2162696 | tf_op jit(solution)/shard_map/ppermute | solution.py:719
  267.5 35.3 %collective-permute-start.39 = (bf16[704,512]{1,0:T(8,128)(2,1)}, bf16[704,512]{1,0:T(8,128)(2,1)}, u32[]{:S(2)}, u32[]{:S(2)}) collective-permute-start(bf16[704,512]{1,0:T(8,128)(2,1)} %get-tuple-element.206.refs_5_), channel_id=1, source_target_pairs={{0,8},{4,12},{8,0},{12,4},{16,24},{20,28},{24,16},{28,20},{1,9},{5... | collective-permute-start | bytes 2162696 | tf_op jit(solution)/shard_map/ppermute | solution.py:716
  294.5 23.1 %collective-permute-start.50 = (bf16[704,512]{1,0:T(8,128)(2,1)}, bf16[704,512]{1,0:T(8,128)(2,1)}, u32[]{:S(2)}, u32[]{:S(2)}) collective-permute-start(bf16[704,512]{1,0:T(8,128)(2,1)} %get-tuple-element.228.refs_5_), channel_id=1, source_target_pairs={{0,8},{4,12},{8,0},{12,4},{16,24},{20,28},{24,16},{28,20},{1,9},{5... | collective-permute-start | bytes 2162696 | tf_op jit(solution)/shard_map/ppermute | solution.py:716
  308.7 63.2 %all-to-all-start.3 = ((bf16[4,896,512]{2,1,0:T(8,128)(2,1)}), bf16[4,896,512]{2,1,0:T(8,128)(2,1)}, u32[]{:S(2)}, u32[]{:S(2)}) async-start(bf16[4,896,512]{2,1,0:T(8,128)(2,1)} %get-tuple-element.248), calls=%async_computation.3 | async-start | bytes 7340032 | tf_op jit(solution)/shard_map/all_to_all | solution.py:896
  324.4 25.7 %collective-permute-start.54 = (bf16[704,512]{1,0:T(8,128)(2,1)}, bf16[704,512]{1,0:T(8,128)(2,1)S(1)}, u32[]{:S(2)}, u32[]{:S(2)}) collective-permute-start(bf16[704,512]{1,0:T(8,128)(2,1)} %get-tuple-element.240.refs_5_), channel_id=1, source_target_pairs={{0,8},{4,12},{8,0},{12,4},{16,24},{20,28},{24,16},{28,20},{1,9},{5... | collective-permute-start | bytes 2162696 | tf_op jit(solution)/shard_map/ppermute | solution.py:716
  326.2 24.0 %collective-permute-start.55 = (bf16[704,512]{1,0:T(8,128)(2,1)}, bf16[704,512]{1,0:T(8,128)(2,1)S(1)}, u32[]{:S(2)}, u32[]{:S(2)}) collective-permute-start(bf16[704,512]{1,0:T(8,128)(2,1)} %get-tuple-element.241.refs_2_), channel_id=1, source_target_pairs={{8,16},{12,20},{16,8},{20,12},{9,17},{13,21},{17,9},{21,13},{10,18... | collective-permute-start | bytes 2162696 | tf_op jit(solution)/shard_map/ppermute | solution.py:719
  339.7 24.2 %collective-permute-start.59 = (bf16[704,512]{1,0:T(8,128)(2,1)}, bf16[704,512]{1,0:T(8,128)(2,1)S(1)}, u32[]{:S(2)}, u32[]{:S(2)}) collective-permute-start(bf16[704,512]{1,0:T(8,128)(2,1)} %get-tuple-element.250.refs_5_), channel_id=1, source_target_pairs={{0,8},{4,12},{8,0},{12,4},{16,24},{20,28},{24,16},{28,20},{1,9},{5... | collective-permute-start | bytes 2162696 | tf_op jit(solution)/shard_map/ppermute | solution.py:716
  356.8 24.0 %collective-permute-start.57 = (bf16[704,512]{1,0:T(8,128)(2,1)}, bf16[704,512]{1,0:T(8,128)(2,1)S(1)}, u32[]{:S(2)}, u32[]{:S(2)}) collective-permute-start(bf16[704,512]{1,0:T(8,128)(2,1)} %get-tuple-element.246.refs_4_), channel_id=1, source_target_pairs={{0,8},{4,12},{8,0},{12,4},{16,24},{20,28},{24,16},{28,20},{1,9},{5... | collective-permute-start | bytes 2162696 | tf_op jit(solution)/shard_map/ppermute | solution.py:716
  387.1 25.3 %collective-permute-start.63 = (bf16[704,512]{1,0:T(8,128)(2,1)}, bf16[704,512]{1,0:T(8,128)(2,1)S(1)}, u32[]{:S(2)}, u32[]{:S(2)}) collective-permute-start(bf16[704,512]{1,0:T(8,128)(2,1)} %get-tuple-element.259.refs_3_), channel_id=1, source_target_pairs={{0,8},{4,12},{8,0},{12,4},{16,24},{20,28},{24,16},{28,20},{1,9},{5... | collective-permute-start | bytes 2162696 | tf_op jit(solution)/shard_map/ppermute | solution.py:716
  403.4 31.8 %all-to-all-start.2 = ((bf16[4,256,1024]{2,1,0:T(8,128)(2,1)}), bf16[4,256,1024]{2,1,0:T(8,128)(2,1)S(1)}, u32[]{:S(2)}, u32[]{:S(2)}) async-start(bf16[4,256,1024]{2,1,0:T(8,128)(2,1)} %get-tuple-element.238), calls=%async_computation.2 | async-start | bytes 4194304 | tf_op jit(solution)/shard_map/all_to_all | solution.py:896
  448.2 28.2 %collective-permute-start.74 = (bf16[704,512]{1,0:T(8,128)(2,1)}, bf16[704,512]{1,0:T(8,128)(2,1)S(1)}, u32[]{:S(2)}, u32[]{:S(2)}) collective-permute-start(bf16[704,512]{1,0:T(8,128)(2,1)} %get-tuple-element.283.refs_2_), channel_id=1, source_target_pairs={{0,8},{4,12},{8,0},{12,4},{16,24},{20,28},{24,16},{28,20},{1,9},{5... | collective-permute-start | bytes 2162696 | tf_op jit(solution)/shard_map/ppermute | solution.py:716
  (110 other events, 1084.6 us)

commit v6 on v5

--- a/solution.py
+++ b/solution.py
@@ -964,14 +964,16 @@
     stack = rows_for_core(0)
     blocks = relay_gather(stack, rows_for_core(cut), S)
     count = len(blocks[-1])
-    pieces, places = [], []
+    pieces, places, late = [], [], []
     for m in range(1, S):
         place = 2 * count * (me ^ m)
         each = count // len(blocks[m])
         pieces += blocks[m]
         places += [place + count * core + j * each for j in range(len(blocks[m]))]
         for j, block in enumerate(blocks[m]):
-            pieces.append(swap_core(block, R))
+            if m == S - 1:
+                late.append(len(pieces))
+            pieces.append(block if m == S - 1 else swap_core(block, R))
             places.append(place + count * (1 - core) + j * each)
     offsets = jnp.stack(places + [2 * count * me]).astype(jnp.int32)
     ct_all = relay_whole(after(ct_low, *blocks[-1]), S)
@@ -997,6 +999,8 @@
     turned = jnp.arange(n, dtype=jnp.int32)
     hot = (bucket_of((n - turned) % n)[None, :] == jnp.arange(BUCKETS)[:, None]).astype(bf16)
     base = dot_tn(bias_table, hot)
+    for i in late:
+        pieces[i] = swap_core(after(pieces[i], base, gain_one, gain_two), R)
 
     normed_low, qkv, context, middle, ffn_in, dense_w, bias = attn_fwd(
         offsets, length, x_low, gain_one[None], gain_two[None], base, dense, pieces

time: 498 us -> 498 us (level)
  transfers between devices with their start and end apart: 82 -> 82, of which waited for: 22 -> 24; matrix products, arithmetic and copies ran while one was open for 5% -> 5% of each run, Pallas kernels for 40% -> 40%
where the time goes in v6:
time: 498 us; the launch traced here: 491 us
  Pallas kernels  231 us (46%)
  starting transfers between devices  114 us (23%)
  waiting for transfers between devices  96.8 us (19%)
  local copies, waits for them, and re-layouts  35.4 us (7%)
  other arithmetic  10.8 us (2%)
    pallas_call x20, Pallas kernels, kernel(): pl.pallas_call(functools.partial(wave_kernel, tuple(ins), tuple(outs) + (...  94.7 us
    pallas_call x2, Pallas kernels, ffn(): pl.pallas_call(functools.partial(ffn_kernel, shape, experts, groups, len(...  61 us
    ppermute x18, starting transfers between devices, step(): ins['got_pair'] = lax.ppermute(state['pair'], rep_axis, pairs)  52 us
    ppermute x18, waiting for transfers between devices, step(): ins['got_pair'] = lax.ppermute(state['pair'], rep_axis, pairs)  49.7 us
    ppermute x14, waiting for transfers between devices, swap_shard(): return lax.ppermute(x, 'shard', [(i, i ^ mask) for i in range(size)])  37.6 us
    all_to_all x5, starting transfers between devices, deal_out(): return lax.all_to_all(x, 'shard', 0, 0, tiled=True)  22.1 us
    unnamed x122, local copies, waits for them, and re-layouts  20.4 us
    ppermute x14, starting transfers between devices, step(): lax.ppermute(state['mid'], rep_axis, line_perm([(1, 2), (2, 1)]))  17.3 us
  transfers between devices with their start and end apart: 82, of which 24 were waited for; matrix products, arithmetic and copies ran while one was open for 5% of the time, Pallas kernels for 40%

profile of v6, /device:TPU:0, one launch (start us, length us, event | category | flops | bytes accessed | tf_op | source)
XLA Modules:
  0.0 490.9 jit_solution(6615287502996481409)
XLA Ops:
  22.1 7.9 %collective-permute-done.4.refs_14_ = bf16[64,4096]{1,0:T(8,128)(2,1)S(1)} collective-permute-done((bf16[64,4096]{1,0:T(8,128)(2,1)S(1)}, bf16[64,4096]{1,0:T(8,128)(2,1)S(1)}, u32[]{:S(2)}, u32[]{:S(2)}) %collective-permute-start.4) | collective-permute-done | bytes 524320 | tf_op jit(solution)/shard_map/ppermute | solution.py:853
  34.7 8.4 %collective-permute-done.9.refs_19_ = bf16[64,4096]{1,0:T(8,128)(2,1)} collective-permute-done((bf16[64,4096]{1,0:T(8,128)(2,1)S(1)}, bf16[64,4096]{1,0:T(8,128)(2,1)}, u32[]{:S(2)}, u32[]{:S(2)}) %collective-permute-start.9) | collective-permute-done | bytes 524320 | tf_op jit(solution)/shard_map/ppermute | solution.py:853
  51.7 17.0 %attn_fwd.1 = (bf16[256,1024]{1,0:T(8,128)(2,1)}, bf16[256,3072]{1,0:T(8,128)(2,1)}, bf16[256,1024]{1,0:T(8,128)(2,1)}, f32[256,1024]{1,0:T(8,128)}, bf16[256,10...) custom-call(s32[13]{0:T(128)} %stack.69.refs_0_, s32[1]{0:T(128)} %bitcast.13.refs_1_, ...), custom_call_target="tpu_custom_call" | custom-call | flops 1 | bytes 1 | tf_op jit(solution)/shard_map/attn_fwd/pallas_call | solution.py:150
  76.2 7.6 %collective-permute-done.13.refs_5_ = bf16[256,1024]{1,0:T(8,128)(2,1)S(1)} collective-permute-done((bf16[256,1024]{1,0:T(8,128)(2,1)}, bf16[256,1024]{1,0:T(8,128)(2,1)S(1)}, u32[]{:S(2)}, u32[]{:S(2)}) %collective-permute-start.13) | collective-permute-done | bytes 524320 | tf_op jit(solution)/shard_map/ppermute | solution.py:853
  95.1 30.7 %ffn0.1 = (bf16[6,704,512]{2,1,0:T(8,128)(2,1)}, bf16[2,704,512]{2,1,0:T(8,128)(2,1)}, bf16[2,704,512]{2,1,0:T(8,128)(2,1)}, bf16[2,704,512]{2,1,0:T(8,128)(2,1)...) custom-call(s32[2]{0:T(128)} %pad_add_fusion.refs_0_, ...), custom_call_target="tpu_custom_call" | custom-call | flops 1 | bytes 1 | tf_op jit(solution)/shard_map/ffn0/pallas_call | solution.py:356
  139.1 30.3 %ffn2.1 = (bf16[6,704,512]{2,1,0:T(8,128)(2,1)}, bf16[2,704,512]{2,1,0:T(8,128)(2,1)}, bf16[2,704,512]{2,1,0:T(8,128)(2,1)}, bf16[2,704,512]{2,1,0:T(8,128)(2,1)...) custom-call(s32[2]{0:T(128)} %pad_add_fusion.refs_0_, ...), custom_call_target="tpu_custom_call", output_to_operand_aliasing={{4}: (19, {}), {5}: (20, {})} | custom-call | flops 1 | bytes 1 | tf_op jit(solution)/shard_map/ffn2/pallas_call | solution.py:356
  182.6 6.6 %combine.2 = (bf16[4,256,1152]{2,1,0:T(8,128)(2,1)}, f32[8,128]{1,0:T(8,128)}) custom-call(s32[1]{0:T(128)} %bitcast.21.me_ref, s32[4,256,128]{2,1,0:T(8,128)} %pad.17.pos_ref, bf16[4,576,1152]{2,1,0:T(8,128)(2,1)} %get-tuple-element.186.src_ref, f32[8,128]{1,0:T(8,128)} %get-tuple-element.187.refs_0_), custom_call_target="tpu_custom_call" | custom-call | flops 1 | bytes 1 | tf_op jit(solution)/shard_map/combine/pallas_call | solution.py:402
  189.2 4.6 all-to-all-start.1
  203.9 11.2 %collective-permute-done.26.refs_1_ = bf16[704,512]{1,0:T(8,128)(2,1)} collective-permute-done((bf16[704,512]{1,0:T(8,128)(2,1)}, bf16[704,512]{1,0:T(8,128)(2,1)}, u32[]{:S(2)}, u32[]{:S(2)}) %collective-permute-start.26) | collective-permute-done | bytes 720928 | tf_op jit(solution)/shard_map/ppermute | solution.py:716
  228.6 6.0 %back_mid.1 = (f32[256,1024]{1,0:T(8,128)}, bf16[256,1024]{1,0:T(8,128)(2,1)}, bf16[256,1024]{1,0:T(8,128)(2,1)}, f32[1024,128]{1,0:T(8,128)}, f32[8,128]{1,0:T(8,128)}) custom-call(f32[256,1024]{1,0:T(8,128)} %get-tuple-element.160.refs_0_, bf16[256,1024]{1,0:T(8,128)(2,1)} %bitcast.57, f32[1,1024]{1,0:T(1,128)} %bitcast.68, ...), custom_call_target="tpu_custom_call" | custom-call | flops 1 | bytes 1 | tf_op jit(solution)/shard_map/back_mid/pallas_call | solution.py:485
  234.6 13.8 %attn_bwd.1 = (bf16[3,256,1024]{2,1,0:T(8,128)(2,1)}, f32[4,4,256]{2,1,0:T(4,128)}, f32[8,128]{1,0:T(8,128)}) custom-call(bf16[256,3072]{1,0:T(8,128)(2,1)} %get-tuple-element.200.q_ref.k_ref.v_ref, bf16[256,3072]{1,0:T(8,128)(2,1)} %get-tuple-element.200.q_ref.k_ref.v_ref, bf16[256,3072]{1,0:T(8,128)(2,1)} %get-tuple-element.200.q_ref.k_ref.v_ref, ...), custom_call_target="tpu_custom_call" | custom-call | flops 1 | bytes 1 | tf_op jit(solution)/shard_map/attn_bwd/pallas_call | solution.py:201
  249.3 4.7 wave.24
  257.8 5.8 %wave.25 = (bf16[704,512]{1,0:T(8,128)(2,1)}, bf16[704,512]{1,0:T(8,128)(2,1)}, bf16[704,512]{1,0:T(8,128)(2,1)}, bf16[704,512]{1,0:T(8,128)(2,1)}, f32[4,704,1024]{2,1,0:T(8,128)}, /*index=5*/f32[8,128]{1,0:T(8,128)}) custom-call(s32[2]{0:T(128)} %pad_add_fusion.1.refs_0_.place_ref, bf16[704,512]{1,0:T(8,128)(2,1)} %collective-permute-done.34.refs_1_, ...), custom_call_target="tpu_custom_call" | custom-call | flops 1 | bytes 1 | tf_op jit(solution)/shard_map/wave/pallas_call | solution.py:791
  272.2 8.3 %back_in.1 = (bf16[256,1024]{1,0:T(8,128)(2,1)}, bf16[1024,128]{1,0:T(8,128)(2,1)}, f32[8,128]{1,0:T(8,128)}) custom-call(bf16[256,1024]{1,0:T(8,128)(2,1)} %bitcast.62, f32[1,1024]{1,0:T(1,128)} %bitcast.66, bf16[3,256,1024]{2,1,0:T(8,128)(2,1)} %get-tuple-element.217.d_ref.refs_2_.refs_3_.refs_4_, f32[16,256]{1,0:T(8,128)} %reshape.175.diag_ref, ...), custom_call_target="tpu_custom_call" | custom-call | flops 1 | bytes 1 | tf_op jit(solution)/shard_map/back_in/pallas_call | solution.py:541
  282.0 5.8 %wave.26 = (bf16[704,512]{1,0:T(8,128)(2,1)}, bf16[704,512]{1,0:T(8,128)(2,1)}, bf16[704,512]{1,0:T(8,128)(2,1)}, bf16[704,512]{1,0:T(8,128)(2,1)}, f32[4,704,1024]{2,1,0:T(8,128)}, /*index=5*/f32[8,128]{1,0:T(8,128)}) custom-call(s32[2]{0:T(128)} %pad_add_fusion.1.refs_0_.place_ref, bf16[704,512]{1,0:T(8,128)(2,1)} %collective-permute-done.41.refs_1_, ...), custom_call_target="tpu_custom_call" | custom-call | flops 1 | bytes 1 | tf_op jit(solution)/shard_map/wave/pallas_call | solution.py:791
  296.2 6.0 %dense.3 = (bf16[4,896,512]{2,1,0:T(8,128)(2,1)}, f32[8,128]{1,0:T(8,128)}) custom-call(s32[1]{0:T(128)} %bitcast.27.core_ref, bf16[256,1024]{1,0:T(8,128)(2,1)} %get-tuple-element.169.refs_0_, bf16[256,1024]{1,0:T(8,128)(2,1)} %copy-done.14, bf16[3,256,1024]{2,1,0:T(8,128)(2,1)} %get-tuple-element.217.d_ref.refs_2_.refs_3_.refs_4_, ...), custom_call_target="tpu_custom_call" | custom-call | flops 1 | bytes 1 | tf_op jit(solution)/shard_map/dense/pallas_call | solution.py:596
  302.2 5.8 %wave.27 = (bf16[704,512]{1,0:T(8,128)(2,1)}, bf16[704,512]{1,0:T(8,128)(2,1)}, bf16[704,512]{1,0:T(8,128)(2,1)}, bf16[704,512]{1,0:T(8,128)(2,1)}, f32[4,704,1024]{2,1,0:T(8,128)}, /*index=5*/f32[8,128]{1,0:T(8,128)}) custom-call(s32[2]{0:T(128)} %pad_add_fusion.1.refs_0_.place_ref, bf16[704,512]{1,0:T(8,128)(2,1)} %collective-permute-done.39.refs_1_, ...), custom_call_target="tpu_custom_call" | custom-call | flops 1 | bytes 1 | tf_op jit(solution)/shard_map/wave/pallas_call | solution.py:791
  308.1 4.9 all-to-all-start.3
  317.9 5.7 %wave.28 = (bf16[704,512]{1,0:T(8,128)(2,1)}, bf16[704,512]{1,0:T(8,128)(2,1)}, bf16[704,512]{1,0:T(8,128)(2,1)}, bf16[704,512]{1,0:T(8,128)(2,1)}, f32[4,704,1024]{2,1,0:T(8,128)}, /*index=5*/f32[8,128]{1,0:T(8,128)}) custom-call(s32[2]{0:T(128)} %pad_add_fusion.1.refs_0_.place_ref, ...), custom_call_target="tpu_custom_call", output_to_operand_aliasing={{4}: (10, {})} | custom-call | flops 1 | bytes 1 | tf_op jit(solution)/shard_map/wave/pallas_call | solution.py:791
  326.3 6.2 %collective-permute-done.48.refs_1_ = bf16[704,512]{1,0:T(8,128)(2,1)S(1)} collective-permute-done((bf16[704,512]{1,0:T(8,128)(2,1)S(1)}, bf16[704,512]{1,0:T(8,128)(2,1)S(1)}, u32[]{:S(2)}, u32[]{:S(2)}) %collective-permute-start.48) | collective-permute-done | bytes 720928 | tf_op jit(solution)/shard_map/ppermute | solution.py:716
  333.3 5.7 %wave.29 = (bf16[704,512]{1,0:T(8,128)(2,1)}, bf16[704,512]{1,0:T(8,128)(2,1)}, bf16[704,512]{1,0:T(8,128)(2,1)}, bf16[704,512]{1,0:T(8,128)(2,1)}, f32[4,704,1024]{2,1,0:T(8,128)}, /*index=5*/f32[8,128]{1,0:T(8,128)}) custom-call(s32[2]{0:T(128)} %pad_add_fusion.1.refs_0_.place_ref, bf16[704,512]{1,0:T(8,128)(2,1)} %copy-done.44, ...), custom_call_target="tpu_custom_call", output_to_operand_aliasing={{4}: (10, {})} | custom-call | flops 1 | bytes 1 | tf_op jit(solution)/shard_map/wave/pallas_call | solution.py:791
  343.0 6.5 %combine.3 = (bf16[4,256,1024]{2,1,0:T(8,128)(2,1)}, f32[8,128]{1,0:T(8,128)}) custom-call(s32[1]{0:T(128)} %bitcast.21.me_ref, s32[4,256,128]{2,1,0:T(8,128)} %pad.17.pos_ref, bf16[4,576,1024]{2,1,0:T(8,128)(2,1)} %get-tuple-element.173.src_ref, f32[8,128]{1,0:T(8,128)} %get-tuple-element.241.refs_0_), custom_call_target="tpu_custom_call" | custom-call | flops 1 | bytes 1 | tf_op jit(solution)/shard_map/combine/pallas_call | solution.py:402
  350.9 5.1 %wave.30 = (bf16[704,512]{1,0:T(8,128)(2,1)}, bf16[704,512]{1,0:T(8,128)(2,1)}, bf16[704,512]{1,0:T(8,128)(2,1)}, f32[4,704,1024]{2,1,0:T(8,128)}, f32[8,128]{1,0:T(8,128)}) custom-call(s32[2]{0:T(128)} %pad_add_fusion.1.refs_0_.place_ref, bf16[704,512]{1,0:T(8,128)(2,1)} %copy-done.23, ...), custom_call_target="tpu_custom_call", output_to_operand_aliasing={{3}: (8, {})} | custom-call | flops 1 | bytes 1 | tf_op jit(solution)/shard_map/wave/pallas_call | solution.py:791
  364.7 5.1 %wave.31 = (bf16[704,512]{1,0:T(8,128)(2,1)}, bf16[704,512]{1,0:T(8,128)(2,1)}, bf16[704,512]{1,0:T(8,128)(2,1)}, f32[4,704,1024]{2,1,0:T(8,128)}, f32[8,128]{1,0:T(8,128)}) custom-call(s32[2]{0:T(128)} %pad_add_fusion.1.refs_0_.place_ref, bf16[704,512]{1,0:T(8,128)(2,1)} %copy-done.25, ...), custom_call_target="tpu_custom_call", output_to_operand_aliasing={{3}: (8, {})} | custom-call | flops 1 | bytes 1 | tf_op jit(solution)/shard_map/wave/pallas_call | solution.py:791
  381.1 5.1 %wave.32 = (bf16[704,512]{1,0:T(8,128)(2,1)}, bf16[704,512]{1,0:T(8,128)(2,1)}, bf16[704,512]{1,0:T(8,128)(2,1)}, f32[4,704,1024]{2,1,0:T(8,128)}, f32[8,128]{1,0:T(8,128)}) custom-call(s32[2]{0:T(128)} %pad_add_fusion.1.refs_0_.place_ref, bf16[704,512]{1,0:T(8,128)(2,1)} %copy-done.22, ...), custom_call_target="tpu_custom_call", output_to_operand_aliasing={{3}: (8, {})} | custom-call | flops 1 | bytes 1 | tf_op jit(solution)/shard_map/wave/pallas_call | solution.py:791
  389.5 7.0 %collective-permute-done.64.refs_1_ = bf16[704,512]{1,0:T(8,128)(2,1)S(1)} collective-permute-done((bf16[704,512]{1,0:T(8,128)(2,1)S(1)}, bf16[704,512]{1,0:T(8,128)(2,1)S(1)}, u32[]{:S(2)}, u32[]{:S(2)}) %collective-permute-start.64) | collective-permute-done | bytes 720928 | tf_op jit(solution)/shard_map/ppermute | solution.py:716
  397.6 5.1 %wave.33 = (bf16[704,512]{1,0:T(8,128)(2,1)}, bf16[704,512]{1,0:T(8,128)(2,1)}, bf16[704,512]{1,0:T(8,128)(2,1)}, f32[4,704,1024]{2,1,0:T(8,128)}, f32[8,128]{1,0:T(8,128)}) custom-call(s32[2]{0:T(128)} %pad_add_fusion.1.refs_0_.place_ref, bf16[704,512]{1,0:T(8,128)(2,1)} %copy-done.28, ...), custom_call_target="tpu_custom_call", output_to_operand_aliasing={{3}: (8, {})} | custom-call | flops 1 | bytes 1 | tf_op jit(solution)/shard_map/wave/pallas_call | solution.py:791
  412.6 4.6 wave.34
  418.8 8.5 %collective-permute-done.69.refs_1_ = bf16[704,512]{1,0:T(8,128)(2,1)} collective-permute-done((bf16[704,512]{1,0:T(8,128)(2,1)S(1)}, bf16[704,512]{1,0:T(8,128)(2,1)}, u32[]{:S(2)}, u32[]{:S(2)}) %collective-permute-start.69) | collective-permute-done | bytes 720928 | tf_op jit(solution)/shard_map/ppermute | solution.py:716
  428.2 4.6 wave.35
  447.6 11.2 %collective-permute-start.74 = (bf16[704,512]{1,0:T(8,128)(2,1)}, bf16[704,512]{1,0:T(8,128)(2,1)S(1)}, u32[]{:S(2)}, u32[]{:S(2)}) collective-permute-start(bf16[704,512]{1,0:T(8,128)(2,1)} %get-tuple-element.287.refs_2_), channel_id=1, source_target_pairs={{0,8},{4,12},{8,0},{12,4},{16,24},{20,28},{24,16},{28,20},{1,9},{5... | collective-permute-start | bytes 2162696 | tf_op jit(solution)/shard_map/ppermute | solution.py:716
  465.5 10.3 %collective-permute-done.74.refs_1_ = bf16[704,512]{1,0:T(8,128)(2,1)S(1)} collective-permute-done((bf16[704,512]{1,0:T(8,128)(2,1)}, bf16[704,512]{1,0:T(8,128)(2,1)S(1)}, u32[]{:S(2)}, u32[]{:S(2)}) %collective-permute-start.74) | collective-permute-done | bytes 720928 | tf_op jit(solution)/shard_map/ppermute | solution.py:716
  (352 shorter events, 212.8 us)
Async XLA Ops:
  8.9 24.0 %collective-permute-start = (bf16[64,4096]{1,0:T(8,128)(2,1)S(1)}, bf16[64,4096]{1,0:T(8,128)(2,1)}, u32[]{:S(2)}, u32[]{:S(2)}) collective-permute-start(bf16[64,4096]{1,0:T(8,128)(2,1)S(1)} %maximum_select_fusion), channel_id=1, source_target_pairs={{0,1},{1,0},{2,3},{3,2},{4,5},{5,4},{6,7},{7,6},{8,9},{9,8},{10,11... | collective-permute-start | bytes 1572872 | tf_op jit(solution)/shard_map/ppermute | solution.py:853
  10.0 23.2 %all-to-all-start = ((bf16[4,256,10]{1,2,0:T(8,128)(2,1)}), bf16[4,256,10]{1,2,0:T(8,128)(2,1)S(1)}, u32[]{:S(2)}, u32[]{:S(2)}) async-start(bf16[4,256,10]{1,2,0:T(8,128)(2,1)} %broadcast_in_dim.68), calls=%async_computation | async-start | bytes 65536 | tf_op jit(solution)/shard_map/all_to_all | solution.py:896
  19.5 23.6 %collective-permute-start.9 = (bf16[64,4096]{1,0:T(8,128)(2,1)S(1)}, bf16[64,4096]{1,0:T(8,128)(2,1)}, u32[]{:S(2)}, u32[]{:S(2)}) collective-permute-start(bf16[64,4096]{1,0:T(8,128)(2,1)S(1)} %collective-permute-done.5.refs_15_), channel_id=1, source_target_pairs={{0,1},{1,0},{2,3},{3,2},{4,5},{5,4},{6,7},{7,6},{8,9},{9,8},{10,11... | collective-permute-start | bytes 1572872 | tf_op jit(solution)/shard_map/ppermute | solution.py:853
  21.5 25.6 %collective-permute-start.7 = (bf16[64,4096]{1,0:T(8,128)(2,1)S(1)}, bf16[64,4096]{1,0:T(8,128)(2,1)}, u32[]{:S(2)}, u32[]{:S(2)}) collective-permute-start(bf16[64,4096]{1,0:T(8,128)(2,1)S(1)} %collective-permute-done.5.refs_15_), channel_id=1, source_target_pairs={{0,4},{4,0},{8,12},{12,8},{16,20},{20,16},{24,28},{28,24},{1,5},{5... | collective-permute-start | bytes 1572872 | tf_op jit(solution)/shard_map/ppermute | solution.py:849
  21.6 27.1 %collective-permute-start.3 = (bf16[64,4096]{1,0:T(8,128)(2,1)S(1)}, bf16[64,4096]{1,0:T(8,128)(2,1)}, u32[]{:S(2)}, u32[]{:S(2)}) collective-permute-start(bf16[64,4096]{1,0:T(8,128)(2,1)S(1)} %collective-permute-done.1.refs_11_), channel_id=1, source_target_pairs={{0,4},{4,0},{8,12},{12,8},{16,20},{20,16},{24,28},{28,24},{1,5},{5... | collective-permute-start | bytes 1572872 | tf_op jit(solution)/shard_map/ppermute | solution.py:849
  45.4 24.2 %collective-permute-start.17 = (bf16[256,1024]{1,0:T(8,128)(2,1)S(1)}, bf16[256,1024]{1,0:T(8,128)(2,1)S(1)}, u32[]{:S(2)}, u32[]{:S(2)}) collective-permute-start(bf16[256,1024]{1,0:T(8,128)(2,1)S(1)} %bitcast.58), channel_id=1, source_target_pairs={{0,2},{1,3},{2,0},{3,1},{4,6},{5,7},{6,4},{7,5},{8,10},{9,11},{10,... | collective-permute-start | bytes 1572872 | tf_op jit(solution)/shard_map/ppermute | solution.py:853
  47.2 24.9 %collective-permute-start.16 = (bf16[256,1024]{1,0:T(8,128)(2,1)S(1)}, bf16[256,1024]{1,0:T(8,128)(2,1)S(1)}, u32[]{:S(2)}, u32[]{:S(2)}) collective-permute-start(bf16[256,1024]{1,0:T(8,128)(2,1)S(1)} %bitcast.59), channel_id=1, source_target_pairs={{0,1},{1,0},{2,3},{3,2},{4,5},{5,4},{6,7},{7,6},{8,9},{9,8},{10,11... | collective-permute-start | bytes 1572872 | tf_op jit(solution)/shard_map/ppermute | solution.py:853
  126.0 43.4 %collective-permute-start.24 = (bf16[2,704,512]{2,1,0:T(8,128)(2,1)}, bf16[2,704,512]{2,1,0:T(8,128)(2,1)S(1)}, u32[]{:S(2)}, u32[]{:S(2)}) collective-permute-start(bf16[2,704,512]{2,1,0:T(8,128)(2,1)} %get-tuple-element.175), channel_id=1, source_target_pairs={{0,4},{4,0},{8,12},{12,8},{16,20},{20,16},{24,28},{28,24},{1,5},{5... | collective-permute-start | bytes 4325384 | tf_op jit(solution)/shard_map/ppermute | solution.py:849
  126.6 67.9 %collective-permute-start.28 = (bf16[2,704,512]{2,1,0:T(8,128)(2,1)}, bf16[2,704,512]{2,1,0:T(8,128)(2,1)}, u32[]{:S(2)}, u32[]{:S(2)}) collective-permute-start(bf16[2,704,512]{2,1,0:T(8,128)(2,1)} %get-tuple-element.182), channel_id=1, source_target_pairs={{0,4},{4,0},{8,12},{12,8},{16,20},{20,16},{24,28},{28,24},{1,5},{5... | collective-permute-start | bytes 4325384 | tf_op jit(solution)/shard_map/ppermute | solution.py:849
  134.5 34.9 %collective-permute-start.25 = (bf16[704,512]{1,0:T(8,128)(2,1)}, bf16[704,512]{1,0:T(8,128)(2,1)}, u32[]{:S(2)}, u32[]{:S(2)}) collective-permute-start(bf16[704,512]{1,0:T(8,128)(2,1)} %get-tuple-element.176.refs_2_), channel_id=1, source_target_pairs={{0,8},{4,12},{8,0},{12,4},{16,24},{20,28},{24,16},{28,20},{1,9},{5... | collective-permute-start | bytes 2162696 | tf_op jit(solution)/shard_map/ppermute | solution.py:716
  136.2 41.5 %collective-permute-start.23 = (bf16[704,512]{1,0:T(8,128)(2,1)}, bf16[704,512]{1,0:T(8,128)(2,1)S(1)}, u32[]{:S(2)}, u32[]{:S(2)}) collective-permute-start(bf16[704,512]{1,0:T(8,128)(2,1)} %get-tuple-element.174.refs_2_), channel_id=1, source_target_pairs={{0,8},{4,12},{8,0},{12,4},{16,24},{20,28},{24,16},{28,20},{1,9},{5... | collective-permute-start | bytes 2162696 | tf_op jit(solution)/shard_map/ppermute | solution.py:716
  189.2 39.4 %all-to-all-start.1 = ((bf16[4,256,1152]{2,1,0:T(8,128)(2,1)}), bf16[4,256,1152]{2,1,0:T(8,128)(2,1)}, u32[]{:S(2)}, u32[]{:S(2)}) async-start(bf16[4,256,1152]{2,1,0:T(8,128)(2,1)} %get-tuple-element.203), calls=%async_computation.1 | async-start | bytes 4718592 | tf_op jit(solution)/shard_map/all_to_all | solution.py:896
  193.8 23.7 %collective-permute-start.31 = (bf16[2,704,512]{2,1,0:T(8,128)(2,1)}, bf16[2,704,512]{2,1,0:T(8,128)(2,1)S(1)}, u32[]{:S(2)}, u32[]{:S(2)}) collective-permute-start(bf16[2,704,512]{2,1,0:T(8,128)(2,1)} %get-tuple-element.190), channel_id=1, source_target_pairs={{0,4},{4,0},{8,12},{12,8},{16,20},{20,16},{24,28},{28,24},{1,5},{5... | collective-permute-start | bytes 4325384 | tf_op jit(solution)/shard_map/ppermute | solution.py:849
  193.9 23.6 %collective-permute-start.32 = (bf16[2,704,512]{2,1,0:T(8,128)(2,1)}, bf16[2,704,512]{2,1,0:T(8,128)(2,1)S(1)}, u32[]{:S(2)}, u32[]{:S(2)}) collective-permute-start(bf16[2,704,512]{2,1,0:T(8,128)(2,1)} %get-tuple-element.191), channel_id=1, source_target_pairs={{0,4},{4,0},{8,12},{12,8},{16,20},{20,16},{24,28},{28,24},{1,5},{5... | collective-permute-start | bytes 4325384 | tf_op jit(solution)/shard_map/ppermute | solution.py:849
  194.4 23.2 %collective-permute-start.33 = (bf16[2,704,512]{2,1,0:T(8,128)(2,1)}, bf16[2,704,512]{2,1,0:T(8,128)(2,1)}, u32[]{:S(2)}, u32[]{:S(2)}) collective-permute-start(bf16[2,704,512]{2,1,0:T(8,128)(2,1)} %get-tuple-element.192), channel_id=1, source_target_pairs={{0,4},{4,0},{8,12},{12,8},{16,20},{20,16},{24,28},{28,24},{1,5},{5... | collective-permute-start | bytes 4325384 | tf_op jit(solution)/shard_map/ppermute | solution.py:849
  215.1 33.4 %collective-permute-start.36 = (bf16[704,512]{1,0:T(8,128)(2,1)}, bf16[704,512]{1,0:T(8,128)(2,1)}, u32[]{:S(2)}, u32[]{:S(2)}) collective-permute-start(bf16[704,512]{1,0:T(8,128)(2,1)} %get-tuple-element.197.refs_5_), channel_id=1, source_target_pairs={{0,8},{4,12},{8,0},{12,4},{16,24},{20,28},{24,16},{28,20},{1,9},{5... | collective-permute-start | bytes 2162696 | tf_op jit(solution)/shard_map/ppermute | solution.py:716
  216.8 31.6 %collective-permute-start.37 = (bf16[704,512]{1,0:T(8,128)(2,1)}, bf16[704,512]{1,0:T(8,128)(2,1)S(1)}, u32[]{:S(2)}, u32[]{:S(2)}) collective-permute-start(bf16[704,512]{1,0:T(8,128)(2,1)} %get-tuple-element.198.refs_2_), channel_id=1, source_target_pairs={{8,16},{12,20},{16,8},{20,12},{9,17},{13,21},{17,9},{21,13},{10,18... | collective-permute-start | bytes 2162696 | tf_op jit(solution)/shard_map/ppermute | solution.py:719
  223.5 32.9 %collective-permute-start.34 = (bf16[704,512]{1,0:T(8,128)(2,1)}, bf16[704,512]{1,0:T(8,128)(2,1)}, u32[]{:S(2)}, u32[]{:S(2)}) collective-permute-start(bf16[704,512]{1,0:T(8,128)(2,1)} %get-tuple-element.193.refs_5_), channel_id=1, source_target_pairs={{0,8},{4,12},{8,0},{12,4},{16,24},{20,28},{24,16},{28,20},{1,9},{5... | collective-permute-start | bytes 2162696 | tf_op jit(solution)/shard_map/ppermute | solution.py:716
  227.1 30.7 %collective-permute-start.35 = (bf16[704,512]{1,0:T(8,128)(2,1)}, bf16[704,512]{1,0:T(8,128)(2,1)}, u32[]{:S(2)}, u32[]{:S(2)}) collective-permute-start(bf16[704,512]{1,0:T(8,128)(2,1)} %get-tuple-element.194.refs_2_), channel_id=1, source_target_pairs={{8,16},{12,20},{16,8},{20,12},{9,17},{13,21},{17,9},{21,13},{10,18... | collective-permute-start | bytes 2162696 | tf_op jit(solution)/shard_map/ppermute | solution.py:719
  254.1 40.9 %collective-permute-start.46 = (bf16[3,256,1024]{2,1,0:T(8,128)(2,1)S(1)}, bf16[3,256,1024]{2,1,0:T(8,128)(2,1)S(1)}, u32[]{:S(2)}, u32[]{:S(2)}) collective-permute-start(bf16[3,256,1024]{2,1,0:T(8,128)(2,1)S(1)} %copy-done.2), channel_id=1, source_target_pairs={{0,4},{4,0},{8,12},{12,8},{16,20},{20,16},{24,28},{28,24},{1,5},{5... | collective-permute-start | bytes 4718600 | tf_op jit(solution)/shard_map/ppermute | solution.py:849
  254.6 25.9 %collective-permute-start.41 = (bf16[704,512]{1,0:T(8,128)(2,1)}, bf16[704,512]{1,0:T(8,128)(2,1)}, u32[]{:S(2)}, u32[]{:S(2)}) collective-permute-start(bf16[704,512]{1,0:T(8,128)(2,1)} %get-tuple-element.213.refs_5_), channel_id=1, source_target_pairs={{0,8},{4,12},{8,0},{12,4},{16,24},{20,28},{24,16},{28,20},{1,9},{5... | collective-permute-start | bytes 2162696 | tf_op jit(solution)/shard_map/ppermute | solution.py:716
  256.3 25.7 %collective-permute-start.42 = (bf16[704,512]{1,0:T(8,128)(2,1)}, bf16[704,512]{1,0:T(8,128)(2,1)}, u32[]{:S(2)}, u32[]{:S(2)}) collective-permute-start(bf16[704,512]{1,0:T(8,128)(2,1)} %get-tuple-element.214.refs_2_), channel_id=1, source_target_pairs={{8,16},{12,20},{16,8},{20,12},{9,17},{13,21},{17,9},{21,13},{10,18... | collective-permute-start | bytes 2162696 | tf_op jit(solution)/shard_map/ppermute | solution.py:719
  267.0 35.3 %collective-permute-start.39 = (bf16[704,512]{1,0:T(8,128)(2,1)}, bf16[704,512]{1,0:T(8,128)(2,1)}, u32[]{:S(2)}, u32[]{:S(2)}) collective-permute-start(bf16[704,512]{1,0:T(8,128)(2,1)} %get-tuple-element.210.refs_5_), channel_id=1, source_target_pairs={{0,8},{4,12},{8,0},{12,4},{16,24},{20,28},{24,16},{28,20},{1,9},{5... | collective-permute-start | bytes 2162696 | tf_op jit(solution)/shard_map/ppermute | solution.py:716
  293.9 23.1 %collective-permute-start.50 = (bf16[704,512]{1,0:T(8,128)(2,1)}, bf16[704,512]{1,0:T(8,128)(2,1)}, u32[]{:S(2)}, u32[]{:S(2)}) collective-permute-start(bf16[704,512]{1,0:T(8,128)(2,1)} %get-tuple-element.232.refs_5_), channel_id=1, source_target_pairs={{0,8},{4,12},{8,0},{12,4},{16,24},{20,28},{24,16},{28,20},{1,9},{5... | collective-permute-start | bytes 2162696 | tf_op jit(solution)/shard_map/ppermute | solution.py:716
  308.1 63.2 %all-to-all-start.3 = ((bf16[4,896,512]{2,1,0:T(8,128)(2,1)}), bf16[4,896,512]{2,1,0:T(8,128)(2,1)}, u32[]{:S(2)}, u32[]{:S(2)}) async-start(bf16[4,896,512]{2,1,0:T(8,128)(2,1)} %get-tuple-element.252), calls=%async_computation.3 | async-start | bytes 7340032 | tf_op jit(solution)/shard_map/all_to_all | solution.py:896
  323.9 25.7 %collective-permute-start.54 = (bf16[704,512]{1,0:T(8,128)(2,1)}, bf16[704,512]{1,0:T(8,128)(2,1)S(1)}, u32[]{:S(2)}, u32[]{:S(2)}) collective-permute-start(bf16[704,512]{1,0:T(8,128)(2,1)} %get-tuple-element.244.refs_5_), channel_id=1, source_target_pairs={{0,8},{4,12},{8,0},{12,4},{16,24},{20,28},{24,16},{28,20},{1,9},{5... | collective-permute-start | bytes 2162696 | tf_op jit(solution)/shard_map/ppermute | solution.py:716
  325.6 24.0 %collective-permute-start.55 = (bf16[704,512]{1,0:T(8,128)(2,1)}, bf16[704,512]{1,0:T(8,128)(2,1)S(1)}, u32[]{:S(2)}, u32[]{:S(2)}) collective-permute-start(bf16[704,512]{1,0:T(8,128)(2,1)} %get-tuple-element.245.refs_2_), channel_id=1, source_target_pairs={{8,16},{12,20},{16,8},{20,12},{9,17},{13,21},{17,9},{21,13},{10,18... | collective-permute-start | bytes 2162696 | tf_op jit(solution)/shard_map/ppermute | solution.py:719
  339.1 24.2 %collective-permute-start.59 = (bf16[704,512]{1,0:T(8,128)(2,1)}, bf16[704,512]{1,0:T(8,128)(2,1)S(1)}, u32[]{:S(2)}, u32[]{:S(2)}) collective-permute-start(bf16[704,512]{1,0:T(8,128)(2,1)} %get-tuple-element.254.refs_5_), channel_id=1, source_target_pairs={{0,8},{4,12},{8,0},{12,4},{16,24},{20,28},{24,16},{28,20},{1,9},{5... | collective-permute-start | bytes 2162696 | tf_op jit(solution)/shard_map/ppermute | solution.py:716
  356.2 24.0 %collective-permute-start.57 = (bf16[704,512]{1,0:T(8,128)(2,1)}, bf16[704,512]{1,0:T(8,128)(2,1)S(1)}, u32[]{:S(2)}, u32[]{:S(2)}) collective-permute-start(bf16[704,512]{1,0:T(8,128)(2,1)} %get-tuple-element.250.refs_4_), channel_id=1, source_target_pairs={{0,8},{4,12},{8,0},{12,4},{16,24},{20,28},{24,16},{28,20},{1,9},{5... | collective-permute-start | bytes 2162696 | tf_op jit(solution)/shard_map/ppermute | solution.py:716
  386.5 25.3 %collective-permute-start.63 = (bf16[704,512]{1,0:T(8,128)(2,1)}, bf16[704,512]{1,0:T(8,128)(2,1)S(1)}, u32[]{:S(2)}, u32[]{:S(2)}) collective-permute-start(bf16[704,512]{1,0:T(8,128)(2,1)} %get-tuple-element.263.refs_3_), channel_id=1, source_target_pairs={{0,8},{4,12},{8,0},{12,4},{16,24},{20,28},{24,16},{28,20},{1,9},{5... | collective-permute-start | bytes 2162696 | tf_op jit(solution)/shard_map/ppermute | solution.py:716
  402.8 31.8 %all-to-all-start.2 = ((bf16[4,256,1024]{2,1,0:T(8,128)(2,1)}), bf16[4,256,1024]{2,1,0:T(8,128)(2,1)S(1)}, u32[]{:S(2)}, u32[]{:S(2)}) async-start(bf16[4,256,1024]{2,1,0:T(8,128)(2,1)} %get-tuple-element.242), calls=%async_computation.2 | async-start | bytes 4194304 | tf_op jit(solution)/shard_map/all_to_all | solution.py:896
  447.6 28.2 %collective-permute-start.74 = (bf16[704,512]{1,0:T(8,128)(2,1)}, bf16[704,512]{1,0:T(8,128)(2,1)S(1)}, u32[]{:S(2)}, u32[]{:S(2)}) collective-permute-start(bf16[704,512]{1,0:T(8,128)(2,1)} %get-tuple-element.287.refs_2_), channel_id=1, source_target_pairs={{0,8},{4,12},{8,0},{12,4},{16,24},{20,28},{24,16},{28,20},{1,9},{5... | collective-permute-start | bytes 2162696 | tf_op jit(solution)/shard_map/ppermute | solution.py:716
  (110 other events, 1079.9 us)
